TPU v7x, 1024 devices: a whole 4x8x16 slice. The times are simulated.
1024 devices in a mesh: ctx: 64 (over y, z_hi, core), tp: 16 (over x, z_lo).
Axes of the slice: x: 4, y: 8, z: 16 (z_hi: 4, z_lo: 4; z = z_hi * 4 + z_lo), core: 2. Of those that a mesh axis runs over, the one named last changes fastest.
Arguments:
- tokens: bfloat16 [8192, 4096], P('ctx', 'tp'), may hold values from -6 to 6
- cotangent: bfloat16 [8192, 4096], P('ctx', 'tp'), may hold values from -6 to 6
- input_weight: bfloat16 [4096, 3, 4096], P(None, None, 'tp'), may hold values from -0.09375 to 0.09375
- output_weight: bfloat16 [4096, 4096], P('tp'), may hold values from -0.09375 to 0.09375
- short_taps: float32 [3, 4096, 3], P(None, 'tp'), may hold values from -3 to 3
- residues: float32 [4096, 16], P('tp'), may hold values from -0.34 to 0.34
- decay_rates: float32 [4096, 16], P('tp'), may hold values from 6.1035156e-05 to 0.05
- skip_gain: float32 [4096], P('tp'), may hold values from 0.1 to 1.9
Outputs:
- mixed: bfloat16 [8192, 4096], P('ctx', 'tp')
- grad_tokens: bfloat16 [8192, 4096], P('ctx', 'tp')
All inputs are finite; a program needn't handle non-finite values.
Results may differ from a plain program's by a relative error of at most 0.022.
Values may be sent and summed in bfloat16 or wider, within the bound.
No kernel may reach another device: no remote copies, remote signals or barrier semaphores. Data moves between devices by JAX's collectives and lax.ppermute only.
A program may use at most 64 MiB of HBM per device.

v0:
```python
import math

import jax
import jax.numpy as jnp
from jax import lax
from jax.sharding import PartitionSpec as P

HIGHEST = lax.Precision.HIGHEST


def short_forward(pieces, short_taps, before):
    tap_count = short_taps.shape[2]
    length = pieces.shape[2]
    padded = jnp.concatenate([before, pieces], axis=2)
    total_sum = jnp.zeros(pieces.shape, jnp.float32)
    for tap_index in range(tap_count):
        start_at = tap_count - 1 - tap_index
        total_sum = (
            total_sum
            + short_taps[:, :, tap_index : tap_index + 1]
            * padded[:, :, start_at : start_at + length]
        )
    return total_sum


def short_adjoint(grads, short_taps, after):
    tap_count = short_taps.shape[2]
    length = grads.shape[2]
    padded = jnp.concatenate([grads, after], axis=2)
    total_sum = jnp.zeros(grads.shape, jnp.float32)
    for tap_index in range(tap_count):
        total_sum = (
            total_sum
            + short_taps[:, :, tap_index : tap_index + 1]
            * padded[:, :, tap_index : tap_index + length]
        )
    return total_sum


def causal_local(signal, residues, decay_rates):
    channels, length = signal.shape
    block_len = math.gcd(length, 64)
    block_count = length // block_len
    offsets = jnp.arange(block_len).astype(jnp.float32)
    rate_col = decay_rates[:, :, None]
    kernel = jnp.einsum("cr,crm->cm", residues, jnp.exp(-rate_col * offsets), precision=HIGHEST)
    row_index = jnp.arange(block_len)[:, None]
    col_index = jnp.arange(block_len)[None, :]
    lag_index = jnp.maximum(row_index - col_index, 0)
    toeplitz = jnp.where((row_index >= col_index)[None], kernel[:, lag_index], 0.0)
    blocks = signal.reshape(channels, block_count, block_len)
    inner_part = jnp.einsum("cbs,cts->cbt", blocks, toeplitz, precision=HIGHEST)
    tail_pows = jnp.exp(-rate_col * (block_len - 1.0 - offsets))
    end_states = jnp.einsum("cbs,crs->cbr", blocks, tail_pows, precision=HIGHEST)
    block_index = jnp.arange(block_count)
    gap_blocks = block_index[:, None] - 1 - block_index[None, :]
    valid_gap = gap_blocks >= 0
    gap_tokens = (block_len * jnp.maximum(gap_blocks, 0)).astype(jnp.float32)
    carry_weights = jnp.where(
        valid_gap[None, None], jnp.exp(-decay_rates[:, :, None, None] * gap_tokens[None, None]), 0.0
    )
    entering = jnp.einsum("crba,car->cbr", carry_weights, end_states, precision=HIGHEST)
    head_pows = residues[:, :, None] * jnp.exp(-rate_col * (offsets + 1.0))
    outer_part = jnp.einsum("cbr,crt->cbt", entering, head_pows, precision=HIGHEST)
    result = (inner_part + outer_part).reshape(channels, length)
    last_tokens = (block_len * (block_count - 1 - block_index)).astype(jnp.float32)
    last_weights = jnp.exp(-rate_col * last_tokens[None, None, :])
    final_state = jnp.einsum("cbr,crb->cr", end_states, last_weights, precision=HIGHEST)
    return (result, final_state)


def shards(
    tokens, cotangent, input_weight, output_weight, short_taps, residues, decay_rates, skip_gain
):
    whole_in, whole_grad = (
        lax.all_gather(tokens, "tp", axis=1, tiled=True),
        lax.all_gather(cotangent, "tp", axis=1, tiled=True),
    )
    projected = jnp.einsum(
        "td,dpc->pct", whole_in, input_weight, preferred_element_type=jnp.float32
    ).astype(jnp.bfloat16)
    back_grad = jnp.einsum(
        "td,cd->ct", whole_grad, output_weight, preferred_element_type=jnp.float32
    ).astype(jnp.bfloat16)
    reach_back = short_taps.shape[2] - 1
    spread = lax.all_to_all(
        jnp.concatenate([projected, back_grad[None]], axis=0),
        "ctx",
        split_axis=1,
        concat_axis=2,
        tiled=True,
    )
    chan_width = spread.shape[1]
    first_channel = lax.axis_index("ctx") * chan_width
    local_taps = lax.dynamic_slice_in_dim(short_taps, first_channel, chan_width, 1)
    local_res = lax.dynamic_slice_in_dim(residues, first_channel, chan_width, 0)
    local_decay = lax.dynamic_slice_in_dim(decay_rates, first_channel, chan_width, 0)
    local_skip = lax.dynamic_slice_in_dim(skip_gain, first_channel, chan_width, 0)[:, None]
    no_edge = jnp.zeros((3, chan_width, reach_back), jnp.float32)
    featured = short_forward(spread[:3].astype(jnp.float32), local_taps, no_edge)
    query, key_part, value_part = (featured[0], featured[1], featured[2])
    gated_in = key_part * value_part
    conv_raw, spare_state = causal_local(gated_in, local_res, local_decay)
    conv_out = conv_raw + local_skip * gated_in
    hidden = (query * conv_out).astype(jnp.bfloat16)
    back_float = spread[3].astype(jnp.float32)
    grad_conv = back_float * query
    grad_query = back_float * conv_out
    flipped, spare_back = causal_local(jnp.flip(grad_conv, 1), local_res, local_decay)
    grad_gated = jnp.flip(flipped, 1) + local_skip * grad_conv
    grad_feat = jnp.stack([grad_query, grad_gated * value_part, grad_gated * key_part])
    grad_proj = short_adjoint(grad_feat, local_taps, no_edge).astype(jnp.bfloat16)
    packed = jnp.concatenate([hidden[None], grad_proj], axis=0)
    returned = lax.all_to_all(packed, "ctx", split_axis=2, concat_axis=1, tiled=True)
    hidden_tok = returned[0]
    grad_tok = returned[1:]
    mixed_terms = jnp.einsum(
        "ct,cd->td", hidden_tok, output_weight, preferred_element_type=jnp.float32
    )
    grad_terms = jnp.einsum(
        "pct,epc->te", grad_tok, input_weight, preferred_element_type=jnp.float32
    )
    mixed, grad_tokens = (
        lax.psum_scatter(
            mixed_terms.astype(jnp.bfloat16), "tp", scatter_dimension=1, tiled=True
        ).astype(jnp.float32),
        lax.psum_scatter(
            grad_terms.astype(jnp.bfloat16), "tp", scatter_dimension=1, tiled=True
        ).astype(jnp.float32),
    )
    return (mixed.astype(jnp.bfloat16), grad_tokens.astype(jnp.bfloat16))


def solution(mesh):
    return jax.shard_map(
        shards,
        mesh=mesh,
        in_specs=(
            P("ctx", "tp"),
            P("ctx", "tp"),
            P(None, None, "tp"),
            P("tp", None),
            P(None, "tp", None),
            P("tp", None),
            P("tp", None),
            P("tp"),
        ),
        out_specs=(P("ctx", "tp"), P("ctx", "tp")),
        check_vma=False,
    )
```

profile of v0, /device:TPU:6, one launch (start us, length us, event | category | flops | bytes accessed | tf_op | source)
XLA Modules:
  0.0 534.9 jit_solution(5836328264297125456)
XLA Ops:
  7.2 0.7 all-gather.3.cloned.1.call-update
  8.0 0.7 all-gather.5.cloned.1.call-update
  8.7 0.8 constant_dynamic-slice_fusion.2
  9.7 0.9 constant_dynamic-slice_fusion.1
  10.7 86.5 %all-gather.3.cloned.1.call-done = bf16[128,4096]{1,0:T(8,128)(2,1)} async-done(((bf16[128,256]{1,0:T(8,128)(2,1)}), bf16[128,4096]{1,0:T(8,128)(2,1)}) %all-gather.3.cloned.1.call-update) | async-done | bytes 1048592 | tf_op jit(solution)/shard_map/all_gather | solution.py:76
  97.3 4.9 convolution_convert_fusion.1
  102.2 76.2 %all-gather.5.cloned.1.call-done = bf16[128,4096]{1,0:T(8,128)(2,1)} async-done(((bf16[128,256]{1,0:T(8,128)(2,1)}), bf16[128,4096]{1,0:T(8,128)(2,1)}) %all-gather.5.cloned.1.call-update) | async-done | bytes 1048592 | tf_op jit(solution)/shard_map/all_gather | solution.py:77
  178.4 1.9 fusion.11
  180.4 0.9 copy.46
  181.3 16.5 %all-to-all-start = ((bf16[4,256,128]{2,0,1:T(4,128)(2,1)}), bf16[4,256,128]{2,0,1:T(4,128)(2,1)S(1)}, u32[]{:S(2)}, u32[]{:S(2)}) async-start(bf16[4,256,128]{2,0,1:T(4,128)(2,1)} %copy.46), calls=%async_computation | async-start | bytes 524288 | tf_op jit(solution)/shard_map/all_to_all | solution.py:86
  197.8 0.5 broadcast_subtract_fusion
  198.4 0.6 dynamic_slice.15
  199.1 14.1 %gather_fusion = f32[4096,4]{1,0:T(8,128)} fusion(f32[4,64]{0,1:T(8,128)S(1)} %copy.66, s32[4096]{0:T(1024)S(1)} %broadcast_clamp_fusion), kind=kCustom, calls=%fused_computation | custom fusion | bytes 147456 | tf_op jit(solution)/shard_map/gather | solution.py:50
  213.2 2.3 copy.49
  215.5 0.6 broadcast_add_fusion
  216.1 0.7 fusion.21
  216.8 0.7 multiply_convert_fusion.1
  217.5 2.4 all-to-all-done
  220.1 0.1 reshape.145
  220.3 0.5 multiply_add_fusion
  220.9 5.6 %rev.7 = f32[4,8192]{1,0:T(4,128)S(1)} reverse(f32[4,8192]{1,0:T(4,128)S(1)} %bitcast_multiply_fusion), dimensions={1} | reverse | bytes 262144 | tf_op jit(solution)/shard_map/jit(_flip)/rev | solution.py:109
  226.6 0.2 reshape.143
  226.8 0.2 mul.97
  226.9 1.3 fusion.26
  228.3 1.3 fusion.27
  229.5 7.7 %fusion.1 = f32[4,16,1,128]{3,2,1,0:T(1,128)S(1)} fusion(f32[4,128,16,1]{1,3,2,0:T(1,128)S(1)} %bitcast.93, f32[128,128]{1,0:T(8,128)} %multiply_convert_fusion.1, f32[4,16]{1,0:T(4,128)} %copy-done.3, pred[128,128]{1,0:T(8,128)(4,1)} %fusion.21), kind=kOutput, calls=%fused_computation.5 | convolution fusion | flops 14680064 | bytes 147712 | tf_op jit(solution)/shard_map/crba,car->cbr/dot_general | solution.py:62
  237.2 7.5 %fusion.2 = f32[4,16,1,128]{3,2,1,0:T(1,128)S(1)} fusion(f32[4,128,16,1]{1,3,2,0:T(1,128)S(1)} %bitcast.92, f32[128,128]{1,0:T(8,128)S(1)} %copy-done.1, f32[4,16]{1,0:T(4,128)} %copy-done.3, pred[128,128]{1,0:T(8,128)(4,1)S(1)} %copy-done.5), kind=kOutput, calls=%fused_computation.6 | convolution fusion | flops 14680064 | bytes 147712 | tf_op jit(solution)/shard_map/crba,car->cbr/dot_general | solution.py:62
  244.7 0.5 fusion.24
  245.2 0.5 fusion.25
  245.7 0.6 convolution_add_fusion
  246.3 0.8 convolution_add_fusion.1
  247.3 0.1 reshape.142
  247.5 0.1 reshape.144
  247.7 5.6 %rev.8 = f32[4,8192]{1,0:T(4,128)S(1)} reverse(f32[4,8192]{1,0:T(4,128)S(1)} %reshape.144), dimensions={1} | reverse | bytes 262144 | tf_op jit(solution)/shard_map/jit(_flip)/rev | solution.py:110
  253.3 0.8 fusion.14
  254.0 0.8 multiply_convert_fusion
  254.9 1.1 add_convert_fusion
  256.1 0.2 pad_maximum_fusion.2
  256.3 8.5 %copy.57 = bf16[4,4,8192]{1,0,2:T(4,128)(2,1)} copy(bf16[4,4,8192]{2,1,0:T(4,128)(2,1)S(1)} %pad_maximum_fusion.2) | data formatting | bytes 524288 | tf_op jit(solution)/shard_map/concatenate | solution.py:113
  264.8 16.2 %reshape.165 = bf16[64,2,1024]{2,1,0:T(2,128)(2,1)S(1)} reshape(bf16[8192,4,4]{2,1,0:T(4,128)(2,1)} %bitcast.82) | data formatting | bytes 524288
  281.0 37.0 %all_to_all.30 = bf16[64,2,1024]{2,1,0:T(2,128)(2,1)S(1)} all-to-all(bf16[64,2,1024]{2,1,0:T(2,128)(2,1)S(1)} %reshape.165), channel_id=1, replica_groups=mesh['ctx'=64,'tp'=16] {'ctx'}, dimensions={0} | all-to-all | bytes 524288 | tf_op jit(solution)/shard_map/all_to_all | solution.py:114
  318.0 19.1 %reshape.166 = bf16[8192,4,4]{2,1,0:T(4,128)(2,1)} reshape(bf16[64,2,1024]{2,1,0:T(2,128)(2,1)S(1)} %all_to_all.30) | data formatting | bytes 524288
  337.1 8.6 %copy.76 = bf16[4,4,64,128]{3,2,1,0:T(8,128)(2,1)S(1)} copy(bf16[4,4,64,128]{1,0,3,2:T(4,128)(2,1)} %bitcast.83) | data formatting | bytes 524288 | tf_op jit(solution)/shard_map/all_to_all | solution.py:114
  345.8 0.2 copy.60
  345.9 6.0 %fusion = bf16[128,4096]{1,0:T(8,128)(2,1)} fusion(bf16[3,256,128]{2,1,0:T(8,128)(2,1)S(1)} %bitcast.90, bf16[4096,3,256]{2,0,1:T(8,128)(2,1)} %param.10), kind=kOutput, calls=%fused_computation.2 | convolution fusion | flops 805830656 | bytes 7536640 | tf_op jit(solution)/shard_map/pct,epc->te/dot_general | solution.py:120
  352.0 1.5 convolution_convert_fusion
  353.5 79.1 %reduce-scatter.5.cloned.1.call-done = bf16[128,256]{1,0:T(8,128)(2,1)} async-done(((bf16[128,4096]{1,0:T(8,128)(2,1)}), bf16[128,256]{1,0:T(8,128)(2,1)}) %reduce-scatter.5.cloned.1.call-update) | async-done | bytes 65552 | tf_op jit(solution)/shard_map/reduce_scatter | solution.py:127
  432.7 95.7 %reduce-scatter.3.cloned.1.call-done = bf16[128,256]{1,0:T(8,128)(2,1)} async-done(((bf16[128,4096]{1,0:T(8,128)(2,1)}), bf16[128,256]{1,0:T(8,128)(2,1)}) %reduce-scatter.3.cloned.1.call-update) | async-done | bytes 65552 | tf_op jit(solution)/shard_map/reduce_scatter | solution.py:124
  (52 shorter events, 1.5 us)
Async XLA Ops:
  7.2 171.2 %copy-start = (bf16[256,4096]{1,0:T(8,128)(2,1)S(1)}, bf16[256,4096]{1,0:T(8,128)(2,1)}, u32[]{:S(2)}) copy-start(bf16[256,4096]{1,0:T(8,128)(2,1)} %param.11) | copy-start | bytes 6291460
  7.2 90.1 %all-gather.3.cloned.1.call-start = ((), (), s32[]{:S(2)}) async-start(), calls=%async_computation.4 | async-start | bytes 1114112 | tf_op jit(solution)/shard_map/all_gather | solution.py:76
  7.9 170.5 %all-gather.5.cloned.1.call-start = ((), (), s32[]{:S(2)}) async-start(), calls=%async_computation.5 | async-start | bytes 1114112 | tf_op jit(solution)/shard_map/all_gather | solution.py:77
  9.5 1.2 copy-start.3
  9.6 1.1 copy-start.6
  102.2 96.2 %copy-start.8 = (f32[256]{0:T(256)S(1)}, f32[256]{0:T(256)}, u32[]{:S(2)}) copy-start(f32[256]{0:T(256)} %param.15) | copy-start | bytes 3076
  181.3 38.7 %all-to-all-start = ((bf16[4,256,128]{2,0,1:T(4,128)(2,1)}), bf16[4,256,128]{2,0,1:T(4,128)(2,1)S(1)}, u32[]{:S(2)}, u32[]{:S(2)}) async-start(bf16[4,256,128]{2,0,1:T(4,128)(2,1)} %copy.46), calls=%async_computation | async-start | bytes 524288 | tf_op jit(solution)/shard_map/all_to_all | solution.py:86
  197.8 234.9 %reduce-scatter.5.cloned.1.call-start = ((), (), s32[]{:S(2)}) async-start(), calls=%async_computation.7 | async-start | bytes 1114112 | tf_op jit(solution)/shard_map/reduce_scatter | solution.py:127
  216.1 4.7 copy-start.2
  226.9 10.3 %copy-start.1 = (f32[128,128]{1,0:T(8,128)S(1)}, f32[128,128]{1,0:T(8,128)}, u32[]{:S(2)}) copy-start(f32[128,128]{1,0:T(8,128)} %multiply_convert_fusion.1) | copy-start | bytes 196612
  226.9 10.3 %copy-start.5 = (pred[128,128]{1,0:T(8,128)(4,1)S(1)}, pred[128,128]{1,0:T(8,128)(4,1)}, u32[]{:S(2)}) copy-start(pred[128,128]{1,0:T(8,128)(4,1)} %fusion.21) | copy-start | bytes 49156
  228.2 16.5 %copy-start.4 = (f32[4,16]{1,0:T(4,128)S(1)}, f32[4,16]{1,0:T(4,128)}, u32[]{:S(2)}) copy-start(f32[4,16]{1,0:T(4,128)} %copy-done.3) | copy-start | bytes 772
  228.2 16.5 %copy-start.7 = (f32[4,16]{1,0:T(4,128)S(1)}, f32[4,16]{1,0:T(4,128)}, u32[]{:S(2)}) copy-start(f32[4,16]{1,0:T(4,128)} %copy-done.6) | copy-start | bytes 772
  228.2 16.5 %copy-start.9 = (f32[64]{0:T(128)S(1)}, f32[64]{0:T(128)}, u32[]{:S(2)}) copy-start(f32[64]{0:T(128)} %broadcast_add_fusion) | copy-start | bytes 772
  351.9 176.5 %reduce-scatter.3.cloned.1.call-start = ((), (), s32[]{:S(2)}) async-start(), calls=%async_computation.6 | async-start | bytes 1114112 | tf_op jit(solution)/shard_map/reduce_scatter | solution.py:124
Sparse Core Ops, SparseCore 0:
  10.6 86.6 all-gather.2
  99.9 78.4 all-gather.4
  352.0 80.5 reduce-scatter.4
  436.9 91.5 reduce-scatter.2
where the time goes:
time: 542 us; the launch traced here: 535 us
  waiting for transfers between devices  341 us (63%)
  local copies, waits for them, and re-layouts  85 us (16%)
  blocking collectives  37 us (7%)
  matrix products  34.3 us (6%)
  starting transfers between devices  16.7 us (3%)
  between operations  14.1 us (3%)
  other arithmetic  6.32 us (1%)
    reduce_scatter x1, waiting for transfers between devices, shards(): lax.psum_scatter(mixed_terms.astype(jnp.bfloat16), 'tp', scatter_dimensio...  95.7 us
    all_gather x1, waiting for transfers between devices, shards(): lax.all_gather(tokens, 'tp', axis=1, tiled=True)  86.5 us
    reduce_scatter x1, waiting for transfers between devices, shards(): lax.psum_scatter(grad_terms.astype(jnp.bfloat16), 'tp', scatter_dimension...  79.1 us
    all_gather x1, waiting for transfers between devices, shards(): lax.all_gather(cotangent, 'tp', axis=1, tiled=True)  76.2 us
    all_to_all x1, blocking collectives, shards(): lax.all_to_all(packed, 'ctx', split_axis=2, concat_axis=1, tiled=True)  37 us
    unnamed x26, local copies, waits for them, and re-layouts  35.5 us
    all_to_all x1, starting transfers between devices, shards(): lax.all_to_all(jnp.concatenate([projected, back_grad[None]], axis=0), 'ct...  16.5 us
    gather x2, local copies, waits for them, and re-layouts, causal_local(): kernel[:, lag_index]  16.4 us
  transfers between devices with their start and end apart: 5, of which 5 were waited for; matrix products, arithmetic and copies ran while one was open for 5% of the time, Pallas kernels for 0%

commit v1 on v0

v1 whole, which is shorter than its diff:
```python
import functools

import jax
import jax.numpy as jnp
from jax import lax
from jax.experimental import pallas as pl
from jax.experimental.pallas import tpu as pltpu
from jax.sharding import Mesh
from jax.sharding import PartitionSpec as P

CTX = ("y", "zh", "core")
TP = ("x", "zl")
EDGE = 16
AHEAD = 2
BF16 = jnp.bfloat16
F32 = jnp.float32


def table_kernel(rates_ref, res_ref, up_ref, down_ref, filt_ref):
    order, rows, _ = up_ref.shape
    row = lax.broadcasted_iota(jnp.int32, (rows, 1), 0).astype(F32)
    span = rows - 8 + AHEAD
    total = jnp.zeros(filt_ref.shape, F32)
    for r in range(order):
        rate = rates_ref[r : r + 1, :]
        up = jnp.exp(-rate * (row + 1.0))
        up_ref[r] = up
        down_ref[r] = jnp.exp(-rate * (span - row))
        total = total + res_ref[r : r + 1, :] * up
    filt_ref[...] = total


def features(ext, proj_ref, prev_ref, next_ref, taps_ref, rows):
    block = proj_ref.shape[1]
    out = []
    for p in range(3):
        ext[p, :EDGE] = prev_ref[p].astype(F32)
        ext[p, EDGE : EDGE + block] = proj_ref[p].astype(F32)
        ext[p, EDGE + block :] = next_ref[p].astype(F32)
        total = taps_ref[p, 0:1, :] * ext[p, EDGE : EDGE + rows]
        for k in range(1, 3):
            total = total + taps_ref[p, k : k + 1, :] * ext[p, EDGE - k : EDGE - k + rows]
        out.append(total)
    return out


def back_rows(back_ref, back_next_ref, rows):
    whole = jnp.concatenate([back_ref[...].astype(F32), back_next_ref[...].astype(F32)], axis=0)
    row = lax.broadcasted_iota(jnp.int32, (rows, 1), 0)
    return jnp.where(row < back_ref.shape[0] + AHEAD, whole[:rows], 0.0), row


def state_kernel(
    proj_ref, prev_ref, next_ref, back_ref, back_next_ref, taps_ref, rates_ref, up_ref, down_ref,
    fwd_ref, bwd_ref, ext,
):
    order, rows, _ = up_ref.shape
    block = proj_ref.shape[1]
    query, key_part, value_part = features(ext, proj_ref, prev_ref, next_ref, taps_ref, rows)
    back, row = back_rows(back_ref, back_next_ref, rows)
    gated = jnp.where(row < block, key_part * value_part, 0.0)
    grad_conv = jnp.where(row >= AHEAD, back * query, 0.0)
    for r in range(order):
        scale = jnp.exp(rates_ref[r : r + 1, :] * (AHEAD + 1.0))
        fwd_ref[r : r + 1, :] = scale * jnp.sum(down_ref[r] * gated, axis=0, keepdims=True)
        bwd_ref[r : r + 1, :] = scale * jnp.sum(up_ref[r] * grad_conv, axis=0, keepdims=True)


def local_kernel(
    proj_ref, prev_ref, next_ref, back_ref, back_next_ref, taps_ref, res_ref, skip_ref, filt_ref,
    conv_ref, grad_ref, ext, pad,
):
    rows, width = conv_ref.shape
    query, key_part, value_part = features(ext, proj_ref, prev_ref, next_ref, taps_ref, rows)
    back, _ = back_rows(back_ref, back_next_ref, rows)
    zero = jnp.zeros((8, width), F32)
    pad[0, :8] = zero
    pad[0, 8:] = key_part * value_part
    pad[1, :rows] = back * query
    pad[1, rows:] = zero
    direct = skip_ref[...] + jnp.sum(res_ref[...], axis=0, keepdims=True)
    for lane in range(0, width, 128):
        lanes = slice(lane, lane + 128)
        total = direct[:, lanes] * pad[0, 8:, lanes]
        for m in range(1, 9):
            moved = pad[0, 8 - m : 8 - m + rows, lanes]
            for q in range(0, rows, 8):
                tap = filt_ref[q + m - 1 : q + m, lanes]
                part = total[q:] + tap * moved[: rows - q]
                total = part if q == 0 else jnp.concatenate([total[:q], part], axis=0)
        conv_ref[:, lanes] = total
        total = direct[:, lanes] * pad[1, :rows, lanes]
        for m in range(1, 9):
            moved = pad[1, m : m + rows, lanes]
            for q in range(0, rows, 8):
                tap = filt_ref[q + m - 1 : q + m, lanes]
                part = total[: rows - q] + tap * moved[q:]
                total = part if q == 0 else jnp.concatenate([part, total[rows - q :]], axis=0)
        grad_ref[:, lanes] = total


def finish_kernel(
    proj_ref, prev_ref, next_ref, back_ref, back_next_ref, taps_ref, res_ref, up_ref, down_ref,
    conv_ref, grad_ref, ahead_ref, behind_ref,
    hidden_ref, out_ref, ext, feat,
):
    order, rows, _ = up_ref.shape
    block = proj_ref.shape[1]
    query, key_part, value_part = features(ext, proj_ref, prev_ref, next_ref, taps_ref, rows)
    back, _ = back_rows(back_ref, back_next_ref, rows)
    conv_out = conv_ref[...]
    grad_gated = grad_ref[...]
    for r in range(order):
        res = res_ref[r : r + 1, :]
        conv_out = conv_out + (res * ahead_ref[r : r + 1, :]) * up_ref[r]
        grad_gated = grad_gated + (res * behind_ref[r : r + 1, :]) * down_ref[r]
    hidden_ref[...] = (query * conv_out)[:block].astype(BF16)
    feat[0] = back * conv_out
    feat[1] = grad_gated * value_part
    feat[2] = grad_gated * key_part
    for p in range(3):
        total = taps_ref[p, 0:1, :] * feat[p, :block]
        for k in range(1, 3):
            total = total + taps_ref[p, k : k + 1, :] * feat[p, k : k + block]
        out_ref[p] = total.astype(BF16)


def call(kernel, outs, scratch, *args):
    return pl.pallas_call(
        kernel,
        out_shape=outs,
        scratch_shapes=scratch,
        in_specs=[pl.BlockSpec(memory_space=pltpu.VMEM)] * len(args),
        out_specs=jax.tree.map(lambda _: pl.BlockSpec(memory_space=pltpu.VMEM), outs),
        compiler_params=pltpu.CompilerParams(vmem_limit_bytes=40 * 2**20),
    )(*args)


def shape(*dims, dtype=F32):
    return jax.ShapeDtypeStruct(dims, dtype)


def spread(array, axis, count):
    copies = jnp.broadcast_to(array[None], (count,) + array.shape)
    return lax.all_to_all(copies, axis, 0, 0, tiled=True)


def scan_states(sizes, fwd, bwd, rates, block):
    n_y, n_z = sizes["y"], sizes["zh"]
    core = lax.axis_index("core")
    y = lax.axis_index("y")
    zh = lax.axis_index("zh")
    later = core == 1
    swap = [(0, 1), (1, 0)]

    def fade(tokens):
        return jnp.exp(-rates * jnp.asarray(tokens, F32))

    beside = lax.ppermute(jnp.where(later, bwd, fwd), "core", swap)
    chip = jnp.where(later, fwd, bwd) + fade(block) * beside
    place = jnp.where(later, zh, n_z - 1 - zh)
    before = jnp.zeros_like(chip)
    whole = fade(2 * block * (n_z - 1 - place)) * chip
    for k in range(1, n_z):
        pairs = [
            (2 * i + c, 2 * ((i + k if c else i - k) % n_z) + c)
            for i in range(n_z)
            for c in range(2)
        ]
        got = lax.ppermute(chip, ("zh", "core"), pairs)
        source = lax.rem(place - k + n_z, n_z)
        whole = whole + fade(2 * block * (n_z - 1 - source)) * got
        before = before + jnp.where(k <= place, fade(2 * block * (k - 1)) * got, 0.0)
    groups = spread(whole, "y", n_y)
    mine = jnp.where(later, y, n_y - 1 - y)
    far = jnp.zeros_like(chip)
    for i in range(n_y):
        source = jnp.where(later, i, n_y - 1 - i)
        gap = 2 * n_z * block * jnp.maximum(mine - 1 - source, 0)
        far = far + jnp.where(source < mine, fade(gap) * groups[i], 0.0)
    enter = before + fade(2 * block * place) * far
    other = lax.ppermute(enter, "core", swap)
    own = beside + fade(block) * enter
    return jnp.where(later, own, other), jnp.where(later, other, own)


def shards(
    sizes,
    tokens,
    cotangent,
    input_weight,
    output_weight,
    short_taps,
    residues,
    decay_rates,
    skip_gain,
):
    n_x, n_zl = sizes["x"], sizes["zl"]
    n_ctx = sizes["y"] * sizes["zh"] * sizes["core"]
    block, part = tokens.shape
    width = output_weight.shape[0]
    order = residues.shape[1]
    rows = block + 8
    taps = short_taps.transpose(0, 2, 1)
    rates = decay_rates.T
    res = residues.T
    skip = skip_gain[None]
    up, down, filt = call(
        table_kernel,
        [shape(order, rows, width), shape(order, rows, width), shape(rows, width)],
        [],
        rates,
        res,
    )
    both = jnp.concatenate([tokens, cotangent], axis=0)
    both = spread(spread(both, "zl", n_zl), "x", n_x)
    weight_in = input_weight.reshape(n_x, n_zl, part, 3, width)
    weight_out = output_weight.reshape(width, n_x, n_zl, part)
    proj = jnp.einsum(
        "xztf,xzfpc->ptc", both[:, :, :block], weight_in, preferred_element_type=F32
    ).astype(BF16)
    back = jnp.einsum(
        "xztf,cxzf->tc", both[:, :, block:], weight_out, preferred_element_type=F32
    ).astype(BF16)
    to_next = [(i, i + 1) for i in range(n_ctx - 1)]
    to_prev = [(i + 1, i) for i in range(n_ctx - 1)]
    prev = lax.ppermute(proj[:, block - EDGE :], CTX, to_next)
    first = jnp.concatenate([proj[:, :EDGE], back[None, :EDGE]], axis=0)
    first = lax.ppermute(first, CTX, to_prev)
    common = (proj, prev, first[:3], back, first[3], taps)
    ext = pltpu.VMEM((3, block + 2 * EDGE, width), F32)
    fwd, bwd = call(
        state_kernel,
        [shape(order, width), shape(order, width)],
        [ext],
        *common,
        rates,
        up,
        down,
    )
    conv, grad = call(
        local_kernel,
        [shape(rows, width), shape(rows, width)],
        [ext, pltpu.VMEM((2, rows + 8, width), F32)],
        *common,
        res,
        skip,
        filt,
    )
    ahead, behind = scan_states(sizes, fwd, bwd, rates, block)
    hidden, grad_proj = call(
        finish_kernel,
        [shape(block, width, dtype=BF16), shape(3, block, width, dtype=BF16)],
        [ext, pltpu.VMEM((3, rows, width), F32)],
        *common,
        res,
        up,
        down,
        conv,
        grad,
        ahead,
        behind,
    )
    mixed = jnp.einsum("tc,cxzf->xztf", hidden, weight_out, preferred_element_type=F32)
    grad_tok = jnp.einsum("ptc,xzfpc->xztf", grad_proj, weight_in, preferred_element_type=F32)
    terms = jnp.concatenate([mixed.astype(BF16), grad_tok.astype(BF16)], axis=2)
    terms = lax.all_to_all(terms, "x", 0, 0, tiled=True)
    terms = jnp.sum(terms.astype(F32), axis=0).astype(BF16)
    terms = lax.all_to_all(terms, "zl", 0, 0, tiled=True)
    total = jnp.sum(terms.astype(F32), axis=0).astype(BF16)
    return total[:block], total[block:]


def solution(mesh, dims=(8, 4, 2, 4, 4)):
    fine = Mesh(mesh.devices.reshape(dims), CTX + TP)
    sizes = dict(zip(CTX + TP, dims))
    return jax.shard_map(
        functools.partial(shards, sizes),
        mesh=fine,
        in_specs=(
            P(CTX, TP),
            P(CTX, TP),
            P(None, None, TP),
            P(TP, None),
            P(None, TP, None),
            P(TP, None),
            P(TP, None),
            P(TP),
        ),
        out_specs=(P(CTX, TP), P(CTX, TP)),
        check_vma=False,
    )
```

time: 542 us -> 189 us (0.35)
  waiting for transfers between devices: 341 us -> 33 us
  local copies, waits for them, and re-layouts: 85 us -> 8.63 us
  starting transfers between devices: 16.7 us -> 56.8 us
  blocking collectives: 37 us -> 68.2 us
  matrix products: 34.3 us -> 12.4 us
  between operations: 14.1 us -> 0.97 us
    reduce_scatter x2 -> x0, waiting for transfers between devices: 175 us -> none  [the longest x1 95.7 us: shards(): lax.psum_scatter(mixed_terms.astype(jnp.bfloat16), 'tp', scatter_dimensio...]
    all_gather x2 -> x0, waiting for transfers between devices: 163 us -> none  [the longest x1 86.5 us: shards(): lax.all_gather(tokens, 'tp', axis=1, tiled=True)]
    ppermute x0 -> x7, starting transfers between devices: none -> 41 us  [the longest x3 23.8 us: scan_states(): got = lax.ppermute(chip, ('zh', 'core'), pairs)]
    unnamed x26 -> x16, local copies, waits for them, and re-layouts: 35.5 us -> 2.37 us
    all_to_all x1 -> x3, blocking collectives: 37 us -> 68.2 us  [the longest x1 29.8 us: shards(): terms = lax.all_to_all(terms, 'x', 0, 0, tiled=True)]
    all_to_all x1 -> x2, waiting for transfers between devices: 2.41 us -> 25.2 us  [spread(): return lax.all_to_all(copies, axis, 0, 0, tiled=True)]
    dot_general x12 -> x4, matrix products: 34.3 us -> 12.4 us  [the longest x1 4.91 us: shards(): jnp.einsum('ptc,xzfpc->xztf', grad_proj, weight_in, preferred_element_typ...]
    gather x2 -> x0, local copies, waits for them, and re-layouts: 16.4 us -> none  [causal_local(): kernel[:, lag_index]]
  transfers between devices with their start and end apart: 5 -> 9, of which waited for: 5 -> 5; matrix products, arithmetic and copies ran while one was open for 5% -> 2% of each run, Pallas kernels for 0% -> 2%
where the time goes in v1:
time: 189 us; the launch traced here: 187 us
  blocking collectives  68.2 us (36%)
  starting transfers between devices  56.8 us (30%)
  waiting for transfers between devices  33 us (17%)
  matrix products  12.4 us (7%)
  local copies, waits for them, and re-layouts  8.63 us (5%)
  Pallas kernels  5.04 us (3%)
    all_to_all x1, blocking collectives, shards(): terms = lax.all_to_all(terms, 'x', 0, 0, tiled=True)  29.8 us
    all_to_all x2, waiting for transfers between devices, spread(): return lax.all_to_all(copies, axis, 0, 0, tiled=True)  25.2 us
    ppermute x3, starting transfers between devices, scan_states(): got = lax.ppermute(chip, ('zh', 'core'), pairs)  23.8 us
    all_to_all x1, blocking collectives, spread(): return lax.all_to_all(copies, axis, 0, 0, tiled=True)  21.5 us
    all_to_all x1, blocking collectives, shards(): terms = lax.all_to_all(terms, 'zl', 0, 0, tiled=True)  16.9 us
    all_to_all x2, starting transfers between devices, spread(): return lax.all_to_all(copies, axis, 0, 0, tiled=True)  15.8 us
    ppermute x1, starting transfers between devices, scan_states(): beside = lax.ppermute(jnp.where(later, bwd, fwd), 'core', swap)  10.9 us
    ppermute x3, waiting for transfers between devices, scan_states(): got = lax.ppermute(chip, ('zh', 'core'), pairs)  6.15 us
  transfers between devices with their start and end apart: 9, of which 5 were waited for; matrix products, arithmetic and copies ran while one was open for 2% of the time, Pallas kernels for 2%

profile of v1, /device:TPU:6, one launch (start us, length us, event | category | flops | bytes accessed | tf_op | source)
XLA Modules:
  0.0 186.9 jit_solution(16077766318439039873)
XLA Ops:
  0.6 0.9 pad_maximum_fusion.1
  1.6 21.5 %all_to_all.25 = bf16[4,256,256]{2,1,0:T(8,128)(2,1)S(1)} all-to-all(bf16[4,256,256]{2,1,0:T(8,128)(2,1)S(1)} %broadcast_in_dim.36), channel_id=1, replica_groups=mesh['y'=8,'zh'=4,'core'=2,'x'=4,'zl'=4] {'zl'}, dimensions={0} | all-to-all | bytes 1048576 | tf_op jit(solution)/shard_map/all_to_all | solution.py:145
  23.1 1.6 broadcast_in_dim.37
  24.7 8.7 %all-to-all-start.1 = ((bf16[4,4,256,256]{3,2,1,0:T(8,128)(2,1)}), bf16[4,4,256,256]{3,2,1,0:T(8,128)(2,1)}, u32[]{:S(2)}, u32[]{:S(2)}) async-start(bf16[4,4,256,256]{3,2,1,0:T(8,128)(2,1)} %broadcast_in_dim.37), calls=%async_computation.1 | async-start | bytes 4194304 | tf_op jit(solution)/shard_map/all_to_all | solution.py:145
  33.3 3.3 %reshape.14 = bf16[256,4,4,256]{3,2,1,0:T(4,128)(2,1)S(1)} reshape(bf16[256,4096]{1,0:T(8,128)(2,1)} %param.11) | data formatting | bytes 4194304 | tf_op jit(solution)/shard_map/reshape | solution.py:218
  36.7 0.0 copy-start.6
  36.7 16.2 %all-to-all-done.1 = bf16[4,4,256,256]{3,2,1,0:T(8,128)(2,1)} async-done(((bf16[4,4,256,256]{3,2,1,0:T(8,128)(2,1)}), bf16[4,4,256,256]{3,2,1,0:T(8,128)(2,1)}, u32[]{:S(2)}, u32[]{:S(2)}) %all-to-all-start.1) | async-done | bytes 2097184 | tf_op jit(solution)/shard_map/all_to_all | solution.py:145
  52.8 4.1 %fusion.12.proj_ref = bf16[3,128,256]{2,1,0:T(8,128)(2,1)S(1)} fusion(bf16[4,4,256,3,256]{4,2,1,0,3:T(8,128)(2,1)} %bitcast.156, bf16[4,4,256,256]{3,2,1,0:T(8,128)(2,1)} %all-to-all-done.1), kind=kOutput, calls=%fused_computation.11 | convolution fusion | flops 805404672 | bytes 7536640 | tf_op jit(solution)/shard_map/xztf,xzfpc->ptc/dot_general | solution.py:219
  57.0 0.0 copy-done.6
  57.0 0.0 copy-start.2
  57.0 0.0 copy-start.3
  57.0 0.0 copy-start.4
  57.0 2.6 %fusion.16.back_ref = bf16[128,256]{1,0:T(8,128)(2,1)S(1)} fusion(bf16[256,4,4,256]{3,2,1,0:T(4,128)(2,1)S(1)} %reshape.14, bf16[4,4,256,256]{3,2,1,0:T(8,128)(2,1)} %all-to-all-done.1), kind=kOutput, calls=%fused_computation.13 | convolution fusion | flops 268468224 | bytes 3211264 | tf_op jit(solution)/shard_map/xztf,cxzf->tc/dot_general | solution.py:222
  59.6 1.3 collective-permute-start.1
  60.9 0.8 shard_map.95
  61.7 3.0 %collective-permute-start = (bf16[3,16,256]{2,1,0:T(8,128)(2,1)S(1)}, bf16[3,16,256]{2,1,0:T(8,128)(2,1)S(1)}, u32[]{:S(2)}, u32[]{:S(2)}) collective-permute-start(bf16[3,16,256]{2,1,0:T(8,128)(2,1)S(1)} %get-tuple-element.21), channel_id=1, source_target_pairs={{0,16},{16,32},{32,48},{48,64},{64,80},{80,96},{96,112},{112,128},... | collective-permute-start | bytes 73736 | tf_op jit(solution)/shard_map/ppermute | solution.py:227
  64.7 0.0 collective-permute-done.1
  64.8 0.8 collective-permute-done.prev_ref
  65.6 0.6 shard_map.97
  66.2 0.0 copy-done
  66.2 10.9 %collective-permute-start.2 = (f32[16,256]{1,0:T(8,128)S(1)}, f32[16,256]{1,0:T(8,128)S(1)}, u32[]{:S(2)}, u32[]{:S(2)}) collective-permute-start(f32[16,256]{1,0:T(8,128)S(1)} %broadcast_select_fusion.2), channel_id=1, source_target_pairs={{0,16},{16,0},{1,17},{17,1},{2,18},{18,2},{3,19},{19,3},{4,20},{20... | collective-permute-start | bytes 49160 | tf_op jit(solution)/shard_map/ppermute | solution.py:159
  77.1 0.8 collective-permute-done.2
  77.9 8.4 %collective-permute-start.5 = (f32[16,256]{1,0:T(8,128)S(1)}, f32[16,256]{1,0:T(8,128)S(1)}, u32[]{:S(2)}, u32[]{:S(2)}) collective-permute-start(f32[16,256]{1,0:T(8,128)S(1)} %multiply_add_fusion.2), channel_id=1, source_target_pairs={{0,32},{16,112},{32,64},{48,16},{64,96},{80,48},{96,0},{112,80},{1... | collective-permute-start | bytes 49160 | tf_op jit(solution)/shard_map/ppermute | solution.py:170
  86.3 12.2 %collective-permute-start.4 = (f32[16,256]{1,0:T(8,128)S(1)}, f32[16,256]{1,0:T(8,128)S(1)}, u32[]{:S(2)}, u32[]{:S(2)}) collective-permute-start(f32[16,256]{1,0:T(8,128)S(1)} %multiply_add_fusion.2), channel_id=1, source_target_pairs={{0,64},{16,80},{32,96},{48,112},{64,0},{80,16},{96,32},{112,48},{1... | collective-permute-start | bytes 49160 | tf_op jit(solution)/shard_map/ppermute | solution.py:170
  98.5 3.3 %collective-permute-start.3 = (f32[16,256]{1,0:T(8,128)S(1)}, f32[16,256]{1,0:T(8,128)S(1)}, u32[]{:S(2)}, u32[]{:S(2)}) collective-permute-start(f32[16,256]{1,0:T(8,128)S(1)} %multiply_add_fusion.2), channel_id=1, source_target_pairs={{0,96},{16,48},{32,0},{48,80},{64,32},{80,112},{96,64},{112,16},{1... | collective-permute-start | bytes 49160 | tf_op jit(solution)/shard_map/ppermute | solution.py:170
  101.8 0.0 collective-permute-done.5
  101.9 0.0 collective-permute-done.4
  101.9 6.1 %collective-permute-done.3 = f32[16,256]{1,0:T(8,128)S(1)} collective-permute-done((f32[16,256]{1,0:T(8,128)S(1)}, f32[16,256]{1,0:T(8,128)S(1)}, u32[]{:S(2)}, u32[]{:S(2)}) %collective-permute-start.3) | collective-permute-done | bytes 16416 | tf_op jit(solution)/shard_map/ppermute | solution.py:170
  108.0 0.7 broadcast_in_dim.40
  108.7 7.1 %all-to-all-start.2 = ((f32[8,16,256]{2,1,0:T(8,128)}), f32[8,16,256]{2,1,0:T(8,128)S(1)}, u32[]{:S(2)}, u32[]{:S(2)}) async-start(f32[8,16,256]{2,1,0:T(8,128)} %broadcast_in_dim.40), calls=%async_computation.2 | async-start | bytes 262144 | tf_op jit(solution)/shard_map/all_to_all | solution.py:145
  115.8 9.1 %all-to-all-done.2 = f32[8,16,256]{2,1,0:T(8,128)S(1)} async-done(((f32[8,16,256]{2,1,0:T(8,128)}), f32[8,16,256]{2,1,0:T(8,128)S(1)}, u32[]{:S(2)}, u32[]{:S(2)}) %all-to-all-start.2) | async-done | bytes 131104 | tf_op jit(solution)/shard_map/all_to_all | solution.py:145
  124.9 0.1 fusion.26
  125.0 1.9 %collective-permute-start.6 = (f32[16,256]{1,0:T(8,128)S(1)}, f32[16,256]{1,0:T(8,128)S(1)}, u32[]{:S(2)}, u32[]{:S(2)}) collective-permute-start(f32[16,256]{1,0:T(8,128)S(1)} %fusion.26), channel_id=1, source_target_pairs={{0,16},{16,0},{1,17},{17,1},{2,18},{18,2},{3,19},{19,3},{4,20},{20... | collective-permute-start | bytes 49160 | tf_op jit(solution)/shard_map/ppermute | solution.py:182
  126.9 0.0 copy-done.5
  126.9 2.8 %shard_map.96 = (f32[136,256]{1,0:T(8,128)S(1)}, f32[136,256]{1,0:T(8,128)S(1)}) custom-call(bf16[3,128,256]{2,1,0:T(8,128)(2,1)S(1)} %fusion.12.proj_ref, bf16[3,16,256]{2,1,0:T(8,128)(2,1)S(1)} %collective-permute-done.prev_ref, bf16[3,16,256]{2,1,0:T(8,128)(2,1)S(1)} %slice.73.next_ref, bf16[128,256]{1,0:T(8,128)(2,1)S(1)} %fusion.16.back_ref, ...), custom_call_target="tpu_custom_call" | custom-call | tf_op jit(solution)/shard_map/pallas_call | solution.py:129
  129.7 0.0 collective-permute-done.6
  129.7 0.0 copy-start.1
  129.7 1.6 copy-done.1
  131.3 0.9 shard_map.98
  132.2 0.7 copy-done.7
  132.9 0.9 fusion.7
  133.8 4.9 %fusion.10 = bf16[4,4,128,256]{3,2,1,0:T(8,128)(2,1)S(1)} fusion(bf16[4,4,256,3,256]{4,2,1,0,3:T(8,128)(2,1)} %bitcast.157, bf16[3,128,256]{2,1,0:T(8,128)(2,1)S(1)} %get-tuple-element.19), kind=kOutput, calls=%fused_computation.8 | convolution fusion | flops 805830656 | bytes 7536640 | tf_op jit(solution)/shard_map/ptc,xzfpc->xztf/dot_general | solution.py:265
  138.7 0.1 pad_maximum_fusion
  138.9 29.8 %all_to_all.26 = bf16[4,4,256,256]{3,2,1,0:T(8,128)(2,1)S(1)} all-to-all(bf16[4,4,256,256]{3,2,1,0:T(8,128)(2,1)S(1)} %pad_maximum_fusion), channel_id=1, replica_groups=mesh['y'=8,'zh'=4,'core'=2,'x'=4,'zl'=4] {'x'}, dimensions={0} | all-to-all | bytes 4194304 | tf_op jit(solution)/shard_map/all_to_all | solution.py:267
  168.6 0.6 reduce_sum.24
  169.2 16.9 %all_to_all.27 = bf16[4,256,256]{2,1,0:T(8,128)(2,1)S(1)} all-to-all(bf16[4,256,256]{2,1,0:T(8,128)(2,1)S(1)} %reduce_sum.24), channel_id=1, replica_groups=mesh['y'=8,'zh'=4,'core'=2,'x'=4,'zl'=4] {'zl'}, dimensions={0} | all-to-all | bytes 1048576 | tf_op jit(solution)/shard_map/all_to_all | solution.py:269
  186.2 0.1 reduce_sum.25
  186.2 0.7 fusion.48
  (16 shorter events, 0.1 us)
Async XLA Ops:
  24.7 28.2 %all-to-all-start.1 = ((bf16[4,4,256,256]{3,2,1,0:T(8,128)(2,1)}), bf16[4,4,256,256]{3,2,1,0:T(8,128)(2,1)}, u32[]{:S(2)}, u32[]{:S(2)}) async-start(bf16[4,4,256,256]{3,2,1,0:T(8,128)(2,1)} %broadcast_in_dim.37), calls=%async_computation.1 | async-start | bytes 4194304 | tf_op jit(solution)/shard_map/all_to_all | solution.py:145
  36.7 20.3 %copy-start.6 = (bf16[256,4,4,256]{3,2,1,0:T(4,128)(2,1)}, bf16[256,4,4,256]{3,2,1,0:T(4,128)(2,1)S(1)}, u32[]{:S(2)}) copy-start(bf16[256,4,4,256]{3,2,1,0:T(4,128)(2,1)S(1)} %reshape.14) | copy-start | bytes 6291460
  57.0 3.9 %copy-start.2 = (f32[256,16]{0,1:T(8,128)S(1)}, f32[256,16]{0,1:T(8,128)}, u32[]{:S(2)}) copy-start(f32[256,16]{0,1:T(8,128)} %param.14) | copy-start | bytes 49156
  57.0 3.9 %copy-start.3 = (f32[256,16]{0,1:T(8,128)S(1)}, f32[256,16]{0,1:T(8,128)}, u32[]{:S(2)}) copy-start(f32[256,16]{0,1:T(8,128)} %param.13) | copy-start | bytes 49156
  57.0 8.6 %copy-start.4 = (f32[3,256,3]{1,2,0:T(4,128)S(1)}, f32[3,256,3]{1,2,0:T(4,128)}, u32[]{:S(2)}) copy-start(f32[3,256,3]{1,2,0:T(4,128)} %param.12) | copy-start | bytes 27652
  59.6 5.1 %collective-permute-start.1 = (bf16[4,16,256]{2,1,0:T(8,128)(2,1)S(1)}, bf16[4,16,256]{2,1,0:T(8,128)(2,1)S(1)}, u32[]{:S(2)}, u32[]{:S(2)}) collective-permute-start(bf16[4,16,256]{2,1,0:T(8,128)(2,1)S(1)} %pad_maximum_fusion.2), channel_id=1, source_target_pairs={{16,0},{32,16},{48,32},{64,48},{80,64},{96,80},{112,96},{128,112},... | collective-permute-start | bytes 98312 | tf_op jit(solution)/shard_map/ppermute | solution.py:229
  61.7 4.5 %copy-start = (f32[16,136,256]{2,1,0:T(8,128)}, f32[16,136,256]{2,1,0:T(8,128)S(1)}, u32[]{:S(2)}) copy-start(f32[16,136,256]{2,1,0:T(8,128)S(1)} %get-tuple-element.12.down_ref) | copy-start | bytes 6684676
  61.7 3.9 %collective-permute-start = (bf16[3,16,256]{2,1,0:T(8,128)(2,1)S(1)}, bf16[3,16,256]{2,1,0:T(8,128)(2,1)S(1)}, u32[]{:S(2)}, u32[]{:S(2)}) collective-permute-start(bf16[3,16,256]{2,1,0:T(8,128)(2,1)S(1)} %get-tuple-element.21), channel_id=1, source_target_pairs={{0,16},{16,32},{32,48},{48,64},{64,80},{80,96},{96,112},{112,128},... | collective-permute-start | bytes 73736 | tf_op jit(solution)/shard_map/ppermute | solution.py:227
  65.6 61.3 %copy-start.5 = (f32[256]{0:T(256)S(1)}, f32[256]{0:T(256)}, u32[]{:S(2)}) copy-start(f32[256]{0:T(256)} %param.15) | copy-start | bytes 3076
  66.2 11.7 %collective-permute-start.2 = (f32[16,256]{1,0:T(8,128)S(1)}, f32[16,256]{1,0:T(8,128)S(1)}, u32[]{:S(2)}, u32[]{:S(2)}) collective-permute-start(f32[16,256]{1,0:T(8,128)S(1)} %broadcast_select_fusion.2), channel_id=1, source_target_pairs={{0,16},{16,0},{1,17},{17,1},{2,18},{18,2},{3,19},{19,3},{4,20},{20... | collective-permute-start | bytes 49160 | tf_op jit(solution)/shard_map/ppermute | solution.py:159
  77.9 23.9 %collective-permute-start.5 = (f32[16,256]{1,0:T(8,128)S(1)}, f32[16,256]{1,0:T(8,128)S(1)}, u32[]{:S(2)}, u32[]{:S(2)}) collective-permute-start(f32[16,256]{1,0:T(8,128)S(1)} %multiply_add_fusion.2), channel_id=1, source_target_pairs={{0,32},{16,112},{32,64},{48,16},{64,96},{80,48},{96,0},{112,80},{1... | collective-permute-start | bytes 49160 | tf_op jit(solution)/shard_map/ppermute | solution.py:170
  86.3 15.5 %collective-permute-start.4 = (f32[16,256]{1,0:T(8,128)S(1)}, f32[16,256]{1,0:T(8,128)S(1)}, u32[]{:S(2)}, u32[]{:S(2)}) collective-permute-start(f32[16,256]{1,0:T(8,128)S(1)} %multiply_add_fusion.2), channel_id=1, source_target_pairs={{0,64},{16,80},{32,96},{48,112},{64,0},{80,16},{96,32},{112,48},{1... | collective-permute-start | bytes 49160 | tf_op jit(solution)/shard_map/ppermute | solution.py:170
  98.5 9.5 %collective-permute-start.3 = (f32[16,256]{1,0:T(8,128)S(1)}, f32[16,256]{1,0:T(8,128)S(1)}, u32[]{:S(2)}, u32[]{:S(2)}) collective-permute-start(f32[16,256]{1,0:T(8,128)S(1)} %multiply_add_fusion.2), channel_id=1, source_target_pairs={{0,96},{16,48},{32,0},{48,80},{64,32},{80,112},{96,64},{112,16},{1... | collective-permute-start | bytes 49160 | tf_op jit(solution)/shard_map/ppermute | solution.py:170
  108.7 16.2 %all-to-all-start.2 = ((f32[8,16,256]{2,1,0:T(8,128)}), f32[8,16,256]{2,1,0:T(8,128)S(1)}, u32[]{:S(2)}, u32[]{:S(2)}) async-start(f32[8,16,256]{2,1,0:T(8,128)} %broadcast_in_dim.40), calls=%async_computation.2 | async-start | bytes 262144 | tf_op jit(solution)/shard_map/all_to_all | solution.py:145
  125.0 4.7 %collective-permute-start.6 = (f32[16,256]{1,0:T(8,128)S(1)}, f32[16,256]{1,0:T(8,128)S(1)}, u32[]{:S(2)}, u32[]{:S(2)}) collective-permute-start(f32[16,256]{1,0:T(8,128)S(1)} %fusion.26), channel_id=1, source_target_pairs={{0,16},{16,0},{1,17},{17,1},{2,18},{18,2},{3,19},{19,3},{4,20},{20... | collective-permute-start | bytes 49160 | tf_op jit(solution)/shard_map/ppermute | solution.py:182
  129.7 1.6 copy-start.1
  131.3 1.6 copy-start.7

commit v2 on v1

--- a/solution.py
+++ b/solution.py
@@ -51,8 +51,8 @@
 
 
 def state_kernel(
-    proj_ref, prev_ref, next_ref, back_ref, back_next_ref, taps_ref, rates_ref, up_ref, down_ref,
-    fwd_ref, bwd_ref, ext,
+    place_ref, proj_ref, prev_ref, next_ref, back_ref, back_next_ref, taps_ref, rates_ref, up_ref, down_ref,
+    fwd_ref, bwd_ref, send_ref, ext,
 ):
     order, rows, _ = up_ref.shape
     block = proj_ref.shape[1]
@@ -64,6 +64,33 @@
         scale = jnp.exp(rates_ref[r : r + 1, :] * (AHEAD + 1.0))
         fwd_ref[r : r + 1, :] = scale * jnp.sum(down_ref[r] * gated, axis=0, keepdims=True)
         bwd_ref[r : r + 1, :] = scale * jnp.sum(up_ref[r] * grad_conv, axis=0, keepdims=True)
+    for i in range(send_ref.shape[0]):
+        send_ref[i] = jnp.where(place_ref[0] < i, fwd_ref[...], bwd_ref[...]).astype(BF16)
+
+
+def chain_kernel(block, place_ref, rates_ref, fwd_ref, bwd_ref, got_ref, send_ref):
+    rates = rates_ref[...]
+    order = rates.shape[0]
+    groups, members = got_ref.shape[0], send_ref.shape[0]
+    group, member = place_ref[0], place_ref[1]
+
+    def fade(blocks):
+        return jnp.exp(-rates * (block * jnp.maximum(blocks, 0)).astype(F32))
+
+    fwd, bwd = fwd_ref[...], bwd_ref[...]
+    before = jnp.zeros_like(fwd)
+    after = jnp.zeros_like(bwd)
+    for i in range(groups):
+        got = got_ref[i].astype(F32)
+        before = before + jnp.where(i < group, fade(members * (group - 1 - i)) * got, 0.0)
+        after = after + jnp.where(i > group, fade(members * (i - 1 - group)) * got, 0.0)
+    for i in range(members):
+        ahead = fade(members - 1 + i - member) * before
+        ahead = ahead + jnp.where(i > member, fade(i - member - 1) * fwd, 0.0)
+        behind = fade(members - 1 + member - i) * after
+        behind = behind + jnp.where(i < member, fade(member - i - 1) * bwd, 0.0)
+        send_ref[i, :order] = ahead.astype(BF16)
+        send_ref[i, order:] = behind.astype(BF16)
 
 
 def local_kernel(
@@ -101,7 +128,7 @@
 
 def finish_kernel(
     proj_ref, prev_ref, next_ref, back_ref, back_next_ref, taps_ref, res_ref, up_ref, down_ref,
-    conv_ref, grad_ref, ahead_ref, behind_ref,
+    conv_ref, grad_ref, got_ref,
     hidden_ref, out_ref, ext, feat,
 ):
     order, rows, _ = up_ref.shape
@@ -110,10 +137,12 @@
     back, _ = back_rows(back_ref, back_next_ref, rows)
     conv_out = conv_ref[...]
     grad_gated = grad_ref[...]
+    states = jnp.sum(got_ref[...].astype(F32), axis=0)
+    ahead, behind = states[:order], states[order:]
     for r in range(order):
         res = res_ref[r : r + 1, :]
-        conv_out = conv_out + (res * ahead_ref[r : r + 1, :]) * up_ref[r]
-        grad_gated = grad_gated + (res * behind_ref[r : r + 1, :]) * down_ref[r]
+        conv_out = conv_out + (res * ahead[r : r + 1]) * up_ref[r]
+        grad_gated = grad_gated + (res * behind[r : r + 1]) * down_ref[r]
     hidden_ref[...] = (query * conv_out)[:block].astype(BF16)
     feat[0] = back * conv_out
     feat[1] = grad_gated * value_part
@@ -125,13 +154,19 @@
         out_ref[p] = total.astype(BF16)
 
 
-def call(kernel, outs, scratch, *args):
+def call(kernel, outs, scratch, *args, flops=0):
+    whole = pl.BlockSpec(memory_space=pltpu.VMEM)
+    specs = [
+        pl.BlockSpec(memory_space=pltpu.SMEM) if a.dtype == jnp.int32 else whole for a in args
+    ]
+    cost = pl.CostEstimate(flops=flops, bytes_accessed=0, transcendentals=0) if flops else None
     return pl.pallas_call(
         kernel,
         out_shape=outs,
         scratch_shapes=scratch,
-        in_specs=[pl.BlockSpec(memory_space=pltpu.VMEM)] * len(args),
-        out_specs=jax.tree.map(lambda _: pl.BlockSpec(memory_space=pltpu.VMEM), outs),
+        in_specs=specs,
+        out_specs=jax.tree.map(lambda _: whole, outs),
+        cost_estimate=cost,
         compiler_params=pltpu.CompilerParams(vmem_limit_bytes=40 * 2**20),
     )(*args)
 
@@ -143,45 +178,6 @@
 def spread(array, axis, count):
     copies = jnp.broadcast_to(array[None], (count,) + array.shape)
     return lax.all_to_all(copies, axis, 0, 0, tiled=True)
-
-
-def scan_states(sizes, fwd, bwd, rates, block):
-    n_y, n_z = sizes["y"], sizes["zh"]
-    core = lax.axis_index("core")
-    y = lax.axis_index("y")
-    zh = lax.axis_index("zh")
-    later = core == 1
-    swap = [(0, 1), (1, 0)]
-
-    def fade(tokens):
-        return jnp.exp(-rates * jnp.asarray(tokens, F32))
-
-    beside = lax.ppermute(jnp.where(later, bwd, fwd), "core", swap)
-    chip = jnp.where(later, fwd, bwd) + fade(block) * beside
-    place = jnp.where(later, zh, n_z - 1 - zh)
-    before = jnp.zeros_like(chip)
-    whole = fade(2 * block * (n_z - 1 - place)) * chip
-    for k in range(1, n_z):
-        pairs = [
-            (2 * i + c, 2 * ((i + k if c else i - k) % n_z) + c)
-            for i in range(n_z)
-            for c in range(2)
-        ]
-        got = lax.ppermute(chip, ("zh", "core"), pairs)
-        source = lax.rem(place - k + n_z, n_z)
-        whole = whole + fade(2 * block * (n_z - 1 - source)) * got
-        before = before + jnp.where(k <= place, fade(2 * block * (k - 1)) * got, 0.0)
-    groups = spread(whole, "y", n_y)
-    mine = jnp.where(later, y, n_y - 1 - y)
-    far = jnp.zeros_like(chip)
-    for i in range(n_y):
-        source = jnp.where(later, i, n_y - 1 - i)
-        gap = 2 * n_z * block * jnp.maximum(mine - 1 - source, 0)
-        far = far + jnp.where(source < mine, fade(gap) * groups[i], 0.0)
-    enter = before + fade(2 * block * place) * far
-    other = lax.ppermute(enter, "core", swap)
-    own = beside + fade(block) * enter
-    return jnp.where(later, own, other), jnp.where(later, other, own)
 
 
 def shards(
@@ -229,10 +225,14 @@
     first = lax.ppermute(first, CTX, to_prev)
     common = (proj, prev, first[:3], back, first[3], taps)
     ext = pltpu.VMEM((3, block + 2 * EDGE, width), F32)
-    fwd, bwd = call(
+    group = lax.axis_index("y")
+    member = lax.axis_index("zh") * sizes["core"] + lax.axis_index("core")
+    place = jnp.stack([group, member]).astype(jnp.int32)
+    fwd, bwd, send = call(
         state_kernel,
-        [shape(order, width), shape(order, width)],
+        [shape(order, width), shape(order, width), shape(sizes["y"], order, width, dtype=BF16)],
         [ext],
+        place,
         *common,
         rates,
         up,
@@ -246,8 +246,20 @@
         res,
         skip,
         filt,
-    )
-    ahead, behind = scan_states(sizes, fwd, bwd, rates, block)
+        flops=3 * 10**9,
+    )
+    got = lax.all_to_all(send, "y", 0, 0, tiled=True)
+    send = call(
+        functools.partial(chain_kernel, block),
+        shape(sizes["zh"] * sizes["core"], 2 * order, width, dtype=BF16),
+        [],
+        place,
+        rates,
+        fwd,
+        bwd,
+        got,
+    )
+    states = lax.all_to_all(send, ("zh", "core"), 0, 0, tiled=True)
     hidden, grad_proj = call(
         finish_kernel,
         [shape(block, width, dtype=BF16), shape(3, block, width, dtype=BF16)],
@@ -258,8 +270,7 @@
         down,
         conv,
         grad,
-        ahead,
-        behind,
+        states,
     )
     mixed = jnp.einsum("tc,cxzf->xztf", hidden, weight_out, preferred_element_type=F32)
     grad_tok = jnp.einsum("ptc,xzfpc->xztf", grad_proj, weight_in, preferred_element_type=F32)

time: 189 us -> 178 us (0.942)
  starting transfers between devices: 56.8 us -> 16.4 us
  blocking collectives: 68.2 us -> 99.8 us
  waiting for transfers between devices: 33 us -> 30.3 us
  Pallas kernels: 5.04 us -> 7.05 us
    ppermute x5 -> x0, starting transfers between devices: 36.6 us -> none  [the longest x3 23.8 us: scan_states(): got = lax.ppermute(chip, ('zh', 'core'), pairs)]
    all_to_all x0 -> x1, blocking collectives: none -> 34.3 us  [shards(): got = lax.all_to_all(send, 'y', 0, 0, tiled=True)]
    all_to_all x0 -> x1, waiting for transfers between devices: none -> 13.3 us  [shards(): states = lax.all_to_all(send, ('zh', 'core'), 0, 0, tiled=True)]
    all_to_all x2 -> x1, waiting for transfers between devices: 25.2 us -> 16.1 us  [spread(): return lax.all_to_all(copies, axis, 0, 0, tiled=True)]
    all_to_all x2 -> x1, starting transfers between devices: 15.8 us -> 8.67 us  [spread(): return lax.all_to_all(copies, axis, 0, 0, tiled=True)]
    ppermute x5 -> x0, waiting for transfers between devices: 6.97 us -> none  [the longest x3 6.15 us: scan_states(): got = lax.ppermute(chip, ('zh', 'core'), pairs)]
    all_to_all x1, blocking collectives: 29.8 us -> 26.3 us  [shards(): terms = lax.all_to_all(terms, 'x', 0, 0, tiled=True)]
    all_to_all x0 -> x1, starting transfers between devices: none -> 3.37 us  [shards(): states = lax.all_to_all(send, ('zh', 'core'), 0, 0, tiled=True)]
  transfers between devices with their start and end apart: 9 -> 4, of which waited for: 5 -> 3; matrix products, arithmetic and copies ran while one was open for 2% -> 2% of each run, Pallas kernels for 2% -> 2%
where the time goes in v2:
time: 178 us; the launch traced here: 176 us
  blocking collectives  99.8 us (56%)
  waiting for transfers between devices  30.3 us (17%)
  starting transfers between devices  16.4 us (9%)
  matrix products  12.5 us (7%)
  local copies, waits for them, and re-layouts  7.93 us (4%)
  Pallas kernels  7.05 us (4%)
    all_to_all x1, blocking collectives, shards(): got = lax.all_to_all(send, 'y', 0, 0, tiled=True)  34.3 us
    all_to_all x1, blocking collectives, shards(): terms = lax.all_to_all(terms, 'x', 0, 0, tiled=True)  26.3 us
    all_to_all x1, blocking collectives, spread(): return lax.all_to_all(copies, axis, 0, 0, tiled=True)  21.5 us
    all_to_all x1, blocking collectives, shards(): terms = lax.all_to_all(terms, 'zl', 0, 0, tiled=True)  17.7 us
    all_to_all x1, waiting for transfers between devices, spread(): return lax.all_to_all(copies, axis, 0, 0, tiled=True)  16.1 us
    all_to_all x1, waiting for transfers between devices, shards(): states = lax.all_to_all(send, ('zh', 'core'), 0, 0, tiled=True)  13.3 us
    all_to_all x1, starting transfers between devices, spread(): return lax.all_to_all(copies, axis, 0, 0, tiled=True)  8.67 us
    pallas_call x5, Pallas kernels, call(): pl.pallas_call(kernel, out_shape=outs, scratch_shapes=scratch, in_specs=s...  7.05 us
  transfers between devices with their start and end apart: 4, of which 3 were waited for; matrix products, arithmetic and copies ran while one was open for 2% of the time, Pallas kernels for 2%

profile of v2, /device:TPU:6, one launch (start us, length us, event | category | flops | bytes accessed | tf_op | source)
XLA Modules:
  0.0 176.5 jit_solution(14904222163000124738)
XLA Ops:
  0.6 0.9 pad_maximum_fusion.1
  1.6 21.5 %all_to_all.30 = bf16[4,256,256]{2,1,0:T(8,128)(2,1)S(1)} all-to-all(bf16[4,256,256]{2,1,0:T(8,128)(2,1)S(1)} %broadcast_in_dim.8), channel_id=1, replica_groups=mesh['y'=8,'zh'=4,'core'=2,'x'=4,'zl'=4] {'zl'}, dimensions={0} | all-to-all | bytes 1048576 | tf_op jit(solution)/shard_map/all_to_all | solution.py:180
  23.1 1.5 broadcast_in_dim.9
  24.7 8.7 %all-to-all-start.1 = ((bf16[4,4,256,256]{3,2,1,0:T(8,128)(2,1)}), bf16[4,4,256,256]{3,2,1,0:T(8,128)(2,1)}, u32[]{:S(2)}, u32[]{:S(2)}) async-start(bf16[4,4,256,256]{3,2,1,0:T(8,128)(2,1)} %broadcast_in_dim.9), calls=%async_computation.1 | async-start | bytes 4194304 | tf_op jit(solution)/shard_map/all_to_all | solution.py:180
  33.3 3.3 %reshape.13 = bf16[256,4,4,256]{3,2,1,0:T(4,128)(2,1)S(1)} reshape(bf16[256,4096]{1,0:T(8,128)(2,1)} %param.11) | data formatting | bytes 4194304 | tf_op jit(solution)/shard_map/reshape | solution.py:214
  36.7 0.0 copy-start.6
  36.7 16.1 %all-to-all-done.1 = bf16[4,4,256,256]{3,2,1,0:T(8,128)(2,1)} async-done(((bf16[4,4,256,256]{3,2,1,0:T(8,128)(2,1)}), bf16[4,4,256,256]{3,2,1,0:T(8,128)(2,1)}, u32[]{:S(2)}, u32[]{:S(2)}) %all-to-all-start.1) | async-done | bytes 2097184 | tf_op jit(solution)/shard_map/all_to_all | solution.py:180
  52.8 4.1 %fusion.12.proj_ref = bf16[3,128,256]{2,1,0:T(8,128)(2,1)S(1)} fusion(bf16[4,4,256,3,256]{4,2,1,0,3:T(8,128)(2,1)} %bitcast.71, bf16[4,4,256,256]{3,2,1,0:T(8,128)(2,1)} %all-to-all-done.1), kind=kOutput, calls=%fused_computation.11 | convolution fusion | flops 805404672 | bytes 7536640 | tf_op jit(solution)/shard_map/xztf,xzfpc->ptc/dot_general | solution.py:215
  56.9 0.0 copy-done.6
  57.0 0.0 copy-start.2
  57.0 0.0 copy-start.3
  57.0 0.0 copy-start.4
  57.0 2.6 %fusion.16.back_ref = bf16[128,256]{1,0:T(8,128)(2,1)S(1)} fusion(bf16[256,4,4,256]{3,2,1,0:T(4,128)(2,1)S(1)} %reshape.13, bf16[4,4,256,256]{3,2,1,0:T(8,128)(2,1)} %all-to-all-done.1), kind=kOutput, calls=%fused_computation.13 | convolution fusion | flops 268468224 | bytes 3211264 | tf_op jit(solution)/shard_map/xztf,cxzf->tc/dot_general | solution.py:218
  59.6 1.3 collective-permute-start.1
  60.9 0.1 pad_add_fusion.place_ref
  61.0 0.0 copy-done.2
  61.0 0.0 copy-done.3
  61.0 0.8 shard_map.95
  61.7 0.0 copy-start
  61.7 3.0 %collective-permute-start = (bf16[3,16,256]{2,1,0:T(8,128)(2,1)S(1)}, bf16[3,16,256]{2,1,0:T(8,128)(2,1)S(1)}, u32[]{:S(2)}, u32[]{:S(2)}) collective-permute-start(bf16[3,16,256]{2,1,0:T(8,128)(2,1)S(1)} %get-tuple-element.23), channel_id=1, source_target_pairs={{0,16},{16,32},{32,48},{48,64},{64,80},{80,96},{96,112},{112,128},... | collective-permute-start | bytes 73736 | tf_op jit(solution)/shard_map/ppermute | solution.py:223
  64.8 0.0 collective-permute-done.1
  64.8 0.8 collective-permute-done.prev_ref
  65.6 0.0 copy-done.4
  65.6 0.0 copy-start.5
  65.6 1.2 shard_map.97
  66.9 0.0 copy-done
  66.9 34.3 %all_to_all.31.got_ref = bf16[8,16,256]{2,1,0:T(8,128)(2,1)S(1)} all-to-all(bf16[8,16,256]{2,1,0:T(8,128)(2,1)S(1)} %get-tuple-element.19), channel_id=1, replica_groups=mesh['y'=8,'zh'=4,'core'=2,'x'=4,'zl'=4] {'y'}, dimensions={0} | all-to-all | bytes 131072 | tf_op jit(solution)/shard_map/all_to_all | solution.py:251
  101.1 1.4 shard_map.98
  102.5 3.4 %all-to-all-start.3 = ((bf16[8,32,256]{2,1,0:T(8,128)(2,1)}), bf16[8,32,256]{2,1,0:T(8,128)(2,1)S(1)}, u32[]{:S(2)}, u32[]{:S(2)}) async-start(bf16[8,32,256]{2,1,0:T(8,128)(2,1)} %shard_map.98), calls=%async_computation.3 | async-start | bytes 262144 | tf_op jit(solution)/shard_map/all_to_all | solution.py:262
  105.9 0.0 copy-done.5
  105.9 2.8 %shard_map.96 = (f32[136,256]{1,0:T(8,128)S(1)}, f32[136,256]{1,0:T(8,128)S(1)}) custom-call(bf16[3,128,256]{2,1,0:T(8,128)(2,1)S(1)} %fusion.12.proj_ref, bf16[3,16,256]{2,1,0:T(8,128)(2,1)S(1)} %collective-permute-done.prev_ref, bf16[3,16,256]{2,1,0:T(8,128)(2,1)S(1)} %slice.41.next_ref, bf16[128,256]{1,0:T(8,128)(2,1)S(1)} %fusion.16.back_ref, ...), custom_call_target="tpu_custom_call" | custom-call | flops 3000000000 | tf_op jit(solution)/shard_map/pallas_call | solution.py:163
  108.7 13.3 %all-to-all-done.3.got_ref = bf16[8,32,256]{2,1,0:T(8,128)(2,1)S(1)} async-done(((bf16[8,32,256]{2,1,0:T(8,128)(2,1)}), bf16[8,32,256]{2,1,0:T(8,128)(2,1)S(1)}, u32[]{:S(2)}, u32[]{:S(2)}) %all-to-all-start.3) | async-done | bytes 131104 | tf_op jit(solution)/shard_map/all_to_all | solution.py:262
  122.0 0.0 copy-start.1
  122.0 1.6 copy-done.1
  123.6 0.0 copy-start.7
  123.6 0.9 shard_map.99
  124.5 0.7 copy-done.7
  125.2 0.9 fusion.7
  126.1 4.9 %fusion.10 = bf16[4,4,128,256]{3,2,1,0:T(8,128)(2,1)S(1)} fusion(bf16[4,4,256,3,256]{4,2,1,0,3:T(8,128)(2,1)} %bitcast.72, bf16[3,128,256]{2,1,0:T(8,128)(2,1)S(1)} %get-tuple-element.21), kind=kOutput, calls=%fused_computation.8 | convolution fusion | flops 805830656 | bytes 7536640 | tf_op jit(solution)/shard_map/ptc,xzfpc->xztf/dot_general | solution.py:276
  131.0 0.1 pad_maximum_fusion
  131.2 26.3 %all_to_all.32 = bf16[4,4,256,256]{3,2,1,0:T(8,128)(2,1)S(1)} all-to-all(bf16[4,4,256,256]{3,2,1,0:T(8,128)(2,1)S(1)} %pad_maximum_fusion), channel_id=1, replica_groups=mesh['y'=8,'zh'=4,'core'=2,'x'=4,'zl'=4] {'x'}, dimensions={0} | all-to-all | bytes 4194304 | tf_op jit(solution)/shard_map/all_to_all | solution.py:278
  157.5 0.6 reduce_sum.24
  158.1 17.7 %all_to_all.33 = bf16[4,256,256]{2,1,0:T(8,128)(2,1)S(1)} all-to-all(bf16[4,256,256]{2,1,0:T(8,128)(2,1)S(1)} %reduce_sum.24), channel_id=1, replica_groups=mesh['y'=8,'zh'=4,'core'=2,'x'=4,'zl'=4] {'zl'}, dimensions={0} | all-to-all | bytes 1048576 | tf_op jit(solution)/shard_map/all_to_all | solution.py:280
  175.8 0.1 reduce_sum.25
  175.8 0.7 fusion.23
  (6 shorter events, 0.1 us)
Async XLA Ops:
  24.7 28.2 %all-to-all-start.1 = ((bf16[4,4,256,256]{3,2,1,0:T(8,128)(2,1)}), bf16[4,4,256,256]{3,2,1,0:T(8,128)(2,1)}, u32[]{:S(2)}, u32[]{:S(2)}) async-start(bf16[4,4,256,256]{3,2,1,0:T(8,128)(2,1)} %broadcast_in_dim.9), calls=%async_computation.1 | async-start | bytes 4194304 | tf_op jit(solution)/shard_map/all_to_all | solution.py:180
  36.7 20.3 %copy-start.6 = (bf16[256,4,4,256]{3,2,1,0:T(4,128)(2,1)}, bf16[256,4,4,256]{3,2,1,0:T(4,128)(2,1)S(1)}, u32[]{:S(2)}) copy-start(bf16[256,4,4,256]{3,2,1,0:T(4,128)(2,1)S(1)} %reshape.13) | copy-start | bytes 6291460
  57.0 4.0 %copy-start.2 = (f32[256,16]{0,1:T(8,128)S(1)}, f32[256,16]{0,1:T(8,128)}, u32[]{:S(2)}) copy-start(f32[256,16]{0,1:T(8,128)} %param.14) | copy-start | bytes 49156
  57.0 4.0 %copy-start.3 = (f32[256,16]{0,1:T(8,128)S(1)}, f32[256,16]{0,1:T(8,128)}, u32[]{:S(2)}) copy-start(f32[256,16]{0,1:T(8,128)} %param.13) | copy-start | bytes 49156
  57.0 8.6 %copy-start.4 = (f32[3,256,3]{1,2,0:T(4,128)S(1)}, f32[3,256,3]{1,2,0:T(4,128)}, u32[]{:S(2)}) copy-start(f32[3,256,3]{1,2,0:T(4,128)} %param.12) | copy-start | bytes 27652
  59.6 5.2 %collective-permute-start.1 = (bf16[4,16,256]{2,1,0:T(8,128)(2,1)S(1)}, bf16[4,16,256]{2,1,0:T(8,128)(2,1)S(1)}, u32[]{:S(2)}, u32[]{:S(2)}) collective-permute-start(bf16[4,16,256]{2,1,0:T(8,128)(2,1)S(1)} %pad_maximum_fusion.2), channel_id=1, source_target_pairs={{16,0},{32,16},{48,32},{64,48},{80,64},{96,80},{112,96},{128,112},... | collective-permute-start | bytes 98312 | tf_op jit(solution)/shard_map/ppermute | solution.py:225
  61.7 5.1 %copy-start = (f32[16,136,256]{2,1,0:T(8,128)}, f32[16,136,256]{2,1,0:T(8,128)S(1)}, u32[]{:S(2)}) copy-start(f32[16,136,256]{2,1,0:T(8,128)S(1)} %get-tuple-element.13.down_ref) | copy-start | bytes 6684676
  61.7 3.9 %collective-permute-start = (bf16[3,16,256]{2,1,0:T(8,128)(2,1)S(1)}, bf16[3,16,256]{2,1,0:T(8,128)(2,1)S(1)}, u32[]{:S(2)}, u32[]{:S(2)}) collective-permute-start(bf16[3,16,256]{2,1,0:T(8,128)(2,1)S(1)} %get-tuple-element.23), channel_id=1, source_target_pairs={{0,16},{16,32},{32,48},{48,64},{64,80},{80,96},{96,112},{112,128},... | collective-permute-start | bytes 73736 | tf_op jit(solution)/shard_map/ppermute | solution.py:223
  65.6 40.3 %copy-start.5 = (f32[256]{0:T(256)S(1)}, f32[256]{0:T(256)}, u32[]{:S(2)}) copy-start(f32[256]{0:T(256)} %param.15) | copy-start | bytes 3076
  102.5 19.5 %all-to-all-start.3 = ((bf16[8,32,256]{2,1,0:T(8,128)(2,1)}), bf16[8,32,256]{2,1,0:T(8,128)(2,1)S(1)}, u32[]{:S(2)}, u32[]{:S(2)}) async-start(bf16[8,32,256]{2,1,0:T(8,128)(2,1)} %shard_map.98), calls=%async_computation.3 | async-start | bytes 262144 | tf_op jit(solution)/shard_map/all_to_all | solution.py:262
  122.0 1.6 copy-start.1
  123.6 1.6 copy-start.7

commit v3 on v2

--- a/solution.py
+++ b/solution.py
@@ -10,7 +10,8 @@
 
 CTX = ("y", "zh", "core")
 TP = ("x", "zl")
-EDGE = 16
+EDGE = 8
+NEAR = 4
 AHEAD = 2
 BF16 = jnp.bfloat16
 F32 = jnp.float32
@@ -30,13 +31,16 @@
     filt_ref[...] = total
 
 
-def features(ext, proj_ref, prev_ref, next_ref, taps_ref, rows):
-    block = proj_ref.shape[1]
+def features(ext, proj_ref, taps_ref, rows):
+    block = proj_ref.shape[1] - EDGE - 2 * NEAR
     out = []
     for p in range(3):
-        ext[p, :EDGE] = prev_ref[p].astype(F32)
-        ext[p, EDGE : EDGE + block] = proj_ref[p].astype(F32)
-        ext[p, EDGE + block :] = next_ref[p].astype(F32)
+        proj = proj_ref[p].astype(F32)
+        edge = proj[block : block + EDGE]
+        near = proj[block + EDGE :]
+        ext[p, :EDGE] = edge
+        ext[p, EDGE : EDGE + block] = proj[:block]
+        ext[p, EDGE + block :] = near
         total = taps_ref[p, 0:1, :] * ext[p, EDGE : EDGE + rows]
         for k in range(1, 3):
             total = total + taps_ref[p, k : k + 1, :] * ext[p, EDGE - k : EDGE - k + rows]
@@ -44,20 +48,23 @@
     return out
 
 
-def back_rows(back_ref, back_next_ref, rows):
-    whole = jnp.concatenate([back_ref[...].astype(F32), back_next_ref[...].astype(F32)], axis=0)
+def back_rows(back_ref, rows):
+    block = back_ref.shape[0] - EDGE - 2 * NEAR
+    back = back_ref[...].astype(F32)
+    near = pltpu.roll(back[block + EDGE :], NEAR, 0)
     row = lax.broadcasted_iota(jnp.int32, (rows, 1), 0)
-    return jnp.where(row < back_ref.shape[0] + AHEAD, whole[:rows], 0.0), row
+    whole = jnp.concatenate([back[:block], near], axis=0)
+    return jnp.where(row < block + AHEAD, whole, 0.0), row
 
 
 def state_kernel(
-    place_ref, proj_ref, prev_ref, next_ref, back_ref, back_next_ref, taps_ref, rates_ref, up_ref, down_ref,
+    place_ref, proj_ref, back_ref, taps_ref, rates_ref, up_ref, down_ref,
     fwd_ref, bwd_ref, send_ref, ext,
 ):
     order, rows, _ = up_ref.shape
-    block = proj_ref.shape[1]
-    query, key_part, value_part = features(ext, proj_ref, prev_ref, next_ref, taps_ref, rows)
-    back, row = back_rows(back_ref, back_next_ref, rows)
+    block = rows - 8
+    query, key_part, value_part = features(ext, proj_ref, taps_ref, rows)
+    back, row = back_rows(back_ref, rows)
     gated = jnp.where(row < block, key_part * value_part, 0.0)
     grad_conv = jnp.where(row >= AHEAD, back * query, 0.0)
     for r in range(order):
@@ -94,12 +101,12 @@
 
 
 def local_kernel(
-    proj_ref, prev_ref, next_ref, back_ref, back_next_ref, taps_ref, res_ref, skip_ref, filt_ref,
+    proj_ref, back_ref, taps_ref, res_ref, skip_ref, filt_ref,
     conv_ref, grad_ref, ext, pad,
 ):
     rows, width = conv_ref.shape
-    query, key_part, value_part = features(ext, proj_ref, prev_ref, next_ref, taps_ref, rows)
-    back, _ = back_rows(back_ref, back_next_ref, rows)
+    query, key_part, value_part = features(ext, proj_ref, taps_ref, rows)
+    back, _ = back_rows(back_ref, rows)
     zero = jnp.zeros((8, width), F32)
     pad[0, :8] = zero
     pad[0, 8:] = key_part * value_part
@@ -127,14 +134,14 @@
 
 
 def finish_kernel(
-    proj_ref, prev_ref, next_ref, back_ref, back_next_ref, taps_ref, res_ref, up_ref, down_ref,
+    proj_ref, back_ref, taps_ref, res_ref, up_ref, down_ref,
     conv_ref, grad_ref, got_ref,
     hidden_ref, out_ref, ext, feat,
 ):
     order, rows, _ = up_ref.shape
-    block = proj_ref.shape[1]
-    query, key_part, value_part = features(ext, proj_ref, prev_ref, next_ref, taps_ref, rows)
-    back, _ = back_rows(back_ref, back_next_ref, rows)
+    block = rows - 8
+    query, key_part, value_part = features(ext, proj_ref, taps_ref, rows)
+    back, _ = back_rows(back_ref, rows)
     conv_out = conv_ref[...]
     grad_gated = grad_ref[...]
     states = jnp.sum(got_ref[...].astype(F32), axis=0)
@@ -208,23 +215,26 @@
         rates,
         res,
     )
-    both = jnp.concatenate([tokens, cotangent], axis=0)
+    to_next = [(i, i + 1) for i in range(n_ctx - 1)]
+    to_prev = [(i + 1, i) for i in range(n_ctx - 1)]
+    edge = lax.ppermute(tokens[block - EDGE :], CTX, to_next)
+    near = jnp.concatenate([tokens[:NEAR], cotangent[:NEAR]], axis=0)
+    near = lax.ppermute(near, CTX, to_prev)
+    both = jnp.concatenate([tokens, edge, near, cotangent], axis=0)
     both = spread(spread(both, "zl", n_zl), "x", n_x)
+    ends = block + EDGE + 2 * NEAR
+    whole_in = both[:, :, :ends]
+    whole_grad = jnp.concatenate([both[:, :, ends:], both[:, :, block:ends]], axis=2)
     weight_in = input_weight.reshape(n_x, n_zl, part, 3, width)
     weight_out = output_weight.reshape(width, n_x, n_zl, part)
     proj = jnp.einsum(
-        "xztf,xzfpc->ptc", both[:, :, :block], weight_in, preferred_element_type=F32
+        "xztf,xzfpc->ptc", whole_in, weight_in, preferred_element_type=F32
     ).astype(BF16)
     back = jnp.einsum(
-        "xztf,cxzf->tc", both[:, :, block:], weight_out, preferred_element_type=F32
+        "xztf,cxzf->tc", whole_grad, weight_out, preferred_element_type=F32
     ).astype(BF16)
-    to_next = [(i, i + 1) for i in range(n_ctx - 1)]
-    to_prev = [(i + 1, i) for i in range(n_ctx - 1)]
-    prev = lax.ppermute(proj[:, block - EDGE :], CTX, to_next)
-    first = jnp.concatenate([proj[:, :EDGE], back[None, :EDGE]], axis=0)
-    first = lax.ppermute(first, CTX, to_prev)
-    common = (proj, prev, first[:3], back, first[3], taps)
-    ext = pltpu.VMEM((3, block + 2 * EDGE, width), F32)
+    common = (proj, back, taps)
+    ext = pltpu.VMEM((3, rows + EDGE, width), F32)
     group = lax.axis_index("y")
     member = lax.axis_index("zh") * sizes["core"] + lax.axis_index("core")
     place = jnp.stack([group, member]).astype(jnp.int32)

time: 178 us -> 184 us (1.034)
  waiting for transfers between devices: 30.3 us -> 41.9 us
  blocking collectives: 99.8 us -> 90.3 us
  local copies, waits for them, and re-layouts: 7.93 us -> 13.3 us
    ppermute x2, waiting for transfers between devices: 0.8 us -> 10.5 us  [the longest x1 10.5 us: shards(): near = lax.ppermute(near, CTX, to_prev)]
    all_to_all x1, blocking collectives: 34.3 us -> 26.1 us  [shards(): got = lax.all_to_all(send, 'y', 0, 0, tiled=True)]
    slice x2 -> x5, local copies, waits for them, and re-layouts: 0.01 us -> 4.44 us  [the longest x2 1.38 us: shards(): near = jnp.concatenate([tokens[:NEAR], cotangent[:NEAR]], axis=0)]
    all_to_all x1, starting transfers between devices: 3.37 us -> 7.72 us  [shards(): states = lax.all_to_all(send, ('zh', 'core'), 0, 0, tiled=True)]
    all_to_all x1, starting transfers between devices: 8.67 us -> 5.04 us  [spread(): return lax.all_to_all(copies, axis, 0, 0, tiled=True)]
    all_to_all x1, waiting for transfers between devices: 16.1 us -> 19 us  [spread(): return lax.all_to_all(copies, axis, 0, 0, tiled=True)]
    all_to_all x1, blocking collectives: 21.5 us -> 19.3 us  [spread(): return lax.all_to_all(copies, axis, 0, 0, tiled=True)]
    unnamed x16 -> x20, local copies, waits for them, and re-layouts: 2.36 us -> 3.77 us
where the time goes in v3:
time: 184 us; the launch traced here: 182 us
  blocking collectives  90.3 us (49%)
  waiting for transfers between devices  41.9 us (23%)
  starting transfers between devices  15.8 us (9%)
  local copies, waits for them, and re-layouts  13.3 us (7%)
  matrix products  11.5 us (6%)
  Pallas kernels  6.85 us (4%)
    all_to_all x1, blocking collectives, shards(): terms = lax.all_to_all(terms, 'x', 0, 0, tiled=True)  27.2 us
    all_to_all x1, blocking collectives, shards(): got = lax.all_to_all(send, 'y', 0, 0, tiled=True)  26.1 us
    all_to_all x1, blocking collectives, spread(): return lax.all_to_all(copies, axis, 0, 0, tiled=True)  19.3 us
    all_to_all x1, waiting for transfers between devices, spread(): return lax.all_to_all(copies, axis, 0, 0, tiled=True)  19 us
    all_to_all x1, blocking collectives, shards(): terms = lax.all_to_all(terms, 'zl', 0, 0, tiled=True)  17.5 us
    all_to_all x1, waiting for transfers between devices, shards(): states = lax.all_to_all(send, ('zh', 'core'), 0, 0, tiled=True)  12.4 us
    ppermute x1, waiting for transfers between devices, shards(): near = lax.ppermute(near, CTX, to_prev)  10.5 us
    all_to_all x1, starting transfers between devices, shards(): states = lax.all_to_all(send, ('zh', 'core'), 0, 0, tiled=True)  7.72 us
  transfers between devices with their start and end apart: 4, of which 3 were waited for; matrix products, arithmetic and copies ran while one was open for 2% of the time, Pallas kernels for 2%

profile of v3, /device:TPU:6, one launch (start us, length us, event | category | flops | bytes accessed | tf_op | source)
XLA Modules:
  0.0 182.2 jit_solution(7810906777839354379)
XLA Ops:
  0.6 0.7 slice.24
  1.3 1.7 collective-permute-start
  3.1 0.7 slice.25
  3.7 0.7 slice.26
  4.4 1.3 collective-permute-start.1
  5.7 0.0 collective-permute-done
  5.8 10.5 %collective-permute-done.1 = bf16[8,256]{1,0:T(8,128)(2,1)S(1)} collective-permute-done((bf16[8,256]{1,0:T(8,128)(2,1)S(1)}, bf16[8,256]{1,0:T(8,128)(2,1)S(1)}, u32[]{:S(2)}, u32[]{:S(2)}) %collective-permute-start.1) | collective-permute-done | bytes 4128 | tf_op jit(solution)/shard_map/ppermute | solution.py:222
  16.3 0.9 pad_maximum_fusion.1
  17.2 19.3 %all_to_all.30 = bf16[4,272,256]{2,1,0:T(8,128)(2,1)S(1)} all-to-all(bf16[4,272,256]{2,1,0:T(8,128)(2,1)S(1)} %broadcast_in_dim.6), channel_id=1, replica_groups=mesh['y'=8,'zh'=4,'core'=2,'x'=4,'zl'=4] {'zl'}, dimensions={0} | all-to-all | bytes 1114112 | tf_op jit(solution)/shard_map/all_to_all | solution.py:187
  36.6 1.6 broadcast_in_dim.7
  38.2 5.0 %all-to-all-start.1 = ((bf16[4,4,272,256]{3,2,1,0:T(8,128)(2,1)}), bf16[4,4,272,256]{3,2,1,0:T(8,128)(2,1)}, u32[]{:S(2)}, u32[]{:S(2)}) async-start(bf16[4,4,272,256]{3,2,1,0:T(8,128)(2,1)} %broadcast_in_dim.7), calls=%async_computation.1 | async-start | bytes 4456448 | tf_op jit(solution)/shard_map/all_to_all | solution.py:187
  43.2 0.0 copy-done.9
  43.2 2.8 %reshape.13 = bf16[256,4,4,256]{3,2,1,0:T(4,128)(2,1)} reshape(bf16[256,4096]{1,0:T(8,128)(2,1)S(1)} %copy-done.9) | data formatting | bytes 4194304 | tf_op jit(solution)/shard_map/reshape | solution.py:229
  46.0 0.0 copy-done.3
  46.0 0.0 copy-done.4
  46.0 0.7 shard_map.95
  46.7 0.0 copy-start
  46.7 1.4 copy-done
  48.1 0.1 pad_add_fusion.place_ref
  48.2 19.0 %all-to-all-done.1 = bf16[4,4,272,256]{3,2,1,0:T(8,128)(2,1)} async-done(((bf16[4,4,272,256]{3,2,1,0:T(8,128)(2,1)}), bf16[4,4,272,256]{3,2,1,0:T(8,128)(2,1)}, u32[]{:S(2)}, u32[]{:S(2)}) %all-to-all-start.1) | async-done | bytes 2228256 | tf_op jit(solution)/shard_map/all_to_all | solution.py:187
  67.1 1.1 slice.34
  68.2 1.3 slice.33
  69.5 0.0 copy-done.7
  69.5 1.3 fusion.21.back_ref
  70.9 0.0 copy-start.1
  70.9 0.0 copy-start.5
  70.9 4.4 %fusion.15.proj_ref = bf16[3,144,256]{2,1,0:T(8,128)(2,1)S(1)} fusion(bf16[4,4,256,3,256]{4,2,1,0,3:T(8,128)(2,1)} %bitcast.69, bf16[4,4,272,256]{3,2,1,0:T(8,128)(2,1)} %all-to-all-done.1), kind=kOutput, calls=%fused_computation.15 | convolution fusion | flops 906080256 | bytes 7692288 | tf_op jit(solution)/shard_map/xztf,xzfpc->ptc/dot_general | solution.py:230
  75.3 0.0 copy-done.1
  75.3 0.0 copy-done.5
  75.3 0.0 copy-start.6
  75.3 1.2 shard_map.97
  76.5 26.1 %all_to_all.31.got_ref = bf16[8,16,256]{2,1,0:T(8,128)(2,1)S(1)} all-to-all(bf16[8,16,256]{2,1,0:T(8,128)(2,1)S(1)} %get-tuple-element.19), channel_id=1, replica_groups=mesh['y'=8,'zh'=4,'core'=2,'x'=4,'zl'=4] {'y'}, dimensions={0} | all-to-all | bytes 131072 | tf_op jit(solution)/shard_map/all_to_all | solution.py:261
  102.6 1.4 shard_map.98
  104.0 7.7 %all-to-all-start.3 = ((bf16[8,32,256]{2,1,0:T(8,128)(2,1)}), bf16[8,32,256]{2,1,0:T(8,128)(2,1)S(1)}, u32[]{:S(2)}, u32[]{:S(2)}) async-start(bf16[8,32,256]{2,1,0:T(8,128)(2,1)} %shard_map.98), calls=%async_computation.3 | async-start | bytes 262144 | tf_op jit(solution)/shard_map/all_to_all | solution.py:272
  111.7 0.0 copy-done.6
  111.7 2.8 %shard_map.96 = (f32[136,256]{1,0:T(8,128)S(1)}, f32[136,256]{1,0:T(8,128)S(1)}) custom-call(bf16[3,144,256]{2,1,0:T(8,128)(2,1)S(1)} %fusion.15.proj_ref, bf16[144,256]{1,0:T(8,128)(2,1)S(1)} %fusion.21.back_ref, f32[3,3,256]{2,1,0:T(4,128)S(1)} %bitcast.66, f32[16,256]{1,0:T(8,128)S(1)} %bitcast.63, f32[1,256]{1,0:T(1,128)S(1)} %bitcast.68, ...), custom_call_target="tpu_custom_call" | custom-call | flops 3000000000 | tf_op jit(solution)/shard_map/pallas_call | solution.py:170
  114.5 12.4 %all-to-all-done.3.got_ref = bf16[8,32,256]{2,1,0:T(8,128)(2,1)S(1)} async-done(((bf16[8,32,256]{2,1,0:T(8,128)(2,1)}), bf16[8,32,256]{2,1,0:T(8,128)(2,1)S(1)}, u32[]{:S(2)}, u32[]{:S(2)}) %all-to-all-start.3) | async-done | bytes 131104 | tf_op jit(solution)/shard_map/all_to_all | solution.py:272
  126.9 1.6 copy-done.2
  128.5 0.8 shard_map.99
  129.4 0.8 copy-done.8
  130.1 0.9 fusion.7
  131.0 4.9 %fusion.10 = bf16[4,4,128,256]{3,2,1,0:T(8,128)(2,1)S(1)} fusion(bf16[4,4,256,3,256]{4,2,1,0,3:T(8,128)(2,1)} %bitcast.70, bf16[3,128,256]{2,1,0:T(8,128)(2,1)S(1)} %get-tuple-element.21), kind=kOutput, calls=%fused_computation.8 | convolution fusion | flops 805830656 | bytes 7536640 | tf_op jit(solution)/shard_map/ptc,xzfpc->xztf/dot_general | solution.py:286
  135.9 0.2 pad_maximum_fusion
  136.1 27.2 %all_to_all.32 = bf16[4,4,256,256]{3,2,1,0:T(8,128)(2,1)S(1)} all-to-all(bf16[4,4,256,256]{3,2,1,0:T(8,128)(2,1)S(1)} %pad_maximum_fusion), channel_id=1, replica_groups=mesh['y'=8,'zh'=4,'core'=2,'x'=4,'zl'=4] {'x'}, dimensions={0} | all-to-all | bytes 4194304 | tf_op jit(solution)/shard_map/all_to_all | solution.py:288
  163.3 0.6 reduce_sum.24
  163.9 17.5 %all_to_all.33 = bf16[4,256,256]{2,1,0:T(8,128)(2,1)S(1)} all-to-all(bf16[4,256,256]{2,1,0:T(8,128)(2,1)S(1)} %reduce_sum.24), channel_id=1, replica_groups=mesh['y'=8,'zh'=4,'core'=2,'x'=4,'zl'=4] {'zl'}, dimensions={0} | all-to-all | bytes 1048576 | tf_op jit(solution)/shard_map/all_to_all | solution.py:290
  181.4 0.1 reduce_sum.25
  181.5 0.7 fusion.29
  (8 shorter events, 0.1 us)
Async XLA Ops:
  1.3 4.4 %collective-permute-start = (bf16[8,256]{1,0:T(8,128)(2,1)S(1)}, bf16[8,256]{1,0:T(8,128)(2,1)S(1)}, u32[]{:S(2)}, u32[]{:S(2)}) collective-permute-start(bf16[8,256]{1,0:T(8,128)(2,1)S(1)} %slice.24), channel_id=1, source_target_pairs={{0,16},{16,32},{32,48},{48,64},{64,80},{80,96},{96,112},{112,128},... | collective-permute-start | bytes 12296 | tf_op jit(solution)/shard_map/ppermute | solution.py:220
  4.4 11.9 %collective-permute-start.1 = (bf16[8,256]{1,0:T(8,128)(2,1)S(1)}, bf16[8,256]{1,0:T(8,128)(2,1)S(1)}, u32[]{:S(2)}, u32[]{:S(2)}) collective-permute-start(bf16[8,256]{1,0:T(8,128)(2,1)S(1)} %pad_maximum_fusion.2), channel_id=1, source_target_pairs={{16,0},{32,16},{48,32},{64,48},{80,64},{96,80},{112,96},{128,112},... | collective-permute-start | bytes 12296 | tf_op jit(solution)/shard_map/ppermute | solution.py:222
  38.1 5.0 %copy-start.9 = (bf16[256,4096]{1,0:T(8,128)(2,1)S(1)}, bf16[256,4096]{1,0:T(8,128)(2,1)}, u32[]{:S(2)}) copy-start(bf16[256,4096]{1,0:T(8,128)(2,1)} %param.11) | copy-start | bytes 6291460
  38.2 29.0 %all-to-all-start.1 = ((bf16[4,4,272,256]{3,2,1,0:T(8,128)(2,1)}), bf16[4,4,272,256]{3,2,1,0:T(8,128)(2,1)}, u32[]{:S(2)}, u32[]{:S(2)}) async-start(bf16[4,4,272,256]{3,2,1,0:T(8,128)(2,1)} %broadcast_in_dim.7), calls=%async_computation.1 | async-start | bytes 4456448 | tf_op jit(solution)/shard_map/all_to_all | solution.py:187
  43.2 2.8 %copy-start.3 = (f32[256,16]{0,1:T(8,128)S(1)}, f32[256,16]{0,1:T(8,128)}, u32[]{:S(2)}) copy-start(f32[256,16]{0,1:T(8,128)} %param.14) | copy-start | bytes 49156
  43.2 2.8 %copy-start.4 = (f32[256,16]{0,1:T(8,128)S(1)}, f32[256,16]{0,1:T(8,128)}, u32[]{:S(2)}) copy-start(f32[256,16]{0,1:T(8,128)} %param.13) | copy-start | bytes 49156
  46.7 1.4 copy-start
  67.1 2.4 %copy-start.7 = (bf16[256,4,4,256]{3,2,1,0:T(4,128)(2,1)S(1)}, bf16[256,4,4,256]{3,2,1,0:T(4,128)(2,1)}, u32[]{:S(2)}) copy-start(bf16[256,4,4,256]{3,2,1,0:T(4,128)(2,1)} %reshape.13) | copy-start | bytes 6291460
  70.9 4.4 %copy-start.1 = (f32[16,136,256]{2,1,0:T(8,128)S(1)}, f32[16,136,256]{2,1,0:T(8,128)}, u32[]{:S(2)}) copy-start(f32[16,136,256]{2,1,0:T(8,128)} %copy-done) | copy-start | bytes 6684676
  70.9 4.4 %copy-start.5 = (f32[3,256,3]{1,2,0:T(4,128)S(1)}, f32[3,256,3]{1,2,0:T(4,128)}, u32[]{:S(2)}) copy-start(f32[3,256,3]{1,2,0:T(4,128)} %param.12) | copy-start | bytes 27652
  75.3 36.4 %copy-start.6 = (f32[256]{0:T(256)S(1)}, f32[256]{0:T(256)}, u32[]{:S(2)}) copy-start(f32[256]{0:T(256)} %param.15) | copy-start | bytes 3076
  104.0 22.9 %all-to-all-start.3 = ((bf16[8,32,256]{2,1,0:T(8,128)(2,1)}), bf16[8,32,256]{2,1,0:T(8,128)(2,1)S(1)}, u32[]{:S(2)}, u32[]{:S(2)}) async-start(bf16[8,32,256]{2,1,0:T(8,128)(2,1)} %shard_map.98), calls=%async_computation.3 | async-start | bytes 262144 | tf_op jit(solution)/shard_map/all_to_all | solution.py:272
  126.9 1.6 copy-start.2
  128.5 1.6 copy-start.8

commit v4 on v3

--- a/solution.py
+++ b/solution.py
@@ -13,6 +13,7 @@
 EDGE = 8
 NEAR = 4
 AHEAD = 2
+GRANT = 16 * 2**20
 BF16 = jnp.bfloat16
 F32 = jnp.float32
 
@@ -49,12 +50,12 @@
 
 
 def back_rows(back_ref, rows):
-    block = back_ref.shape[0] - EDGE - 2 * NEAR
+    ends = EDGE + 2 * NEAR
     back = back_ref[...].astype(F32)
-    near = pltpu.roll(back[block + EDGE :], NEAR, 0)
+    near = pltpu.roll(back[EDGE:ends], NEAR, 0)
     row = lax.broadcasted_iota(jnp.int32, (rows, 1), 0)
-    whole = jnp.concatenate([back[:block], near], axis=0)
-    return jnp.where(row < block + AHEAD, whole, 0.0), row
+    whole = jnp.concatenate([back[ends:], near], axis=0)
+    return jnp.where(row < back_ref.shape[0] - ends + AHEAD, whole, 0.0), row
 
 
 def state_kernel(
@@ -174,8 +175,114 @@
         in_specs=specs,
         out_specs=jax.tree.map(lambda _: whole, outs),
         cost_estimate=cost,
-        compiler_params=pltpu.CompilerParams(vmem_limit_bytes=40 * 2**20),
+        compiler_params=pltpu.CompilerParams(vmem_limit_bytes=GRANT),
     )(*args)
+
+
+def project_kernel(counts, rows, first, index_ref, *refs):
+    pieces, refs = refs[: len(counts)], refs[len(counts) :]
+    weight_in, weight_out = refs[:2]
+    old = refs[2] if not first else None
+    total = refs[-2] if len(refs) == 5 else refs[-1]
+    step = pl.program_id(0)
+
+    @pl.when(step == 0)
+    def _():
+        total[...] = jnp.zeros_like(total) if first else old[...]
+
+    start = 0
+    for piece, count in zip(pieces, counts):
+
+        @pl.when((step >= start) & (step < start + count))
+        def _(piece=piece, start=start):
+            part = piece[step - start]
+            for p in range(3):
+                total[p] += jnp.dot(part[:rows], weight_in[p], preferred_element_type=F32)
+            total[3] += lax.dot_general(
+                part[-rows:], weight_out[...], (((1,), (1,)), ((), ())), preferred_element_type=F32
+            )
+
+        start += count
+
+
+def project_last_kernel(counts, rows, index_ref, *refs):
+    out, total = refs[-2:]
+    project_kernel(counts, rows, False, index_ref, *refs[:-2], total)
+
+    @pl.when(pl.program_id(0) == sum(counts) - 1)
+    def _():
+        out[...] = total[...].astype(BF16)
+
+
+def project(index, pieces, weight_in, weight_out, rows, old=None, last=False):
+    counts = [piece.shape[0] for piece in pieces]
+    width = weight_out.shape[0]
+    part = pieces[0].shape[2]
+    whole = pl.BlockSpec(memory_space=pltpu.VMEM)
+    if last:
+        kernel = functools.partial(project_last_kernel, counts, rows)
+    else:
+        kernel = functools.partial(project_kernel, counts, rows, old is None)
+    return pl.pallas_call(
+        kernel,
+        grid_spec=pltpu.PrefetchScalarGridSpec(
+            num_scalar_prefetch=1,
+            grid=(sum(counts),),
+            in_specs=[whole] * len(pieces)
+            + [
+                pl.BlockSpec((3, part, width), lambda s, index: (0, index[s], 0)),
+                pl.BlockSpec((width, part), lambda s, index: (0, index[s])),
+            ]
+            + [whole] * (old is not None),
+            out_specs=whole,
+            scratch_shapes=[pltpu.VMEM((4, rows, width), F32)] if last else [],
+        ),
+        out_shape=shape(4, rows, width, dtype=BF16 if last else F32),
+        cost_estimate=pl.CostEstimate(
+            flops=8 * sum(counts) * rows * part * width,
+            bytes_accessed=8 * sum(counts) * part * width,
+            transcendentals=0,
+        ),
+        compiler_params=pltpu.CompilerParams(vmem_limit_bytes=GRANT),
+    )(index, *pieces, weight_in, weight_out, *([] if old is None else [old]))
+
+
+def partials_kernel(index_ref, hidden, grad, weight_in, weight_out, out):
+    block = hidden.shape[0]
+    mixed = jnp.dot(hidden[...], weight_out[...], preferred_element_type=F32)
+    out[0, :block] = mixed.astype(BF16)
+    total = jnp.zeros_like(mixed)
+    for p in range(3):
+        total = total + lax.dot_general(
+            grad[p], weight_in[p], (((1,), (1,)), ((), ())), preferred_element_type=F32
+        )
+    out[0, block:] = total.astype(BF16)
+
+
+def partials(index, count, hidden, grad, weight_in, weight_out, part):
+    block, width = hidden.shape
+    whole = pl.BlockSpec(memory_space=pltpu.VMEM)
+    return pl.pallas_call(
+        partials_kernel,
+        grid_spec=pltpu.PrefetchScalarGridSpec(
+            num_scalar_prefetch=1,
+            grid=(count,),
+            in_specs=[
+                whole,
+                whole,
+                pl.BlockSpec((3, part, width), lambda s, index: (0, index[s], 0)),
+                pl.BlockSpec((width, part), lambda s, index: (0, index[s])),
+            ],
+            out_specs=pl.BlockSpec((1, 2 * block, part), lambda s, index: (s, 0, 0)),
+        ),
+        out_shape=shape(count, 2 * block, part, dtype=BF16),
+        cost_estimate=pl.CostEstimate(
+            flops=8 * count * block * part * width,
+            bytes_accessed=8 * count * part * width,
+            transcendentals=0,
+        ),
+        compiler_params=pltpu.CompilerParams(vmem_limit_bytes=GRANT),
+    )(index, hidden, grad, weight_in, weight_out)
 
 
 def shape(*dims, dtype=F32):
@@ -221,18 +328,26 @@
     near = jnp.concatenate([tokens[:NEAR], cotangent[:NEAR]], axis=0)
     near = lax.ppermute(near, CTX, to_prev)
     both = jnp.concatenate([tokens, edge, near, cotangent], axis=0)
-    both = spread(spread(both, "zl", n_zl), "x", n_x)
-    ends = block + EDGE + 2 * NEAR
-    whole_in = both[:, :, :ends]
-    whole_grad = jnp.concatenate([both[:, :, ends:], both[:, :, block:ends]], axis=2)
-    weight_in = input_weight.reshape(n_x, n_zl, part, 3, width)
-    weight_out = output_weight.reshape(width, n_x, n_zl, part)
-    proj = jnp.einsum(
-        "xztf,xzfpc->ptc", whole_in, weight_in, preferred_element_type=F32
-    ).astype(BF16)
-    back = jnp.einsum(
-        "xztf,cxzf->tc", whole_grad, weight_out, preferred_element_type=F32
-    ).astype(BF16)
+    near_pieces = spread(both, "zl", n_zl)
+    half = n_zl // 2
+    right = [(i, (i + 1) % n_x) for i in range(n_x)]
+    left = [(i, (i - 1) % n_x) for i in range(n_x)]
+    from_left = lax.ppermute(near_pieces, "x", right)
+    from_right = lax.ppermute(near_pieces, "x", left)
+    far_left = lax.ppermute(from_left[:half], "x", right)
+    far_right = lax.ppermute(from_right[half:], "x", left)
+    x = lax.axis_index("x")
+    own, after, far, before = (
+        (lax.rem(x + k, n_x) * n_zl + jnp.arange(n_zl)).astype(jnp.int32) for k in range(n_x)
+    )
+    weight_in = input_weight.transpose(1, 0, 2)
+    weights = (weight_in, output_weight, block + EDGE + 2 * NEAR)
+    total = project(own, [near_pieces], *weights)
+    total = project(
+        jnp.concatenate([before, after]), [from_left, from_right], *weights, old=total
+    )
+    total = project(far, [far_left, far_right], *weights, old=total, last=True)
+    proj, back = total[:3], total[3]
     common = (proj, back, taps)
     ext = pltpu.VMEM((3, rows + EDGE, width), F32)
     group = lax.axis_index("y")
@@ -282,13 +397,25 @@
         grad,
         states,
     )
-    mixed = jnp.einsum("tc,cxzf->xztf", hidden, weight_out, preferred_element_type=F32)
-    grad_tok = jnp.einsum("ptc,xzfpc->xztf", grad_proj, weight_in, preferred_element_type=F32)
-    terms = jnp.concatenate([mixed.astype(BF16), grad_tok.astype(BF16)], axis=2)
-    terms = lax.all_to_all(terms, "x", 0, 0, tiled=True)
-    terms = jnp.sum(terms.astype(F32), axis=0).astype(BF16)
-    terms = lax.all_to_all(terms, "zl", 0, 0, tiled=True)
-    total = jnp.sum(terms.astype(F32), axis=0).astype(BF16)
+    def terms(index):
+        return partials(
+            index, index.shape[0], hidden, grad_proj, weight_in, output_weight, part
+        )
+
+    def add(*arrays):
+        return sum(a.astype(F32) for a in arrays).astype(BF16)
+
+    far_right = lax.ppermute(terms(far[:half]), "x", right)
+    far_left = lax.ppermute(terms(far[half:]), "x", left)
+    to_right = terms(after)
+    to_left = terms(before)
+    to_right = jnp.concatenate([add(to_right[:half], far_right), to_right[half:]], axis=0)
+    to_left = jnp.concatenate([to_left[:half], add(to_left[half:], far_left)], axis=0)
+    from_left = lax.ppermute(to_right, "x", right)
+    from_right = lax.ppermute(to_left, "x", left)
+    summed = add(terms(own), from_left, from_right)
+    summed = lax.all_to_all(summed, "zl", 0, 0, tiled=True)
+    total = jnp.sum(summed.astype(F32), axis=0).astype(BF16)
     return total[:block], total[block:]
 
 

time: 184 us -> 177 us (0.962)
  blocking collectives: 90.3 us -> 54.9 us
  starting transfers between devices: 15.8 us -> 48.6 us
  Pallas kernels: 6.85 us -> 24 us
  matrix products: 11.5 us -> 0 us
  waiting for transfers between devices: 41.9 us -> 30.7 us
    ppermute x0 -> x8, starting transfers between devices: none -> 39 us  [the longest x1 15.7 us: shards(): from_left = lax.ppermute(near_pieces, 'x', right)]
    all_to_all x2 -> x1, blocking collectives: 44.8 us -> 15.2 us  [shards(): summed = lax.all_to_all(summed, 'zl', 0, 0, tiled=True)]
    all_to_all x1 -> x0, waiting for transfers between devices: 19 us -> none  [spread(): return lax.all_to_all(copies, axis, 0, 0, tiled=True)]
    ppermute x0 -> x8, waiting for transfers between devices: none -> 17.4 us  [the longest x1 7.06 us: shards(): from_left = lax.ppermute(near_pieces, 'x', right)]
    pallas_call x0 -> x8, Pallas kernels: none -> 17 us  [the longest x3 8.49 us: project(): pl.pallas_call(kernel, grid_spec=pltpu.PrefetchScalarGridSpec(num_scalar_...]
    dot_general x4 -> x0, matrix products: 11.5 us -> none  [the longest x1 4.92 us: shards(): jnp.einsum('ptc,xzfpc->xztf', grad_proj, weight_in, preferred_element_typ...]
    ppermute x1, waiting for transfers between devices: 10.5 us -> 0.01 us  [shards(): near = lax.ppermute(near, CTX, to_prev)]
    unnamed x20 -> x32, local copies, waits for them, and re-layouts: 3.77 us -> 11.1 us
  transfers between devices with their start and end apart: 4 -> 11, of which waited for: 3 -> 6; matrix products, arithmetic and copies ran while one was open for 2% -> 1% of each run, Pallas kernels for 2% -> 10%
where the time goes in v4:
time: 177 us; the launch traced here: 176 us
  blocking collectives  54.9 us (31%)
  starting transfers between devices  48.6 us (27%)
  waiting for transfers between devices  30.7 us (17%)
  Pallas kernels  24 us (14%)
  local copies, waits for them, and re-layouts  15.1 us (9%)
    all_to_all x1, blocking collectives, shards(): got = lax.all_to_all(send, 'y', 0, 0, tiled=True)  22 us
    all_to_all x1, blocking collectives, spread(): return lax.all_to_all(copies, axis, 0, 0, tiled=True)  17.7 us
    ppermute x1, starting transfers between devices, shards(): from_left = lax.ppermute(near_pieces, 'x', right)  15.7 us
    all_to_all x1, blocking collectives, shards(): summed = lax.all_to_all(summed, 'zl', 0, 0, tiled=True)  15.2 us
    all_to_all x1, waiting for transfers between devices, shards(): states = lax.all_to_all(send, ('zh', 'core'), 0, 0, tiled=True)  12.5 us
    unnamed x32, local copies, waits for them, and re-layouts  11.1 us
    pallas_call x3, Pallas kernels, project(): pl.pallas_call(kernel, grid_spec=pltpu.PrefetchScalarGridSpec(num_scalar_...  8.49 us
    pallas_call x5, Pallas kernels, partials(): pl.pallas_call(partials_kernel, grid_spec=pltpu.PrefetchScalarGridSpec(nu...  8.47 us
  transfers between devices with their start and end apart: 11, of which 6 were waited for; matrix products, arithmetic and copies ran while one was open for 1% of the time, Pallas kernels for 10%

profile of v4, /device:TPU:6, one launch (start us, length us, event | category | flops | bytes accessed | tf_op | source)
XLA Modules:
  0.0 176.0 jit_solution(6089104339788252814)
XLA Ops:
  0.6 0.8 slice.46
  1.5 0.7 slice.47
  2.2 1.3 collective-permute-start.1
  3.5 0.7 slice.45
  4.2 3.0 %collective-permute-start = (bf16[8,256]{1,0:T(8,128)(2,1)S(1)}, bf16[8,256]{1,0:T(8,128)(2,1)S(1)}, u32[]{:S(2)}, u32[]{:S(2)}) collective-permute-start(bf16[8,256]{1,0:T(8,128)(2,1)S(1)} %slice.45), channel_id=1, source_target_pairs={{0,16},{16,32},{32,48},{48,64},{64,80},{80,96},{96,112},{112,128},... | collective-permute-start | bytes 12296 | tf_op jit(solution)/shard_map/ppermute | solution.py:327
  7.2 0.8 collective-permute-done
  8.0 0.9 pad_maximum_fusion.2
  8.9 17.7 %all_to_all.20.refs_0_ = bf16[4,272,256]{2,1,0:T(8,128)(2,1)S(1)} all-to-all(bf16[4,272,256]{2,1,0:T(8,128)(2,1)S(1)} %broadcast_in_dim.4), channel_id=1, replica_groups=mesh['y'=8,'zh'=4,'core'=2,'x'=4,'zl'=4] {'zl'}, dimensions={0} | all-to-all | bytes 1114112 | tf_op jit(solution)/shard_map/all_to_all | solution.py:294
  26.6 15.7 %collective-permute-start.2 = (bf16[4,272,256]{2,1,0:T(8,128)(2,1)S(1)}, bf16[4,272,256]{2,1,0:T(8,128)(2,1)S(1)}, u32[]{:S(2)}, u32[]{:S(2)}) collective-permute-start(bf16[4,272,256]{2,1,0:T(8,128)(2,1)S(1)} %all_to_all.20.refs_0_), channel_id=1, source_target_pairs={{0,4},{4,8},{8,12},{12,0},{1,5},{5,9},{9,13},{13,1},{2,6},{6,10},{... | collective-permute-start | bytes 1671176 | tf_op jit(solution)/shard_map/ppermute | solution.py:335
  42.3 1.9 %collective-permute-start.4 = (bf16[4,272,256]{2,1,0:T(8,128)(2,1)S(1)}, bf16[4,272,256]{2,1,0:T(8,128)(2,1)}, u32[]{:S(2)}, u32[]{:S(2)}) collective-permute-start(bf16[4,272,256]{2,1,0:T(8,128)(2,1)S(1)} %all_to_all.20.refs_0_), channel_id=1, source_target_pairs={{0,12},{4,0},{8,4},{12,8},{1,13},{5,1},{9,5},{13,9},{2,14},{6,2},{... | collective-permute-start | bytes 1671176 | tf_op jit(solution)/shard_map/ppermute | solution.py:336
  44.3 0.7 copy-done.8
  45.0 0.7 copy-done.10
  45.7 0.8 shard_map.98
  46.5 7.1 %collective-permute-done.2.refs_0_ = bf16[4,272,256]{2,1,0:T(8,128)(2,1)S(1)} collective-permute-done((bf16[4,272,256]{2,1,0:T(8,128)(2,1)S(1)}, bf16[4,272,256]{2,1,0:T(8,128)(2,1)S(1)}, u32[]{:S(2)}, u32[]{:S(2)}) %collective-permute-start.2) | collective-permute-done | bytes 557088 | tf_op jit(solution)/shard_map/ppermute | solution.py:335
  53.6 5.6 %collective-permute-start.3 = (bf16[2,272,256]{2,1,0:T(8,128)(2,1)S(1)}, bf16[2,272,256]{2,1,0:T(8,128)(2,1)S(1)}, u32[]{:S(2)}, u32[]{:S(2)}) collective-permute-start(bf16[2,272,256]{2,1,0:T(8,128)(2,1)S(1)} %slice.60), channel_id=1, source_target_pairs={{0,4},{4,8},{8,12},{12,0},{1,5},{5,9},{9,13},{13,1},{2,6},{6,10},{... | collective-permute-start | bytes 835592 | tf_op jit(solution)/shard_map/ppermute | solution.py:337
  59.2 1.0 slice.61
  60.2 1.9 %collective-permute-start.5 = (bf16[2,272,256]{2,1,0:T(8,128)(2,1)S(1)}, bf16[2,272,256]{2,1,0:T(8,128)(2,1)S(1)}, u32[]{:S(2)}, u32[]{:S(2)}) collective-permute-start(bf16[2,272,256]{2,1,0:T(8,128)(2,1)S(1)} %slice.61), channel_id=1, source_target_pairs={{0,12},{4,0},{8,4},{12,8},{1,13},{5,1},{9,5},{13,9},{2,14},{6,2},{... | collective-permute-start | bytes 835592 | tf_op jit(solution)/shard_map/ppermute | solution.py:338
  62.3 2.8 %copy-done = bf16[4096,3,256]{2,0,1:T(8,128)(2,1)S(1)} copy-done((bf16[4096,3,256]{2,0,1:T(8,128)(2,1)S(1)}, bf16[4096,3,256]{2,0,1:T(8,128)(2,1)}, u32[]{:S(2)}) %copy-start) | copy-done | bytes 6291480
  65.1 2.0 %shard_map.95.refs_4_ = f32[4,144,256]{2,1,0:T(8,128)S(1)} custom-call(s32[4]{0:T(128)S(1)} %iota_add_fusion.3.index_ref, bf16[4,272,256]{2,1,0:T(8,128)(2,1)S(1)} %all_to_all.20.refs_0_, bf16[3,4096,256]{2,1,0:T(8,128)(2,1)S(1)} %bitcast.9, bf16[256,4096]{1,0:T(8,128)(2,1)S(1)} %copy-done.3), custom_call_target="tpu_custom_call" | custom-call | flops 301989888 | bytes 2097152 | tf_op jit(solution)/shard_map/pallas_call | solution.py:226
  67.1 0.8 copy-done.1
  67.9 4.4 %shard_map.96.refs_4_ = f32[4,144,256]{2,1,0:T(8,128)S(1)} custom-call(s32[8]{0:T(128)S(1)} %pad_add_fusion.index_ref, bf16[4,272,256]{2,1,0:T(8,128)(2,1)S(1)} %collective-permute-done.2.refs_0_, bf16[4,272,256]{2,1,0:T(8,128)(2,1)} %collective-permute-done.4.refs_1_, bf16[3,4096,256]{2,1,0:T(8,128)(2,1)S(1)} %bitcast.10, bf16[256,4096]{1,0:T(8,128)(2,1)S(1)} %copy-done.3, ...), custom_call_target="tpu_custom_call" | custom-call | flops 603979776 | bytes 4194304 | tf_op jit(solution)/shard_map/pallas_call | solution.py:226
  72.3 2.1 %shard_map.97 = bf16[4,144,256]{2,1,0:T(8,128)(2,1)S(1)} custom-call(s32[4]{0:T(128)S(1)} %iota_add_fusion.2.index_ref, bf16[2,272,256]{2,1,0:T(8,128)(2,1)S(1)} %collective-permute-done.3.refs_0_, bf16[2,272,256]{2,1,0:T(8,128)(2,1)S(1)} %collective-permute-done.5.refs_1_, bf16[3,4096,256]{2,1,0:T(8,128)(2,1)S(1)} %bitcast.11, ...), custom_call_target="tpu_custom_call" | custom-call | flops 301989888 | bytes 2097152 | tf_op jit(solution)/shard_map/pallas_call | solution.py:226
  74.5 1.3 shard_map.100
  75.8 22.0 %all_to_all.21.got_ref = bf16[8,16,256]{2,1,0:T(8,128)(2,1)S(1)} all-to-all(bf16[8,16,256]{2,1,0:T(8,128)(2,1)S(1)} %get-tuple-element.19), channel_id=1, replica_groups=mesh['y'=8,'zh'=4,'core'=2,'x'=4,'zl'=4] {'y'}, dimensions={0} | all-to-all | bytes 131072 | tf_op jit(solution)/shard_map/all_to_all | solution.py:376
  97.8 1.4 shard_map.101
  99.2 5.2 %all-to-all-start.2 = ((bf16[8,32,256]{2,1,0:T(8,128)(2,1)}), bf16[8,32,256]{2,1,0:T(8,128)(2,1)S(1)}, u32[]{:S(2)}, u32[]{:S(2)}) async-start(bf16[8,32,256]{2,1,0:T(8,128)(2,1)} %shard_map.101), calls=%async_computation.2 | async-start | bytes 262144 | tf_op jit(solution)/shard_map/all_to_all | solution.py:387
  104.5 2.8 %shard_map.99 = (f32[136,256]{1,0:T(8,128)S(1)}, f32[136,256]{1,0:T(8,128)S(1)}) custom-call(bf16[3,144,256]{2,1,0:T(8,128)(2,1)S(1)} %slice.62.proj_ref, bf16[144,256]{1,0:T(8,128)(2,1)S(1)} %slice_bitcast_fusion.back_ref, f32[3,3,256]{2,1,0:T(4,128)S(1)} %bitcast.26, f32[16,256]{1,0:T(8,128)S(1)} %bitcast.23, f32[1,256]{1,0:T(1,128)S(1)} %bitcast.28, ...), custom_call_target="tpu_custom_call" | custom-call | flops 3000000000 | tf_op jit(solution)/shard_map/pallas_call | solution.py:171
  107.3 12.5 %all-to-all-done.2.got_ref = bf16[8,32,256]{2,1,0:T(8,128)(2,1)S(1)} async-done(((bf16[8,32,256]{2,1,0:T(8,128)(2,1)}), bf16[8,32,256]{2,1,0:T(8,128)(2,1)S(1)}, u32[]{:S(2)}, u32[]{:S(2)}) %all-to-all-start.2) | async-done | bytes 131104 | tf_op jit(solution)/shard_map/all_to_all | solution.py:387
  119.7 1.6 copy-done.5
  121.4 1.6 copy-done.7
  123.0 0.8 shard_map.102
  123.8 2.8 %copy-done.2 = bf16[4096,3,256]{2,0,1:T(8,128)(2,1)S(1)} copy-done((bf16[4096,3,256]{2,0,1:T(8,128)(2,1)S(1)}, bf16[4096,3,256]{2,0,1:T(8,128)(2,1)}, u32[]{:S(2)}) %copy-start.2) | copy-done | bytes 6291480
  126.6 1.3 shard_map.105
  127.9 4.8 %collective-permute-start.6 = (bf16[2,256,256]{2,1,0:T(8,128)(2,1)S(1)}, bf16[2,256,256]{2,1,0:T(8,128)(2,1)S(1)}, u32[]{:S(2)}, u32[]{:S(2)}) collective-permute-start(bf16[2,256,256]{2,1,0:T(8,128)(2,1)S(1)} %shard_map.105), channel_id=1, source_target_pairs={{0,4},{4,8},{8,12},{12,0},{1,5},{5,9},{9,13},{13,1},{2,6},{6,10},{... | collective-permute-start | bytes 786440 | tf_op jit(solution)/shard_map/ppermute | solution.py:408
  132.7 2.0 %shard_map.104 = bf16[4,256,256]{2,1,0:T(8,128)(2,1)S(1)} custom-call(s32[4]{0:T(128)S(1)} %get-tuple-element.26.index_ref, bf16[128,256]{1,0:T(8,128)(2,1)S(1)} %get-tuple-element.20.hidden, bf16[3,128,256]{2,1,0:T(8,128)(2,1)S(1)} %get-tuple-element.21.grad, bf16[3,4096,256]{2,1,0:T(8,128)(2,1)S(1)} %bitcast.13, bf16[256,4096]{1,0:T(8,128)(2,1)S(1)} %copy-done.3), custom_call_target="tpu_custom_call" | custom-call | flops 268435456 | bytes 2097152 | tf_op jit(solution)/shard_map/pallas_call | solution.py:265
  134.7 1.3 shard_map.107
  136.0 2.1 %collective-permute-start.8 = (bf16[2,256,256]{2,1,0:T(8,128)(2,1)S(1)}, bf16[2,256,256]{2,1,0:T(8,128)(2,1)S(1)}, u32[]{:S(2)}, u32[]{:S(2)}) collective-permute-start(bf16[2,256,256]{2,1,0:T(8,128)(2,1)S(1)} %shard_map.107), channel_id=1, source_target_pairs={{0,12},{4,0},{8,4},{12,8},{1,13},{5,1},{9,5},{13,9},{2,14},{6,2},{... | collective-permute-start | bytes 786440 | tf_op jit(solution)/shard_map/ppermute | solution.py:409
  138.1 2.0 %shard_map.106 = bf16[4,256,256]{2,1,0:T(8,128)(2,1)S(1)} custom-call(s32[4]{0:T(128)S(1)} %get-tuple-element.27.index_ref, bf16[128,256]{1,0:T(8,128)(2,1)S(1)} %get-tuple-element.20.hidden, bf16[3,128,256]{2,1,0:T(8,128)(2,1)S(1)} %get-tuple-element.21.grad, bf16[3,4096,256]{2,1,0:T(8,128)(2,1)S(1)} %bitcast.15, bf16[256,4096]{1,0:T(8,128)(2,1)S(1)} %copy-done.3), custom_call_target="tpu_custom_call" | custom-call | flops 268435456 | bytes 2097152 | tf_op jit(solution)/shard_map/pallas_call | solution.py:265
  140.2 5.1 %collective-permute-start.7 = (bf16[4,256,256]{2,1,0:T(8,128)(2,1)S(1)}, bf16[4,256,256]{2,1,0:T(8,128)(2,1)S(1)}, u32[]{:S(2)}, u32[]{:S(2)}) collective-permute-start(bf16[4,256,256]{2,1,0:T(8,128)(2,1)S(1)} %pad_maximum_fusion), channel_id=1, source_target_pairs={{0,4},{4,8},{8,12},{12,0},{1,5},{5,9},{9,13},{13,1},{2,6},{6,10},{... | collective-permute-start | bytes 1572872 | tf_op jit(solution)/shard_map/ppermute | solution.py:414
  145.4 0.3 collective-permute-done.8
  145.8 1.9 %collective-permute-start.9 = (bf16[4,256,256]{2,1,0:T(8,128)(2,1)S(1)}, bf16[4,256,256]{2,1,0:T(8,128)(2,1)S(1)}, u32[]{:S(2)}, u32[]{:S(2)}) collective-permute-start(bf16[4,256,256]{2,1,0:T(8,128)(2,1)S(1)} %pad_maximum_fusion.1), channel_id=1, source_target_pairs={{0,12},{4,0},{8,4},{12,8},{1,13},{5,1},{9,5},{13,9},{2,14},{6,2},{... | collective-permute-start | bytes 1572872 | tf_op jit(solution)/shard_map/ppermute | solution.py:415
  147.7 2.0 %shard_map.103 = bf16[4,256,256]{2,1,0:T(8,128)(2,1)S(1)} custom-call(s32[4]{0:T(128)S(1)} %iota_add_fusion.3.index_ref, bf16[128,256]{1,0:T(8,128)(2,1)S(1)} %get-tuple-element.20.hidden, bf16[3,128,256]{2,1,0:T(8,128)(2,1)S(1)} %get-tuple-element.21.grad, bf16[3,4096,256]{2,1,0:T(8,128)(2,1)S(1)} %bitcast.18, bf16[256,4096]{1,0:T(8,128)(2,1)S(1)} %copy-done.3), custom_call_target="tpu_custom_call" | custom-call | flops 268435456 | bytes 2097152 | tf_op jit(solution)/shard_map/pallas_call | solution.py:265
  149.7 4.6 %collective-permute-done.7 = bf16[4,256,256]{2,1,0:T(8,128)(2,1)S(1)} collective-permute-done((bf16[4,256,256]{2,1,0:T(8,128)(2,1)S(1)}, bf16[4,256,256]{2,1,0:T(8,128)(2,1)S(1)}, u32[]{:S(2)}, u32[]{:S(2)}) %collective-permute-start.7) | collective-permute-done | bytes 524320 | tf_op jit(solution)/shard_map/ppermute | solution.py:414
  154.3 5.5 %collective-permute-done.9 = bf16[4,256,256]{2,1,0:T(8,128)(2,1)S(1)} collective-permute-done((bf16[4,256,256]{2,1,0:T(8,128)(2,1)S(1)}, bf16[4,256,256]{2,1,0:T(8,128)(2,1)S(1)}, u32[]{:S(2)}, u32[]{:S(2)}) %collective-permute-start.9) | collective-permute-done | bytes 524320 | tf_op jit(solution)/shard_map/ppermute | solution.py:415
  159.8 0.2 add_convert_fusion
  160.0 15.2 %all_to_all.22 = bf16[4,256,256]{2,1,0:T(8,128)(2,1)S(1)} all-to-all(bf16[4,256,256]{2,1,0:T(8,128)(2,1)S(1)} %add_convert_fusion), channel_id=1, replica_groups=mesh['y'=8,'zh'=4,'core'=2,'x'=4,'zl'=4] {'zl'}, dimensions={0} | all-to-all | bytes 1048576 | tf_op jit(solution)/shard_map/all_to_all | solution.py:417
  175.2 0.1 reduce_sum.12
  175.3 0.7 fusion
  (48 shorter events, 0.7 us)
Async XLA Ops:
  0.6 61.7 %copy-start.3 = (bf16[256,4096]{1,0:T(8,128)(2,1)S(1)}, bf16[256,4096]{1,0:T(8,128)(2,1)}, u32[]{:S(2)}) copy-start(bf16[256,4096]{1,0:T(8,128)(2,1)} %weight_out.9) | copy-start | bytes 6291460
  2.2 5.0 %collective-permute-start.1 = (bf16[8,256]{1,0:T(8,128)(2,1)S(1)}, bf16[8,256]{1,0:T(8,128)(2,1)S(1)}, u32[]{:S(2)}, u32[]{:S(2)}) collective-permute-start(bf16[8,256]{1,0:T(8,128)(2,1)S(1)} %pad_maximum_fusion.3), channel_id=1, source_target_pairs={{16,0},{32,16},{48,32},{64,48},{80,64},{96,80},{112,96},{128,112},... | collective-permute-start | bytes 12296 | tf_op jit(solution)/shard_map/ppermute | solution.py:329
  4.2 3.8 %collective-permute-start = (bf16[8,256]{1,0:T(8,128)(2,1)S(1)}, bf16[8,256]{1,0:T(8,128)(2,1)S(1)}, u32[]{:S(2)}, u32[]{:S(2)}) collective-permute-start(bf16[8,256]{1,0:T(8,128)(2,1)S(1)} %slice.45), channel_id=1, source_target_pairs={{0,16},{16,32},{32,48},{48,64},{64,80},{80,96},{96,112},{112,128},... | collective-permute-start | bytes 12296 | tf_op jit(solution)/shard_map/ppermute | solution.py:327
  26.6 27.0 %collective-permute-start.2 = (bf16[4,272,256]{2,1,0:T(8,128)(2,1)S(1)}, bf16[4,272,256]{2,1,0:T(8,128)(2,1)S(1)}, u32[]{:S(2)}, u32[]{:S(2)}) collective-permute-start(bf16[4,272,256]{2,1,0:T(8,128)(2,1)S(1)} %all_to_all.20.refs_0_), channel_id=1, source_target_pairs={{0,4},{4,8},{8,12},{12,0},{1,5},{5,9},{9,13},{13,1},{2,6},{6,10},{... | collective-permute-start | bytes 1671176 | tf_op jit(solution)/shard_map/ppermute | solution.py:335
  42.3 16.9 %collective-permute-start.4 = (bf16[4,272,256]{2,1,0:T(8,128)(2,1)S(1)}, bf16[4,272,256]{2,1,0:T(8,128)(2,1)}, u32[]{:S(2)}, u32[]{:S(2)}) collective-permute-start(bf16[4,272,256]{2,1,0:T(8,128)(2,1)S(1)} %all_to_all.20.refs_0_), channel_id=1, source_target_pairs={{0,12},{4,0},{8,4},{12,8},{1,13},{5,1},{9,5},{13,9},{2,14},{6,2},{... | collective-permute-start | bytes 1671176 | tf_op jit(solution)/shard_map/ppermute | solution.py:336
  44.3 0.7 copy-start.8
  45.0 0.7 copy-start.10
  46.5 28.0 %copy-start.4 = (f32[16,136,256]{2,1,0:T(8,128)}, f32[16,136,256]{2,1,0:T(8,128)S(1)}, u32[]{:S(2)}) copy-start(f32[16,136,256]{2,1,0:T(8,128)S(1)} %get-tuple-element.12.up_ref) | copy-start | bytes 6684676
  46.5 28.0 %copy-start.6 = (f32[16,136,256]{2,1,0:T(8,128)}, f32[16,136,256]{2,1,0:T(8,128)S(1)}, u32[]{:S(2)}) copy-start(f32[16,136,256]{2,1,0:T(8,128)S(1)} %get-tuple-element.13.down_ref) | copy-start | bytes 6684676
  53.6 18.7 %collective-permute-start.3 = (bf16[2,272,256]{2,1,0:T(8,128)(2,1)S(1)}, bf16[2,272,256]{2,1,0:T(8,128)(2,1)S(1)}, u32[]{:S(2)}, u32[]{:S(2)}) collective-permute-start(bf16[2,272,256]{2,1,0:T(8,128)(2,1)S(1)} %slice.60), channel_id=1, source_target_pairs={{0,4},{4,8},{8,12},{12,0},{1,5},{5,9},{9,13},{13,1},{2,6},{6,10},{... | collective-permute-start | bytes 835592 | tf_op jit(solution)/shard_map/ppermute | solution.py:337
  60.2 12.1 %collective-permute-start.5 = (bf16[2,272,256]{2,1,0:T(8,128)(2,1)S(1)}, bf16[2,272,256]{2,1,0:T(8,128)(2,1)S(1)}, u32[]{:S(2)}, u32[]{:S(2)}) collective-permute-start(bf16[2,272,256]{2,1,0:T(8,128)(2,1)S(1)} %slice.61), channel_id=1, source_target_pairs={{0,12},{4,0},{8,4},{12,8},{1,13},{5,1},{9,5},{13,9},{2,14},{6,2},{... | collective-permute-start | bytes 835592 | tf_op jit(solution)/shard_map/ppermute | solution.py:338
  62.3 2.8 %copy-start = (bf16[4096,3,256]{2,0,1:T(8,128)(2,1)S(1)}, bf16[4096,3,256]{2,0,1:T(8,128)(2,1)}, u32[]{:S(2)}) copy-start(bf16[4096,3,256]{2,0,1:T(8,128)(2,1)} %param.10) | copy-start | bytes 18874372
  65.1 2.8 %copy-start.1 = (bf16[4096,3,256]{2,0,1:T(8,128)(2,1)S(1)}, bf16[4096,3,256]{2,0,1:T(8,128)(2,1)}, u32[]{:S(2)}) copy-start(bf16[4096,3,256]{2,0,1:T(8,128)(2,1)} %param.10) | copy-start | bytes 18874372
  72.3 2.2 %copy-start.9 = (f32[256,16]{0,1:T(8,128)S(1)}, f32[256,16]{0,1:T(8,128)}, u32[]{:S(2)}) copy-start(f32[256,16]{0,1:T(8,128)} %param.14) | copy-start | bytes 49156
  72.3 2.2 %copy-start.12 = (f32[3,256,3]{1,2,0:T(4,128)S(1)}, f32[3,256,3]{1,2,0:T(4,128)}, u32[]{:S(2)}) copy-start(f32[3,256,3]{1,2,0:T(4,128)} %param.12) | copy-start | bytes 27652
  74.5 30.0 %copy-start.11 = (f32[256,16]{0,1:T(8,128)S(1)}, f32[256,16]{0,1:T(8,128)}, u32[]{:S(2)}) copy-start(f32[256,16]{0,1:T(8,128)} %param.13) | copy-start | bytes 49156
  74.5 30.0 %copy-start.13 = (f32[256]{0:T(256)S(1)}, f32[256]{0:T(256)}, u32[]{:S(2)}) copy-start(f32[256]{0:T(256)} %param.15) | copy-start | bytes 3076
  99.2 20.5 %all-to-all-start.2 = ((bf16[8,32,256]{2,1,0:T(8,128)(2,1)}), bf16[8,32,256]{2,1,0:T(8,128)(2,1)S(1)}, u32[]{:S(2)}, u32[]{:S(2)}) async-start(bf16[8,32,256]{2,1,0:T(8,128)(2,1)} %shard_map.101), calls=%async_computation.2 | async-start | bytes 262144 | tf_op jit(solution)/shard_map/all_to_all | solution.py:387
  119.7 1.6 copy-start.5
  121.4 1.6 copy-start.7
  123.8 2.8 %copy-start.2 = (bf16[4096,3,256]{2,0,1:T(8,128)(2,1)S(1)}, bf16[4096,3,256]{2,0,1:T(8,128)(2,1)}, u32[]{:S(2)}) copy-start(bf16[4096,3,256]{2,0,1:T(8,128)(2,1)} %param.10) | copy-start | bytes 18874372
  127.9 12.2 %collective-permute-start.6 = (bf16[2,256,256]{2,1,0:T(8,128)(2,1)S(1)}, bf16[2,256,256]{2,1,0:T(8,128)(2,1)S(1)}, u32[]{:S(2)}, u32[]{:S(2)}) collective-permute-start(bf16[2,256,256]{2,1,0:T(8,128)(2,1)S(1)} %shard_map.105), channel_id=1, source_target_pairs={{0,4},{4,8},{8,12},{12,0},{1,5},{5,9},{9,13},{13,1},{2,6},{6,10},{... | collective-permute-start | bytes 786440 | tf_op jit(solution)/shard_map/ppermute | solution.py:408
  134.7 13.0 %slice-start = ((s8[6291456]{0:T(1024)(128)(4,1)}), s8[4194304]{0:T(1024)(128)(4,1)S(1)}, s32[]{:S(2)}) async-start(s8[6291456]{0:T(1024)(128)(4,1)} %bitcast.16), calls=%async_computation.4 | async-start | bytes 8388608
  136.0 11.7 %slice-start.1 = ((s8[6291456]{0:T(1024)(128)(4,1)}), s8[2097152]{0:T(1024)(128)(4,1)S(1)}, s32[]{:S(2)}) async-start(s8[6291456]{0:T(1024)(128)(4,1)} %bitcast.16), calls=%async_computation.5 | async-start | bytes 4194304
  136.0 9.6 %collective-permute-start.8 = (bf16[2,256,256]{2,1,0:T(8,128)(2,1)S(1)}, bf16[2,256,256]{2,1,0:T(8,128)(2,1)S(1)}, u32[]{:S(2)}, u32[]{:S(2)}) collective-permute-start(bf16[2,256,256]{2,1,0:T(8,128)(2,1)S(1)} %shard_map.107), channel_id=1, source_target_pairs={{0,12},{4,0},{8,4},{12,8},{1,13},{5,1},{9,5},{13,9},{2,14},{6,2},{... | collective-permute-start | bytes 786440 | tf_op jit(solution)/shard_map/ppermute | solution.py:409
  140.2 14.0 %collective-permute-start.7 = (bf16[4,256,256]{2,1,0:T(8,128)(2,1)S(1)}, bf16[4,256,256]{2,1,0:T(8,128)(2,1)S(1)}, u32[]{:S(2)}, u32[]{:S(2)}) collective-permute-start(bf16[4,256,256]{2,1,0:T(8,128)(2,1)S(1)} %pad_maximum_fusion), channel_id=1, source_target_pairs={{0,4},{4,8},{8,12},{12,0},{1,5},{5,9},{9,13},{13,1},{2,6},{6,10},{... | collective-permute-start | bytes 1572872 | tf_op jit(solution)/shard_map/ppermute | solution.py:414
  145.8 14.0 %collective-permute-start.9 = (bf16[4,256,256]{2,1,0:T(8,128)(2,1)S(1)}, bf16[4,256,256]{2,1,0:T(8,128)(2,1)S(1)}, u32[]{:S(2)}, u32[]{:S(2)}) collective-permute-start(bf16[4,256,256]{2,1,0:T(8,128)(2,1)S(1)} %pad_maximum_fusion.1), channel_id=1, source_target_pairs={{0,12},{4,0},{8,4},{12,8},{1,13},{5,1},{9,5},{13,9},{2,14},{6,2},{... | collective-permute-start | bytes 1572872 | tf_op jit(solution)/shard_map/ppermute | solution.py:415

commit v5 on v3

--- a/solution.py
+++ b/solution.py
@@ -13,22 +13,27 @@
 EDGE = 8
 NEAR = 4
 AHEAD = 2
+GRANT = 16 * 2**20
 BF16 = jnp.bfloat16
 F32 = jnp.float32
 
 
-def table_kernel(rates_ref, res_ref, up_ref, down_ref, filt_ref):
-    order, rows, _ = up_ref.shape
-    row = lax.broadcasted_iota(jnp.int32, (rows, 1), 0).astype(F32)
-    span = rows - 8 + AHEAD
-    total = jnp.zeros(filt_ref.shape, F32)
-    for r in range(order):
-        rate = rates_ref[r : r + 1, :]
-        up = jnp.exp(-rate * (row + 1.0))
-        up_ref[r] = up
-        down_ref[r] = jnp.exp(-rate * (span - row))
-        total = total + res_ref[r : r + 1, :] * up
-    filt_ref[...] = total
+def edge_kernel(tokens, cotangent, copies, edge, near):
+    block = tokens.shape[0]
+    for i in range(copies.shape[0]):
+        copies[i, :block] = tokens[...]
+        copies[i, block:] = cotangent[...]
+    edge[...] = tokens[block - 2 * EDGE :]
+    ours = tokens[: 2 * EDGE].astype(F32)
+    other = pltpu.roll(cotangent[: 2 * EDGE].astype(F32), NEAR, 0)
+    row = lax.broadcasted_iota(jnp.int32, ours.shape, 0)
+    near[...] = jnp.where(row < NEAR, ours, other).astype(BF16)
+
+
+def halo_kernel(edge, near, copies):
+    both = jnp.concatenate([edge[...].astype(F32)[EDGE:], near[...].astype(F32)[:EDGE]], axis=0)
+    for i in range(copies.shape[0]):
+        copies[i] = both.astype(BF16)
 
 
 def features(ext, proj_ref, taps_ref, rows):
@@ -49,28 +54,32 @@
 
 
 def back_rows(back_ref, rows):
-    block = back_ref.shape[0] - EDGE - 2 * NEAR
+    ends = EDGE + 2 * NEAR
     back = back_ref[...].astype(F32)
-    near = pltpu.roll(back[block + EDGE :], NEAR, 0)
+    near = pltpu.roll(back[EDGE:ends], NEAR, 0)
     row = lax.broadcasted_iota(jnp.int32, (rows, 1), 0)
-    whole = jnp.concatenate([back[:block], near], axis=0)
-    return jnp.where(row < block + AHEAD, whole, 0.0), row
+    whole = jnp.concatenate([back[ends:], near], axis=0)
+    return jnp.where(row < back_ref.shape[0] - ends + AHEAD, whole, 0.0), row
 
 
 def state_kernel(
-    place_ref, proj_ref, back_ref, taps_ref, rates_ref, up_ref, down_ref,
+    place_ref, proj_ref, back_ref, taps_ref, rates_ref,
     fwd_ref, bwd_ref, send_ref, ext,
 ):
-    order, rows, _ = up_ref.shape
-    block = rows - 8
+    order = rates_ref.shape[0]
+    block = proj_ref.shape[1] - EDGE - 2 * NEAR
+    rows = block + 8
     query, key_part, value_part = features(ext, proj_ref, taps_ref, rows)
     back, row = back_rows(back_ref, rows)
     gated = jnp.where(row < block, key_part * value_part, 0.0)
     grad_conv = jnp.where(row >= AHEAD, back * query, 0.0)
+    time = row.astype(F32)
     for r in range(order):
-        scale = jnp.exp(rates_ref[r : r + 1, :] * (AHEAD + 1.0))
-        fwd_ref[r : r + 1, :] = scale * jnp.sum(down_ref[r] * gated, axis=0, keepdims=True)
-        bwd_ref[r : r + 1, :] = scale * jnp.sum(up_ref[r] * grad_conv, axis=0, keepdims=True)
+        rate = rates_ref[r : r + 1, :]
+        fwd = jnp.exp(-rate * (block - 1.0 - time)) * gated
+        bwd = jnp.exp(-rate * (time - AHEAD)) * grad_conv
+        fwd_ref[r : r + 1, :] = jnp.sum(fwd, axis=0, keepdims=True)
+        bwd_ref[r : r + 1, :] = jnp.sum(bwd, axis=0, keepdims=True)
     for i in range(send_ref.shape[0]):
         send_ref[i] = jnp.where(place_ref[0] < i, fwd_ref[...], bwd_ref[...]).astype(BF16)
 
@@ -101,10 +110,15 @@
 
 
 def local_kernel(
-    proj_ref, back_ref, taps_ref, res_ref, skip_ref, filt_ref,
-    conv_ref, grad_ref, ext, pad,
+    proj_ref, back_ref, taps_ref, rates_ref, res_ref, skip_ref,
+    conv_ref, grad_ref, ext, pad, filt_ref,
 ):
     rows, width = conv_ref.shape
+    time = lax.broadcasted_iota(jnp.int32, (rows, 1), 0).astype(F32)
+    taps = jnp.zeros((rows, width), F32)
+    for r in range(rates_ref.shape[0]):
+        taps = taps + res_ref[r : r + 1, :] * jnp.exp(-rates_ref[r : r + 1, :] * (time + 1.0))
+    filt_ref[...] = taps
     query, key_part, value_part = features(ext, proj_ref, taps_ref, rows)
     back, _ = back_rows(back_ref, rows)
     zero = jnp.zeros((8, width), F32)
@@ -134,22 +148,26 @@
 
 
 def finish_kernel(
-    proj_ref, back_ref, taps_ref, res_ref, up_ref, down_ref,
+    proj_ref, back_ref, taps_ref, rates_ref, res_ref,
     conv_ref, grad_ref, got_ref,
     hidden_ref, out_ref, ext, feat,
 ):
-    order, rows, _ = up_ref.shape
+    order = rates_ref.shape[0]
+    rows = conv_ref.shape[0]
     block = rows - 8
     query, key_part, value_part = features(ext, proj_ref, taps_ref, rows)
-    back, _ = back_rows(back_ref, rows)
+    back, row = back_rows(back_ref, rows)
+    time = row.astype(F32)
     conv_out = conv_ref[...]
     grad_gated = grad_ref[...]
     states = jnp.sum(got_ref[...].astype(F32), axis=0)
     ahead, behind = states[:order], states[order:]
     for r in range(order):
         res = res_ref[r : r + 1, :]
-        conv_out = conv_out + (res * ahead[r : r + 1]) * up_ref[r]
-        grad_gated = grad_gated + (res * behind[r : r + 1]) * down_ref[r]
+        rate = rates_ref[r : r + 1, :]
+        conv_out = conv_out + (res * ahead[r : r + 1]) * jnp.exp(-rate * (time + 1.0))
+        past = jnp.exp(-rate * (block + AHEAD - time))
+        grad_gated = grad_gated + (res * behind[r : r + 1]) * past
     hidden_ref[...] = (query * conv_out)[:block].astype(BF16)
     feat[0] = back * conv_out
     feat[1] = grad_gated * value_part
@@ -174,17 +192,148 @@
         in_specs=specs,
         out_specs=jax.tree.map(lambda _: whole, outs),
         cost_estimate=cost,
-        compiler_params=pltpu.CompilerParams(vmem_limit_bytes=40 * 2**20),
+        compiler_params=pltpu.CompilerParams(vmem_limit_bytes=GRANT),
     )(*args)
+
+
+def load_weights(blocks, weight_in, weight_out, held_in, held_out, sems):
+    part = held_in.shape[2]
+    copies = []
+    for s, block in enumerate(blocks):
+        at = pl.ds(pl.multiple_of(block * part, part), part)
+        copies.append(
+            (
+                pltpu.make_async_copy(weight_in.at[:, at, :], held_in.at[s], sems.at[s, 0]),
+                pltpu.make_async_copy(weight_out.at[:, at], held_out.at[s], sems.at[s, 1]),
+            )
+        )
+        for copy in copies[-1]:
+            copy.start()
+
+    def ready(s):
+        for copy in copies[s]:
+            copy.wait()
+
+    return ready
+
+
+def project_kernel(sizes, offsets, first, last, place_ref, *refs):
+    n_x, n_zl = sizes["x"], sizes["zl"]
+    pieces, refs = refs[: len(offsets)], refs[len(offsets) :]
+    halo, weight_in, weight_out = refs[:3]
+    old = None if first else refs[3]
+    out, held_in, held_out, sems = refs[3 + (not first) : 7 + (not first)]
+    total = refs[-1] if last else out
+    block = pieces[0].shape[1] // 2
+    work = [
+        (piece, j, lax.rem(place_ref[2] + k, n_x) * n_zl + start + j)
+        for piece, (k, start) in zip(pieces, offsets)
+        for j in range(piece.shape[0])
+    ]
+    ready = load_weights([w[2] for w in work], weight_in, weight_out, held_in, held_out, sems)
+    for s, (piece, j, index) in enumerate(work):
+        ready(s)
+        ends = halo[index]
+        part_in = jnp.concatenate([piece[j, :block], ends], axis=0)
+        part_grad = jnp.concatenate([ends, piece[j, block:]], axis=0)
+        for p in range(4):
+            if p < 3:
+                term = jnp.dot(part_in, held_in[s, p], preferred_element_type=F32)
+            else:
+                term = lax.dot_general(
+                    part_grad,
+                    held_out[s],
+                    (((1,), (1,)), ((), ())),
+                    preferred_element_type=F32,
+                )
+            if s == 0 and first:
+                total[p] = term
+            else:
+                total[p] = (old if s == 0 else total)[p] + term
+    if last:
+        out[...] = total[...].astype(BF16)
+
+
+def project(sizes, place, offsets, pieces, halo, weights, old=None, last=False):
+    weight_in, weight_out = weights
+    count = sum(piece.shape[0] for piece in pieces)
+    rows = pieces[0].shape[1] // 2 + halo.shape[1]
+    part = pieces[0].shape[2]
+    width = weight_out.shape[0]
+    whole = pl.BlockSpec(memory_space=pltpu.VMEM)
+    far = pl.BlockSpec(memory_space=pltpu.HBM)
+    scratch = [
+        pltpu.VMEM((count, 3, part, width), BF16),
+        pltpu.VMEM((count, width, part), BF16),
+        pltpu.SemaphoreType.DMA((count, 2)),
+    ]
+    return pl.pallas_call(
+        functools.partial(project_kernel, sizes, offsets, old is None, last),
+        in_specs=[pl.BlockSpec(memory_space=pltpu.SMEM)]
+        + [whole] * (len(pieces) + 1)
+        + [far, far]
+        + [whole] * (old is not None),
+        out_specs=whole,
+        scratch_shapes=scratch + ([pltpu.VMEM((4, rows, width), F32)] if last else []),
+        out_shape=shape(4, rows, width, dtype=BF16 if last else F32),
+        cost_estimate=pl.CostEstimate(
+            flops=8 * count * rows * part * width,
+            bytes_accessed=8 * count * part * width,
+            transcendentals=0,
+        ),
+        compiler_params=pltpu.CompilerParams(vmem_limit_bytes=GRANT),
+    )(place, *pieces, halo, weight_in, weight_out, *([] if old is None else [old]))
+
+
+def partials_kernel(
+    sizes, offset, place_ref, hidden, grad, weight_in, weight_out, out, held_in, held_out, sems
+):
+    n_x, n_zl = sizes["x"], sizes["zl"]
+    block = hidden.shape[0]
+    k, start = offset
+    base = lax.rem(place_ref[2] + k, n_x) * n_zl + start
+    count = out.shape[0]
+    ready = load_weights(
+        [base + j for j in range(count)], weight_in, weight_out, held_in, held_out, sems
+    )
+    for s in range(count):
+        ready(s)
+        mixed = jnp.dot(hidden[...], held_out[s], preferred_element_type=F32)
+        out[s, :block] = mixed.astype(BF16)
+        total = None
+        for p in range(3):
+            term = lax.dot_general(
+                grad[p], held_in[s, p], (((1,), (1,)), ((), ())), preferred_element_type=F32
+            )
+            total = term if p == 0 else total + term
+        out[s, block:] = total.astype(BF16)
+
+
+def partials(sizes, place, offset, count, hidden, grad, weights, part):
+    block, width = hidden.shape
+    whole = pl.BlockSpec(memory_space=pltpu.VMEM)
+    far = pl.BlockSpec(memory_space=pltpu.HBM)
+    return pl.pallas_call(
+        functools.partial(partials_kernel, sizes, offset),
+        in_specs=[pl.BlockSpec(memory_space=pltpu.SMEM), whole, whole, far, far],
+        out_specs=whole,
+        scratch_shapes=[
+            pltpu.VMEM((count, 3, part, width), BF16),
+            pltpu.VMEM((count, width, part), BF16),
+            pltpu.SemaphoreType.DMA((count, 2)),
+        ],
+        out_shape=shape(count, 2 * block, part, dtype=BF16),
+        cost_estimate=pl.CostEstimate(
+            flops=8 * count * block * part * width,
+            bytes_accessed=8 * count * part * width,
+            transcendentals=0,
+        ),
+        compiler_params=pltpu.CompilerParams(vmem_limit_bytes=GRANT),
+    )(place, hidden, grad, *weights)
 
 
 def shape(*dims, dtype=F32):
     return jax.ShapeDtypeStruct(dims, dtype)
-
-
-def spread(array, axis, count):
-    copies = jnp.broadcast_to(array[None], (count,) + array.shape)
-    return lax.all_to_all(copies, axis, 0, 0, tiled=True)
 
 
 def shards(
@@ -208,54 +357,64 @@
     rates = decay_rates.T
     res = residues.T
     skip = skip_gain[None]
-    up, down, filt = call(
-        table_kernel,
-        [shape(order, rows, width), shape(order, rows, width), shape(rows, width)],
-        [],
-        rates,
-        res,
-    )
+    place = jnp.stack(
+        [
+            lax.axis_index("y"),
+            lax.axis_index("zh") * sizes["core"] + lax.axis_index("core"),
+            lax.axis_index("x"),
+        ]
+    ).astype(jnp.int32)
     to_next = [(i, i + 1) for i in range(n_ctx - 1)]
     to_prev = [(i + 1, i) for i in range(n_ctx - 1)]
-    edge = lax.ppermute(tokens[block - EDGE :], CTX, to_next)
-    near = jnp.concatenate([tokens[:NEAR], cotangent[:NEAR]], axis=0)
+    copies, edge, near = call(
+        edge_kernel,
+        [
+            shape(n_zl, 2 * block, part, dtype=BF16),
+            shape(2 * EDGE, part, dtype=BF16),
+            shape(2 * EDGE, part, dtype=BF16),
+        ],
+        [],
+        tokens,
+        cotangent,
+    )
+    edge = lax.ppermute(edge, CTX, to_next)
     near = lax.ppermute(near, CTX, to_prev)
-    both = jnp.concatenate([tokens, edge, near, cotangent], axis=0)
-    both = spread(spread(both, "zl", n_zl), "x", n_x)
-    ends = block + EDGE + 2 * NEAR
-    whole_in = both[:, :, :ends]
-    whole_grad = jnp.concatenate([both[:, :, ends:], both[:, :, block:ends]], axis=2)
-    weight_in = input_weight.reshape(n_x, n_zl, part, 3, width)
-    weight_out = output_weight.reshape(width, n_x, n_zl, part)
-    proj = jnp.einsum(
-        "xztf,xzfpc->ptc", whole_in, weight_in, preferred_element_type=F32
-    ).astype(BF16)
-    back = jnp.einsum(
-        "xztf,cxzf->tc", whole_grad, weight_out, preferred_element_type=F32
-    ).astype(BF16)
-    common = (proj, back, taps)
+    pieces = lax.all_to_all(copies, "zl", 0, 0, tiled=True)
+    ends = call(halo_kernel, shape(n_x * n_zl, 2 * EDGE, part, dtype=BF16), [], edge, near)
+    ends, _ = lax.optimization_barrier((ends, pieces))
+    halo = lax.all_to_all(ends, TP, 0, 0, tiled=True)
+    half = n_zl // 2
+    right = [(i, (i + 1) % n_x) for i in range(n_x)]
+    left = [(i, (i - 1) % n_x) for i in range(n_x)]
+    from_left = lax.ppermute(pieces, "x", right)
+    from_right = lax.ppermute(pieces, "x", left)
+    far_left = lax.ppermute(from_left[:half], "x", right)
+    far_right = lax.ppermute(from_right[half:], "x", left)
+    weights = (input_weight.transpose(1, 0, 2), output_weight)
+    total = project(sizes, place, [(0, 0)], [pieces], halo, weights)
+    total = project(
+        sizes, place, [(n_x - 1, 0), (1, 0)], [from_left, from_right], halo, weights, total
+    )
+    total = project(
+        sizes, place, [(2, 0), (2, half)], [far_left, far_right], halo, weights, total, True
+    )
+    proj, back = total[:3], total[3]
+    common = (proj, back, taps, rates)
     ext = pltpu.VMEM((3, rows + EDGE, width), F32)
-    group = lax.axis_index("y")
-    member = lax.axis_index("zh") * sizes["core"] + lax.axis_index("core")
-    place = jnp.stack([group, member]).astype(jnp.int32)
     fwd, bwd, send = call(
         state_kernel,
         [shape(order, width), shape(order, width), shape(sizes["y"], order, width, dtype=BF16)],
         [ext],
         place,
         *common,
-        rates,
-        up,
-        down,
     )
     conv, grad = call(
         local_kernel,
         [shape(rows, width), shape(rows, width)],
-        [ext, pltpu.VMEM((2, rows + 8, width), F32)],
+        [ext, pltpu.VMEM((2, rows + 8, width), F32), pltpu.VMEM((rows, width), F32)],
         *common,
         res,
         skip,
-        filt,
         flops=3 * 10**9,
     )
     got = lax.all_to_all(send, "y", 0, 0, tiled=True)
@@ -276,19 +435,27 @@
         [ext, pltpu.VMEM((3, rows, width), F32)],
         *common,
         res,
-        up,
-        down,
         conv,
         grad,
         states,
     )
-    mixed = jnp.einsum("tc,cxzf->xztf", hidden, weight_out, preferred_element_type=F32)
-    grad_tok = jnp.einsum("ptc,xzfpc->xztf", grad_proj, weight_in, preferred_element_type=F32)
-    terms = jnp.concatenate([mixed.astype(BF16), grad_tok.astype(BF16)], axis=2)
-    terms = lax.all_to_all(terms, "x", 0, 0, tiled=True)
-    terms = jnp.sum(terms.astype(F32), axis=0).astype(BF16)
-    terms = lax.all_to_all(terms, "zl", 0, 0, tiled=True)
-    total = jnp.sum(terms.astype(F32), axis=0).astype(BF16)
+    def terms(offset, count):
+        return partials(sizes, place, offset, count, hidden, grad_proj, weights, part)
+
+    def add(*arrays):
+        return sum(a.astype(F32) for a in arrays).astype(BF16)
+
+    far_right = lax.ppermute(terms((2, 0), half), "x", right)
+    far_left = lax.ppermute(terms((2, half), half), "x", left)
+    to_right = terms((1, 0), n_zl)
+    to_left = terms((n_x - 1, 0), n_zl)
+    to_right = jnp.concatenate([add(to_right[:half], far_right), to_right[half:]], axis=0)
+    to_left = jnp.concatenate([to_left[:half], add(to_left[half:], far_left)], axis=0)
+    from_left = lax.ppermute(to_right, "x", right)
+    from_right = lax.ppermute(to_left, "x", left)
+    summed = add(terms((0, 0), n_zl), from_left, from_right)
+    summed = lax.all_to_all(summed, "zl", 0, 0, tiled=True)
+    total = jnp.sum(summed.astype(F32), axis=0).astype(BF16)
     return total[:block], total[block:]
 
 

time: 184 us -> 176 us (0.957)
  blocking collectives: 90.3 us -> 55.3 us
  starting transfers between devices: 15.8 us -> 45.7 us
  Pallas kernels: 6.85 us -> 26.6 us
  matrix products: 11.5 us -> 0 us
  waiting for transfers between devices: 41.9 us -> 33.1 us
    all_to_all x3 -> x2, blocking collectives: 64.1 us -> 35.9 us  [the longest x1 21.5 us: shards(): pieces = lax.all_to_all(copies, 'zl', 0, 0, tiled=True)]
    ppermute x1 -> x9, starting transfers between devices: 1.73 us -> 28.2 us  [the longest x1 6.16 us: shards(): from_left = lax.ppermute(pieces, 'x', right)]
    all_to_all x1, waiting for transfers between devices: 19 us -> 0.01 us  [shards(): halo = lax.all_to_all(ends, TP, 0, 0, tiled=True)]
    pallas_call x0 -> x8, Pallas kernels: none -> 18.4 us  [the longest x5 10.8 us: partials(): pl.pallas_call(functools.partial(partials_kernel, sizes, offset), in_spec...]
    dot_general x4 -> x0, matrix products: 11.5 us -> none  [the longest x1 4.92 us: shards(): jnp.einsum('ptc,xzfpc->xztf', grad_proj, weight_in, preferred_element_typ...]
    ppermute x1 -> x9, waiting for transfers between devices: 0.01 us -> 10.1 us  [the longest x1 5.38 us: shards(): from_left = lax.ppermute(to_right, 'x', right)]
    all_to_all x1, blocking collectives: 26.1 us -> 19.4 us  [shards(): got = lax.all_to_all(send, 'y', 0, 0, tiled=True)]
    unnamed x20 -> x22, local copies, waits for them, and re-layouts: 3.77 us -> 9.93 us
  transfers between devices with their start and end apart: 4 -> 12, of which waited for: 3 -> 5; matrix products, arithmetic and copies ran while one was open for 2% -> 2% of each run, Pallas kernels for 2% -> 11%
where the time goes in v5:
time: 176 us; the launch traced here: 175 us
  blocking collectives  55.3 us (31%)
  starting transfers between devices  45.7 us (26%)
  waiting for transfers between devices  33.1 us (19%)
  Pallas kernels  26.6 us (15%)
  local copies, waits for them, and re-layouts  13 us (7%)
    all_to_all x1, blocking collectives, shards(): pieces = lax.all_to_all(copies, 'zl', 0, 0, tiled=True)  21.5 us
    all_to_all x1, blocking collectives, shards(): got = lax.all_to_all(send, 'y', 0, 0, tiled=True)  19.4 us
    all_to_all x1, blocking collectives, shards(): summed = lax.all_to_all(summed, 'zl', 0, 0, tiled=True)  14.4 us
    all_to_all x1, waiting for transfers between devices, shards(): states = lax.all_to_all(send, ('zh', 'core'), 0, 0, tiled=True)  14.3 us
    pallas_call x5, Pallas kernels, partials(): pl.pallas_call(functools.partial(partials_kernel, sizes, offset), in_spec...  10.8 us
    all_to_all x1, starting transfers between devices, shards(): states = lax.all_to_all(send, ('zh', 'core'), 0, 0, tiled=True)  10.5 us
    unnamed x22, local copies, waits for them, and re-layouts  9.93 us
    ppermute x1, waiting for transfers between devices, shards(): near = lax.ppermute(near, CTX, to_prev)  8.75 us
  transfers between devices with their start and end apart: 12, of which 5 were waited for; matrix products, arithmetic and copies ran while one was open for 2% of the time, Pallas kernels for 11%

profile of v5, /device:TPU:6, one launch (start us, length us, event | category | flops | bytes accessed | tf_op | source)
XLA Modules:
  0.0 175.4 jit_solution(2014694528988985995)
XLA Ops:
  0.6 0.0 copy-start.4
  0.7 1.0 copy-done.6
  1.6 0.8 copy-done.7
  2.5 21.5 %all_to_all.25.refs_0_ = bf16[4,256,256]{2,1,0:T(8,128)(2,1)S(1)} all-to-all(bf16[4,256,256]{2,1,0:T(8,128)(2,1)S(1)} %get-tuple-element.13), channel_id=1, replica_groups=mesh['y'=8,'zh'=4,'core'=2,'x'=4,'zl'=4] {'zl'}, dimensions={0} | all-to-all | bytes 1048576 | tf_op jit(solution)/shard_map/all_to_all | solution.py:382
  24.1 6.2 %collective-permute-start = (bf16[4,256,256]{2,1,0:T(8,128)(2,1)S(1)}, bf16[4,256,256]{2,1,0:T(8,128)(2,1)S(1)}, u32[]{:S(2)}, u32[]{:S(2)}) collective-permute-start(bf16[4,256,256]{2,1,0:T(8,128)(2,1)S(1)} %all_to_all.25.refs_0_), channel_id=1, source_target_pairs={{0,4},{4,8},{8,12},{12,0},{1,5},{5,9},{9,13},{13,1},{2,6},{6,10},{... | collective-permute-start | bytes 1572872 | tf_op jit(solution)/shard_map/ppermute | solution.py:389
  30.2 1.9 %collective-permute-start.2 = (bf16[4,256,256]{2,1,0:T(8,128)(2,1)S(1)}, bf16[4,256,256]{2,1,0:T(8,128)(2,1)}, u32[]{:S(2)}, u32[]{:S(2)}) collective-permute-start(bf16[4,256,256]{2,1,0:T(8,128)(2,1)S(1)} %all_to_all.25.refs_0_), channel_id=1, source_target_pairs={{0,12},{4,0},{8,4},{12,8},{1,13},{5,1},{9,5},{13,9},{2,14},{6,2},{... | collective-permute-start | bytes 1572872 | tf_op jit(solution)/shard_map/ppermute | solution.py:390
  32.2 1.3 collective-permute-start.4
  33.5 1.3 collective-permute-start.5
  34.8 8.7 %collective-permute-done.5.near = bf16[16,256]{1,0:T(8,128)(2,1)S(1)} collective-permute-done((bf16[16,256]{1,0:T(8,128)(2,1)S(1)}, bf16[16,256]{1,0:T(8,128)(2,1)S(1)}, u32[]{:S(2)}, u32[]{:S(2)}) %collective-permute-start.5) | collective-permute-done | bytes 8224 | tf_op jit(solution)/shard_map/ppermute | solution.py:381
  43.5 0.7 shard_map.96
  44.2 5.7 %all-to-all-start.1 = ((bf16[16,16,256]{2,1,0:T(8,128)(2,1)}), bf16[16,16,256]{2,1,0:T(8,128)(2,1)S(1)}, u32[]{:S(2)}, u32[]{:S(2)}) async-start(bf16[16,16,256]{2,1,0:T(8,128)(2,1)} %shard_map.96), calls=%async_computation.1 | async-start | bytes 262144 | tf_op jit(solution)/shard_map/all_to_all | solution.py:385
  49.9 0.7 slice.40
  50.6 2.0 %collective-permute-start.1 = (bf16[2,256,256]{2,1,0:T(8,128)(2,1)}, bf16[2,256,256]{2,1,0:T(8,128)(2,1)S(1)}, u32[]{:S(2)}, u32[]{:S(2)}) collective-permute-start(bf16[2,256,256]{2,1,0:T(8,128)(2,1)} %slice.40), channel_id=1, source_target_pairs={{0,4},{4,8},{8,12},{12,0},{1,5},{5,9},{9,13},{13,1},{2,6},{6,10},{... | collective-permute-start | bytes 786440 | tf_op jit(solution)/shard_map/ppermute | solution.py:391
  52.6 1.7 slice.41
  54.3 3.8 %collective-permute-start.3 = (bf16[2,256,256]{2,1,0:T(8,128)(2,1)}, bf16[2,256,256]{2,1,0:T(8,128)(2,1)}, u32[]{:S(2)}, u32[]{:S(2)}) collective-permute-start(bf16[2,256,256]{2,1,0:T(8,128)(2,1)} %slice.41), channel_id=1, source_target_pairs={{0,12},{4,0},{8,4},{12,8},{1,13},{5,1},{9,5},{13,9},{2,14},{6,2},{... | collective-permute-start | bytes 786440 | tf_op jit(solution)/shard_map/ppermute | solution.py:392
  58.1 0.1 pad_add_fusion.place_ref
  58.2 2.8 %copy-done = bf16[4096,3,256]{2,0,1:T(8,128)(2,1)S(1)} copy-done((bf16[4096,3,256]{2,0,1:T(8,128)(2,1)S(1)}, bf16[4096,3,256]{2,0,1:T(8,128)(2,1)}, u32[]{:S(2)}) %copy-start) | copy-done | bytes 6291480
  61.0 1.6 copy-done.3
  62.6 1.8 %shard_map.97.refs_5_ = f32[4,144,256]{2,1,0:T(8,128)S(1)} custom-call(s32[3]{0:T(128)S(1)} %pad_add_fusion.place_ref, bf16[4,256,256]{2,1,0:T(8,128)(2,1)S(1)} %all_to_all.25.refs_0_, bf16[16,16,256]{2,1,0:T(8,128)(2,1)S(1)} %all-to-all-done.1.refs_1_.refs_2_, bf16[3,4096,256]{2,1,0:T(8,128)(2,1)S(1)} %bitcast.10, bf16[256,4096]{1,0:T(8,128)(2,1)S(1)} %copy-done.3), custom_call_target="tpu_custom_call" | custom-call | flops 301989888 | bytes 2097152 | tf_op jit(solution)/shard_map/pallas_call | solution.py:270
  64.5 0.9 copy-done.1
  65.4 3.5 %shard_map.98.refs_5_ = f32[4,144,256]{2,1,0:T(8,128)S(1)} custom-call(s32[3]{0:T(128)S(1)} %pad_add_fusion.place_ref, bf16[4,256,256]{2,1,0:T(8,128)(2,1)S(1)} %collective-permute-done.refs_0_, bf16[4,256,256]{2,1,0:T(8,128)(2,1)} %collective-permute-done.2.refs_1_, bf16[16,16,256]{2,1,0:T(8,128)(2,1)S(1)} %all-to-all-done.1.refs_1_.refs_2_, ...), custom_call_target="tpu_custom_call" | custom-call | flops 603979776 | bytes 4194304 | tf_op jit(solution)/shard_map/pallas_call | solution.py:270
  68.9 2.3 %shard_map.99 = bf16[4,144,256]{2,1,0:T(8,128)(2,1)S(1)} custom-call(s32[3]{0:T(128)S(1)} %pad_add_fusion.place_ref, bf16[2,256,256]{2,1,0:T(8,128)(2,1)S(1)} %collective-permute-done.1.refs_0_, bf16[2,256,256]{2,1,0:T(8,128)(2,1)} %collective-permute-done.3.refs_1_, bf16[16,16,256]{2,1,0:T(8,128)(2,1)S(1)} %all-to-all-done.1.refs_1_.refs_2_, ...), custom_call_target="tpu_custom_call" | custom-call | flops 301989888 | bytes 2097152 | tf_op jit(solution)/shard_map/pallas_call | solution.py:270
  71.3 1.7 shard_map.101
  72.9 19.4 %all_to_all.26.got_ref = bf16[8,16,256]{2,1,0:T(8,128)(2,1)S(1)} all-to-all(bf16[8,16,256]{2,1,0:T(8,128)(2,1)S(1)} %get-tuple-element.21), channel_id=1, replica_groups=mesh['y'=8,'zh'=4,'core'=2,'x'=4,'zl'=4] {'y'}, dimensions={0} | all-to-all | bytes 131072 | tf_op jit(solution)/shard_map/all_to_all | solution.py:420
  92.3 1.4 shard_map.102
  93.7 10.5 %all-to-all-start.3 = ((bf16[8,32,256]{2,1,0:T(8,128)(2,1)}), bf16[8,32,256]{2,1,0:T(8,128)(2,1)S(1)}, u32[]{:S(2)}, u32[]{:S(2)}) async-start(bf16[8,32,256]{2,1,0:T(8,128)(2,1)} %shard_map.102), calls=%async_computation.3 | async-start | bytes 262144 | tf_op jit(solution)/shard_map/all_to_all | solution.py:431
  104.2 3.2 %shard_map.100 = (f32[136,256]{1,0:T(8,128)S(1)}, f32[136,256]{1,0:T(8,128)S(1)}) custom-call(bf16[3,144,256]{2,1,0:T(8,128)(2,1)S(1)} %slice.42.proj_ref, bf16[144,256]{1,0:T(8,128)(2,1)S(1)} %slice_bitcast_fusion.back_ref, f32[3,3,256]{2,1,0:T(4,128)S(1)} %bitcast.23, f32[16,256]{1,0:T(8,128)S(1)} %bitcast.20, f32[16,256]{1,0:T(8,128)S(1)} %bitcast.25, ...), custom_call_target="tpu_custom_call" | custom-call | flops 3000000000 | tf_op jit(solution)/shard_map/pallas_call | solution.py:188
  107.4 14.3 %all-to-all-done.3.got_ref = bf16[8,32,256]{2,1,0:T(8,128)(2,1)S(1)} async-done(((bf16[8,32,256]{2,1,0:T(8,128)(2,1)}), bf16[8,32,256]{2,1,0:T(8,128)(2,1)S(1)}, u32[]{:S(2)}, u32[]{:S(2)}) %all-to-all-start.3) | async-done | bytes 131104 | tf_op jit(solution)/shard_map/all_to_all | solution.py:431
  121.7 1.2 shard_map.103
  123.0 2.8 %copy-done.2 = bf16[4096,3,256]{2,0,1:T(8,128)(2,1)S(1)} copy-done((bf16[4096,3,256]{2,0,1:T(8,128)(2,1)S(1)}, bf16[4096,3,256]{2,0,1:T(8,128)(2,1)}, u32[]{:S(2)}) %copy-start.2) | copy-done | bytes 6291480
  125.8 1.6 shard_map.106
  127.3 3.7 %collective-permute-start.6 = (bf16[2,256,256]{2,1,0:T(8,128)(2,1)S(1)}, bf16[2,256,256]{2,1,0:T(8,128)(2,1)S(1)}, u32[]{:S(2)}, u32[]{:S(2)}) collective-permute-start(bf16[2,256,256]{2,1,0:T(8,128)(2,1)S(1)} %shard_map.106), channel_id=1, source_target_pairs={{0,4},{4,8},{8,12},{12,0},{1,5},{5,9},{9,13},{13,1},{2,6},{6,10},{... | collective-permute-start | bytes 786440 | tf_op jit(solution)/shard_map/ppermute | solution.py:448
  131.0 2.6 %shard_map.105 = bf16[4,256,256]{2,1,0:T(8,128)(2,1)S(1)} custom-call(s32[3]{0:T(128)S(1)} %pad_add_fusion.place_ref, bf16[128,256]{1,0:T(8,128)(2,1)S(1)} %get-tuple-element.22.hidden, bf16[3,128,256]{2,1,0:T(8,128)(2,1)S(1)} %get-tuple-element.23.grad, bf16[3,4096,256]{2,1,0:T(8,128)(2,1)S(1)} %bitcast.14, bf16[256,4096]{1,0:T(8,128)(2,1)S(1)} %copy-done.4), custom_call_target="tpu_custom_call" | custom-call | flops 268435456 | bytes 2097152 | tf_op jit(solution)/shard_map/pallas_call | solution.py:316
  133.6 1.6 shard_map.108
  135.2 2.3 %collective-permute-start.8 = (bf16[2,256,256]{2,1,0:T(8,128)(2,1)S(1)}, bf16[2,256,256]{2,1,0:T(8,128)(2,1)S(1)}, u32[]{:S(2)}, u32[]{:S(2)}) collective-permute-start(bf16[2,256,256]{2,1,0:T(8,128)(2,1)S(1)} %shard_map.108), channel_id=1, source_target_pairs={{0,12},{4,0},{8,4},{12,8},{1,13},{5,1},{9,5},{13,9},{2,14},{6,2},{... | collective-permute-start | bytes 786440 | tf_op jit(solution)/shard_map/ppermute | solution.py:449
  137.5 2.6 %shard_map.107 = bf16[4,256,256]{2,1,0:T(8,128)(2,1)S(1)} custom-call(s32[3]{0:T(128)S(1)} %pad_add_fusion.place_ref, bf16[128,256]{1,0:T(8,128)(2,1)S(1)} %get-tuple-element.22.hidden, bf16[3,128,256]{2,1,0:T(8,128)(2,1)S(1)} %get-tuple-element.23.grad, bf16[3,4096,256]{2,1,0:T(8,128)(2,1)S(1)} %bitcast.16, bf16[256,4096]{1,0:T(8,128)(2,1)S(1)} %copy-done.4), custom_call_target="tpu_custom_call" | custom-call | flops 268435456 | bytes 2097152 | tf_op jit(solution)/shard_map/pallas_call | solution.py:316
  140.1 0.1 add_convert_fusion.2
  140.3 4.7 %collective-permute-start.7 = (bf16[4,256,256]{2,1,0:T(8,128)(2,1)S(1)}, bf16[4,256,256]{2,1,0:T(8,128)(2,1)S(1)}, u32[]{:S(2)}, u32[]{:S(2)}) collective-permute-start(bf16[4,256,256]{2,1,0:T(8,128)(2,1)S(1)} %pad_maximum_fusion), channel_id=1, source_target_pairs={{0,4},{4,8},{8,12},{12,0},{1,5},{5,9},{9,13},{13,1},{2,6},{6,10},{... | collective-permute-start | bytes 1572872 | tf_op jit(solution)/shard_map/ppermute | solution.py:454
  145.0 0.1 collective-permute-done.8
  145.0 0.1 add_convert_fusion.1
  145.2 2.3 %collective-permute-start.9 = (bf16[4,256,256]{2,1,0:T(8,128)(2,1)S(1)}, bf16[4,256,256]{2,1,0:T(8,128)(2,1)S(1)}, u32[]{:S(2)}, u32[]{:S(2)}) collective-permute-start(bf16[4,256,256]{2,1,0:T(8,128)(2,1)S(1)} %pad_maximum_fusion.1), channel_id=1, source_target_pairs={{0,12},{4,0},{8,4},{12,8},{1,13},{5,1},{9,5},{13,9},{2,14},{6,2},{... | collective-permute-start | bytes 1572872 | tf_op jit(solution)/shard_map/ppermute | solution.py:455
  147.5 2.6 %shard_map.104 = bf16[4,256,256]{2,1,0:T(8,128)(2,1)S(1)} custom-call(s32[3]{0:T(128)S(1)} %pad_add_fusion.place_ref, bf16[128,256]{1,0:T(8,128)(2,1)S(1)} %get-tuple-element.22.hidden, bf16[3,128,256]{2,1,0:T(8,128)(2,1)S(1)} %get-tuple-element.23.grad, bf16[3,4096,256]{2,1,0:T(8,128)(2,1)S(1)} %bitcast.17, bf16[256,4096]{1,0:T(8,128)(2,1)S(1)} %copy-done.4), custom_call_target="tpu_custom_call" | custom-call | flops 268435456 | bytes 2097152 | tf_op jit(solution)/shard_map/pallas_call | solution.py:316
  150.1 5.4 %collective-permute-done.7 = bf16[4,256,256]{2,1,0:T(8,128)(2,1)S(1)} collective-permute-done((bf16[4,256,256]{2,1,0:T(8,128)(2,1)S(1)}, bf16[4,256,256]{2,1,0:T(8,128)(2,1)S(1)}, u32[]{:S(2)}, u32[]{:S(2)}) %collective-permute-start.7) | collective-permute-done | bytes 524320 | tf_op jit(solution)/shard_map/ppermute | solution.py:454
  155.4 4.6 %collective-permute-done.9 = bf16[4,256,256]{2,1,0:T(8,128)(2,1)S(1)} collective-permute-done((bf16[4,256,256]{2,1,0:T(8,128)(2,1)S(1)}, bf16[4,256,256]{2,1,0:T(8,128)(2,1)S(1)}, u32[]{:S(2)}, u32[]{:S(2)}) %collective-permute-start.9) | collective-permute-done | bytes 524320 | tf_op jit(solution)/shard_map/ppermute | solution.py:455
  160.1 0.2 add_convert_fusion
  160.3 14.4 %all_to_all.27 = bf16[4,256,256]{2,1,0:T(8,128)(2,1)S(1)} all-to-all(bf16[4,256,256]{2,1,0:T(8,128)(2,1)S(1)} %add_convert_fusion), channel_id=1, replica_groups=mesh['y'=8,'zh'=4,'core'=2,'x'=4,'zl'=4] {'zl'}, dimensions={0} | all-to-all | bytes 1048576 | tf_op jit(solution)/shard_map/all_to_all | solution.py:457
  174.6 0.1 reduce_sum.12
  174.7 0.7 fusion
  (29 shorter events, 0.3 us)
Async XLA Ops:
  0.6 63.8 %copy-start.4 = (bf16[256,4096]{1,0:T(8,128)(2,1)S(1)}, bf16[256,4096]{1,0:T(8,128)(2,1)}, u32[]{:S(2)}) copy-start(bf16[256,4096]{1,0:T(8,128)(2,1)} %weight_out.9) | copy-start | bytes 6291460
  0.6 1.0 copy-start.6
  1.6 0.8 copy-start.7
  24.1 25.8 %collective-permute-start = (bf16[4,256,256]{2,1,0:T(8,128)(2,1)S(1)}, bf16[4,256,256]{2,1,0:T(8,128)(2,1)S(1)}, u32[]{:S(2)}, u32[]{:S(2)}) collective-permute-start(bf16[4,256,256]{2,1,0:T(8,128)(2,1)S(1)} %all_to_all.25.refs_0_), channel_id=1, source_target_pairs={{0,4},{4,8},{8,12},{12,0},{1,5},{5,9},{9,13},{13,1},{2,6},{6,10},{... | collective-permute-start | bytes 1572872 | tf_op jit(solution)/shard_map/ppermute | solution.py:389
  30.2 22.4 %collective-permute-start.2 = (bf16[4,256,256]{2,1,0:T(8,128)(2,1)S(1)}, bf16[4,256,256]{2,1,0:T(8,128)(2,1)}, u32[]{:S(2)}, u32[]{:S(2)}) collective-permute-start(bf16[4,256,256]{2,1,0:T(8,128)(2,1)S(1)} %all_to_all.25.refs_0_), channel_id=1, source_target_pairs={{0,12},{4,0},{8,4},{12,8},{1,13},{5,1},{9,5},{13,9},{2,14},{6,2},{... | collective-permute-start | bytes 1572872 | tf_op jit(solution)/shard_map/ppermute | solution.py:390
  32.2 2.6 %collective-permute-start.4 = (bf16[16,256]{1,0:T(8,128)(2,1)S(1)}, bf16[16,256]{1,0:T(8,128)(2,1)S(1)}, u32[]{:S(2)}, u32[]{:S(2)}) collective-permute-start(bf16[16,256]{1,0:T(8,128)(2,1)S(1)} %get-tuple-element.14), channel_id=1, source_target_pairs={{0,16},{16,32},{32,48},{48,64},{64,80},{80,96},{96,112},{112,128},... | collective-permute-start | bytes 24584 | tf_op jit(solution)/shard_map/ppermute | solution.py:380
  33.5 10.1 %collective-permute-start.5 = (bf16[16,256]{1,0:T(8,128)(2,1)S(1)}, bf16[16,256]{1,0:T(8,128)(2,1)S(1)}, u32[]{:S(2)}, u32[]{:S(2)}) collective-permute-start(bf16[16,256]{1,0:T(8,128)(2,1)S(1)} %get-tuple-element.15), channel_id=1, source_target_pairs={{16,0},{32,16},{48,32},{64,48},{80,64},{96,80},{112,96},{128,112},... | collective-permute-start | bytes 24584 | tf_op jit(solution)/shard_map/ppermute | solution.py:381
  44.2 14.0 %all-to-all-start.1 = ((bf16[16,16,256]{2,1,0:T(8,128)(2,1)}), bf16[16,16,256]{2,1,0:T(8,128)(2,1)S(1)}, u32[]{:S(2)}, u32[]{:S(2)}) async-start(bf16[16,16,256]{2,1,0:T(8,128)(2,1)} %shard_map.96), calls=%async_computation.1 | async-start | bytes 262144 | tf_op jit(solution)/shard_map/all_to_all | solution.py:385
  50.6 18.3 %collective-permute-start.1 = (bf16[2,256,256]{2,1,0:T(8,128)(2,1)}, bf16[2,256,256]{2,1,0:T(8,128)(2,1)S(1)}, u32[]{:S(2)}, u32[]{:S(2)}) collective-permute-start(bf16[2,256,256]{2,1,0:T(8,128)(2,1)} %slice.40), channel_id=1, source_target_pairs={{0,4},{4,8},{8,12},{12,0},{1,5},{5,9},{9,13},{13,1},{2,6},{6,10},{... | collective-permute-start | bytes 786440 | tf_op jit(solution)/shard_map/ppermute | solution.py:391
  54.3 14.6 %collective-permute-start.3 = (bf16[2,256,256]{2,1,0:T(8,128)(2,1)}, bf16[2,256,256]{2,1,0:T(8,128)(2,1)}, u32[]{:S(2)}, u32[]{:S(2)}) collective-permute-start(bf16[2,256,256]{2,1,0:T(8,128)(2,1)} %slice.41), channel_id=1, source_target_pairs={{0,12},{4,0},{8,4},{12,8},{1,13},{5,1},{9,5},{13,9},{2,14},{6,2},{... | collective-permute-start | bytes 786440 | tf_op jit(solution)/shard_map/ppermute | solution.py:392
  58.2 2.8 %copy-start = (bf16[4096,3,256]{2,0,1:T(8,128)(2,1)S(1)}, bf16[4096,3,256]{2,0,1:T(8,128)(2,1)}, u32[]{:S(2)}) copy-start(bf16[4096,3,256]{2,0,1:T(8,128)(2,1)} %param.10) | copy-start | bytes 18874372
  61.0 1.6 copy-start.3
  62.6 2.8 %copy-start.1 = (bf16[4096,3,256]{2,0,1:T(8,128)(2,1)S(1)}, bf16[4096,3,256]{2,0,1:T(8,128)(2,1)}, u32[]{:S(2)}) copy-start(bf16[4096,3,256]{2,0,1:T(8,128)(2,1)} %param.10) | copy-start | bytes 18874372
  68.8 2.4 %copy-start.5 = (f32[256,16]{0,1:T(8,128)S(1)}, f32[256,16]{0,1:T(8,128)}, u32[]{:S(2)}) copy-start(f32[256,16]{0,1:T(8,128)} %param.14) | copy-start | bytes 49156
  68.8 2.4 %copy-start.8 = (f32[3,256,3]{1,2,0:T(4,128)S(1)}, f32[3,256,3]{1,2,0:T(4,128)}, u32[]{:S(2)}) copy-start(f32[3,256,3]{1,2,0:T(4,128)} %param.12) | copy-start | bytes 27652
  68.9 35.3 %copy-start.9 = (f32[256,16]{0,1:T(8,128)S(1)}, f32[256,16]{0,1:T(8,128)}, u32[]{:S(2)}) copy-start(f32[256,16]{0,1:T(8,128)} %param.13) | copy-start | bytes 49156
  68.9 35.3 %copy-start.10 = (f32[256]{0:T(256)S(1)}, f32[256]{0:T(256)}, u32[]{:S(2)}) copy-start(f32[256]{0:T(256)} %param.15) | copy-start | bytes 3076
  93.7 28.0 %all-to-all-start.3 = ((bf16[8,32,256]{2,1,0:T(8,128)(2,1)}), bf16[8,32,256]{2,1,0:T(8,128)(2,1)S(1)}, u32[]{:S(2)}, u32[]{:S(2)}) async-start(bf16[8,32,256]{2,1,0:T(8,128)(2,1)} %shard_map.102), calls=%async_computation.3 | async-start | bytes 262144 | tf_op jit(solution)/shard_map/all_to_all | solution.py:431
  123.0 2.8 %copy-start.2 = (bf16[4096,3,256]{2,0,1:T(8,128)(2,1)S(1)}, bf16[4096,3,256]{2,0,1:T(8,128)(2,1)}, u32[]{:S(2)}) copy-start(bf16[4096,3,256]{2,0,1:T(8,128)(2,1)} %param.10) | copy-start | bytes 18874372
  127.3 12.8 %collective-permute-start.6 = (bf16[2,256,256]{2,1,0:T(8,128)(2,1)S(1)}, bf16[2,256,256]{2,1,0:T(8,128)(2,1)S(1)}, u32[]{:S(2)}, u32[]{:S(2)}) collective-permute-start(bf16[2,256,256]{2,1,0:T(8,128)(2,1)S(1)} %shard_map.106), channel_id=1, source_target_pairs={{0,4},{4,8},{8,12},{12,0},{1,5},{5,9},{9,13},{13,1},{2,6},{6,10},{... | collective-permute-start | bytes 786440 | tf_op jit(solution)/shard_map/ppermute | solution.py:448
  135.2 9.9 %collective-permute-start.8 = (bf16[2,256,256]{2,1,0:T(8,128)(2,1)S(1)}, bf16[2,256,256]{2,1,0:T(8,128)(2,1)S(1)}, u32[]{:S(2)}, u32[]{:S(2)}) collective-permute-start(bf16[2,256,256]{2,1,0:T(8,128)(2,1)S(1)} %shard_map.108), channel_id=1, source_target_pairs={{0,12},{4,0},{8,4},{12,8},{1,13},{5,1},{9,5},{13,9},{2,14},{6,2},{... | collective-permute-start | bytes 786440 | tf_op jit(solution)/shard_map/ppermute | solution.py:449
  140.3 15.2 %collective-permute-start.7 = (bf16[4,256,256]{2,1,0:T(8,128)(2,1)S(1)}, bf16[4,256,256]{2,1,0:T(8,128)(2,1)S(1)}, u32[]{:S(2)}, u32[]{:S(2)}) collective-permute-start(bf16[4,256,256]{2,1,0:T(8,128)(2,1)S(1)} %pad_maximum_fusion), channel_id=1, source_target_pairs={{0,4},{4,8},{8,12},{12,0},{1,5},{5,9},{9,13},{13,1},{2,6},{6,10},{... | collective-permute-start | bytes 1572872 | tf_op jit(solution)/shard_map/ppermute | solution.py:454
  145.2 14.9 %collective-permute-start.9 = (bf16[4,256,256]{2,1,0:T(8,128)(2,1)S(1)}, bf16[4,256,256]{2,1,0:T(8,128)(2,1)S(1)}, u32[]{:S(2)}, u32[]{:S(2)}) collective-permute-start(bf16[4,256,256]{2,1,0:T(8,128)(2,1)S(1)} %pad_maximum_fusion.1), channel_id=1, source_target_pairs={{0,12},{4,0},{8,4},{12,8},{1,13},{5,1},{9,5},{13,9},{2,14},{6,2},{... | collective-permute-start | bytes 1572872 | tf_op jit(solution)/shard_map/ppermute | solution.py:455

commit v6 on v5

v6 whole, which is shorter than its diff:
```python
import functools

import jax
import jax.numpy as jnp
from jax import lax
from jax.experimental import pallas as pl
from jax.experimental.pallas import tpu as pltpu
from jax.sharding import Mesh
from jax.sharding import PartitionSpec as P

CTX = ("y", "zh", "core")
TP = ("x", "zl")
TILE = 8
AHEAD = 2
GRANT = 16 * 2**20
BF16 = jnp.bfloat16
F32 = jnp.float32


def copy_kernel(tokens, cotangent, copies):
    block = tokens.shape[0]
    for i in range(copies.shape[0]):
        copies[i, :block] = tokens[...]
        copies[i, block:] = cotangent[...]


def features(ext, proj_ref, taps_ref, rows, last=None, first=None):
    block, width = proj_ref.shape[1:]
    zero = jnp.zeros((TILE, width), F32)
    out = []
    for p in range(3):
        ext[p, :TILE] = zero
        ext[p, TILE : TILE + block] = proj_ref[p].astype(F32)
        ext[p, TILE + block :] = zero
        if last is not None:
            ext[p, TILE - AHEAD : TILE] = last[AHEAD * p : AHEAD * (p + 1)]
            ext[p, TILE + block : TILE + block + AHEAD] = first[AHEAD * p : AHEAD * (p + 1)]
        total = taps_ref[p, 0:1, :] * ext[p, TILE : TILE + rows]
        for k in range(1, 3):
            total = total + taps_ref[p, k : k + 1, :] * ext[p, TILE - k : TILE - k + rows]
        out.append(total)
    return out


def inner_rows(ext, proj_ref, taps_ref, rows):
    block, width = proj_ref.shape[1:]
    query, key_part, value_part = features(ext, proj_ref, taps_ref, rows)
    row = lax.broadcasted_iota(jnp.int32, (rows, 1), 0)
    inside = (row >= AHEAD) & (row < block)
    back = jnp.concatenate([proj_ref[3].astype(F32), jnp.zeros((TILE, width), F32)], axis=0)
    gated = jnp.where(inside, key_part * value_part, 0.0)
    return gated, jnp.where(inside, back * query, 0.0), row.astype(F32)


def state_kernel(proj_ref, taps_ref, rates_ref, send_ref, ext, pack):
    order = rates_ref.shape[0]
    block = proj_ref.shape[1]
    gated, grad_conv, time = inner_rows(ext, proj_ref, taps_ref, block + TILE)
    for r in range(order):
        rate = rates_ref[r : r + 1, :]
        fwd = jnp.exp(-rate * (block - 1.0 - time)) * gated
        bwd = jnp.exp(-rate * (time - AHEAD)) * grad_conv
        pack[r : r + 1] = jnp.sum(fwd, axis=0, keepdims=True)
        pack[order + r : order + r + 1] = jnp.sum(bwd, axis=0, keepdims=True)
    at = 2 * order
    pack[at + TILE :] = jnp.zeros((TILE, pack.shape[1]), F32)
    for p in range(4):
        rows = proj_ref[p].astype(F32)
        pack[at + AHEAD * p : at + AHEAD * (p + 1)] = rows[:AHEAD]
        if p < 3:
            ends = at + TILE + AHEAD * p
            pack[ends : ends + AHEAD] = rows[block - AHEAD :]
    for i in range(send_ref.shape[0]):
        send_ref[i] = pack[...].astype(BF16)


def joint(taps_ref, first, last):
    row = []
    for p in range(3):
        a, b = first[AHEAD * p : AHEAD * p + 1], first[AHEAD * p + 1 : AHEAD * p + 2]
        c, d = last[AHEAD * p : AHEAD * p + 1], last[AHEAD * p + 1 : AHEAD * p + 2]
        t = [taps_ref[p, k : k + 1, :] for k in range(3)]
        row.append((t[0] * a + t[1] * d + t[2] * c, t[0] * b + t[1] * a + t[2] * d))
    back = (first[3 * AHEAD : 3 * AHEAD + 1], first[3 * AHEAD + 1 : 3 * AHEAD + 2])
    gated = tuple(row[1][i] * row[2][i] for i in range(AHEAD))
    return gated, tuple(back[i] * row[0][i] for i in range(AHEAD))


def fader(rates, block):
    def fade(blocks):
        if isinstance(blocks, int):
            return jnp.exp(-rates * float(block * blocks))
        return jnp.exp(-rates * (block * jnp.maximum(blocks, 0)).astype(F32))

    return fade


def group_states(block, taps_ref, rates, got_ref):
    order = rates.shape[0]
    members = got_ref.shape[0]
    fwd, bwd, firsts, lasts = [], [], [], []
    for j in range(members):
        got = got_ref[j].astype(F32)
        fwd.append(got[:order])
        bwd.append(got[order : 2 * order])
        firsts.append(got[2 * order : 2 * order + TILE])
        lasts.append(got[2 * order + TILE :])
    near, far = jnp.exp(-rates * (block - 2.0)), jnp.exp(-rates * (block - 1.0))
    for j in range(1, members):
        gated, grad_conv = joint(taps_ref, firsts[j], lasts[j - 1])
        fwd[j] = fwd[j] + far * gated[0] + near * gated[1]
        bwd[j - 1] = bwd[j - 1] + near * grad_conv[0] + far * grad_conv[1]
    return fwd, bwd, firsts, lasts, near, far


def chain_kernel(block, place_ref, taps_ref, rates_ref, got_ref, send_ref):
    rates = rates_ref[...]
    order = rates.shape[0]
    fade = fader(rates, block)
    fwd, bwd, firsts, lasts, _, _ = group_states(block, taps_ref, rates, got_ref)
    members = len(fwd)
    total_fwd = sum(fade(members - 1 - j) * fwd[j] for j in range(members))
    total_bwd = sum(fade(j) * bwd[j] for j in range(members))
    ends = jnp.concatenate([firsts[0], lasts[-1]], axis=0).astype(BF16)
    for i in range(send_ref.shape[0]):
        send_ref[i, :order] = jnp.where(place_ref[0] < i, total_fwd, total_bwd).astype(BF16)
        send_ref[i, order:] = ends


def local_kernel(
    proj_ref, taps_ref, rates_ref, res_ref, skip_ref, conv_ref, grad_ref, ext, pad, filt_ref
):
    rows, width = conv_ref.shape
    gated, grad_conv, time = inner_rows(ext, proj_ref, taps_ref, rows)
    taps = jnp.zeros((rows, width), F32)
    for r in range(rates_ref.shape[0]):
        taps = taps + res_ref[r : r + 1, :] * jnp.exp(-rates_ref[r : r + 1, :] * (time + 1.0))
    filt_ref[...] = taps
    zero = jnp.zeros((TILE, width), F32)
    pad[0, :TILE] = zero
    pad[0, TILE:] = gated
    pad[1, :rows] = grad_conv
    pad[1, rows:] = zero
    direct = skip_ref[...] + jnp.sum(res_ref[...], axis=0, keepdims=True)
    for lane in range(0, width, 128):
        lanes = slice(lane, lane + 128)
        total = direct[:, lanes] * pad[0, TILE:, lanes]
        for m in range(1, TILE + 1):
            moved = pad[0, TILE - m : TILE - m + rows, lanes]
            for q in range(0, rows, TILE):
                tap = filt_ref[q + m - 1 : q + m, lanes]
                part = total[q:] + tap * moved[: rows - q]
                total = part if q == 0 else jnp.concatenate([total[:q], part], axis=0)
        conv_ref[:, lanes] = total
        total = direct[:, lanes] * pad[1, :rows, lanes]
        for m in range(1, TILE + 1):
            moved = pad[1, m : m + rows, lanes]
            for q in range(0, rows, TILE):
                tap = filt_ref[q + m - 1 : q + m, lanes]
                part = total[: rows - q] + tap * moved[q:]
                total = part if q == 0 else jnp.concatenate([part, total[rows - q :]], axis=0)
        grad_ref[:, lanes] = total


def finish_kernel(
    place_ref, proj_ref, taps_ref, rates_ref, res_ref, skip_ref, conv_ref, grad_ref,
    near_ref, far_ref, hidden_ref, out_ref, ext, feat,
):
    rates = rates_ref[...]
    res_all = res_ref[...]
    skip = skip_ref[...]
    order, width = rates.shape
    rows = conv_ref.shape[0]
    block = rows - TILE
    group, member = place_ref[0], place_ref[1]
    groups, members = far_ref.shape[0], near_ref.shape[0]
    fade = fader(rates, block)
    fwd, bwd, firsts, lasts, near, far = group_states(block, taps_ref, rates, near_ref)

    def rows_of(ref, index, start, there):
        got = ref[jnp.where(there, index, 0)].astype(F32)
        return jnp.where(there, got[start : start + TILE], 0.0)

    nothing = jnp.zeros((TILE, width), F32)
    whole = [far_ref[i].astype(F32) for i in range(groups)]
    head = [w[order : order + TILE] for w in whole] + [nothing]
    tail = [nothing] + [w[order + TILE :] for w in whole]
    ahead = jnp.zeros_like(rates)
    behind = jnp.zeros_like(rates)
    for i in range(groups):
        gated, _ = joint(taps_ref, head[i], tail[i])
        total = whole[i][:order] + fade(members - 1) * (far * gated[0] + near * gated[1])
        ahead = ahead + jnp.where(i < group, fade(members * (group - 1 - i)) * total, 0.0)
        _, grad_conv = joint(taps_ref, head[i + 1], tail[i + 1])
        total = whole[i][:order] + fade(members - 1) * (near * grad_conv[0] + far * grad_conv[1])
        behind = behind + jnp.where(i > group, fade(members * (i - 1 - group)) * total, 0.0)
    tail_before = rows_of(far_ref, group - 1, order + TILE, group > 0)
    head_behind = rows_of(far_ref, group + 1, order, group < groups - 1)
    gated, _ = joint(taps_ref, firsts[0], tail_before)
    _, grad_conv = joint(taps_ref, head_behind, lasts[-1])
    fwd[0] = fwd[0] + far * gated[0] + near * gated[1]
    bwd[-1] = bwd[-1] + near * grad_conv[0] + far * grad_conv[1]
    ahead = fade(member) * ahead
    behind = fade(members - 1 - member) * behind
    for j in range(members):
        ahead = ahead + jnp.where(j < member, fade(member - 1 - j) * fwd[j], 0.0)
        behind = behind + jnp.where(j > member, fade(j - 1 - member) * bwd[j], 0.0)

    last = rows_of(near_ref, member - 1, 2 * order + TILE, member > 0)
    last = jnp.where(member > 0, last, tail_before)
    first = rows_of(near_ref, member + 1, 2 * order, member < members - 1)
    first = jnp.where(member < members - 1, first, head_behind)
    query, key_part, value_part = features(ext, proj_ref, taps_ref, rows, last, first)
    row = lax.broadcasted_iota(jnp.int32, (TILE, 1), 0)
    next_back = jnp.where(row < AHEAD, pltpu.roll(first, AHEAD, 0), 0.0)
    back = jnp.concatenate([proj_ref[3].astype(F32), next_back], axis=0)
    gated = key_part * value_part
    grad_conv = back * query

    g = [gated[i : i + 1] for i in (0, 1, block, block + 1)]
    h = [grad_conv[i : i + 1] for i in (0, 1, block, block + 1)]
    grow = jnp.exp(rates)
    ahead = ahead + grow * g[0] + (grow * grow) * g[1]
    behind = behind + (grow * grow) * h[2] + grow * h[3]
    lag0 = skip + jnp.sum(res_all, axis=0, keepdims=True)
    lag1 = jnp.sum(res_all * jnp.exp(-rates), axis=0, keepdims=True)
    less = jnp.sum(res_all * grow, axis=0, keepdims=True)

    def two(a, b):
        return jnp.where(row == 0, a, jnp.where(row == 1, b, 0.0))

    def with_ends(array, top, bottom):
        return jnp.concatenate(
            [array[:TILE] + top, array[TILE:block], array[block:] + bottom], axis=0
        )

    conv_out = with_ends(
        conv_ref[...],
        two(skip * g[0] - less * g[1], skip * g[1]),
        two(lag0 * g[2], lag0 * g[3] + lag1 * g[2]),
    )
    grad_gated = with_ends(
        grad_ref[...],
        two(lag0 * h[0] + lag1 * h[1], lag0 * h[1]),
        two(skip * h[2], skip * h[3] - less * h[2]),
    )
    time = lax.broadcasted_iota(jnp.int32, (rows, 1), 0).astype(F32)
    ahead = res_all * ahead
    behind = res_all * behind
    for r in range(order):
        rate = rates[r : r + 1]
        conv_out = conv_out + ahead[r : r + 1] * jnp.exp(-rate * (time + 1.0))
        past = jnp.exp(-rate * (block + AHEAD - time))
        grad_gated = grad_gated + behind[r : r + 1] * past
    hidden_ref[...] = (query * conv_out)[:block].astype(BF16)
    feat[0] = back * conv_out
    feat[1] = grad_gated * value_part
    feat[2] = grad_gated * key_part
    for p in range(3):
        total = taps_ref[p, 0:1, :] * feat[p, :block]
        for k in range(1, 3):
            total = total + taps_ref[p, k : k + 1, :] * feat[p, k : k + block]
        out_ref[p] = total.astype(BF16)


def call(kernel, outs, scratch, *args, flops=0):
    whole = pl.BlockSpec(memory_space=pltpu.VMEM)
    specs = [
        pl.BlockSpec(memory_space=pltpu.SMEM) if a.dtype == jnp.int32 else whole for a in args
    ]
    cost = pl.CostEstimate(flops=flops, bytes_accessed=0, transcendentals=0) if flops else None
    return pl.pallas_call(
        kernel,
        out_shape=outs,
        scratch_shapes=scratch,
        in_specs=specs,
        out_specs=jax.tree.map(lambda _: whole, outs),
        cost_estimate=cost,
        compiler_params=pltpu.CompilerParams(vmem_limit_bytes=GRANT),
    )(*args)


def load_weights(blocks, weight_in, weight_out, held_in, held_out, sems):
    part = held_in.shape[2]
    copies = []
    for s, block in enumerate(blocks):
        at = pl.ds(pl.multiple_of(block * part, part), part)
        copies.append(
            (
                pltpu.make_async_copy(weight_in.at[:, at, :], held_in.at[s], sems.at[s, 0]),
                pltpu.make_async_copy(weight_out.at[:, at], held_out.at[s], sems.at[s, 1]),
            )
        )
        for copy in copies[-1]:
            copy.start()

    def ready(s):
        for copy in copies[s]:
            copy.wait()

    return ready


def project_kernel(sizes, offsets, first, last, place_ref, *refs):
    n_x, n_zl = sizes["x"], sizes["zl"]
    pieces, refs = refs[: len(offsets)], refs[len(offsets) :]
    weight_in, weight_out = refs[:2]
    old = None if first else refs[2]
    out, held_in, held_out, sems = refs[2 + (not first) : 6 + (not first)]
    total = refs[-1] if last else out
    block = pieces[0].shape[1] // 2
    work = [
        (piece, j, lax.rem(place_ref[2] + k, n_x) * n_zl + start + j)
        for piece, (k, start) in zip(pieces, offsets)
        for j in range(piece.shape[0])
    ]
    ready = load_weights([w[2] for w in work], weight_in, weight_out, held_in, held_out, sems)
    for s, (piece, j, _) in enumerate(work):
        ready(s)
        part_in = piece[j, :block]
        part_grad = piece[j, block:]
        for p in range(4):
            if p < 3:
                term = jnp.dot(part_in, held_in[s, p], preferred_element_type=F32)
            else:
                term = lax.dot_general(
                    part_grad,
                    held_out[s],
                    (((1,), (1,)), ((), ())),
                    preferred_element_type=F32,
                )
            if s == 0 and first:
                total[p] = term
            else:
                total[p] = (old if s == 0 else total)[p] + term
    if last:
        out[...] = total[...].astype(BF16)


def project(sizes, place, offsets, pieces, weights, old=None, last=False):
    weight_in, weight_out = weights
    count = sum(piece.shape[0] for piece in pieces)
    rows = pieces[0].shape[1] // 2
    part = pieces[0].shape[2]
    width = weight_out.shape[0]
    whole = pl.BlockSpec(memory_space=pltpu.VMEM)
    far = pl.BlockSpec(memory_space=pltpu.HBM)
    scratch = [
        pltpu.VMEM((count, 3, part, width), BF16),
        pltpu.VMEM((count, width, part), BF16),
        pltpu.SemaphoreType.DMA((count, 2)),
    ]
    return pl.pallas_call(
        functools.partial(project_kernel, sizes, offsets, old is None, last),
        in_specs=[pl.BlockSpec(memory_space=pltpu.SMEM)]
        + [whole] * len(pieces)
        + [far, far]
        + [whole] * (old is not None),
        out_specs=whole,
        scratch_shapes=scratch + ([pltpu.VMEM((4, rows, width), F32)] if last else []),
        out_shape=shape(4, rows, width, dtype=BF16 if last else F32),
        cost_estimate=pl.CostEstimate(
            flops=8 * count * rows * part * width,
            bytes_accessed=8 * count * part * width,
            transcendentals=0,
        ),
        compiler_params=pltpu.CompilerParams(vmem_limit_bytes=GRANT),
    )(place, *pieces, weight_in, weight_out, *([] if old is None else [old]))


def partials_kernel(
    sizes, offset, place_ref, hidden, grad, weight_in, weight_out, out, held_in, held_out, sems
):
    n_x, n_zl = sizes["x"], sizes["zl"]
    block = hidden.shape[0]
    k, start = offset
    base = lax.rem(place_ref[2] + k, n_x) * n_zl + start
    count = out.shape[0]
    ready = load_weights(
        [base + j for j in range(count)], weight_in, weight_out, held_in, held_out, sems
    )
    for s in range(count):
        ready(s)
        mixed = jnp.dot(hidden[...], held_out[s], preferred_element_type=F32)
        out[s, :block] = mixed.astype(BF16)
        total = None
        for p in range(3):
            term = lax.dot_general(
                grad[p], held_in[s, p], (((1,), (1,)), ((), ())), preferred_element_type=F32
            )
            total = term if p == 0 else total + term
        out[s, block:] = total.astype(BF16)


def partials(sizes, place, offset, count, hidden, grad, weights, part):
    block, width = hidden.shape
    whole = pl.BlockSpec(memory_space=pltpu.VMEM)
    far = pl.BlockSpec(memory_space=pltpu.HBM)
    return pl.pallas_call(
        functools.partial(partials_kernel, sizes, offset),
        in_specs=[pl.BlockSpec(memory_space=pltpu.SMEM), whole, whole, far, far],
        out_specs=whole,
        scratch_shapes=[
            pltpu.VMEM((count, 3, part, width), BF16),
            pltpu.VMEM((count, width, part), BF16),
            pltpu.SemaphoreType.DMA((count, 2)),
        ],
        out_shape=shape(count, 2 * block, part, dtype=BF16),
        cost_estimate=pl.CostEstimate(
            flops=8 * count * block * part * width,
            bytes_accessed=8 * count * part * width,
            transcendentals=0,
        ),
        compiler_params=pltpu.CompilerParams(vmem_limit_bytes=GRANT),
    )(place, hidden, grad, *weights)


def shape(*dims, dtype=F32):
    return jax.ShapeDtypeStruct(dims, dtype)


def shards(
    sizes,
    tokens,
    cotangent,
    input_weight,
    output_weight,
    short_taps,
    residues,
    decay_rates,
    skip_gain,
):
    n_x, n_zl = sizes["x"], sizes["zl"]
    block, part = tokens.shape
    width = output_weight.shape[0]
    order = residues.shape[1]
    rows = block + TILE
    taps = short_taps.transpose(0, 2, 1)
    rates = decay_rates.T
    res = residues.T
    skip = skip_gain[None]
    place = jnp.stack(
        [
            lax.axis_index("y"),
            lax.axis_index("zh") * sizes["core"] + lax.axis_index("core"),
            lax.axis_index("x"),
        ]
    ).astype(jnp.int32)
    copies = call(
        copy_kernel, shape(n_zl, 2 * block, part, dtype=BF16), [], tokens, cotangent
    )
    pieces = lax.all_to_all(copies, "zl", 0, 0, tiled=True)
    half = n_zl // 2
    right = [(i, (i + 1) % n_x) for i in range(n_x)]
    left = [(i, (i - 1) % n_x) for i in range(n_x)]
    from_left = lax.ppermute(pieces, "x", right)
    from_right = lax.ppermute(pieces, "x", left)
    weights = tuple(
        pltpu.with_memory_space_constraint(w, pltpu.HBM)
        for w in (input_weight.transpose(1, 0, 2), output_weight)
    )
    total = project(sizes, place, [(0, 0)], [pieces], weights)
    from_left, from_right, total = lax.optimization_barrier((from_left, from_right, total))
    far_left = lax.ppermute(from_left[:half], "x", right)
    far_right = lax.ppermute(from_right[half:], "x", left)
    total = project(
        sizes, place, [(n_x - 1, 0), (1, 0)], [from_left, from_right], weights, total
    )
    total = project(
        sizes, place, [(2, 0), (2, half)], [far_left, far_right], weights, total, True
    )
    proj = total
    ext = pltpu.VMEM((3, rows + TILE, width), F32)
    members = sizes["zh"] * sizes["core"]
    pack = 2 * order + 2 * TILE
    send = call(
        state_kernel,
        shape(members, pack, width, dtype=BF16),
        [ext, pltpu.VMEM((pack, width), F32)],
        proj,
        taps,
        rates,
    )
    conv, grad = call(
        local_kernel,
        [shape(rows, width), shape(rows, width)],
        [ext, pltpu.VMEM((2, rows + TILE, width), F32), pltpu.VMEM((rows, width), F32)],
        proj,
        taps,
        rates,
        res,
        skip,
        flops=3 * 10**9,
    )
    near_states = lax.all_to_all(send, ("zh", "core"), 0, 0, tiled=True)
    send = call(
        functools.partial(chain_kernel, block),
        shape(sizes["y"], order + 2 * TILE, width, dtype=BF16),
        [],
        place,
        taps,
        rates,
        near_states,
    )
    far_states = lax.all_to_all(send, "y", 0, 0, tiled=True)
    hidden, grad_proj = call(
        finish_kernel,
        [shape(block, width, dtype=BF16), shape(3, block, width, dtype=BF16)],
        [ext, pltpu.VMEM((3, rows, width), F32)],
        place,
        proj,
        taps,
        rates,
        res,
        skip,
        conv,
        grad,
        near_states,
        far_states,
    )

    def terms(offset, count, order_by=place):
        return partials(sizes, order_by, offset, count, hidden, grad_proj, weights, part)

    def add(*arrays):
        return sum(a.astype(F32) for a in arrays).astype(BF16)

    far_right = lax.ppermute(terms((2, 0), half), "x", right)
    far_left, later = lax.optimization_barrier((terms((2, half), half), place))
    far_left = lax.ppermute(far_left, "x", left)
    to_right = terms((1, 0), n_zl, later)
    to_left = terms((n_x - 1, 0), n_zl, later)
    to_right = jnp.concatenate([add(to_right[:half], far_right), to_right[half:]], axis=0)
    to_left = jnp.concatenate([to_left[:half], add(to_left[half:], far_left)], axis=0)
    from_left = lax.ppermute(to_right, "x", right)
    from_right = lax.ppermute(to_left, "x", left)
    summed = add(terms((0, 0), n_zl, later), from_left, from_right)
    summed = lax.all_to_all(summed, "zl", 0, 0, tiled=True)
    total = jnp.sum(summed.astype(F32), axis=0).astype(BF16)
    return total[:block], total[block:]


def solution(mesh, dims=(8, 4, 2, 4, 4)):
    fine = Mesh(mesh.devices.reshape(dims), CTX + TP)
    sizes = dict(zip(CTX + TP, dims))
    return jax.shard_map(
        functools.partial(shards, sizes),
        mesh=fine,
        in_specs=(
            P(CTX, TP),
            P(CTX, TP),
            P(None, None, TP),
            P(TP, None),
            P(None, TP, None),
            P(TP, None),
            P(TP, None),
            P(TP),
        ),
        out_specs=(P(CTX, TP), P(CTX, TP)),
        check_vma=False,
    )
```

time: 176 us -> 162 us (0.920)
  blocking collectives: 55.3 us -> 69.8 us
  starting transfers between devices: 45.7 us -> 34.5 us
  local copies, waits for them, and re-layouts: 13 us -> 2.43 us
  waiting for transfers between devices: 33.1 us -> 22.6 us
  Pallas kernels: 26.6 us -> 30.8 us
    all_to_all x1, blocking collectives: 19.4 us -> 34.2 us  [shards(): near_states = lax.all_to_all(send, ('zh', 'core'), 0, 0, tiled=True)]
    all_to_all x2 -> x1, starting transfers between devices: 16.2 us -> 7.1 us  [shards(): far_states = lax.all_to_all(send, 'y', 0, 0, tiled=True)]
    ppermute x3 -> x1, waiting for transfers between devices: 8.8 us -> 0.01 us  [shards(): far_left = lax.ppermute(far_left, 'x', left)]
    all_to_all x2 -> x1, waiting for transfers between devices: 14.3 us -> 5.87 us  [shards(): far_states = lax.all_to_all(send, 'y', 0, 0, tiled=True)]
    unnamed x22 -> x12, local copies, waits for them, and re-layouts: 9.93 us -> 1.7 us
    ppermute x1, waiting for transfers between devices: 0.01 us -> 4.93 us  [shards(): from_right = lax.ppermute(pieces, 'x', left)]
    ppermute x1, waiting for transfers between devices: 0.01 us -> 4.22 us  [shards(): far_right = lax.ppermute(from_right[half:], 'x', left)]
    pallas_call x5, Pallas kernels: 10.8 us -> 14.6 us  [partials(): pl.pallas_call(functools.partial(partials_kernel, sizes, offset), in_spec...]
  transfers between devices with their start and end apart: 12 -> 9, of which waited for: 5 -> 6; matrix products, arithmetic and copies ran while one was open for 2% -> 0% of each run, Pallas kernels for 11% -> 13%
where the time goes in v6:
time: 162 us
  blocking collectives  69.8 us (43%)
  starting transfers between devices  34.5 us (21%)
  Pallas kernels  30.8 us (19%)
  waiting for transfers between devices  22.6 us (14%)
  local copies, waits for them, and re-layouts  2.43 us (2%)
    all_to_all x1, blocking collectives, shards(): near_states = lax.all_to_all(send, ('zh', 'core'), 0, 0, tiled=True)  34.2 us
    all_to_all x1, blocking collectives, shards(): pieces = lax.all_to_all(copies, 'zl', 0, 0, tiled=True)  21.5 us
    pallas_call x5, Pallas kernels, partials(): pl.pallas_call(functools.partial(partials_kernel, sizes, offset), in_spec...  14.6 us
    all_to_all x1, blocking collectives, shards(): summed = lax.all_to_all(summed, 'zl', 0, 0, tiled=True)  14 us
    pallas_call x3, Pallas kernels, project(): pl.pallas_call(functools.partial(project_kernel, sizes, offsets, old is N...  8.31 us
    pallas_call x5, Pallas kernels, call(): pl.pallas_call(kernel, out_shape=outs, scratch_shapes=scratch, in_specs=s...  7.9 us
    all_to_all x1, starting transfers between devices, shards(): far_states = lax.all_to_all(send, 'y', 0, 0, tiled=True)  7.1 us
    all_to_all x1, waiting for transfers between devices, shards(): far_states = lax.all_to_all(send, 'y', 0, 0, tiled=True)  5.87 us
  transfers between devices with their start and end apart: 9, of which 6 were waited for; matrix products, arithmetic and copies ran while one was open for 0% of the time, Pallas kernels for 13%

profile of v6, /device:TPU:6, one launch (start us, length us, event | category | flops | bytes accessed | tf_op | source)
XLA Modules:
  0.0 161.6 jit_solution(14156617747326805714)
XLA Ops:
  0.6 0.8 copy-done.2
  1.5 0.8 copy-done.3
  2.3 21.5 %all_to_all.20.refs_0_ = bf16[4,256,256]{2,1,0:T(8,128)(2,1)S(1)} all-to-all(bf16[4,256,256]{2,1,0:T(8,128)(2,1)S(1)} %shard_map.95), channel_id=1, replica_groups=mesh['y'=8,'zh'=4,'core'=2,'x'=4,'zl'=4] {'zl'}, dimensions={0} | all-to-all | bytes 1048576 | tf_op jit(solution)/shard_map/all_to_all | solution.py:452
  23.9 2.7 %collective-permute-start.1 = (bf16[4,256,256]{2,1,0:T(8,128)(2,1)S(1)}, bf16[4,256,256]{2,1,0:T(8,128)(2,1)S(1)}, u32[]{:S(2)}, u32[]{:S(2)}) collective-permute-start(bf16[4,256,256]{2,1,0:T(8,128)(2,1)S(1)} %all_to_all.20.refs_0_), channel_id=1, source_target_pairs={{0,12},{4,0},{8,4},{12,8},{1,13},{5,1},{9,5},{13,9},{2,14},{6,2},{... | collective-permute-start | bytes 1572872 | tf_op jit(solution)/shard_map/ppermute | solution.py:457
  26.6 5.4 %collective-permute-start = (bf16[4,256,256]{2,1,0:T(8,128)(2,1)S(1)}, bf16[4,256,256]{2,1,0:T(8,128)(2,1)S(1)}, u32[]{:S(2)}, u32[]{:S(2)}) collective-permute-start(bf16[4,256,256]{2,1,0:T(8,128)(2,1)S(1)} %all_to_all.20.refs_0_), channel_id=1, source_target_pairs={{0,4},{4,8},{8,12},{12,0},{1,5},{5,9},{9,13},{13,1},{2,6},{6,10},{... | collective-permute-start | bytes 1572872 | tf_op jit(solution)/shard_map/ppermute | solution.py:456
  32.0 0.1 pad_add_fusion.place_ref
  32.1 2.5 %shard_map.96.refs_4_ = f32[4,128,256]{2,1,0:T(8,128)S(1)} custom-call(s32[3]{0:T(128)S(1)} %pad_add_fusion.place_ref, bf16[4,256,256]{2,1,0:T(8,128)(2,1)S(1)} %all_to_all.20.refs_0_, bf16[3,4096,256]{2,1,0:T(8,128)(2,1)} %bitcast.20, bf16[256,4096]{1,0:T(8,128)(2,1)} %weight_out.9), custom_call_target="tpu_custom_call" | custom-call | flops 268435456 | bytes 2097152 | tf_op jit(solution)/shard_map/pallas_call | solution.py:353
  34.6 4.9 %collective-permute-done.1.refs_1_ = bf16[4,256,256]{2,1,0:T(8,128)(2,1)S(1)} collective-permute-done((bf16[4,256,256]{2,1,0:T(8,128)(2,1)S(1)}, bf16[4,256,256]{2,1,0:T(8,128)(2,1)S(1)}, u32[]{:S(2)}, u32[]{:S(2)}) %collective-permute-start.1) | collective-permute-done | bytes 524320 | tf_op jit(solution)/shard_map/ppermute | solution.py:457
  39.5 1.3 collective-permute-done.refs_0_
  40.8 5.5 %collective-permute-start.2 = (bf16[2,256,256]{2,1,0:T(8,128)(2,1)S(1)}, bf16[2,256,256]{2,1,0:T(8,128)(2,1)S(1)}, u32[]{:S(2)}, u32[]{:S(2)}) collective-permute-start(bf16[2,256,256]{2,1,0:T(8,128)(2,1)S(1)} %slice.24), channel_id=1, source_target_pairs={{0,4},{4,8},{8,12},{12,0},{1,5},{5,9},{9,13},{13,1},{2,6},{6,10},{... | collective-permute-start | bytes 786440 | tf_op jit(solution)/shard_map/ppermute | solution.py:464
  46.4 1.9 %collective-permute-start.3 = (bf16[2,256,256]{2,1,0:T(8,128)(2,1)S(1)}, bf16[2,256,256]{2,1,0:T(8,128)(2,1)S(1)}, u32[]{:S(2)}, u32[]{:S(2)}) collective-permute-start(bf16[2,256,256]{2,1,0:T(8,128)(2,1)S(1)} %slice.25), channel_id=1, source_target_pairs={{0,12},{4,0},{8,4},{12,8},{1,13},{5,1},{9,5},{13,9},{2,14},{6,2},{... | collective-permute-start | bytes 786440 | tf_op jit(solution)/shard_map/ppermute | solution.py:465
  48.3 3.3 %shard_map.97.refs_4_ = f32[4,128,256]{2,1,0:T(8,128)S(1)} custom-call(s32[3]{0:T(128)S(1)} %pad_add_fusion.place_ref, bf16[4,256,256]{2,1,0:T(8,128)(2,1)S(1)} %collective-permute-done.refs_0_, bf16[4,256,256]{2,1,0:T(8,128)(2,1)S(1)} %collective-permute-done.1.refs_1_, bf16[3,4096,256]{2,1,0:T(8,128)(2,1)} %bitcast.21, bf16[256,4096]{1,0:T(8,128)(2,1)} %weight_out.9, ...), custom_call_target="tpu_custom_call" | custom-call | flops 536870912 | bytes 4194304 | tf_op jit(solution)/shard_map/pallas_call | solution.py:353
  51.6 0.0 copy-start
  51.6 0.0 copy-start.1
  51.6 0.0 copy-start.4
  51.6 0.0 copy-start.5
  51.6 0.0 collective-permute-done.2.refs_0_
  51.6 4.2 %collective-permute-done.3.refs_1_ = bf16[2,256,256]{2,1,0:T(8,128)(2,1)S(1)} collective-permute-done((bf16[2,256,256]{2,1,0:T(8,128)(2,1)S(1)}, bf16[2,256,256]{2,1,0:T(8,128)(2,1)S(1)}, u32[]{:S(2)}, u32[]{:S(2)}) %collective-permute-start.3) | collective-permute-done | bytes 262176 | tf_op jit(solution)/shard_map/ppermute | solution.py:465
  55.8 2.5 %shard_map.98.proj_ref = bf16[4,128,256]{2,1,0:T(8,128)(2,1)S(1)} custom-call(s32[3]{0:T(128)S(1)} %pad_add_fusion.place_ref, bf16[2,256,256]{2,1,0:T(8,128)(2,1)S(1)} %collective-permute-done.2.refs_0_, bf16[2,256,256]{2,1,0:T(8,128)(2,1)S(1)} %collective-permute-done.3.refs_1_, bf16[3,4096,256]{2,1,0:T(8,128)(2,1)} %bitcast.22, ...), custom_call_target="tpu_custom_call" | custom-call | flops 268435456 | bytes 2097152 | tf_op jit(solution)/shard_map/pallas_call | solution.py:353
  58.4 0.0 copy-done
  58.4 0.0 copy-done.1
  58.4 1.1 shard_map.100
  59.5 34.2 %all_to_all.21.got_ref.near_ref = bf16[8,48,256]{2,1,0:T(8,128)(2,1)S(1)} all-to-all(bf16[8,48,256]{2,1,0:T(8,128)(2,1)S(1)} %shard_map.100), channel_id=1, replica_groups=mesh['y'=8,'zh'=4,'core'=2,'x'=4,'zl'=4] {'zh','core'}, dimensions={0} | all-to-all | bytes 393216 | tf_op jit(solution)/shard_map/all_to_all | solution.py:495
  93.7 1.4 shard_map.101
  95.1 7.1 %all-to-all-start.2 = ((bf16[8,32,256]{2,1,0:T(8,128)(2,1)}), bf16[8,32,256]{2,1,0:T(8,128)(2,1)S(1)}, u32[]{:S(2)}, u32[]{:S(2)}) async-start(bf16[8,32,256]{2,1,0:T(8,128)(2,1)} %shard_map.101), calls=%async_computation.2 | async-start | bytes 262144 | tf_op jit(solution)/shard_map/all_to_all | solution.py:505
  102.2 0.0 copy-done.5
  102.2 3.2 %shard_map.99 = (f32[136,256]{1,0:T(8,128)S(1)}, f32[136,256]{1,0:T(8,128)S(1)}) custom-call(bf16[4,128,256]{2,1,0:T(8,128)(2,1)S(1)} %shard_map.98.proj_ref, f32[3,3,256]{2,1,0:T(4,128)S(1)} %bitcast.14, f32[16,256]{1,0:T(8,128)S(1)} %bitcast.10, f32[16,256]{1,0:T(8,128)S(1)} %bitcast.16, f32[1,256]{1,0:T(1,128)S(1)} %bitcast.18), custom_call_target="tpu_custom_call" | custom-call | flops 3000000000 | tf_op jit(solution)/shard_map/pallas_call | solution.py:272
  105.4 5.9 %all-to-all-done.2.far_ref = bf16[8,32,256]{2,1,0:T(8,128)(2,1)S(1)} async-done(((bf16[8,32,256]{2,1,0:T(8,128)(2,1)}), bf16[8,32,256]{2,1,0:T(8,128)(2,1)S(1)}, u32[]{:S(2)}, u32[]{:S(2)}) %all-to-all-start.2) | async-done | bytes 131104 | tf_op jit(solution)/shard_map/all_to_all | solution.py:505
  111.3 2.2 %shard_map.102 = (bf16[128,256]{1,0:T(8,128)(2,1)S(1)}, bf16[3,128,256]{2,1,0:T(8,128)(2,1)S(1)}) custom-call(s32[3]{0:T(128)S(1)} %pad_add_fusion.place_ref, bf16[4,128,256]{2,1,0:T(8,128)(2,1)S(1)} %shard_map.98.proj_ref, f32[3,3,256]{2,1,0:T(4,128)S(1)} %bitcast.15, f32[16,256]{1,0:T(8,128)S(1)} %bitcast.11, f32[16,256]{1,0:T(8,128)S(1)} %bitcast.17, ...), custom_call_target="tpu_custom_call" | custom-call | tf_op jit(solution)/shard_map/pallas_call | solution.py:272
  113.5 2.4 %shard_map.106 = bf16[2,256,256]{2,1,0:T(8,128)(2,1)S(1)} custom-call(s32[3]{0:T(128)S(1)} %pad_add_fusion.place_ref, bf16[128,256]{1,0:T(8,128)(2,1)S(1)} %get-tuple-element.16.hidden, bf16[3,128,256]{2,1,0:T(8,128)(2,1)S(1)} %get-tuple-element.17.grad, bf16[3,4096,256]{2,1,0:T(8,128)(2,1)} %bitcast.23, bf16[256,4096]{1,0:T(8,128)(2,1)} %weight_out.9), custom_call_target="tpu_custom_call" | custom-call | flops 134217728 | bytes 1048576 | tf_op jit(solution)/shard_map/pallas_call | solution.py:399
  115.9 1.9 %collective-permute-start.4 = (bf16[2,256,256]{2,1,0:T(8,128)(2,1)S(1)}, bf16[2,256,256]{2,1,0:T(8,128)(2,1)S(1)}, u32[]{:S(2)}, u32[]{:S(2)}) collective-permute-start(bf16[2,256,256]{2,1,0:T(8,128)(2,1)S(1)} %shard_map.106), channel_id=1, source_target_pairs={{0,4},{4,8},{8,12},{12,0},{1,5},{5,9},{9,13},{13,1},{2,6},{6,10},{... | collective-permute-start | bytes 786440 | tf_op jit(solution)/shard_map/ppermute | solution.py:528
  117.8 2.4 %shard_map.103 = bf16[2,256,256]{2,1,0:T(8,128)(2,1)S(1)} custom-call(s32[3]{0:T(128)S(1)} %pad_add_fusion.place_ref, bf16[128,256]{1,0:T(8,128)(2,1)S(1)} %get-tuple-element.16.hidden, bf16[3,128,256]{2,1,0:T(8,128)(2,1)S(1)} %get-tuple-element.17.grad, bf16[3,4096,256]{2,1,0:T(8,128)(2,1)} %bitcast.24, bf16[256,4096]{1,0:T(8,128)(2,1)} %weight_out.9), custom_call_target="tpu_custom_call" | custom-call | flops 134217728 | bytes 1048576 | tf_op jit(solution)/shard_map/pallas_call | solution.py:399
  120.2 4.1 %collective-permute-start.6 = (bf16[2,256,256]{2,1,0:T(8,128)(2,1)S(1)}, bf16[2,256,256]{2,1,0:T(8,128)(2,1)S(1)}, u32[]{:S(2)}, u32[]{:S(2)}) collective-permute-start(bf16[2,256,256]{2,1,0:T(8,128)(2,1)S(1)} %shard_map.103), channel_id=1, source_target_pairs={{0,12},{4,0},{8,4},{12,8},{1,13},{5,1},{9,5},{13,9},{2,14},{6,2},{... | collective-permute-start | bytes 786440 | tf_op jit(solution)/shard_map/ppermute | solution.py:530
  124.3 3.3 %shard_map.107 = bf16[4,256,256]{2,1,0:T(8,128)(2,1)S(1)} custom-call(s32[3]{0:T(128)S(1)} %pad_add_fusion.place_ref, bf16[128,256]{1,0:T(8,128)(2,1)S(1)} %get-tuple-element.16.hidden, bf16[3,128,256]{2,1,0:T(8,128)(2,1)S(1)} %get-tuple-element.17.grad, bf16[3,4096,256]{2,1,0:T(8,128)(2,1)} %bitcast.25, bf16[256,4096]{1,0:T(8,128)(2,1)} %weight_out.9), custom_call_target="tpu_custom_call" | custom-call | flops 268435456 | bytes 2097152 | tf_op jit(solution)/shard_map/pallas_call | solution.py:399
  127.6 3.3 %shard_map.105 = bf16[4,256,256]{2,1,0:T(8,128)(2,1)S(1)} custom-call(s32[3]{0:T(128)S(1)} %pad_add_fusion.place_ref, bf16[128,256]{1,0:T(8,128)(2,1)S(1)} %get-tuple-element.16.hidden, bf16[3,128,256]{2,1,0:T(8,128)(2,1)S(1)} %get-tuple-element.17.grad, bf16[3,4096,256]{2,1,0:T(8,128)(2,1)} %bitcast.26, bf16[256,4096]{1,0:T(8,128)(2,1)} %weight_out.9), custom_call_target="tpu_custom_call" | custom-call | flops 268435456 | bytes 2097152 | tf_op jit(solution)/shard_map/pallas_call | solution.py:399
  130.9 0.0 collective-permute-done.4
  130.9 0.1 add_convert_fusion.2
  131.1 3.1 %collective-permute-start.5 = (bf16[4,256,256]{2,1,0:T(8,128)(2,1)S(1)}, bf16[4,256,256]{2,1,0:T(8,128)(2,1)S(1)}, u32[]{:S(2)}, u32[]{:S(2)}) collective-permute-start(bf16[4,256,256]{2,1,0:T(8,128)(2,1)S(1)} %pad_maximum_fusion), channel_id=1, source_target_pairs={{0,4},{4,8},{8,12},{12,0},{1,5},{5,9},{9,13},{13,1},{2,6},{6,10},{... | collective-permute-start | bytes 1572872 | tf_op jit(solution)/shard_map/ppermute | solution.py:535
  134.2 0.0 collective-permute-done.6
  134.2 0.1 add_convert_fusion.1
  134.3 2.7 %collective-permute-start.7 = (bf16[4,256,256]{2,1,0:T(8,128)(2,1)S(1)}, bf16[4,256,256]{2,1,0:T(8,128)(2,1)S(1)}, u32[]{:S(2)}, u32[]{:S(2)}) collective-permute-start(bf16[4,256,256]{2,1,0:T(8,128)(2,1)S(1)} %pad_maximum_fusion.1), channel_id=1, source_target_pairs={{0,12},{4,0},{8,4},{12,8},{1,13},{5,1},{9,5},{13,9},{2,14},{6,2},{... | collective-permute-start | bytes 1572872 | tf_op jit(solution)/shard_map/ppermute | solution.py:536
  137.1 3.3 %shard_map.104 = bf16[4,256,256]{2,1,0:T(8,128)(2,1)S(1)} custom-call(s32[3]{0:T(128)S(1)} %pad_add_fusion.place_ref, bf16[128,256]{1,0:T(8,128)(2,1)S(1)} %get-tuple-element.16.hidden, bf16[3,128,256]{2,1,0:T(8,128)(2,1)S(1)} %get-tuple-element.17.grad, bf16[3,4096,256]{2,1,0:T(8,128)(2,1)} %bitcast.27, bf16[256,4096]{1,0:T(8,128)(2,1)} %weight_out.9), custom_call_target="tpu_custom_call" | custom-call | flops 268435456 | bytes 2097152 | tf_op jit(solution)/shard_map/pallas_call | solution.py:399
  140.3 1.8 %collective-permute-done.5 = bf16[4,256,256]{2,1,0:T(8,128)(2,1)S(1)} collective-permute-done((bf16[4,256,256]{2,1,0:T(8,128)(2,1)S(1)}, bf16[4,256,256]{2,1,0:T(8,128)(2,1)S(1)}, u32[]{:S(2)}, u32[]{:S(2)}) %collective-permute-start.5) | collective-permute-done | bytes 524320 | tf_op jit(solution)/shard_map/ppermute | solution.py:535
  142.1 4.5 %collective-permute-done.7 = bf16[4,256,256]{2,1,0:T(8,128)(2,1)S(1)} collective-permute-done((bf16[4,256,256]{2,1,0:T(8,128)(2,1)S(1)}, bf16[4,256,256]{2,1,0:T(8,128)(2,1)S(1)}, u32[]{:S(2)}, u32[]{:S(2)}) %collective-permute-start.7) | collective-permute-done | bytes 524320 | tf_op jit(solution)/shard_map/ppermute | solution.py:536
  146.6 0.2 add_convert_fusion
  146.8 14.0 %all_to_all.22 = bf16[4,256,256]{2,1,0:T(8,128)(2,1)S(1)} all-to-all(bf16[4,256,256]{2,1,0:T(8,128)(2,1)S(1)} %add_convert_fusion), channel_id=1, replica_groups=mesh['y'=8,'zh'=4,'core'=2,'x'=4,'zl'=4] {'zl'}, dimensions={0} | all-to-all | bytes 1048576 | tf_op jit(solution)/shard_map/all_to_all | solution.py:538
  160.9 0.1 reduce_sum.12
  161.0 0.7 fusion
  (10 shorter events, 0.2 us)
Async XLA Ops:
  0.6 0.8 copy-start.2
  1.5 0.8 copy-start.3
  23.9 15.6 %collective-permute-start.1 = (bf16[4,256,256]{2,1,0:T(8,128)(2,1)S(1)}, bf16[4,256,256]{2,1,0:T(8,128)(2,1)S(1)}, u32[]{:S(2)}, u32[]{:S(2)}) collective-permute-start(bf16[4,256,256]{2,1,0:T(8,128)(2,1)S(1)} %all_to_all.20.refs_0_), channel_id=1, source_target_pairs={{0,12},{4,0},{8,4},{12,8},{1,13},{5,1},{9,5},{13,9},{2,14},{6,2},{... | collective-permute-start | bytes 1572872 | tf_op jit(solution)/shard_map/ppermute | solution.py:457
  26.6 14.1 %collective-permute-start = (bf16[4,256,256]{2,1,0:T(8,128)(2,1)S(1)}, bf16[4,256,256]{2,1,0:T(8,128)(2,1)S(1)}, u32[]{:S(2)}, u32[]{:S(2)}) collective-permute-start(bf16[4,256,256]{2,1,0:T(8,128)(2,1)S(1)} %all_to_all.20.refs_0_), channel_id=1, source_target_pairs={{0,4},{4,8},{8,12},{12,0},{1,5},{5,9},{9,13},{13,1},{2,6},{6,10},{... | collective-permute-start | bytes 1572872 | tf_op jit(solution)/shard_map/ppermute | solution.py:456
  40.8 10.8 %collective-permute-start.2 = (bf16[2,256,256]{2,1,0:T(8,128)(2,1)S(1)}, bf16[2,256,256]{2,1,0:T(8,128)(2,1)S(1)}, u32[]{:S(2)}, u32[]{:S(2)}) collective-permute-start(bf16[2,256,256]{2,1,0:T(8,128)(2,1)S(1)} %slice.24), channel_id=1, source_target_pairs={{0,4},{4,8},{8,12},{12,0},{1,5},{5,9},{9,13},{13,1},{2,6},{6,10},{... | collective-permute-start | bytes 786440 | tf_op jit(solution)/shard_map/ppermute | solution.py:464
  46.4 9.5 %collective-permute-start.3 = (bf16[2,256,256]{2,1,0:T(8,128)(2,1)S(1)}, bf16[2,256,256]{2,1,0:T(8,128)(2,1)S(1)}, u32[]{:S(2)}, u32[]{:S(2)}) collective-permute-start(bf16[2,256,256]{2,1,0:T(8,128)(2,1)S(1)} %slice.25), channel_id=1, source_target_pairs={{0,12},{4,0},{8,4},{12,8},{1,13},{5,1},{9,5},{13,9},{2,14},{6,2},{... | collective-permute-start | bytes 786440 | tf_op jit(solution)/shard_map/ppermute | solution.py:465
  51.6 6.8 %copy-start = (f32[256,16]{0,1:T(8,128)S(1)}, f32[256,16]{0,1:T(8,128)}, u32[]{:S(2)}) copy-start(f32[256,16]{0,1:T(8,128)} %param.14) | copy-start | bytes 49156
  51.6 6.8 %copy-start.1 = (f32[3,256,3]{1,2,0:T(4,128)S(1)}, f32[3,256,3]{1,2,0:T(4,128)}, u32[]{:S(2)}) copy-start(f32[3,256,3]{1,2,0:T(4,128)} %param.12) | copy-start | bytes 27652
  51.6 50.6 %copy-start.4 = (f32[256,16]{0,1:T(8,128)S(1)}, f32[256,16]{0,1:T(8,128)}, u32[]{:S(2)}) copy-start(f32[256,16]{0,1:T(8,128)} %param.13) | copy-start | bytes 49156
  51.6 50.6 %copy-start.5 = (f32[256]{0:T(256)S(1)}, f32[256]{0:T(256)}, u32[]{:S(2)}) copy-start(f32[256]{0:T(256)} %param.15) | copy-start | bytes 3076
  95.1 16.2 %all-to-all-start.2 = ((bf16[8,32,256]{2,1,0:T(8,128)(2,1)}), bf16[8,32,256]{2,1,0:T(8,128)(2,1)S(1)}, u32[]{:S(2)}, u32[]{:S(2)}) async-start(bf16[8,32,256]{2,1,0:T(8,128)(2,1)} %shard_map.101), calls=%async_computation.2 | async-start | bytes 262144 | tf_op jit(solution)/shard_map/all_to_all | solution.py:505
  115.9 15.0 %collective-permute-start.4 = (bf16[2,256,256]{2,1,0:T(8,128)(2,1)S(1)}, bf16[2,256,256]{2,1,0:T(8,128)(2,1)S(1)}, u32[]{:S(2)}, u32[]{:S(2)}) collective-permute-start(bf16[2,256,256]{2,1,0:T(8,128)(2,1)S(1)} %shard_map.106), channel_id=1, source_target_pairs={{0,4},{4,8},{8,12},{12,0},{1,5},{5,9},{9,13},{13,1},{2,6},{6,10},{... | collective-permute-start | bytes 786440 | tf_op jit(solution)/shard_map/ppermute | solution.py:528
  120.2 14.0 %collective-permute-start.6 = (bf16[2,256,256]{2,1,0:T(8,128)(2,1)S(1)}, bf16[2,256,256]{2,1,0:T(8,128)(2,1)S(1)}, u32[]{:S(2)}, u32[]{:S(2)}) collective-permute-start(bf16[2,256,256]{2,1,0:T(8,128)(2,1)S(1)} %shard_map.103), channel_id=1, source_target_pairs={{0,12},{4,0},{8,4},{12,8},{1,13},{5,1},{9,5},{13,9},{2,14},{6,2},{... | collective-permute-start | bytes 786440 | tf_op jit(solution)/shard_map/ppermute | solution.py:530
  131.1 11.1 %collective-permute-start.5 = (bf16[4,256,256]{2,1,0:T(8,128)(2,1)S(1)}, bf16[4,256,256]{2,1,0:T(8,128)(2,1)S(1)}, u32[]{:S(2)}, u32[]{:S(2)}) collective-permute-start(bf16[4,256,256]{2,1,0:T(8,128)(2,1)S(1)} %pad_maximum_fusion), channel_id=1, source_target_pairs={{0,4},{4,8},{8,12},{12,0},{1,5},{5,9},{9,13},{13,1},{2,6},{6,10},{... | collective-permute-start | bytes 1572872 | tf_op jit(solution)/shard_map/ppermute | solution.py:535
  134.3 12.3 %collective-permute-start.7 = (bf16[4,256,256]{2,1,0:T(8,128)(2,1)S(1)}, bf16[4,256,256]{2,1,0:T(8,128)(2,1)S(1)}, u32[]{:S(2)}, u32[]{:S(2)}) collective-permute-start(bf16[4,256,256]{2,1,0:T(8,128)(2,1)S(1)} %pad_maximum_fusion.1), channel_id=1, source_target_pairs={{0,12},{4,0},{8,4},{12,8},{1,13},{5,1},{9,5},{13,9},{2,14},{6,2},{... | collective-permute-start | bytes 1572872 | tf_op jit(solution)/shard_map/ppermute | solution.py:536

commit v7 on v6

--- a/solution.py
+++ b/solution.py
@@ -17,11 +17,16 @@
 F32 = jnp.float32
 
 
-def copy_kernel(tokens, cotangent, copies):
+def copy_kernel(tokens, cotangent, copies, sems):
     block = tokens.shape[0]
+    moves = []
     for i in range(copies.shape[0]):
-        copies[i, :block] = tokens[...]
-        copies[i, block:] = cotangent[...]
+        for k, rows in enumerate((tokens, cotangent)):
+            there = copies.at[i, pl.ds(k * block, block)]
+            moves.append(pltpu.make_async_copy(rows, there, sems.at[i, k]))
+            moves[-1].start()
+    for move in moves:
+        move.wait()
 
 
 def features(ext, proj_ref, taps_ref, rows, last=None, first=None):
@@ -263,10 +268,17 @@
         out_ref[p] = total.astype(BF16)
 
 
-def call(kernel, outs, scratch, *args, flops=0):
+def in_hbm(array):
+    return pltpu.with_memory_space_constraint(array, pltpu.HBM)
+
+
+def call(kernel, outs, scratch, *args, flops=0, hbm=0):
     whole = pl.BlockSpec(memory_space=pltpu.VMEM)
+    far = pl.BlockSpec(memory_space=pltpu.HBM)
+    scalar = pl.BlockSpec(memory_space=pltpu.SMEM)
     specs = [
-        pl.BlockSpec(memory_space=pltpu.SMEM) if a.dtype == jnp.int32 else whole for a in args
+        scalar if a.dtype == jnp.int32 else far if i >= len(args) - hbm else whole
+        for i, a in enumerate(args)
     ]
     cost = pl.CostEstimate(flops=flops, bytes_accessed=0, transcendentals=0) if flops else None
     return pl.pallas_call(
@@ -280,7 +292,7 @@
     )(*args)
 
 
-def load_weights(blocks, weight_in, weight_out, held_in, held_out, sems):
+def load_weights(blocks, weight_in, weight_out, held_in, held_out, sems, ahead=3):
     part = held_in.shape[2]
     copies = []
     for s, block in enumerate(blocks):
@@ -291,128 +303,132 @@
                 pltpu.make_async_copy(weight_out.at[:, at], held_out.at[s], sems.at[s, 1]),
             )
         )
-        for copy in copies[-1]:
+
+    def start(s):
+        for copy in copies[s]:
             copy.start()
+
+    for s in range(min(ahead, len(copies))):
+        start(s)
 
     def ready(s):
         for copy in copies[s]:
             copy.wait()
+        if s + ahead < len(copies):
+            start(s + ahead)
 
     return ready
 
 
-def project_kernel(sizes, offsets, first, last, place_ref, *refs):
+def held_weights(count, part, width):
+    return [
+        pltpu.VMEM((count, 3, part, width), BF16),
+        pltpu.VMEM((count, width, part), BF16),
+        pltpu.SemaphoreType.DMA((count, 2)),
+    ]
+
+
+def project(sizes, offsets, place_ref, pieces, weights, old, total, held_in, held_out, sems):
     n_x, n_zl = sizes["x"], sizes["zl"]
-    pieces, refs = refs[: len(offsets)], refs[len(offsets) :]
-    weight_in, weight_out = refs[:2]
-    old = None if first else refs[2]
-    out, held_in, held_out, sems = refs[2 + (not first) : 6 + (not first)]
-    total = refs[-1] if last else out
     block = pieces[0].shape[1] // 2
     work = [
         (piece, j, lax.rem(place_ref[2] + k, n_x) * n_zl + start + j)
         for piece, (k, start) in zip(pieces, offsets)
         for j in range(piece.shape[0])
     ]
-    ready = load_weights([w[2] for w in work], weight_in, weight_out, held_in, held_out, sems)
+    ready = load_weights([w[2] for w in work], *weights, held_in, held_out, sems)
     for s, (piece, j, _) in enumerate(work):
         ready(s)
-        part_in = piece[j, :block]
-        part_grad = piece[j, block:]
         for p in range(4):
             if p < 3:
-                term = jnp.dot(part_in, held_in[s, p], preferred_element_type=F32)
+                term = jnp.dot(piece[j, :block], held_in[s, p], preferred_element_type=F32)
             else:
                 term = lax.dot_general(
-                    part_grad,
+                    piece[j, block:],
                     held_out[s],
                     (((1,), (1,)), ((), ())),
                     preferred_element_type=F32,
                 )
-            if s == 0 and first:
+            if s == 0 and old is None:
                 total[p] = term
             else:
                 total[p] = (old if s == 0 else total)[p] + term
-    if last:
-        out[...] = total[...].astype(BF16)
-
-
-def project(sizes, place, offsets, pieces, weights, old=None, last=False):
-    weight_in, weight_out = weights
-    count = sum(piece.shape[0] for piece in pieces)
-    rows = pieces[0].shape[1] // 2
-    part = pieces[0].shape[2]
-    width = weight_out.shape[0]
-    whole = pl.BlockSpec(memory_space=pltpu.VMEM)
-    far = pl.BlockSpec(memory_space=pltpu.HBM)
-    scratch = [
-        pltpu.VMEM((count, 3, part, width), BF16),
-        pltpu.VMEM((count, width, part), BF16),
-        pltpu.SemaphoreType.DMA((count, 2)),
-    ]
-    return pl.pallas_call(
-        functools.partial(project_kernel, sizes, offsets, old is None, last),
-        in_specs=[pl.BlockSpec(memory_space=pltpu.SMEM)]
-        + [whole] * len(pieces)
-        + [far, far]
-        + [whole] * (old is not None),
-        out_specs=whole,
-        scratch_shapes=scratch + ([pltpu.VMEM((4, rows, width), F32)] if last else []),
-        out_shape=shape(4, rows, width, dtype=BF16 if last else F32),
-        cost_estimate=pl.CostEstimate(
-            flops=8 * count * rows * part * width,
-            bytes_accessed=8 * count * part * width,
-            transcendentals=0,
-        ),
-        compiler_params=pltpu.CompilerParams(vmem_limit_bytes=GRANT),
-    )(place, *pieces, weight_in, weight_out, *([] if old is None else [old]))
-
-
-def partials_kernel(
-    sizes, offset, place_ref, hidden, grad, weight_in, weight_out, out, held_in, held_out, sems
+
+
+def near_kernel(sizes, place, piece, weight_in, weight_out, total, *held):
+    project(sizes, [(0, 0)], place, [piece], (weight_in, weight_out), None, total, *held)
+
+
+def side_kernel(sizes, place, left, right, old, weight_in, weight_out, total, *held):
+    offsets = [(sizes["x"] - 1, 0), (1, 0)]
+    weights = (weight_in, weight_out)
+    project(sizes, offsets, place, [left, right], weights, old, total, *held)
+
+
+def far_kernel(
+    sizes, place, left, right, old, taps, rates, weight_in, weight_out, proj, send, total, ext, pack, *held
 ):
-    n_x, n_zl = sizes["x"], sizes["zl"]
+    offsets = [(2, 0), (2, left.shape[0])]
+    weights = (weight_in, weight_out)
+    project(sizes, offsets, place, [left, right], weights, old, total, *held)
+    proj[...] = total[...].astype(BF16)
+    state_kernel(proj, taps, rates, send, ext, pack)
+
+
+def partials(held, start, out, hidden, grad, ready):
+    held_in, held_out = held[:2]
     block = hidden.shape[0]
-    k, start = offset
-    base = lax.rem(place_ref[2] + k, n_x) * n_zl + start
-    count = out.shape[0]
-    ready = load_weights(
-        [base + j for j in range(count)], weight_in, weight_out, held_in, held_out, sems
-    )
-    for s in range(count):
+    for j in range(out.shape[0]):
+        s = start + j
         ready(s)
         mixed = jnp.dot(hidden[...], held_out[s], preferred_element_type=F32)
-        out[s, :block] = mixed.astype(BF16)
+        out[j, :block] = mixed.astype(BF16)
         total = None
         for p in range(3):
             term = lax.dot_general(
                 grad[p], held_in[s, p], (((1,), (1,)), ((), ())), preferred_element_type=F32
             )
             total = term if p == 0 else total + term
-        out[s, block:] = total.astype(BF16)
-
-
-def partials(sizes, place, offset, count, hidden, grad, weights, part):
-    block, width = hidden.shape
-    whole = pl.BlockSpec(memory_space=pltpu.VMEM)
-    far = pl.BlockSpec(memory_space=pltpu.HBM)
-    return pl.pallas_call(
-        functools.partial(partials_kernel, sizes, offset),
-        in_specs=[pl.BlockSpec(memory_space=pltpu.SMEM), whole, whole, far, far],
-        out_specs=whole,
-        scratch_shapes=[
-            pltpu.VMEM((count, 3, part, width), BF16),
-            pltpu.VMEM((count, width, part), BF16),
-            pltpu.SemaphoreType.DMA((count, 2)),
-        ],
-        out_shape=shape(count, 2 * block, part, dtype=BF16),
-        cost_estimate=pl.CostEstimate(
-            flops=8 * count * block * part * width,
-            bytes_accessed=8 * count * part * width,
-            transcendentals=0,
-        ),
-        compiler_params=pltpu.CompilerParams(vmem_limit_bytes=GRANT),
-    )(place, hidden, grad, *weights)
+        out[j, block:] = total.astype(BF16)
+
+
+def partials_kernel(sizes, offsets, place, hidden, grad, weight_in, weight_out, *refs):
+    outs, held = refs[:-3], refs[-3:]
+    n_x, n_zl = sizes["x"], sizes["zl"]
+    blocks = [
+        lax.rem(place[2] + k, n_x) * n_zl + j
+        for k, out in zip(offsets, outs)
+        for j in range(out.shape[0])
+    ]
+    ready = load_weights(blocks, weight_in, weight_out, *held)
+    start = 0
+    for out in outs:
+        partials(held, start, out, hidden, grad, ready)
+        start += out.shape[0]
+
+
+def last_kernel(
+    sizes, place, proj, taps, rates, res, skip, conv, grad, near, far, weight_in, weight_out,
+    hidden, out, to_right, to_left, ext, feat, *held,
+):
+    n_x, n_zl = sizes["x"], sizes["zl"]
+    blocks = [lax.rem(place[2] + 2, n_x) * n_zl + j for j in range(n_zl)]
+    ready = load_weights(blocks, weight_in, weight_out, *held, ahead=n_zl)
+    finish_kernel(
+        place, proj, taps, rates, res, skip, conv, grad, near, far, hidden, out, ext, feat
+    )
+    partials(held, 0, to_right, hidden, out, ready)
+    partials(held, to_right.shape[0], to_left, hidden, out, ready)
+
+
+def join_kernel(start, terms, got, out):
+    count = got.shape[0]
+    for i in range(terms.shape[0]):
+        if start <= i < start + count:
+            both = terms[i].astype(F32) + got[i - start].astype(F32)
+            out[i] = both.astype(BF16)
+        else:
+            out[i] = terms[i]
 
 
 def shape(*dims, dtype=F32):
@@ -447,39 +463,66 @@
         ]
     ).astype(jnp.int32)
     copies = call(
-        copy_kernel, shape(n_zl, 2 * block, part, dtype=BF16), [], tokens, cotangent
+        copy_kernel,
+        shape(n_zl, 2 * block, part, dtype=BF16),
+        [pltpu.SemaphoreType.DMA((n_zl, 2))],
+        in_hbm(tokens),
+        in_hbm(cotangent),
+        hbm=2,
     )
     pieces = lax.all_to_all(copies, "zl", 0, 0, tiled=True)
     half = n_zl // 2
+
+    def products(count):
+        return 8 * count * block * part * width
+
     right = [(i, (i + 1) % n_x) for i in range(n_x)]
     left = [(i, (i - 1) % n_x) for i in range(n_x)]
     from_left = lax.ppermute(pieces, "x", right)
     from_right = lax.ppermute(pieces, "x", left)
-    weights = tuple(
-        pltpu.with_memory_space_constraint(w, pltpu.HBM)
-        for w in (input_weight.transpose(1, 0, 2), output_weight)
-    )
-    total = project(sizes, place, [(0, 0)], [pieces], weights)
+    weights = (in_hbm(input_weight.transpose(1, 0, 2)), in_hbm(output_weight))
+    total = call(
+        functools.partial(near_kernel, sizes),
+        shape(4, block, width),
+        held_weights(n_zl, part, width),
+        place,
+        pieces,
+        *weights,
+        flops=products(n_zl),
+        hbm=2,
+    )
     from_left, from_right, total = lax.optimization_barrier((from_left, from_right, total))
     far_left = lax.ppermute(from_left[:half], "x", right)
     far_right = lax.ppermute(from_right[half:], "x", left)
-    total = project(
-        sizes, place, [(n_x - 1, 0), (1, 0)], [from_left, from_right], weights, total
-    )
-    total = project(
-        sizes, place, [(2, 0), (2, half)], [far_left, far_right], weights, total, True
-    )
-    proj = total
+    total = call(
+        functools.partial(side_kernel, sizes),
+        shape(4, block, width),
+        held_weights(2 * n_zl, part, width),
+        place,
+        from_left,
+        from_right,
+        total,
+        *weights,
+        flops=products(2 * n_zl),
+        hbm=2,
+    )
     ext = pltpu.VMEM((3, rows + TILE, width), F32)
     members = sizes["zh"] * sizes["core"]
     pack = 2 * order + 2 * TILE
-    send = call(
-        state_kernel,
-        shape(members, pack, width, dtype=BF16),
-        [ext, pltpu.VMEM((pack, width), F32)],
-        proj,
+    proj, send = call(
+        functools.partial(far_kernel, sizes),
+        [shape(4, block, width, dtype=BF16), shape(members, pack, width, dtype=BF16)],
+        [pltpu.VMEM((4, block, width), F32), ext, pltpu.VMEM((pack, width), F32)]
+        + held_weights(n_zl, part, width),
+        place,
+        far_left,
+        far_right,
+        total,
         taps,
         rates,
+        *weights,
+        flops=products(n_zl),
+        hbm=2,
     )
     conv, grad = call(
         local_kernel,
@@ -503,10 +546,17 @@
         near_states,
     )
     far_states = lax.all_to_all(send, "y", 0, 0, tiled=True)
-    hidden, grad_proj = call(
-        finish_kernel,
-        [shape(block, width, dtype=BF16), shape(3, block, width, dtype=BF16)],
-        [ext, pltpu.VMEM((3, rows, width), F32)],
+    piece = shape(n_zl, 2 * block, part, dtype=BF16)
+    half_piece = shape(half, 2 * block, part, dtype=BF16)
+    hidden, grad_proj, to_right, to_left = call(
+        functools.partial(last_kernel, sizes),
+        [
+            shape(block, width, dtype=BF16),
+            shape(3, block, width, dtype=BF16),
+            half_piece,
+            half_piece,
+        ],
+        [ext, pltpu.VMEM((3, rows, width), F32)] + held_weights(n_zl, part, width),
         place,
         proj,
         taps,
@@ -517,24 +567,39 @@
         grad,
         near_states,
         far_states,
-    )
-
-    def terms(offset, count, order_by=place):
-        return partials(sizes, order_by, offset, count, hidden, grad_proj, weights, part)
-
-    def add(*arrays):
-        return sum(a.astype(F32) for a in arrays).astype(BF16)
-
-    far_right = lax.ppermute(terms((2, 0), half), "x", right)
-    far_left, later = lax.optimization_barrier((terms((2, half), half), place))
-    far_left = lax.ppermute(far_left, "x", left)
-    to_right = terms((1, 0), n_zl, later)
-    to_left = terms((n_x - 1, 0), n_zl, later)
-    to_right = jnp.concatenate([add(to_right[:half], far_right), to_right[half:]], axis=0)
-    to_left = jnp.concatenate([to_left[:half], add(to_left[half:], far_left)], axis=0)
+        *weights,
+        flops=products(n_zl),
+        hbm=2,
+    )
+    far_right = lax.ppermute(to_right, "x", right)
+    far_left = lax.ppermute(to_left, "x", left)
+    to_right, to_left = call(
+        functools.partial(partials_kernel, sizes, [1, n_x - 1]),
+        [piece, piece],
+        held_weights(2 * n_zl, part, width),
+        place,
+        hidden,
+        grad_proj,
+        *weights,
+        flops=products(2 * n_zl),
+        hbm=2,
+    )
+    to_right = call(functools.partial(join_kernel, 0), piece, [], to_right, far_right)
     from_left = lax.ppermute(to_right, "x", right)
+    to_left = call(functools.partial(join_kernel, half), piece, [], to_left, far_left)
     from_right = lax.ppermute(to_left, "x", left)
-    summed = add(terms((0, 0), n_zl, later), from_left, from_right)
+    (own,) = call(
+        functools.partial(partials_kernel, sizes, [0]),
+        [piece],
+        held_weights(n_zl, part, width),
+        place,
+        hidden,
+        grad_proj,
+        *weights,
+        flops=products(n_zl),
+        hbm=2,
+    )
+    summed = sum(a.astype(F32) for a in (own, from_left, from_right)).astype(BF16)
     summed = lax.all_to_all(summed, "zl", 0, 0, tiled=True)
     total = jnp.sum(summed.astype(F32), axis=0).astype(BF16)
     return total[:block], total[block:]

time: 162 us -> 159 us (0.981); the launches traced: 162 us -> 156 us
  waiting for transfers between devices: 22.6 us -> 18.1 us
  starting transfers between devices: 34.5 us -> 36.7 us
  local copies, waits for them, and re-layouts: 2.43 us -> 0.72 us
    pallas_call x8 -> x0, Pallas kernels: 22.9 us -> none  [the longest x5 14.6 us: partials(): pl.pallas_call(functools.partial(partials_kernel, sizes, offset), in_spec...]
    pallas_call x5 -> x11, Pallas kernels: 7.9 us -> 29.4 us  [call(): pl.pallas_call(kernel, out_shape=outs, scratch_shapes=scratch, in_specs=s...]
    ppermute x1, waiting for transfers between devices: 4.48 us -> 1.87 us  [shards(): from_right = lax.ppermute(to_left, 'x', left)]
    ppermute x1, starting transfers between devices: 3.13 us -> 5.13 us  [shards(): from_left = lax.ppermute(to_right, 'x', right)]
    unnamed x12 -> x8, local copies, waits for them, and re-layouts: 1.7 us -> 0.03 us
  transfers between devices with their start and end apart: 9 -> 9, of which waited for: 6 -> 6; matrix products, arithmetic and copies ran while one was open for 0% -> 0% of each run, Pallas kernels for 13% -> 12%
where the time goes in v7:
time: 159 us; the launch traced here: 156 us
  blocking collectives  69.6 us (44%)
  starting transfers between devices  36.7 us (23%)
  Pallas kernels  29.4 us (18%)
  waiting for transfers between devices  18.1 us (11%)
    all_to_all x1, blocking collectives, shards(): near_states = lax.all_to_all(send, ('zh', 'core'), 0, 0, tiled=True)  34.2 us
    pallas_call x11, Pallas kernels, call(): pl.pallas_call(kernel, out_shape=outs, scratch_shapes=scratch, in_specs=s...  29.4 us
    all_to_all x1, blocking collectives, shards(): pieces = lax.all_to_all(copies, 'zl', 0, 0, tiled=True)  21.5 us
    all_to_all x1, blocking collectives, shards(): summed = lax.all_to_all(summed, 'zl', 0, 0, tiled=True)  13.9 us
    all_to_all x1, starting transfers between devices, shards(): far_states = lax.all_to_all(send, 'y', 0, 0, tiled=True)  7.1 us
    all_to_all x1, waiting for transfers between devices, shards(): far_states = lax.all_to_all(send, 'y', 0, 0, tiled=True)  5.87 us
    ppermute x1, starting transfers between devices, shards(): far_left = lax.ppermute(from_left[:half], 'x', right)  5.53 us
    ppermute x1, starting transfers between devices, shards(): from_left = lax.ppermute(pieces, 'x', right)  5.36 us
  transfers between devices with their start and end apart: 9, of which 6 were waited for; matrix products, arithmetic and copies ran while one was open for 0% of the time, Pallas kernels for 12%

profile of v7, /device:TPU:6, one launch (start us, length us, event | category | flops | bytes accessed | tf_op | source)
XLA Modules:
  0.0 155.8 jit_solution(3865891731156059939)
XLA Ops:
  0.6 1.3 shard_map.95
  1.9 21.5 %all_to_all.20.piece = bf16[4,256,256]{2,1,0:T(8,128)(2,1)S(1)} all-to-all(bf16[4,256,256]{2,1,0:T(8,128)(2,1)S(1)} %shard_map.95), channel_id=1, replica_groups=mesh['y'=8,'zh'=4,'core'=2,'x'=4,'zl'=4] {'zl'}, dimensions={0} | all-to-all | bytes 1048576 | tf_op jit(solution)/shard_map/all_to_all | solution.py:473
  23.5 2.7 %collective-permute-start.1 = (bf16[4,256,256]{2,1,0:T(8,128)(2,1)S(1)}, bf16[4,256,256]{2,1,0:T(8,128)(2,1)S(1)}, u32[]{:S(2)}, u32[]{:S(2)}) collective-permute-start(bf16[4,256,256]{2,1,0:T(8,128)(2,1)S(1)} %all_to_all.20.piece), channel_id=1, source_target_pairs={{0,12},{4,0},{8,4},{12,8},{1,13},{5,1},{9,5},{13,9},{2,14},{6,2},{... | collective-permute-start | bytes 1572872 | tf_op jit(solution)/shard_map/ppermute | solution.py:482
  26.2 5.4 %collective-permute-start = (bf16[4,256,256]{2,1,0:T(8,128)(2,1)S(1)}, bf16[4,256,256]{2,1,0:T(8,128)(2,1)S(1)}, u32[]{:S(2)}, u32[]{:S(2)}) collective-permute-start(bf16[4,256,256]{2,1,0:T(8,128)(2,1)S(1)} %all_to_all.20.piece), channel_id=1, source_target_pairs={{0,4},{4,8},{8,12},{12,0},{1,5},{5,9},{9,13},{13,1},{2,6},{6,10},{... | collective-permute-start | bytes 1572872 | tf_op jit(solution)/shard_map/ppermute | solution.py:481
  31.6 0.1 pad_add_fusion.place.place_ref
  31.6 3.0 %shard_map.96.old = f32[4,128,256]{2,1,0:T(8,128)S(1)} custom-call(s32[3]{0:T(128)S(1)} %pad_add_fusion.place.place_ref, bf16[4,256,256]{2,1,0:T(8,128)(2,1)S(1)} %all_to_all.20.piece, bf16[3,4096,256]{2,1,0:T(8,128)(2,1)} %bitcast.20, bf16[256,4096]{1,0:T(8,128)(2,1)} %weight_out.11), custom_call_target="tpu_custom_call" | custom-call | flops 268435456 | tf_op jit(solution)/shard_map/pallas_call | solution.py:284
  34.7 0.0 copy-start
  34.7 0.0 copy-start.1
  34.7 4.4 %collective-permute-done.1.right = bf16[4,256,256]{2,1,0:T(8,128)(2,1)S(1)} collective-permute-done((bf16[4,256,256]{2,1,0:T(8,128)(2,1)S(1)}, bf16[4,256,256]{2,1,0:T(8,128)(2,1)S(1)}, u32[]{:S(2)}, u32[]{:S(2)}) %collective-permute-start.1) | collective-permute-done | bytes 524320 | tf_op jit(solution)/shard_map/ppermute | solution.py:482
  39.1 1.3 collective-permute-done.left
  40.4 5.5 %collective-permute-start.2 = (bf16[2,256,256]{2,1,0:T(8,128)(2,1)S(1)}, bf16[2,256,256]{2,1,0:T(8,128)(2,1)S(1)}, u32[]{:S(2)}, u32[]{:S(2)}) collective-permute-start(bf16[2,256,256]{2,1,0:T(8,128)(2,1)S(1)} %slice.12), channel_id=1, source_target_pairs={{0,4},{4,8},{8,12},{12,0},{1,5},{5,9},{9,13},{13,1},{2,6},{6,10},{... | collective-permute-start | bytes 786440 | tf_op jit(solution)/shard_map/ppermute | solution.py:495
  45.9 1.9 %collective-permute-start.3 = (bf16[2,256,256]{2,1,0:T(8,128)(2,1)S(1)}, bf16[2,256,256]{2,1,0:T(8,128)(2,1)S(1)}, u32[]{:S(2)}, u32[]{:S(2)}) collective-permute-start(bf16[2,256,256]{2,1,0:T(8,128)(2,1)S(1)} %slice.13), channel_id=1, source_target_pairs={{0,12},{4,0},{8,4},{12,8},{1,13},{5,1},{9,5},{13,9},{2,14},{6,2},{... | collective-permute-start | bytes 786440 | tf_op jit(solution)/shard_map/ppermute | solution.py:496
  47.8 4.4 %shard_map.97.old = f32[4,128,256]{2,1,0:T(8,128)S(1)} custom-call(s32[3]{0:T(128)S(1)} %pad_add_fusion.place.place_ref, bf16[4,256,256]{2,1,0:T(8,128)(2,1)S(1)} %collective-permute-done.left, bf16[4,256,256]{2,1,0:T(8,128)(2,1)S(1)} %collective-permute-done.1.right, f32[4,128,256]{2,1,0:T(8,128)S(1)} %shard_map.96.old, bf16[3,4096,256]{2,1,0:T(8,128)(2,1)} %bitcast.21, ...), custom_call_target="tpu_custom_call" | custom-call | flops 536870912 | tf_op jit(solution)/shard_map/pallas_call | solution.py:284
  52.2 0.0 copy-start.2
  52.2 0.0 copy-start.3
  52.3 0.0 collective-permute-done.2.left
  52.3 3.1 %collective-permute-done.3.right = bf16[2,256,256]{2,1,0:T(8,128)(2,1)S(1)} collective-permute-done((bf16[2,256,256]{2,1,0:T(8,128)(2,1)S(1)}, bf16[2,256,256]{2,1,0:T(8,128)(2,1)S(1)}, u32[]{:S(2)}, u32[]{:S(2)}) %collective-permute-start.3) | collective-permute-done | bytes 262176 | tf_op jit(solution)/shard_map/ppermute | solution.py:496
  55.4 0.0 copy-done
  55.4 0.0 copy-done.1
  55.4 4.0 %shard_map.98 = (bf16[4,128,256]{2,1,0:T(8,128)(2,1)S(1)}, bf16[8,48,256]{2,1,0:T(8,128)(2,1)S(1)}) custom-call(s32[3]{0:T(128)S(1)} %pad_add_fusion.place.place_ref, bf16[2,256,256]{2,1,0:T(8,128)(2,1)S(1)} %collective-permute-done.2.left, bf16[2,256,256]{2,1,0:T(8,128)(2,1)S(1)} %collective-permute-done.3.right, f32[4,128,256]{2,1,0:T(8,128)S(1)} %shard_map.97.old, ...), custom_call_target="tpu_custom_call" | custom-call | flops 268435456 | tf_op jit(solution)/shard_map/pallas_call | solution.py:284
  59.4 34.2 %all_to_all.21.got_ref.near = bf16[8,48,256]{2,1,0:T(8,128)(2,1)S(1)} all-to-all(bf16[8,48,256]{2,1,0:T(8,128)(2,1)S(1)} %get-tuple-element.21), channel_id=1, replica_groups=mesh['y'=8,'zh'=4,'core'=2,'x'=4,'zl'=4] {'zh','core'}, dimensions={0} | all-to-all | bytes 393216 | tf_op jit(solution)/shard_map/all_to_all | solution.py:538
  93.6 1.4 shard_map.100
  95.0 7.1 %all-to-all-start.2 = ((bf16[8,32,256]{2,1,0:T(8,128)(2,1)}), bf16[8,32,256]{2,1,0:T(8,128)(2,1)S(1)}, u32[]{:S(2)}, u32[]{:S(2)}) async-start(bf16[8,32,256]{2,1,0:T(8,128)(2,1)} %shard_map.100), calls=%async_computation.2 | async-start | bytes 262144 | tf_op jit(solution)/shard_map/all_to_all | solution.py:548
  102.1 0.0 copy-done.2
  102.1 0.0 copy-done.3
  102.1 3.2 %shard_map.99 = (f32[136,256]{1,0:T(8,128)S(1)}, f32[136,256]{1,0:T(8,128)S(1)}) custom-call(bf16[4,128,256]{2,1,0:T(8,128)(2,1)S(1)} %get-tuple-element.18.proj_ref.proj, f32[3,3,256]{2,1,0:T(4,128)S(1)} %bitcast.14, f32[16,256]{1,0:T(8,128)S(1)} %bitcast.10, f32[16,256]{1,0:T(8,128)S(1)} %bitcast.16, f32[1,256]{1,0:T(1,128)S(1)} %bitcast.18), custom_call_target="tpu_custom_call" | custom-call | flops 3000000000 | tf_op jit(solution)/shard_map/pallas_call | solution.py:284
  105.3 5.9 %all-to-all-done.2.far = bf16[8,32,256]{2,1,0:T(8,128)(2,1)S(1)} async-done(((bf16[8,32,256]{2,1,0:T(8,128)(2,1)}), bf16[8,32,256]{2,1,0:T(8,128)(2,1)S(1)}, u32[]{:S(2)}, u32[]{:S(2)}) %all-to-all-start.2) | async-done | bytes 131104 | tf_op jit(solution)/shard_map/all_to_all | solution.py:548
  111.1 3.9 %shard_map.101 = (bf16[128,256]{1,0:T(8,128)(2,1)S(1)}, bf16[3,128,256]{2,1,0:T(8,128)(2,1)S(1)}, bf16[2,256,256]{2,1,0:T(8,128)(2,1)S(1)}, bf16[2,256,256]{2,1,0:T(8,128)(2,1)S(1)}) custom-call(s32[3]{0:T(128)S(1)} %pad_add_fusion.place.place_ref, bf16[4,128,256]{2,1,0:T(8,128)(2,1)S(1)} %get-tuple-element.18.proj_ref.proj, f32[3,3,256]{2,1,0:T(4,128)S(1)} %bitcast.15, ...), custom_call_target="tpu_custom_call" | custom-call | flops 268435456 | tf_op jit(solution)/shard_map/pallas_call | solution.py:284
  115.0 1.9 %collective-permute-start.6 = (bf16[2,256,256]{2,1,0:T(8,128)(2,1)S(1)}, bf16[2,256,256]{2,1,0:T(8,128)(2,1)S(1)}, u32[]{:S(2)}, u32[]{:S(2)}) collective-permute-start(bf16[2,256,256]{2,1,0:T(8,128)(2,1)S(1)} %get-tuple-element.27), channel_id=1, source_target_pairs={{0,12},{4,0},{8,4},{12,8},{1,13},{5,1},{9,5},{13,9},{2,14},{6,2},{... | collective-permute-start | bytes 786440 | tf_op jit(solution)/shard_map/ppermute | solution.py:575
  117.0 5.1 %collective-permute-start.4 = (bf16[2,256,256]{2,1,0:T(8,128)(2,1)S(1)}, bf16[2,256,256]{2,1,0:T(8,128)(2,1)S(1)}, u32[]{:S(2)}, u32[]{:S(2)}) collective-permute-start(bf16[2,256,256]{2,1,0:T(8,128)(2,1)S(1)} %get-tuple-element.25), channel_id=1, source_target_pairs={{0,4},{4,8},{8,12},{12,0},{1,5},{5,9},{9,13},{13,1},{2,6},{6,10},{... | collective-permute-start | bytes 786440 | tf_op jit(solution)/shard_map/ppermute | solution.py:574
  122.1 4.9 %shard_map.103 = (bf16[4,256,256]{2,1,0:T(8,128)(2,1)S(1)}, bf16[4,256,256]{2,1,0:T(8,128)(2,1)S(1)}) custom-call(s32[3]{0:T(128)S(1)} %pad_add_fusion.place.place_ref, bf16[128,256]{1,0:T(8,128)(2,1)S(1)} %get-tuple-element.22.hidden, bf16[3,128,256]{2,1,0:T(8,128)(2,1)S(1)} %get-tuple-element.23.grad, bf16[3,4096,256]{2,1,0:T(8,128)(2,1)} %bitcast.24, ...), custom_call_target="tpu_custom_call" | custom-call | flops 536870912 | tf_op jit(solution)/shard_map/pallas_call | solution.py:284
  127.0 0.0 collective-permute-done.6.got
  127.1 0.1 shard_map.105
  127.2 1.9 %collective-permute-start.7 = (bf16[4,256,256]{2,1,0:T(8,128)(2,1)S(1)}, bf16[4,256,256]{2,1,0:T(8,128)(2,1)S(1)}, u32[]{:S(2)}, u32[]{:S(2)}) collective-permute-start(bf16[4,256,256]{2,1,0:T(8,128)(2,1)S(1)} %shard_map.105), channel_id=1, source_target_pairs={{0,12},{4,0},{8,4},{12,8},{1,13},{5,1},{9,5},{13,9},{2,14},{6,2},{... | collective-permute-start | bytes 1572872 | tf_op jit(solution)/shard_map/ppermute | solution.py:590
  129.1 0.0 collective-permute-done.4.got
  129.1 0.1 shard_map.104
  129.2 5.1 %collective-permute-start.5 = (bf16[4,256,256]{2,1,0:T(8,128)(2,1)S(1)}, bf16[4,256,256]{2,1,0:T(8,128)(2,1)S(1)}, u32[]{:S(2)}, u32[]{:S(2)}) collective-permute-start(bf16[4,256,256]{2,1,0:T(8,128)(2,1)S(1)} %shard_map.104), channel_id=1, source_target_pairs={{0,4},{4,8},{8,12},{12,0},{1,5},{5,9},{9,13},{13,1},{2,6},{6,10},{... | collective-permute-start | bytes 1572872 | tf_op jit(solution)/shard_map/ppermute | solution.py:588
  134.3 3.3 %shard_map.102 = bf16[4,256,256]{2,1,0:T(8,128)(2,1)S(1)} custom-call(s32[3]{0:T(128)S(1)} %pad_add_fusion.place.place_ref, bf16[128,256]{1,0:T(8,128)(2,1)S(1)} %get-tuple-element.22.hidden, bf16[3,128,256]{2,1,0:T(8,128)(2,1)S(1)} %get-tuple-element.23.grad, bf16[3,4096,256]{2,1,0:T(8,128)(2,1)} %bitcast.25, bf16[256,4096]{1,0:T(8,128)(2,1)} %weight_out.11), custom_call_target="tpu_custom_call" | custom-call | flops 268435456 | tf_op jit(solution)/shard_map/pallas_call | solution.py:284
  137.6 1.9 %collective-permute-done.7 = bf16[4,256,256]{2,1,0:T(8,128)(2,1)S(1)} collective-permute-done((bf16[4,256,256]{2,1,0:T(8,128)(2,1)S(1)}, bf16[4,256,256]{2,1,0:T(8,128)(2,1)S(1)}, u32[]{:S(2)}, u32[]{:S(2)}) %collective-permute-start.7) | collective-permute-done | bytes 524320 | tf_op jit(solution)/shard_map/ppermute | solution.py:590
  139.4 1.5 collective-permute-done.5
  141.0 0.2 add_convert_fusion
  141.2 13.9 %all_to_all.22 = bf16[4,256,256]{2,1,0:T(8,128)(2,1)S(1)} all-to-all(bf16[4,256,256]{2,1,0:T(8,128)(2,1)S(1)} %add_convert_fusion), channel_id=1, replica_groups=mesh['y'=8,'zh'=4,'core'=2,'x'=4,'zl'=4] {'zl'}, dimensions={0} | all-to-all | bytes 1048576 | tf_op jit(solution)/shard_map/all_to_all | solution.py:603
  155.1 0.1 reduce_sum.12
  155.2 0.7 fusion
  (2 shorter events, 0.0 us)
Async XLA Ops:
  23.5 15.6 %collective-permute-start.1 = (bf16[4,256,256]{2,1,0:T(8,128)(2,1)S(1)}, bf16[4,256,256]{2,1,0:T(8,128)(2,1)S(1)}, u32[]{:S(2)}, u32[]{:S(2)}) collective-permute-start(bf16[4,256,256]{2,1,0:T(8,128)(2,1)S(1)} %all_to_all.20.piece), channel_id=1, source_target_pairs={{0,12},{4,0},{8,4},{12,8},{1,13},{5,1},{9,5},{13,9},{2,14},{6,2},{... | collective-permute-start | bytes 1572872 | tf_op jit(solution)/shard_map/ppermute | solution.py:482
  26.2 14.1 %collective-permute-start = (bf16[4,256,256]{2,1,0:T(8,128)(2,1)S(1)}, bf16[4,256,256]{2,1,0:T(8,128)(2,1)S(1)}, u32[]{:S(2)}, u32[]{:S(2)}) collective-permute-start(bf16[4,256,256]{2,1,0:T(8,128)(2,1)S(1)} %all_to_all.20.piece), channel_id=1, source_target_pairs={{0,4},{4,8},{8,12},{12,0},{1,5},{5,9},{9,13},{13,1},{2,6},{6,10},{... | collective-permute-start | bytes 1572872 | tf_op jit(solution)/shard_map/ppermute | solution.py:481
  34.7 20.7 %copy-start = (f32[256,16]{0,1:T(8,128)S(1)}, f32[256,16]{0,1:T(8,128)}, u32[]{:S(2)}) copy-start(f32[256,16]{0,1:T(8,128)} %param.14) | copy-start | bytes 49156
  34.7 20.7 %copy-start.1 = (f32[3,256,3]{1,2,0:T(4,128)S(1)}, f32[3,256,3]{1,2,0:T(4,128)}, u32[]{:S(2)}) copy-start(f32[3,256,3]{1,2,0:T(4,128)} %param.12) | copy-start | bytes 27652
  40.4 11.9 %collective-permute-start.2 = (bf16[2,256,256]{2,1,0:T(8,128)(2,1)S(1)}, bf16[2,256,256]{2,1,0:T(8,128)(2,1)S(1)}, u32[]{:S(2)}, u32[]{:S(2)}) collective-permute-start(bf16[2,256,256]{2,1,0:T(8,128)(2,1)S(1)} %slice.12), channel_id=1, source_target_pairs={{0,4},{4,8},{8,12},{12,0},{1,5},{5,9},{9,13},{13,1},{2,6},{6,10},{... | collective-permute-start | bytes 786440 | tf_op jit(solution)/shard_map/ppermute | solution.py:495
  45.9 9.5 %collective-permute-start.3 = (bf16[2,256,256]{2,1,0:T(8,128)(2,1)S(1)}, bf16[2,256,256]{2,1,0:T(8,128)(2,1)S(1)}, u32[]{:S(2)}, u32[]{:S(2)}) collective-permute-start(bf16[2,256,256]{2,1,0:T(8,128)(2,1)S(1)} %slice.13), channel_id=1, source_target_pairs={{0,12},{4,0},{8,4},{12,8},{1,13},{5,1},{9,5},{13,9},{2,14},{6,2},{... | collective-permute-start | bytes 786440 | tf_op jit(solution)/shard_map/ppermute | solution.py:496
  52.2 49.8 %copy-start.2 = (f32[256,16]{0,1:T(8,128)S(1)}, f32[256,16]{0,1:T(8,128)}, u32[]{:S(2)}) copy-start(f32[256,16]{0,1:T(8,128)} %param.13) | copy-start | bytes 49156
  52.2 49.8 %copy-start.3 = (f32[256]{0:T(256)S(1)}, f32[256]{0:T(256)}, u32[]{:S(2)}) copy-start(f32[256]{0:T(256)} %param.15) | copy-start | bytes 3076
  95.0 16.2 %all-to-all-start.2 = ((bf16[8,32,256]{2,1,0:T(8,128)(2,1)}), bf16[8,32,256]{2,1,0:T(8,128)(2,1)S(1)}, u32[]{:S(2)}, u32[]{:S(2)}) async-start(bf16[8,32,256]{2,1,0:T(8,128)(2,1)} %shard_map.100), calls=%async_computation.2 | async-start | bytes 262144 | tf_op jit(solution)/shard_map/all_to_all | solution.py:548
  115.0 12.0 %collective-permute-start.6 = (bf16[2,256,256]{2,1,0:T(8,128)(2,1)S(1)}, bf16[2,256,256]{2,1,0:T(8,128)(2,1)S(1)}, u32[]{:S(2)}, u32[]{:S(2)}) collective-permute-start(bf16[2,256,256]{2,1,0:T(8,128)(2,1)S(1)} %get-tuple-element.27), channel_id=1, source_target_pairs={{0,12},{4,0},{8,4},{12,8},{1,13},{5,1},{9,5},{13,9},{2,14},{6,2},{... | collective-permute-start | bytes 786440 | tf_op jit(solution)/shard_map/ppermute | solution.py:575
  117.0 12.1 %collective-permute-start.4 = (bf16[2,256,256]{2,1,0:T(8,128)(2,1)S(1)}, bf16[2,256,256]{2,1,0:T(8,128)(2,1)S(1)}, u32[]{:S(2)}, u32[]{:S(2)}) collective-permute-start(bf16[2,256,256]{2,1,0:T(8,128)(2,1)S(1)} %get-tuple-element.25), channel_id=1, source_target_pairs={{0,4},{4,8},{8,12},{12,0},{1,5},{5,9},{9,13},{13,1},{2,6},{6,10},{... | collective-permute-start | bytes 786440 | tf_op jit(solution)/shard_map/ppermute | solution.py:574
  127.2 12.3 %collective-permute-start.7 = (bf16[4,256,256]{2,1,0:T(8,128)(2,1)S(1)}, bf16[4,256,256]{2,1,0:T(8,128)(2,1)S(1)}, u32[]{:S(2)}, u32[]{:S(2)}) collective-permute-start(bf16[4,256,256]{2,1,0:T(8,128)(2,1)S(1)} %shard_map.105), channel_id=1, source_target_pairs={{0,12},{4,0},{8,4},{12,8},{1,13},{5,1},{9,5},{13,9},{2,14},{6,2},{... | collective-permute-start | bytes 1572872 | tf_op jit(solution)/shard_map/ppermute | solution.py:590
  129.2 11.8 %collective-permute-start.5 = (bf16[4,256,256]{2,1,0:T(8,128)(2,1)S(1)}, bf16[4,256,256]{2,1,0:T(8,128)(2,1)S(1)}, u32[]{:S(2)}, u32[]{:S(2)}) collective-permute-start(bf16[4,256,256]{2,1,0:T(8,128)(2,1)S(1)} %shard_map.104), channel_id=1, source_target_pairs={{0,4},{4,8},{8,12},{12,0},{1,5},{5,9},{9,13},{13,1},{2,6},{6,10},{... | collective-permute-start | bytes 1572872 | tf_op jit(solution)/shard_map/ppermute | solution.py:588

commit v8 on v7

--- a/solution.py
+++ b/solution.py
@@ -13,6 +13,7 @@
 TILE = 8
 AHEAD = 2
 GRANT = 16 * 2**20
+PAIR = 2
 BF16 = jnp.bfloat16
 F32 = jnp.float32
 
@@ -292,17 +293,25 @@
     )(*args)
 
 
-def load_weights(blocks, weight_in, weight_out, held_in, held_out, sems, ahead=3):
-    part = held_in.shape[2]
+def load_weights(blocks, weight_in, weight_out, held_in, held_out, sems, ahead=2):
+    span = held_in.shape[1]
+    width = weight_out.shape[0]
+    part = span // PAIR
     copies = []
     for s, block in enumerate(blocks):
-        at = pl.ds(pl.multiple_of(block * part, part), part)
-        copies.append(
-            (
-                pltpu.make_async_copy(weight_in.at[:, at, :], held_in.at[s], sems.at[s, 0]),
-                pltpu.make_async_copy(weight_out.at[:, at], held_out.at[s], sems.at[s, 1]),
+        at = pl.ds(pl.multiple_of(block * part, part), span)
+        moves = [
+            pltpu.make_async_copy(
+                weight_in.at[p, at, :],
+                held_in.at[s, :, pl.ds(p * width, width)],
+                sems.at[s, p],
             )
+            for p in range(3)
+        ]
+        moves.append(
+            pltpu.make_async_copy(weight_out.at[:, at], held_out.at[s], sems.at[s, 3])
         )
+        copies.append(moves)
 
     def start(s):
         for copy in copies[s]:
@@ -322,37 +331,37 @@
 
 def held_weights(count, part, width):
     return [
-        pltpu.VMEM((count, 3, part, width), BF16),
-        pltpu.VMEM((count, width, part), BF16),
-        pltpu.SemaphoreType.DMA((count, 2)),
+        pltpu.VMEM((count, PAIR * part, 3 * width), BF16),
+        pltpu.VMEM((count, width, PAIR * part), BF16),
+        pltpu.SemaphoreType.DMA((count, 4)),
     ]
 
 
 def project(sizes, offsets, place_ref, pieces, weights, old, total, held_in, held_out, sems):
     n_x, n_zl = sizes["x"], sizes["zl"]
     block = pieces[0].shape[1] // 2
+    width = total.shape[2]
     work = [
         (piece, j, lax.rem(place_ref[2] + k, n_x) * n_zl + start + j)
         for piece, (k, start) in zip(pieces, offsets)
-        for j in range(piece.shape[0])
+        for j in range(0, piece.shape[0], PAIR)
     ]
     ready = load_weights([w[2] for w in work], *weights, held_in, held_out, sems)
     for s, (piece, j, _) in enumerate(work):
+        run = range(j, j + PAIR)
+        part_in = jnp.concatenate([piece[i, :block] for i in run], axis=1)
+        part_grad = jnp.concatenate([piece[i, block:] for i in run], axis=1)
         ready(s)
+        term = jnp.dot(part_in, held_in[s], preferred_element_type=F32)
+        back = lax.dot_general(
+            part_grad, held_out[s], (((1,), (1,)), ((), ())), preferred_element_type=F32
+        )
+        terms = [term[:, p * width : (p + 1) * width] for p in range(3)] + [back]
         for p in range(4):
-            if p < 3:
-                term = jnp.dot(piece[j, :block], held_in[s, p], preferred_element_type=F32)
+            if s == 0 and old is None:
+                total[p] = terms[p]
             else:
-                term = lax.dot_general(
-                    piece[j, block:],
-                    held_out[s],
-                    (((1,), (1,)), ((), ())),
-                    preferred_element_type=F32,
-                )
-            if s == 0 and old is None:
-                total[p] = term
-            else:
-                total[p] = (old if s == 0 else total)[p] + term
+                total[p] = (old if s == 0 else total)[p] + terms[p]
 
 
 def near_kernel(sizes, place, piece, weight_in, weight_out, total, *held):
@@ -378,18 +387,18 @@
 def partials(held, start, out, hidden, grad, ready):
     held_in, held_out = held[:2]
     block = hidden.shape[0]
-    for j in range(out.shape[0]):
-        s = start + j
+    part = out.shape[2]
+    for j in range(0, out.shape[0], PAIR):
+        s = start + j // PAIR
+        grads = jnp.concatenate([grad[p] for p in range(3)], axis=1)
         ready(s)
         mixed = jnp.dot(hidden[...], held_out[s], preferred_element_type=F32)
-        out[j, :block] = mixed.astype(BF16)
-        total = None
-        for p in range(3):
-            term = lax.dot_general(
-                grad[p], held_in[s, p], (((1,), (1,)), ((), ())), preferred_element_type=F32
-            )
-            total = term if p == 0 else total + term
-        out[j, block:] = total.astype(BF16)
+        total = lax.dot_general(
+            grads, held_in[s], (((1,), (1,)), ((), ())), preferred_element_type=F32
+        )
+        for i in range(PAIR):
+            out[j + i, :block] = mixed[:, i * part : (i + 1) * part].astype(BF16)
+            out[j + i, block:] = total[:, i * part : (i + 1) * part].astype(BF16)
 
 
 def partials_kernel(sizes, offsets, place, hidden, grad, weight_in, weight_out, *refs):
@@ -398,13 +407,13 @@
     blocks = [
         lax.rem(place[2] + k, n_x) * n_zl + j
         for k, out in zip(offsets, outs)
-        for j in range(out.shape[0])
+        for j in range(0, out.shape[0], PAIR)
     ]
     ready = load_weights(blocks, weight_in, weight_out, *held)
     start = 0
     for out in outs:
         partials(held, start, out, hidden, grad, ready)
-        start += out.shape[0]
+        start += out.shape[0] // PAIR
 
 
 def last_kernel(
@@ -412,13 +421,13 @@
     hidden, out, to_right, to_left, ext, feat, *held,
 ):
     n_x, n_zl = sizes["x"], sizes["zl"]
-    blocks = [lax.rem(place[2] + 2, n_x) * n_zl + j for j in range(n_zl)]
-    ready = load_weights(blocks, weight_in, weight_out, *held, ahead=n_zl)
+    blocks = [lax.rem(place[2] + 2, n_x) * n_zl + j for j in range(0, n_zl, PAIR)]
+    ready = load_weights(blocks, weight_in, weight_out, *held)
     finish_kernel(
         place, proj, taps, rates, res, skip, conv, grad, near, far, hidden, out, ext, feat
     )
     partials(held, 0, to_right, hidden, out, ready)
-    partials(held, to_right.shape[0], to_left, hidden, out, ready)
+    partials(held, to_right.shape[0] // PAIR, to_left, hidden, out, ready)
 
 
 def join_kernel(start, terms, got, out):
@@ -484,7 +493,7 @@
     total = call(
         functools.partial(near_kernel, sizes),
         shape(4, block, width),
-        held_weights(n_zl, part, width),
+        held_weights(n_zl // PAIR, part, width),
         place,
         pieces,
         *weights,
@@ -497,7 +506,7 @@
     total = call(
         functools.partial(side_kernel, sizes),
         shape(4, block, width),
-        held_weights(2 * n_zl, part, width),
+        held_weights(2 * n_zl // PAIR, part, width),
         place,
         from_left,
         from_right,
@@ -513,7 +522,7 @@
         functools.partial(far_kernel, sizes),
         [shape(4, block, width, dtype=BF16), shape(members, pack, width, dtype=BF16)],
         [pltpu.VMEM((4, block, width), F32), ext, pltpu.VMEM((pack, width), F32)]
-        + held_weights(n_zl, part, width),
+        + held_weights(n_zl // PAIR, part, width),
         place,
         far_left,
         far_right,
@@ -556,7 +565,7 @@
             half_piece,
             half_piece,
         ],
-        [ext, pltpu.VMEM((3, rows, width), F32)] + held_weights(n_zl, part, width),
+        [ext, pltpu.VMEM((3, rows, width), F32)] + held_weights(n_zl // PAIR, part, width),
         place,
         proj,
         taps,
@@ -576,7 +585,7 @@
     to_right, to_left = call(
         functools.partial(partials_kernel, sizes, [1, n_x - 1]),
         [piece, piece],
-        held_weights(2 * n_zl, part, width),
+        held_weights(2 * n_zl // PAIR, part, width),
         place,
         hidden,
         grad_proj,
@@ -591,7 +600,7 @@
     (own,) = call(
         functools.partial(partials_kernel, sizes, [0]),
         [piece],
-        held_weights(n_zl, part, width),
+        held_weights(n_zl // PAIR, part, width),
         place,
         hidden,
         grad_proj,

time: 159 us -> 157 us (0.987)
  Pallas kernels: 29.4 us -> 26 us
    pallas_call x11, Pallas kernels: 29.4 us -> 26 us  [call(): pl.pallas_call(kernel, out_shape=outs, scratch_shapes=scratch, in_specs=s...]
  transfers between devices with their start and end apart: 9 -> 9, of which waited for: 6 -> 6; matrix products, arithmetic and copies ran while one was open for 0% -> 0% of each run, Pallas kernels for 12% -> 11%
where the time goes in v8:
time: 157 us; the launch traced here: 154 us
  blocking collectives  69.6 us (44%)
  starting transfers between devices  36.7 us (23%)
  Pallas kernels  26 us (17%)
  waiting for transfers between devices  19.4 us (12%)
    all_to_all x1, blocking collectives, shards(): near_states = lax.all_to_all(send, ('zh', 'core'), 0, 0, tiled=True)  34.2 us
    pallas_call x11, Pallas kernels, call(): pl.pallas_call(kernel, out_shape=outs, scratch_shapes=scratch, in_specs=s...  26 us
    all_to_all x1, blocking collectives, shards(): pieces = lax.all_to_all(copies, 'zl', 0, 0, tiled=True)  21.5 us
    all_to_all x1, blocking collectives, shards(): summed = lax.all_to_all(summed, 'zl', 0, 0, tiled=True)  13.9 us
    all_to_all x1, starting transfers between devices, shards(): far_states = lax.all_to_all(send, 'y', 0, 0, tiled=True)  7.1 us
    all_to_all x1, waiting for transfers between devices, shards(): far_states = lax.all_to_all(send, 'y', 0, 0, tiled=True)  5.87 us
    ppermute x1, starting transfers between devices, shards(): far_left = lax.ppermute(from_left[:half], 'x', right)  5.53 us
    ppermute x1, starting transfers between devices, shards(): from_left = lax.ppermute(pieces, 'x', right)  5.36 us
  transfers between devices with their start and end apart: 9, of which 6 were waited for; matrix products, arithmetic and copies ran while one was open for 0% of the time, Pallas kernels for 11%

profile of v8, /device:TPU:6, one launch (start us, length us, event | category | flops | bytes accessed | tf_op | source)
XLA Modules:
  0.0 153.7 jit_solution(11339399143336998295)
XLA Ops:
  0.6 1.3 shard_map.95
  1.9 21.5 %all_to_all.20.piece = bf16[4,256,256]{2,1,0:T(8,128)(2,1)S(1)} all-to-all(bf16[4,256,256]{2,1,0:T(8,128)(2,1)S(1)} %shard_map.95), channel_id=1, replica_groups=mesh['y'=8,'zh'=4,'core'=2,'x'=4,'zl'=4] {'zl'}, dimensions={0} | all-to-all | bytes 1048576 | tf_op jit(solution)/shard_map/all_to_all | solution.py:482
  23.5 2.7 %collective-permute-start.1 = (bf16[4,256,256]{2,1,0:T(8,128)(2,1)S(1)}, bf16[4,256,256]{2,1,0:T(8,128)(2,1)S(1)}, u32[]{:S(2)}, u32[]{:S(2)}) collective-permute-start(bf16[4,256,256]{2,1,0:T(8,128)(2,1)S(1)} %all_to_all.20.piece), channel_id=1, source_target_pairs={{0,12},{4,0},{8,4},{12,8},{1,13},{5,1},{9,5},{13,9},{2,14},{6,2},{... | collective-permute-start | bytes 1572872 | tf_op jit(solution)/shard_map/ppermute | solution.py:491
  26.2 5.4 %collective-permute-start = (bf16[4,256,256]{2,1,0:T(8,128)(2,1)S(1)}, bf16[4,256,256]{2,1,0:T(8,128)(2,1)S(1)}, u32[]{:S(2)}, u32[]{:S(2)}) collective-permute-start(bf16[4,256,256]{2,1,0:T(8,128)(2,1)S(1)} %all_to_all.20.piece), channel_id=1, source_target_pairs={{0,4},{4,8},{8,12},{12,0},{1,5},{5,9},{9,13},{13,1},{2,6},{6,10},{... | collective-permute-start | bytes 1572872 | tf_op jit(solution)/shard_map/ppermute | solution.py:490
  31.6 0.1 pad_add_fusion.place.place_ref
  31.6 2.6 %shard_map.96.old = f32[4,128,256]{2,1,0:T(8,128)S(1)} custom-call(s32[3]{0:T(128)S(1)} %pad_add_fusion.place.place_ref, bf16[4,256,256]{2,1,0:T(8,128)(2,1)S(1)} %all_to_all.20.piece, bf16[3,4096,256]{2,1,0:T(8,128)(2,1)} %bitcast.20, bf16[256,4096]{1,0:T(8,128)(2,1)} %weight_out.11), custom_call_target="tpu_custom_call" | custom-call | flops 268435456 | tf_op jit(solution)/shard_map/pallas_call | solution.py:285
  34.2 0.0 copy-start
  34.2 0.0 copy-start.1
  34.2 4.8 %collective-permute-done.1.right = bf16[4,256,256]{2,1,0:T(8,128)(2,1)S(1)} collective-permute-done((bf16[4,256,256]{2,1,0:T(8,128)(2,1)S(1)}, bf16[4,256,256]{2,1,0:T(8,128)(2,1)S(1)}, u32[]{:S(2)}, u32[]{:S(2)}) %collective-permute-start.1) | collective-permute-done | bytes 524320 | tf_op jit(solution)/shard_map/ppermute | solution.py:491
  39.1 1.3 collective-permute-done.left
  40.4 5.5 %collective-permute-start.2 = (bf16[2,256,256]{2,1,0:T(8,128)(2,1)S(1)}, bf16[2,256,256]{2,1,0:T(8,128)(2,1)S(1)}, u32[]{:S(2)}, u32[]{:S(2)}) collective-permute-start(bf16[2,256,256]{2,1,0:T(8,128)(2,1)S(1)} %slice.12), channel_id=1, source_target_pairs={{0,4},{4,8},{8,12},{12,0},{1,5},{5,9},{9,13},{13,1},{2,6},{6,10},{... | collective-permute-start | bytes 786440 | tf_op jit(solution)/shard_map/ppermute | solution.py:504
  45.9 1.9 %collective-permute-start.3 = (bf16[2,256,256]{2,1,0:T(8,128)(2,1)S(1)}, bf16[2,256,256]{2,1,0:T(8,128)(2,1)S(1)}, u32[]{:S(2)}, u32[]{:S(2)}) collective-permute-start(bf16[2,256,256]{2,1,0:T(8,128)(2,1)S(1)} %slice.13), channel_id=1, source_target_pairs={{0,12},{4,0},{8,4},{12,8},{1,13},{5,1},{9,5},{13,9},{2,14},{6,2},{... | collective-permute-start | bytes 786440 | tf_op jit(solution)/shard_map/ppermute | solution.py:505
  47.8 4.0 %shard_map.97.old = f32[4,128,256]{2,1,0:T(8,128)S(1)} custom-call(s32[3]{0:T(128)S(1)} %pad_add_fusion.place.place_ref, bf16[4,256,256]{2,1,0:T(8,128)(2,1)S(1)} %collective-permute-done.left, bf16[4,256,256]{2,1,0:T(8,128)(2,1)S(1)} %collective-permute-done.1.right, f32[4,128,256]{2,1,0:T(8,128)S(1)} %shard_map.96.old, bf16[3,4096,256]{2,1,0:T(8,128)(2,1)} %bitcast.21, ...), custom_call_target="tpu_custom_call" | custom-call | flops 536870912 | tf_op jit(solution)/shard_map/pallas_call | solution.py:285
  51.9 0.0 copy-start.2
  51.9 0.0 copy-start.3
  51.9 0.0 collective-permute-done.2.left
  51.9 3.5 %collective-permute-done.3.right = bf16[2,256,256]{2,1,0:T(8,128)(2,1)S(1)} collective-permute-done((bf16[2,256,256]{2,1,0:T(8,128)(2,1)S(1)}, bf16[2,256,256]{2,1,0:T(8,128)(2,1)S(1)}, u32[]{:S(2)}, u32[]{:S(2)}) %collective-permute-start.3) | collective-permute-done | bytes 262176 | tf_op jit(solution)/shard_map/ppermute | solution.py:505
  55.4 0.0 copy-done
  55.4 0.0 copy-done.1
  55.4 3.5 %shard_map.98 = (bf16[4,128,256]{2,1,0:T(8,128)(2,1)S(1)}, bf16[8,48,256]{2,1,0:T(8,128)(2,1)S(1)}) custom-call(s32[3]{0:T(128)S(1)} %pad_add_fusion.place.place_ref, bf16[2,256,256]{2,1,0:T(8,128)(2,1)S(1)} %collective-permute-done.2.left, bf16[2,256,256]{2,1,0:T(8,128)(2,1)S(1)} %collective-permute-done.3.right, f32[4,128,256]{2,1,0:T(8,128)S(1)} %shard_map.97.old, ...), custom_call_target="tpu_custom_call" | custom-call | flops 268435456 | tf_op jit(solution)/shard_map/pallas_call | solution.py:285
  58.9 34.2 %all_to_all.21.got_ref.near = bf16[8,48,256]{2,1,0:T(8,128)(2,1)S(1)} all-to-all(bf16[8,48,256]{2,1,0:T(8,128)(2,1)S(1)} %get-tuple-element.21), channel_id=1, replica_groups=mesh['y'=8,'zh'=4,'core'=2,'x'=4,'zl'=4] {'zh','core'}, dimensions={0} | all-to-all | bytes 393216 | tf_op jit(solution)/shard_map/all_to_all | solution.py:547
  93.1 1.4 shard_map.100
  94.5 7.1 %all-to-all-start.2 = ((bf16[8,32,256]{2,1,0:T(8,128)(2,1)}), bf16[8,32,256]{2,1,0:T(8,128)(2,1)S(1)}, u32[]{:S(2)}, u32[]{:S(2)}) async-start(bf16[8,32,256]{2,1,0:T(8,128)(2,1)} %shard_map.100), calls=%async_computation.2 | async-start | bytes 262144 | tf_op jit(solution)/shard_map/all_to_all | solution.py:557
  101.6 0.0 copy-done.2
  101.6 0.0 copy-done.3
  101.6 3.2 %shard_map.99 = (f32[136,256]{1,0:T(8,128)S(1)}, f32[136,256]{1,0:T(8,128)S(1)}) custom-call(bf16[4,128,256]{2,1,0:T(8,128)(2,1)S(1)} %get-tuple-element.18.proj_ref.proj, f32[3,3,256]{2,1,0:T(4,128)S(1)} %bitcast.14, f32[16,256]{1,0:T(8,128)S(1)} %bitcast.10, f32[16,256]{1,0:T(8,128)S(1)} %bitcast.16, f32[1,256]{1,0:T(1,128)S(1)} %bitcast.18), custom_call_target="tpu_custom_call" | custom-call | flops 3000000000 | tf_op jit(solution)/shard_map/pallas_call | solution.py:285
  104.8 5.9 %all-to-all-done.2.far = bf16[8,32,256]{2,1,0:T(8,128)(2,1)S(1)} async-done(((bf16[8,32,256]{2,1,0:T(8,128)(2,1)}), bf16[8,32,256]{2,1,0:T(8,128)(2,1)S(1)}, u32[]{:S(2)}, u32[]{:S(2)}) %all-to-all-start.2) | async-done | bytes 131104 | tf_op jit(solution)/shard_map/all_to_all | solution.py:557
  110.7 3.2 %shard_map.101 = (bf16[128,256]{1,0:T(8,128)(2,1)S(1)}, bf16[3,128,256]{2,1,0:T(8,128)(2,1)S(1)}, bf16[2,256,256]{2,1,0:T(8,128)(2,1)S(1)}, bf16[2,256,256]{2,1,0:T(8,128)(2,1)S(1)}) custom-call(s32[3]{0:T(128)S(1)} %pad_add_fusion.place.place_ref, bf16[4,128,256]{2,1,0:T(8,128)(2,1)S(1)} %get-tuple-element.18.proj_ref.proj, f32[3,3,256]{2,1,0:T(4,128)S(1)} %bitcast.15, ...), custom_call_target="tpu_custom_call" | custom-call | flops 268435456 | tf_op jit(solution)/shard_map/pallas_call | solution.py:285
  113.8 1.9 %collective-permute-start.6 = (bf16[2,256,256]{2,1,0:T(8,128)(2,1)S(1)}, bf16[2,256,256]{2,1,0:T(8,128)(2,1)S(1)}, u32[]{:S(2)}, u32[]{:S(2)}) collective-permute-start(bf16[2,256,256]{2,1,0:T(8,128)(2,1)S(1)} %get-tuple-element.27), channel_id=1, source_target_pairs={{0,12},{4,0},{8,4},{12,8},{1,13},{5,1},{9,5},{13,9},{2,14},{6,2},{... | collective-permute-start | bytes 786440 | tf_op jit(solution)/shard_map/ppermute | solution.py:584
  115.8 5.1 %collective-permute-start.4 = (bf16[2,256,256]{2,1,0:T(8,128)(2,1)S(1)}, bf16[2,256,256]{2,1,0:T(8,128)(2,1)S(1)}, u32[]{:S(2)}, u32[]{:S(2)}) collective-permute-start(bf16[2,256,256]{2,1,0:T(8,128)(2,1)S(1)} %get-tuple-element.25), channel_id=1, source_target_pairs={{0,4},{4,8},{8,12},{12,0},{1,5},{5,9},{9,13},{13,1},{2,6},{6,10},{... | collective-permute-start | bytes 786440 | tf_op jit(solution)/shard_map/ppermute | solution.py:583
  120.9 4.0 %shard_map.103 = (bf16[4,256,256]{2,1,0:T(8,128)(2,1)S(1)}, bf16[4,256,256]{2,1,0:T(8,128)(2,1)S(1)}) custom-call(s32[3]{0:T(128)S(1)} %pad_add_fusion.place.place_ref, bf16[128,256]{1,0:T(8,128)(2,1)S(1)} %get-tuple-element.22.hidden, bf16[3,128,256]{2,1,0:T(8,128)(2,1)S(1)} %get-tuple-element.23.grad, bf16[3,4096,256]{2,1,0:T(8,128)(2,1)} %bitcast.24, ...), custom_call_target="tpu_custom_call" | custom-call | flops 536870912 | tf_op jit(solution)/shard_map/pallas_call | solution.py:285
  125.0 0.0 collective-permute-done.6.got
  125.0 0.1 shard_map.105
  125.1 1.9 %collective-permute-start.7 = (bf16[4,256,256]{2,1,0:T(8,128)(2,1)S(1)}, bf16[4,256,256]{2,1,0:T(8,128)(2,1)S(1)}, u32[]{:S(2)}, u32[]{:S(2)}) collective-permute-start(bf16[4,256,256]{2,1,0:T(8,128)(2,1)S(1)} %shard_map.105), channel_id=1, source_target_pairs={{0,12},{4,0},{8,4},{12,8},{1,13},{5,1},{9,5},{13,9},{2,14},{6,2},{... | collective-permute-start | bytes 1572872 | tf_op jit(solution)/shard_map/ppermute | solution.py:599
  127.0 0.0 collective-permute-done.4.got
  127.0 0.1 shard_map.104
  127.1 5.1 %collective-permute-start.5 = (bf16[4,256,256]{2,1,0:T(8,128)(2,1)S(1)}, bf16[4,256,256]{2,1,0:T(8,128)(2,1)S(1)}, u32[]{:S(2)}, u32[]{:S(2)}) collective-permute-start(bf16[4,256,256]{2,1,0:T(8,128)(2,1)S(1)} %shard_map.104), channel_id=1, source_target_pairs={{0,4},{4,8},{8,12},{12,0},{1,5},{5,9},{9,13},{13,1},{2,6},{6,10},{... | collective-permute-start | bytes 1572872 | tf_op jit(solution)/shard_map/ppermute | solution.py:597
  132.2 2.7 %shard_map.102 = bf16[4,256,256]{2,1,0:T(8,128)(2,1)S(1)} custom-call(s32[3]{0:T(128)S(1)} %pad_add_fusion.place.place_ref, bf16[128,256]{1,0:T(8,128)(2,1)S(1)} %get-tuple-element.22.hidden, bf16[3,128,256]{2,1,0:T(8,128)(2,1)S(1)} %get-tuple-element.23.grad, bf16[3,4096,256]{2,1,0:T(8,128)(2,1)} %bitcast.25, bf16[256,4096]{1,0:T(8,128)(2,1)} %weight_out.11), custom_call_target="tpu_custom_call" | custom-call | flops 268435456 | tf_op jit(solution)/shard_map/pallas_call | solution.py:285
  134.9 2.4 %collective-permute-done.7 = bf16[4,256,256]{2,1,0:T(8,128)(2,1)S(1)} collective-permute-done((bf16[4,256,256]{2,1,0:T(8,128)(2,1)S(1)}, bf16[4,256,256]{2,1,0:T(8,128)(2,1)S(1)}, u32[]{:S(2)}, u32[]{:S(2)}) %collective-permute-start.7) | collective-permute-done | bytes 524320 | tf_op jit(solution)/shard_map/ppermute | solution.py:599
  137.3 1.5 %collective-permute-done.5 = bf16[4,256,256]{2,1,0:T(8,128)(2,1)S(1)} collective-permute-done((bf16[4,256,256]{2,1,0:T(8,128)(2,1)S(1)}, bf16[4,256,256]{2,1,0:T(8,128)(2,1)S(1)}, u32[]{:S(2)}, u32[]{:S(2)}) %collective-permute-start.5) | collective-permute-done | bytes 524320 | tf_op jit(solution)/shard_map/ppermute | solution.py:597
  138.9 0.2 add_convert_fusion
  139.1 13.9 %all_to_all.22 = bf16[4,256,256]{2,1,0:T(8,128)(2,1)S(1)} all-to-all(bf16[4,256,256]{2,1,0:T(8,128)(2,1)S(1)} %add_convert_fusion), channel_id=1, replica_groups=mesh['y'=8,'zh'=4,'core'=2,'x'=4,'zl'=4] {'zl'}, dimensions={0} | all-to-all | bytes 1048576 | tf_op jit(solution)/shard_map/all_to_all | solution.py:612
  153.0 0.1 reduce_sum.12
  153.1 0.7 fusion
  (2 shorter events, 0.0 us)
Async XLA Ops:
  23.5 15.6 %collective-permute-start.1 = (bf16[4,256,256]{2,1,0:T(8,128)(2,1)S(1)}, bf16[4,256,256]{2,1,0:T(8,128)(2,1)S(1)}, u32[]{:S(2)}, u32[]{:S(2)}) collective-permute-start(bf16[4,256,256]{2,1,0:T(8,128)(2,1)S(1)} %all_to_all.20.piece), channel_id=1, source_target_pairs={{0,12},{4,0},{8,4},{12,8},{1,13},{5,1},{9,5},{13,9},{2,14},{6,2},{... | collective-permute-start | bytes 1572872 | tf_op jit(solution)/shard_map/ppermute | solution.py:491
  26.2 14.1 %collective-permute-start = (bf16[4,256,256]{2,1,0:T(8,128)(2,1)S(1)}, bf16[4,256,256]{2,1,0:T(8,128)(2,1)S(1)}, u32[]{:S(2)}, u32[]{:S(2)}) collective-permute-start(bf16[4,256,256]{2,1,0:T(8,128)(2,1)S(1)} %all_to_all.20.piece), channel_id=1, source_target_pairs={{0,4},{4,8},{8,12},{12,0},{1,5},{5,9},{9,13},{13,1},{2,6},{6,10},{... | collective-permute-start | bytes 1572872 | tf_op jit(solution)/shard_map/ppermute | solution.py:490
  34.2 21.2 %copy-start = (f32[256,16]{0,1:T(8,128)S(1)}, f32[256,16]{0,1:T(8,128)}, u32[]{:S(2)}) copy-start(f32[256,16]{0,1:T(8,128)} %param.14) | copy-start | bytes 49156
  34.2 21.2 %copy-start.1 = (f32[3,256,3]{1,2,0:T(4,128)S(1)}, f32[3,256,3]{1,2,0:T(4,128)}, u32[]{:S(2)}) copy-start(f32[3,256,3]{1,2,0:T(4,128)} %param.12) | copy-start | bytes 27652
  40.4 11.5 %collective-permute-start.2 = (bf16[2,256,256]{2,1,0:T(8,128)(2,1)S(1)}, bf16[2,256,256]{2,1,0:T(8,128)(2,1)S(1)}, u32[]{:S(2)}, u32[]{:S(2)}) collective-permute-start(bf16[2,256,256]{2,1,0:T(8,128)(2,1)S(1)} %slice.12), channel_id=1, source_target_pairs={{0,4},{4,8},{8,12},{12,0},{1,5},{5,9},{9,13},{13,1},{2,6},{6,10},{... | collective-permute-start | bytes 786440 | tf_op jit(solution)/shard_map/ppermute | solution.py:504
  45.9 9.5 %collective-permute-start.3 = (bf16[2,256,256]{2,1,0:T(8,128)(2,1)S(1)}, bf16[2,256,256]{2,1,0:T(8,128)(2,1)S(1)}, u32[]{:S(2)}, u32[]{:S(2)}) collective-permute-start(bf16[2,256,256]{2,1,0:T(8,128)(2,1)S(1)} %slice.13), channel_id=1, source_target_pairs={{0,12},{4,0},{8,4},{12,8},{1,13},{5,1},{9,5},{13,9},{2,14},{6,2},{... | collective-permute-start | bytes 786440 | tf_op jit(solution)/shard_map/ppermute | solution.py:505
  51.9 49.7 %copy-start.2 = (f32[256,16]{0,1:T(8,128)S(1)}, f32[256,16]{0,1:T(8,128)}, u32[]{:S(2)}) copy-start(f32[256,16]{0,1:T(8,128)} %param.13) | copy-start | bytes 49156
  51.9 49.7 %copy-start.3 = (f32[256]{0:T(256)S(1)}, f32[256]{0:T(256)}, u32[]{:S(2)}) copy-start(f32[256]{0:T(256)} %param.15) | copy-start | bytes 3076
  94.5 16.2 %all-to-all-start.2 = ((bf16[8,32,256]{2,1,0:T(8,128)(2,1)}), bf16[8,32,256]{2,1,0:T(8,128)(2,1)S(1)}, u32[]{:S(2)}, u32[]{:S(2)}) async-start(bf16[8,32,256]{2,1,0:T(8,128)(2,1)} %shard_map.100), calls=%async_computation.2 | async-start | bytes 262144 | tf_op jit(solution)/shard_map/all_to_all | solution.py:557
  113.8 11.1 %collective-permute-start.6 = (bf16[2,256,256]{2,1,0:T(8,128)(2,1)S(1)}, bf16[2,256,256]{2,1,0:T(8,128)(2,1)S(1)}, u32[]{:S(2)}, u32[]{:S(2)}) collective-permute-start(bf16[2,256,256]{2,1,0:T(8,128)(2,1)S(1)} %get-tuple-element.27), channel_id=1, source_target_pairs={{0,12},{4,0},{8,4},{12,8},{1,13},{5,1},{9,5},{13,9},{2,14},{6,2},{... | collective-permute-start | bytes 786440 | tf_op jit(solution)/shard_map/ppermute | solution.py:584
  115.8 11.2 %collective-permute-start.4 = (bf16[2,256,256]{2,1,0:T(8,128)(2,1)S(1)}, bf16[2,256,256]{2,1,0:T(8,128)(2,1)S(1)}, u32[]{:S(2)}, u32[]{:S(2)}) collective-permute-start(bf16[2,256,256]{2,1,0:T(8,128)(2,1)S(1)} %get-tuple-element.25), channel_id=1, source_target_pairs={{0,4},{4,8},{8,12},{12,0},{1,5},{5,9},{9,13},{13,1},{2,6},{6,10},{... | collective-permute-start | bytes 786440 | tf_op jit(solution)/shard_map/ppermute | solution.py:583
  125.1 12.3 %collective-permute-start.7 = (bf16[4,256,256]{2,1,0:T(8,128)(2,1)S(1)}, bf16[4,256,256]{2,1,0:T(8,128)(2,1)S(1)}, u32[]{:S(2)}, u32[]{:S(2)}) collective-permute-start(bf16[4,256,256]{2,1,0:T(8,128)(2,1)S(1)} %shard_map.105), channel_id=1, source_target_pairs={{0,12},{4,0},{8,4},{12,8},{1,13},{5,1},{9,5},{13,9},{2,14},{6,2},{... | collective-permute-start | bytes 1572872 | tf_op jit(solution)/shard_map/ppermute | solution.py:599
  127.1 11.8 %collective-permute-start.5 = (bf16[4,256,256]{2,1,0:T(8,128)(2,1)S(1)}, bf16[4,256,256]{2,1,0:T(8,128)(2,1)S(1)}, u32[]{:S(2)}, u32[]{:S(2)}) collective-permute-start(bf16[4,256,256]{2,1,0:T(8,128)(2,1)S(1)} %shard_map.104), channel_id=1, source_target_pairs={{0,4},{4,8},{8,12},{12,0},{1,5},{5,9},{9,13},{13,1},{2,6},{6,10},{... | collective-permute-start | bytes 1572872 | tf_op jit(solution)/shard_map/ppermute | solution.py:597

commit v9 on v8

--- a/solution.py
+++ b/solution.py
@@ -337,20 +337,22 @@
     ]
 
 
-def project(sizes, offsets, place_ref, pieces, weights, old, total, held_in, held_out, sems):
+def set_base(sizes, place, steps):
     n_x, n_zl = sizes["x"], sizes["zl"]
-    block = pieces[0].shape[1] // 2
+    x, core = place[2], place[3]
+    return lax.rem(x + jnp.where(core == 0, n_x - steps, steps), n_x) * n_zl
+
+
+def project(sizes, steps, place, pieces, weights, old, total, held_in, held_out, sems):
+    block = pieces.shape[1] // 2
     width = total.shape[2]
-    work = [
-        (piece, j, lax.rem(place_ref[2] + k, n_x) * n_zl + start + j)
-        for piece, (k, start) in zip(pieces, offsets)
-        for j in range(0, piece.shape[0], PAIR)
-    ]
-    ready = load_weights([w[2] for w in work], *weights, held_in, held_out, sems)
-    for s, (piece, j, _) in enumerate(work):
+    starts = range(0, pieces.shape[0], PAIR)
+    base = set_base(sizes, place, steps)
+    ready = load_weights([base + j for j in starts], *weights, held_in, held_out, sems)
+    for s, j in enumerate(starts):
         run = range(j, j + PAIR)
-        part_in = jnp.concatenate([piece[i, :block] for i in run], axis=1)
-        part_grad = jnp.concatenate([piece[i, block:] for i in run], axis=1)
+        part_in = jnp.concatenate([pieces[i, :block] for i in run], axis=1)
+        part_grad = jnp.concatenate([pieces[i, block:] for i in run], axis=1)
         ready(s)
         term = jnp.dot(part_in, held_in[s], preferred_element_type=F32)
         back = lax.dot_general(
@@ -364,32 +366,29 @@
                 total[p] = (old if s == 0 else total)[p] + terms[p]
 
 
-def near_kernel(sizes, place, piece, weight_in, weight_out, total, *held):
-    project(sizes, [(0, 0)], place, [piece], (weight_in, weight_out), None, total, *held)
-
-
-def side_kernel(sizes, place, left, right, old, weight_in, weight_out, total, *held):
-    offsets = [(sizes["x"] - 1, 0), (1, 0)]
-    weights = (weight_in, weight_out)
-    project(sizes, offsets, place, [left, right], weights, old, total, *held)
+def first_kernel(sizes, place, pieces, weight_in, weight_out, total, *held):
+    project(sizes, 0, place, pieces, (weight_in, weight_out), None, total, *held)
+
+
+def next_kernel(sizes, steps, place, pieces, old, weight_in, weight_out, total, *held):
+    project(sizes, steps, place, pieces, (weight_in, weight_out), old, total, *held)
 
 
 def far_kernel(
-    sizes, place, left, right, old, taps, rates, weight_in, weight_out, proj, send, total, ext, pack, *held
+    sizes, steps, place, pieces, old, taps, rates, weight_in, weight_out,
+    proj, send, total, ext, pack, *held,
 ):
-    offsets = [(2, 0), (2, left.shape[0])]
-    weights = (weight_in, weight_out)
-    project(sizes, offsets, place, [left, right], weights, old, total, *held)
+    project(sizes, steps, place, pieces, (weight_in, weight_out), old, total, *held)
     proj[...] = total[...].astype(BF16)
     state_kernel(proj, taps, rates, send, ext, pack)
 
 
-def partials(held, start, out, hidden, grad, ready):
+def partials(held, out, hidden, grad, ready):
     held_in, held_out = held[:2]
     block = hidden.shape[0]
     part = out.shape[2]
     for j in range(0, out.shape[0], PAIR):
-        s = start + j // PAIR
+        s = j // PAIR
         grads = jnp.concatenate([grad[p] for p in range(3)], axis=1)
         ready(s)
         mixed = jnp.dot(hidden[...], held_out[s], preferred_element_type=F32)
@@ -401,43 +400,24 @@
             out[j + i, block:] = total[:, i * part : (i + 1) * part].astype(BF16)
 
 
-def partials_kernel(sizes, offsets, place, hidden, grad, weight_in, weight_out, *refs):
-    outs, held = refs[:-3], refs[-3:]
-    n_x, n_zl = sizes["x"], sizes["zl"]
-    blocks = [
-        lax.rem(place[2] + k, n_x) * n_zl + j
-        for k, out in zip(offsets, outs)
-        for j in range(0, out.shape[0], PAIR)
-    ]
-    ready = load_weights(blocks, weight_in, weight_out, *held)
-    start = 0
-    for out in outs:
-        partials(held, start, out, hidden, grad, ready)
-        start += out.shape[0] // PAIR
+def partials_kernel(sizes, steps, place, hidden, grad, weight_in, weight_out, out, *held):
+    base = set_base(sizes, place, steps)
+    starts = range(0, out.shape[0], PAIR)
+    ready = load_weights([base + j for j in starts], weight_in, weight_out, *held)
+    partials(held, out, hidden, grad, ready)
 
 
 def last_kernel(
     sizes, place, proj, taps, rates, res, skip, conv, grad, near, far, weight_in, weight_out,
-    hidden, out, to_right, to_left, ext, feat, *held,
+    hidden, out, terms, ext, feat, *held,
 ):
-    n_x, n_zl = sizes["x"], sizes["zl"]
-    blocks = [lax.rem(place[2] + 2, n_x) * n_zl + j for j in range(0, n_zl, PAIR)]
-    ready = load_weights(blocks, weight_in, weight_out, *held)
+    base = set_base(sizes, place, 1)
+    starts = range(0, terms.shape[0], PAIR)
+    ready = load_weights([base + j for j in starts], weight_in, weight_out, *held)
     finish_kernel(
         place, proj, taps, rates, res, skip, conv, grad, near, far, hidden, out, ext, feat
     )
-    partials(held, 0, to_right, hidden, out, ready)
-    partials(held, to_right.shape[0] // PAIR, to_left, hidden, out, ready)
-
-
-def join_kernel(start, terms, got, out):
-    count = got.shape[0]
-    for i in range(terms.shape[0]):
-        if start <= i < start + count:
-            both = terms[i].astype(F32) + got[i - start].astype(F32)
-            out[i] = both.astype(BF16)
-        else:
-            out[i] = terms[i]
+    partials(held, terms, hidden, out, ready)
 
 
 def shape(*dims, dtype=F32):
@@ -469,6 +449,7 @@
             lax.axis_index("y"),
             lax.axis_index("zh") * sizes["core"] + lax.axis_index("core"),
             lax.axis_index("x"),
+            lax.axis_index("core"),
         ]
     ).astype(jnp.int32)
     copies = call(
@@ -480,52 +461,56 @@
         hbm=2,
     )
     pieces = lax.all_to_all(copies, "zl", 0, 0, tiled=True)
-    half = n_zl // 2
+    ring = [
+        (c * n_x + i, c * n_x + (i + 1 - 2 * c) % n_x) for c in range(2) for i in range(n_x)
+    ]
+
+    def onward(array):
+        return lax.ppermute(array, ("core", "x"), ring)
 
     def products(count):
         return 8 * count * block * part * width
 
     right = [(i, (i + 1) % n_x) for i in range(n_x)]
     left = [(i, (i - 1) % n_x) for i in range(n_x)]
-    from_left = lax.ppermute(pieces, "x", right)
-    from_right = lax.ppermute(pieces, "x", left)
     weights = (in_hbm(input_weight.transpose(1, 0, 2)), in_hbm(output_weight))
+    held = held_weights(n_zl // PAIR, part, width)
+    arrived = onward(pieces)
     total = call(
-        functools.partial(near_kernel, sizes),
+        functools.partial(first_kernel, sizes),
         shape(4, block, width),
-        held_weights(n_zl // PAIR, part, width),
+        held,
         place,
         pieces,
         *weights,
         flops=products(n_zl),
         hbm=2,
     )
-    from_left, from_right, total = lax.optimization_barrier((from_left, from_right, total))
-    far_left = lax.ppermute(from_left[:half], "x", right)
-    far_right = lax.ppermute(from_right[half:], "x", left)
-    total = call(
-        functools.partial(side_kernel, sizes),
-        shape(4, block, width),
-        held_weights(2 * n_zl // PAIR, part, width),
-        place,
-        from_left,
-        from_right,
-        total,
-        *weights,
-        flops=products(2 * n_zl),
-        hbm=2,
-    )
+    for step in range(1, n_x - 1):
+        arrived, total = lax.optimization_barrier((arrived, total))
+        following = onward(arrived)
+        total = call(
+            functools.partial(next_kernel, sizes, step),
+            shape(4, block, width),
+            held,
+            place,
+            arrived,
+            total,
+            *weights,
+            flops=products(n_zl),
+            hbm=2,
+        )
+        arrived = following
     ext = pltpu.VMEM((3, rows + TILE, width), F32)
     members = sizes["zh"] * sizes["core"]
     pack = 2 * order + 2 * TILE
     proj, send = call(
-        functools.partial(far_kernel, sizes),
+        functools.partial(far_kernel, sizes, n_x - 1),
         [shape(4, block, width, dtype=BF16), shape(members, pack, width, dtype=BF16)],
         [pltpu.VMEM((4, block, width), F32), ext, pltpu.VMEM((pack, width), F32)]
-        + held_weights(n_zl // PAIR, part, width),
+        + held,
         place,
-        far_left,
-        far_right,
+        arrived,
         total,
         taps,
         rates,
@@ -556,16 +541,14 @@
     )
     far_states = lax.all_to_all(send, "y", 0, 0, tiled=True)
     piece = shape(n_zl, 2 * block, part, dtype=BF16)
-    half_piece = shape(half, 2 * block, part, dtype=BF16)
-    hidden, grad_proj, to_right, to_left = call(
+    hidden, grad_proj, terms = call(
         functools.partial(last_kernel, sizes),
         [
             shape(block, width, dtype=BF16),
             shape(3, block, width, dtype=BF16),
-            half_piece,
-            half_piece,
+            piece,
         ],
-        [ext, pltpu.VMEM((3, rows, width), F32)] + held_weights(n_zl // PAIR, part, width),
+        [ext, pltpu.VMEM((3, rows, width), F32)] + held,
         place,
         proj,
         taps,
@@ -580,35 +563,22 @@
         flops=products(n_zl),
         hbm=2,
     )
-    far_right = lax.ppermute(to_right, "x", right)
-    far_left = lax.ppermute(to_left, "x", left)
-    to_right, to_left = call(
-        functools.partial(partials_kernel, sizes, [1, n_x - 1]),
-        [piece, piece],
-        held_weights(2 * n_zl // PAIR, part, width),
-        place,
-        hidden,
-        grad_proj,
-        *weights,
-        flops=products(2 * n_zl),
-        hbm=2,
-    )
-    to_right = call(functools.partial(join_kernel, 0), piece, [], to_right, far_right)
-    from_left = lax.ppermute(to_right, "x", right)
-    to_left = call(functools.partial(join_kernel, half), piece, [], to_left, far_left)
-    from_right = lax.ppermute(to_left, "x", left)
-    (own,) = call(
-        functools.partial(partials_kernel, sizes, [0]),
-        [piece],
-        held_weights(n_zl // PAIR, part, width),
-        place,
-        hidden,
-        grad_proj,
-        *weights,
-        flops=products(n_zl),
-        hbm=2,
-    )
-    summed = sum(a.astype(F32) for a in (own, from_left, from_right)).astype(BF16)
+    for step in range(2, n_x + 1):
+        got = onward(terms)
+        own = call(
+            functools.partial(partials_kernel, sizes, step % n_x),
+            piece,
+            held,
+            place,
+            hidden,
+            grad_proj,
+            *weights,
+            flops=products(n_zl),
+            hbm=2,
+        )
+        got, place = lax.optimization_barrier((got, place))
+        terms = (own.astype(F32) + got.astype(F32)).astype(BF16)
+    summed = terms
     summed = lax.all_to_all(summed, "zl", 0, 0, tiled=True)
     total = jnp.sum(summed.astype(F32), axis=0).astype(BF16)
     return total[:block], total[block:]

time: 157 us -> 170 us (1.083)
  waiting for transfers between devices: 19.4 us -> 29.9 us
  starting transfers between devices: 36.7 us -> 41.2 us
  blocking collectives: 69.6 us -> 65.6 us
  Pallas kernels: 26 us -> 28.3 us
    ppermute x8 -> x6, waiting for transfers between devices: 13.6 us -> 24 us  [onward(): return lax.ppermute(array, ('core', 'x'), ring)]
    ppermute x8 -> x6, starting transfers between devices: 29.6 us -> 34.1 us  [onward(): return lax.ppermute(array, ('core', 'x'), ring)]
    all_to_all x1, blocking collectives: 34.2 us -> 30.2 us  [shards(): near_states = lax.all_to_all(send, ('zh', 'core'), 0, 0, tiled=True)]
    pallas_call x11, Pallas kernels: 26 us -> 28.3 us  [call(): pl.pallas_call(kernel, out_shape=outs, scratch_shapes=scratch, in_specs=s...]
  transfers between devices with their start and end apart: 9 -> 7, of which waited for: 6 -> 7; matrix products, arithmetic and copies ran while one was open for 0% -> 0% of each run, Pallas kernels for 11% -> 11%
where the time goes in v9:
time: 170 us; the launch traced here: 167 us
  blocking collectives  65.6 us (39%)
  starting transfers between devices  41.2 us (24%)
  waiting for transfers between devices  29.9 us (18%)
  Pallas kernels  28.3 us (17%)
    ppermute x6, starting transfers between devices, onward(): return lax.ppermute(array, ('core', 'x'), ring)  34.1 us
    all_to_all x1, blocking collectives, shards(): near_states = lax.all_to_all(send, ('zh', 'core'), 0, 0, tiled=True)  30.2 us
    pallas_call x11, Pallas kernels, call(): pl.pallas_call(kernel, out_shape=outs, scratch_shapes=scratch, in_specs=s...  28.3 us
    ppermute x6, waiting for transfers between devices, onward(): return lax.ppermute(array, ('core', 'x'), ring)  24 us
    all_to_all x1, blocking collectives, shards(): pieces = lax.all_to_all(copies, 'zl', 0, 0, tiled=True)  21.5 us
    all_to_all x1, blocking collectives, shards(): summed = lax.all_to_all(summed, 'zl', 0, 0, tiled=True)  13.9 us
    all_to_all x1, starting transfers between devices, shards(): far_states = lax.all_to_all(send, 'y', 0, 0, tiled=True)  7.1 us
    all_to_all x1, waiting for transfers between devices, shards(): far_states = lax.all_to_all(send, 'y', 0, 0, tiled=True)  5.87 us
  transfers between devices with their start and end apart: 7, of which 7 were waited for; matrix products, arithmetic and copies ran while one was open for 0% of the time, Pallas kernels for 11%

profile of v9, /device:TPU:6, one launch (start us, length us, event | category | flops | bytes accessed | tf_op | source)
XLA Modules:
  0.0 167.2 jit_solution(8908914367299362858)
XLA Ops:
  0.6 1.3 shard_map.95
  1.9 21.5 %all_to_all.20.pieces = bf16[4,256,256]{2,1,0:T(8,128)(2,1)S(1)} all-to-all(bf16[4,256,256]{2,1,0:T(8,128)(2,1)S(1)} %shard_map.95), channel_id=1, replica_groups=mesh['y'=8,'zh'=4,'core'=2,'x'=4,'zl'=4] {'zl'}, dimensions={0} | all-to-all | bytes 1048576 | tf_op jit(solution)/shard_map/all_to_all | solution.py:463
  23.5 6.2 %collective-permute-start = (bf16[4,256,256]{2,1,0:T(8,128)(2,1)S(1)}, bf16[4,256,256]{2,1,0:T(8,128)(2,1)S(1)}, u32[]{:S(2)}, u32[]{:S(2)}) collective-permute-start(bf16[4,256,256]{2,1,0:T(8,128)(2,1)S(1)} %all_to_all.20.pieces), channel_id=1, source_target_pairs={{0,4},{4,8},{8,12},{12,0},{16,28},{20,16},{24,20},{28,24},{1,5},{5... | collective-permute-start | bytes 1572872 | tf_op jit(solution)/shard_map/ppermute | solution.py:469
  29.6 0.1 pad_add_fusion.place.place_ref
  29.7 2.6 %shard_map.96.old = f32[4,128,256]{2,1,0:T(8,128)S(1)} custom-call(s32[4]{0:T(128)S(1)} %pad_add_fusion.place.place_ref, bf16[4,256,256]{2,1,0:T(8,128)(2,1)S(1)} %all_to_all.20.pieces, bf16[3,4096,256]{2,1,0:T(8,128)(2,1)} %bitcast.21, bf16[256,4096]{1,0:T(8,128)(2,1)} %weight_out.15), custom_call_target="tpu_custom_call" | custom-call | flops 268435456 | tf_op jit(solution)/shard_map/pallas_call | solution.py:285
  32.3 4.0 %collective-permute-done.pieces = bf16[4,256,256]{2,1,0:T(8,128)(2,1)S(1)} collective-permute-done((bf16[4,256,256]{2,1,0:T(8,128)(2,1)S(1)}, bf16[4,256,256]{2,1,0:T(8,128)(2,1)S(1)}, u32[]{:S(2)}, u32[]{:S(2)}) %collective-permute-start) | collective-permute-done | bytes 524320 | tf_op jit(solution)/shard_map/ppermute | solution.py:469
  36.3 5.6 %collective-permute-start.1 = (bf16[4,256,256]{2,1,0:T(8,128)(2,1)S(1)}, bf16[4,256,256]{2,1,0:T(8,128)(2,1)S(1)}, u32[]{:S(2)}, u32[]{:S(2)}) collective-permute-start(bf16[4,256,256]{2,1,0:T(8,128)(2,1)S(1)} %collective-permute-done.pieces), channel_id=1, source_target_pairs={{0,4},{4,8},{8,12},{12,0},{16,28},{20,16},{24,20},{28,24},{1,5},{5... | collective-permute-start | bytes 1572872 | tf_op jit(solution)/shard_map/ppermute | solution.py:469
  41.9 2.6 %shard_map.97.old = f32[4,128,256]{2,1,0:T(8,128)S(1)} custom-call(s32[4]{0:T(128)S(1)} %pad_add_fusion.place.place_ref, bf16[4,256,256]{2,1,0:T(8,128)(2,1)S(1)} %collective-permute-done.pieces, f32[4,128,256]{2,1,0:T(8,128)S(1)} %shard_map.96.old, bf16[3,4096,256]{2,1,0:T(8,128)(2,1)} %bitcast.22, bf16[256,4096]{1,0:T(8,128)(2,1)} %weight_out.15), custom_call_target="tpu_custom_call" | custom-call | flops 268435456 | tf_op jit(solution)/shard_map/pallas_call | solution.py:285
  44.5 0.0 copy-start
  44.5 0.0 copy-start.1
  44.5 4.0 %collective-permute-done.1.pieces = bf16[4,256,256]{2,1,0:T(8,128)(2,1)S(1)} collective-permute-done((bf16[4,256,256]{2,1,0:T(8,128)(2,1)S(1)}, bf16[4,256,256]{2,1,0:T(8,128)(2,1)S(1)}, u32[]{:S(2)}, u32[]{:S(2)}) %collective-permute-start.1) | collective-permute-done | bytes 524320 | tf_op jit(solution)/shard_map/ppermute | solution.py:469
  48.6 5.6 %collective-permute-start.2 = (bf16[4,256,256]{2,1,0:T(8,128)(2,1)S(1)}, bf16[4,256,256]{2,1,0:T(8,128)(2,1)S(1)}, u32[]{:S(2)}, u32[]{:S(2)}) collective-permute-start(bf16[4,256,256]{2,1,0:T(8,128)(2,1)S(1)} %collective-permute-done.1.pieces), channel_id=1, source_target_pairs={{0,4},{4,8},{8,12},{12,0},{16,28},{20,16},{24,20},{28,24},{1,5},{5... | collective-permute-start | bytes 1572872 | tf_op jit(solution)/shard_map/ppermute | solution.py:469
  54.2 2.6 %shard_map.98.old = f32[4,128,256]{2,1,0:T(8,128)S(1)} custom-call(s32[4]{0:T(128)S(1)} %pad_add_fusion.place.place_ref, bf16[4,256,256]{2,1,0:T(8,128)(2,1)S(1)} %collective-permute-done.1.pieces, f32[4,128,256]{2,1,0:T(8,128)S(1)} %shard_map.97.old, bf16[3,4096,256]{2,1,0:T(8,128)(2,1)} %bitcast.23, bf16[256,4096]{1,0:T(8,128)(2,1)} %weight_out.15), custom_call_target="tpu_custom_call" | custom-call | flops 268435456 | tf_op jit(solution)/shard_map/pallas_call | solution.py:285
  56.8 0.0 copy-start.2
  56.8 0.0 copy-start.3
  56.8 4.0 %collective-permute-done.2.pieces = bf16[4,256,256]{2,1,0:T(8,128)(2,1)S(1)} collective-permute-done((bf16[4,256,256]{2,1,0:T(8,128)(2,1)S(1)}, bf16[4,256,256]{2,1,0:T(8,128)(2,1)S(1)}, u32[]{:S(2)}, u32[]{:S(2)}) %collective-permute-start.2) | collective-permute-done | bytes 524320 | tf_op jit(solution)/shard_map/ppermute | solution.py:469
  60.9 0.0 copy-done
  60.9 0.0 copy-done.1
  60.9 3.5 %shard_map.99 = (bf16[4,128,256]{2,1,0:T(8,128)(2,1)S(1)}, bf16[8,48,256]{2,1,0:T(8,128)(2,1)S(1)}) custom-call(s32[4]{0:T(128)S(1)} %pad_add_fusion.place.place_ref, bf16[4,256,256]{2,1,0:T(8,128)(2,1)S(1)} %collective-permute-done.2.pieces, f32[4,128,256]{2,1,0:T(8,128)S(1)} %shard_map.98.old, f32[3,3,256]{2,1,0:T(4,128)S(1)} %bitcast.13, ...), custom_call_target="tpu_custom_call" | custom-call | flops 268435456 | tf_op jit(solution)/shard_map/pallas_call | solution.py:285
  64.4 30.2 %all_to_all.21.got_ref.near = bf16[8,48,256]{2,1,0:T(8,128)(2,1)S(1)} all-to-all(bf16[8,48,256]{2,1,0:T(8,128)(2,1)S(1)} %get-tuple-element.25), channel_id=1, replica_groups=mesh['y'=8,'zh'=4,'core'=2,'x'=4,'zl'=4] {'zh','core'}, dimensions={0} | all-to-all | bytes 393216 | tf_op jit(solution)/shard_map/all_to_all | solution.py:532
  94.6 1.4 shard_map.101
  95.9 7.1 %all-to-all-start.2 = ((bf16[8,32,256]{2,1,0:T(8,128)(2,1)}), bf16[8,32,256]{2,1,0:T(8,128)(2,1)S(1)}, u32[]{:S(2)}, u32[]{:S(2)}) async-start(bf16[8,32,256]{2,1,0:T(8,128)(2,1)} %shard_map.101), calls=%async_computation.2 | async-start | bytes 262144 | tf_op jit(solution)/shard_map/all_to_all | solution.py:542
  103.0 0.0 copy-done.2
  103.0 0.0 copy-done.3
  103.1 3.2 %shard_map.100 = (f32[136,256]{1,0:T(8,128)S(1)}, f32[136,256]{1,0:T(8,128)S(1)}) custom-call(bf16[4,128,256]{2,1,0:T(8,128)(2,1)S(1)} %get-tuple-element.22.proj_ref.proj, f32[3,3,256]{2,1,0:T(4,128)S(1)} %bitcast.15, f32[16,256]{1,0:T(8,128)S(1)} %bitcast.11, f32[16,256]{1,0:T(8,128)S(1)} %bitcast.17, f32[1,256]{1,0:T(1,128)S(1)} %bitcast.19), custom_call_target="tpu_custom_call" | custom-call | flops 3000000000 | tf_op jit(solution)/shard_map/pallas_call | solution.py:285
  106.2 5.9 %all-to-all-done.2.far = bf16[8,32,256]{2,1,0:T(8,128)(2,1)S(1)} async-done(((bf16[8,32,256]{2,1,0:T(8,128)(2,1)}), bf16[8,32,256]{2,1,0:T(8,128)(2,1)S(1)}, u32[]{:S(2)}, u32[]{:S(2)}) %all-to-all-start.2) | async-done | bytes 131104 | tf_op jit(solution)/shard_map/all_to_all | solution.py:542
  112.1 3.2 %shard_map.102 = (bf16[128,256]{1,0:T(8,128)(2,1)S(1)}, bf16[3,128,256]{2,1,0:T(8,128)(2,1)S(1)}, bf16[4,256,256]{2,1,0:T(8,128)(2,1)S(1)}) custom-call(s32[4]{0:T(128)S(1)} %pad_add_fusion.place.place_ref, bf16[4,128,256]{2,1,0:T(8,128)(2,1)S(1)} %get-tuple-element.22.proj_ref.proj, f32[3,3,256]{2,1,0:T(4,128)S(1)} %bitcast.16, f32[16,256]{1,0:T(8,128)S(1)} %bitcast.12, ...), custom_call_target="tpu_custom_call" | custom-call | flops 268435456 | tf_op jit(solution)/shard_map/pallas_call | solution.py:285
  115.3 5.6 %collective-permute-start.3 = (bf16[4,256,256]{2,1,0:T(8,128)(2,1)S(1)}, bf16[4,256,256]{2,1,0:T(8,128)(2,1)S(1)}, u32[]{:S(2)}, u32[]{:S(2)}) collective-permute-start(bf16[4,256,256]{2,1,0:T(8,128)(2,1)S(1)} %get-tuple-element.28), channel_id=1, source_target_pairs={{0,4},{4,8},{8,12},{12,0},{16,28},{20,16},{24,20},{28,24},{1,5},{5... | collective-permute-start | bytes 1572872 | tf_op jit(solution)/shard_map/ppermute | solution.py:469
  120.9 2.7 %shard_map.103 = bf16[4,256,256]{2,1,0:T(8,128)(2,1)S(1)} custom-call(s32[4]{0:T(128)S(1)} %pad_add_fusion.place.place_ref, bf16[128,256]{1,0:T(8,128)(2,1)S(1)} %get-tuple-element.26.hidden, bf16[3,128,256]{2,1,0:T(8,128)(2,1)S(1)} %get-tuple-element.27.grad, bf16[3,4096,256]{2,1,0:T(8,128)(2,1)} %bitcast.26, bf16[256,4096]{1,0:T(8,128)(2,1)} %weight_out.15), custom_call_target="tpu_custom_call" | custom-call | flops 268435456 | tf_op jit(solution)/shard_map/pallas_call | solution.py:285
  123.6 4.0 %collective-permute-done.3 = bf16[4,256,256]{2,1,0:T(8,128)(2,1)S(1)} collective-permute-done((bf16[4,256,256]{2,1,0:T(8,128)(2,1)S(1)}, bf16[4,256,256]{2,1,0:T(8,128)(2,1)S(1)}, u32[]{:S(2)}, u32[]{:S(2)}) %collective-permute-start.3) | collective-permute-done | bytes 524320 | tf_op jit(solution)/shard_map/ppermute | solution.py:469
  127.6 0.1 add_convert_fusion.2
  127.7 5.6 %collective-permute-start.4 = (bf16[4,256,256]{2,1,0:T(8,128)(2,1)S(1)}, bf16[4,256,256]{2,1,0:T(8,128)(2,1)S(1)}, u32[]{:S(2)}, u32[]{:S(2)}) collective-permute-start(bf16[4,256,256]{2,1,0:T(8,128)(2,1)S(1)} %add_convert_fusion.2), channel_id=1, source_target_pairs={{0,4},{4,8},{8,12},{12,0},{16,28},{20,16},{24,20},{28,24},{1,5},{5... | collective-permute-start | bytes 1572872 | tf_op jit(solution)/shard_map/ppermute | solution.py:469
  133.3 2.7 %shard_map.105 = bf16[4,256,256]{2,1,0:T(8,128)(2,1)S(1)} custom-call(s32[4]{0:T(128)S(1)} %pad_add_fusion.place.place_ref, bf16[128,256]{1,0:T(8,128)(2,1)S(1)} %get-tuple-element.26.hidden, bf16[3,128,256]{2,1,0:T(8,128)(2,1)S(1)} %get-tuple-element.27.grad, bf16[3,4096,256]{2,1,0:T(8,128)(2,1)} %bitcast.27, bf16[256,4096]{1,0:T(8,128)(2,1)} %weight_out.15), custom_call_target="tpu_custom_call" | custom-call | flops 268435456 | tf_op jit(solution)/shard_map/pallas_call | solution.py:285
  136.0 4.0 %collective-permute-done.4 = bf16[4,256,256]{2,1,0:T(8,128)(2,1)S(1)} collective-permute-done((bf16[4,256,256]{2,1,0:T(8,128)(2,1)S(1)}, bf16[4,256,256]{2,1,0:T(8,128)(2,1)S(1)}, u32[]{:S(2)}, u32[]{:S(2)}) %collective-permute-start.4) | collective-permute-done | bytes 524320 | tf_op jit(solution)/shard_map/ppermute | solution.py:469
  140.0 0.1 add_convert_fusion.1
  140.1 5.6 %collective-permute-start.5 = (bf16[4,256,256]{2,1,0:T(8,128)(2,1)S(1)}, bf16[4,256,256]{2,1,0:T(8,128)(2,1)S(1)}, u32[]{:S(2)}, u32[]{:S(2)}) collective-permute-start(bf16[4,256,256]{2,1,0:T(8,128)(2,1)S(1)} %add_convert_fusion.1), channel_id=1, source_target_pairs={{0,4},{4,8},{8,12},{12,0},{16,28},{20,16},{24,20},{28,24},{1,5},{5... | collective-permute-start | bytes 1572872 | tf_op jit(solution)/shard_map/ppermute | solution.py:469
  145.8 2.7 %shard_map.104 = bf16[4,256,256]{2,1,0:T(8,128)(2,1)S(1)} custom-call(s32[4]{0:T(128)S(1)} %pad_add_fusion.place.place_ref, bf16[128,256]{1,0:T(8,128)(2,1)S(1)} %get-tuple-element.26.hidden, bf16[3,128,256]{2,1,0:T(8,128)(2,1)S(1)} %get-tuple-element.27.grad, bf16[3,4096,256]{2,1,0:T(8,128)(2,1)} %bitcast.28, bf16[256,4096]{1,0:T(8,128)(2,1)} %weight_out.15), custom_call_target="tpu_custom_call" | custom-call | flops 268435456 | tf_op jit(solution)/shard_map/pallas_call | solution.py:285
  148.5 4.0 %collective-permute-done.5 = bf16[4,256,256]{2,1,0:T(8,128)(2,1)S(1)} collective-permute-done((bf16[4,256,256]{2,1,0:T(8,128)(2,1)S(1)}, bf16[4,256,256]{2,1,0:T(8,128)(2,1)S(1)}, u32[]{:S(2)}, u32[]{:S(2)}) %collective-permute-start.5) | collective-permute-done | bytes 524320 | tf_op jit(solution)/shard_map/ppermute | solution.py:469
  152.4 0.1 add_convert_fusion
  152.6 13.9 %all_to_all.22 = bf16[4,256,256]{2,1,0:T(8,128)(2,1)S(1)} all-to-all(bf16[4,256,256]{2,1,0:T(8,128)(2,1)S(1)} %add_convert_fusion), channel_id=1, replica_groups=mesh['y'=8,'zh'=4,'core'=2,'x'=4,'zl'=4] {'zl'}, dimensions={0} | all-to-all | bytes 1048576 | tf_op jit(solution)/shard_map/all_to_all | solution.py:582
  166.4 0.1 reduce_sum.12
  166.5 0.7 fusion
Async XLA Ops:
  23.5 12.8 %collective-permute-start = (bf16[4,256,256]{2,1,0:T(8,128)(2,1)S(1)}, bf16[4,256,256]{2,1,0:T(8,128)(2,1)S(1)}, u32[]{:S(2)}, u32[]{:S(2)}) collective-permute-start(bf16[4,256,256]{2,1,0:T(8,128)(2,1)S(1)} %all_to_all.20.pieces), channel_id=1, source_target_pairs={{0,4},{4,8},{8,12},{12,0},{16,28},{20,16},{24,20},{28,24},{1,5},{5... | collective-permute-start | bytes 1572872 | tf_op jit(solution)/shard_map/ppermute | solution.py:469
  36.3 12.3 %collective-permute-start.1 = (bf16[4,256,256]{2,1,0:T(8,128)(2,1)S(1)}, bf16[4,256,256]{2,1,0:T(8,128)(2,1)S(1)}, u32[]{:S(2)}, u32[]{:S(2)}) collective-permute-start(bf16[4,256,256]{2,1,0:T(8,128)(2,1)S(1)} %collective-permute-done.pieces), channel_id=1, source_target_pairs={{0,4},{4,8},{8,12},{12,0},{16,28},{20,16},{24,20},{28,24},{1,5},{5... | collective-permute-start | bytes 1572872 | tf_op jit(solution)/shard_map/ppermute | solution.py:469
  44.5 16.3 %copy-start = (f32[256,16]{0,1:T(8,128)S(1)}, f32[256,16]{0,1:T(8,128)}, u32[]{:S(2)}) copy-start(f32[256,16]{0,1:T(8,128)} %param.14) | copy-start | bytes 49156
  44.5 16.3 %copy-start.1 = (f32[3,256,3]{1,2,0:T(4,128)S(1)}, f32[3,256,3]{1,2,0:T(4,128)}, u32[]{:S(2)}) copy-start(f32[3,256,3]{1,2,0:T(4,128)} %param.12) | copy-start | bytes 27652
  48.6 12.3 %collective-permute-start.2 = (bf16[4,256,256]{2,1,0:T(8,128)(2,1)S(1)}, bf16[4,256,256]{2,1,0:T(8,128)(2,1)S(1)}, u32[]{:S(2)}, u32[]{:S(2)}) collective-permute-start(bf16[4,256,256]{2,1,0:T(8,128)(2,1)S(1)} %collective-permute-done.1.pieces), channel_id=1, source_target_pairs={{0,4},{4,8},{8,12},{12,0},{16,28},{20,16},{24,20},{28,24},{1,5},{5... | collective-permute-start | bytes 1572872 | tf_op jit(solution)/shard_map/ppermute | solution.py:469
  56.8 46.3 %copy-start.2 = (f32[256,16]{0,1:T(8,128)S(1)}, f32[256,16]{0,1:T(8,128)}, u32[]{:S(2)}) copy-start(f32[256,16]{0,1:T(8,128)} %param.13) | copy-start | bytes 49156
  56.8 46.3 %copy-start.3 = (f32[256]{0:T(256)S(1)}, f32[256]{0:T(256)}, u32[]{:S(2)}) copy-start(f32[256]{0:T(256)} %param.15) | copy-start | bytes 3076
  95.9 16.2 %all-to-all-start.2 = ((bf16[8,32,256]{2,1,0:T(8,128)(2,1)}), bf16[8,32,256]{2,1,0:T(8,128)(2,1)S(1)}, u32[]{:S(2)}, u32[]{:S(2)}) async-start(bf16[8,32,256]{2,1,0:T(8,128)(2,1)} %shard_map.101), calls=%async_computation.2 | async-start | bytes 262144 | tf_op jit(solution)/shard_map/all_to_all | solution.py:542
  115.3 12.3 %collective-permute-start.3 = (bf16[4,256,256]{2,1,0:T(8,128)(2,1)S(1)}, bf16[4,256,256]{2,1,0:T(8,128)(2,1)S(1)}, u32[]{:S(2)}, u32[]{:S(2)}) collective-permute-start(bf16[4,256,256]{2,1,0:T(8,128)(2,1)S(1)} %get-tuple-element.28), channel_id=1, source_target_pairs={{0,4},{4,8},{8,12},{12,0},{16,28},{20,16},{24,20},{28,24},{1,5},{5... | collective-permute-start | bytes 1572872 | tf_op jit(solution)/shard_map/ppermute | solution.py:469
  127.7 12.3 %collective-permute-start.4 = (bf16[4,256,256]{2,1,0:T(8,128)(2,1)S(1)}, bf16[4,256,256]{2,1,0:T(8,128)(2,1)S(1)}, u32[]{:S(2)}, u32[]{:S(2)}) collective-permute-start(bf16[4,256,256]{2,1,0:T(8,128)(2,1)S(1)} %add_convert_fusion.2), channel_id=1, source_target_pairs={{0,4},{4,8},{8,12},{12,0},{16,28},{20,16},{24,20},{28,24},{1,5},{5... | collective-permute-start | bytes 1572872 | tf_op jit(solution)/shard_map/ppermute | solution.py:469
  140.1 12.3 %collective-permute-start.5 = (bf16[4,256,256]{2,1,0:T(8,128)(2,1)S(1)}, bf16[4,256,256]{2,1,0:T(8,128)(2,1)S(1)}, u32[]{:S(2)}, u32[]{:S(2)}) collective-permute-start(bf16[4,256,256]{2,1,0:T(8,128)(2,1)S(1)} %add_convert_fusion.1), channel_id=1, source_target_pairs={{0,4},{4,8},{8,12},{12,0},{16,28},{20,16},{24,20},{28,24},{1,5},{5... | collective-permute-start | bytes 1572872 | tf_op jit(solution)/shard_map/ppermute | solution.py:469

commit v10 on v8

--- a/solution.py
+++ b/solution.py
@@ -62,10 +62,17 @@
     order = rates_ref.shape[0]
     block = proj_ref.shape[1]
     gated, grad_conv, time = inner_rows(ext, proj_ref, taps_ref, block + TILE)
+    time = time[:TILE]
     for r in range(order):
         rate = rates_ref[r : r + 1, :]
-        fwd = jnp.exp(-rate * (block - 1.0 - time)) * gated
-        bwd = jnp.exp(-rate * (time - AHEAD)) * grad_conv
+        fade = jnp.exp(-rate * TILE)
+        fwd = gated[:TILE]
+        bwd = grad_conv[block - TILE : block]
+        for q in range(TILE, block, TILE):
+            fwd = fwd * fade + gated[q : q + TILE]
+            bwd = bwd * fade + grad_conv[block - TILE - q : block - q]
+        fwd = jnp.exp(-rate * (TILE - 1.0 - time)) * fwd
+        bwd = jnp.exp(-rate * (time - AHEAD)) * bwd
         pack[r : r + 1] = jnp.sum(fwd, axis=0, keepdims=True)
         pack[order + r : order + r + 1] = jnp.sum(bwd, axis=0, keepdims=True)
     at = 2 * order
@@ -125,8 +132,11 @@
     fade = fader(rates, block)
     fwd, bwd, firsts, lasts, _, _ = group_states(block, taps_ref, rates, got_ref)
     members = len(fwd)
-    total_fwd = sum(fade(members - 1 - j) * fwd[j] for j in range(members))
-    total_bwd = sum(fade(j) * bwd[j] for j in range(members))
+    step = fade(1)
+    total_fwd, total_bwd = fwd[0], bwd[-1]
+    for j in range(1, members):
+        total_fwd = total_fwd * step + fwd[j]
+        total_bwd = total_bwd * step + bwd[members - 1 - j]
     ends = jnp.concatenate([firsts[0], lasts[-1]], axis=0).astype(BF16)
     for i in range(send_ref.shape[0]):
         send_ref[i, :order] = jnp.where(place_ref[0] < i, total_fwd, total_bwd).astype(BF16)
@@ -193,24 +203,25 @@
     tail = [nothing] + [w[order + TILE :] for w in whole]
     ahead = jnp.zeros_like(rates)
     behind = jnp.zeros_like(rates)
+    step, stride, most = fade(1), fade(members), fade(members - 1)
     for i in range(groups):
         gated, _ = joint(taps_ref, head[i], tail[i])
-        total = whole[i][:order] + fade(members - 1) * (far * gated[0] + near * gated[1])
-        ahead = ahead + jnp.where(i < group, fade(members * (group - 1 - i)) * total, 0.0)
-        _, grad_conv = joint(taps_ref, head[i + 1], tail[i + 1])
-        total = whole[i][:order] + fade(members - 1) * (near * grad_conv[0] + far * grad_conv[1])
-        behind = behind + jnp.where(i > group, fade(members * (i - 1 - group)) * total, 0.0)
+        total = whole[i][:order] + most * (far * gated[0] + near * gated[1])
+        ahead = jnp.where(i < group, ahead * stride + total, ahead)
+        j = groups - 1 - i
+        _, grad_conv = joint(taps_ref, head[j + 1], tail[j + 1])
+        total = whole[j][:order] + most * (near * grad_conv[0] + far * grad_conv[1])
+        behind = jnp.where(j > group, behind * stride + total, behind)
     tail_before = rows_of(far_ref, group - 1, order + TILE, group > 0)
     head_behind = rows_of(far_ref, group + 1, order, group < groups - 1)
     gated, _ = joint(taps_ref, firsts[0], tail_before)
     _, grad_conv = joint(taps_ref, head_behind, lasts[-1])
     fwd[0] = fwd[0] + far * gated[0] + near * gated[1]
     bwd[-1] = bwd[-1] + near * grad_conv[0] + far * grad_conv[1]
-    ahead = fade(member) * ahead
-    behind = fade(members - 1 - member) * behind
     for j in range(members):
-        ahead = ahead + jnp.where(j < member, fade(member - 1 - j) * fwd[j], 0.0)
-        behind = behind + jnp.where(j > member, fade(j - 1 - member) * bwd[j], 0.0)
+        ahead = jnp.where(j < member, ahead * step + fwd[j], ahead)
+        i = members - 1 - j
+        behind = jnp.where(i > member, behind * step + bwd[i], behind)
 
     last = rows_of(near_ref, member - 1, 2 * order + TILE, member > 0)
     last = jnp.where(member > 0, last, tail_before)
@@ -250,14 +261,30 @@
         two(lag0 * h[0] + lag1 * h[1], lag0 * h[1]),
         two(skip * h[2], skip * h[3] - less * h[2]),
     )
-    time = lax.broadcasted_iota(jnp.int32, (rows, 1), 0).astype(F32)
+    time = row.astype(F32)
     ahead = res_all * ahead
     behind = res_all * behind
-    for r in range(order):
-        rate = rates[r : r + 1]
-        conv_out = conv_out + ahead[r : r + 1] * jnp.exp(-rate * (time + 1.0))
-        past = jnp.exp(-rate * (block + AHEAD - time))
-        grad_gated = grad_gated + behind[r : r + 1] * past
+    conv_tiles = [[] for _ in range(0, rows, TILE)]
+    grad_tiles = [[] for _ in range(0, rows, TILE)]
+    for lane in range(0, width, 128):
+        lanes = slice(lane, lane + 128)
+        conv_sum = [conv_out[q : q + TILE, lanes] for q in range(0, rows, TILE)]
+        grad_sum = [grad_gated[q : q + TILE, lanes] for q in range(0, rows, TILE)]
+        for r in range(order):
+            rate = rates[r : r + 1, lanes]
+            fall = jnp.exp(-rate * TILE)
+            later = ahead[r : r + 1, lanes] * jnp.exp(-rate * (time + 1.0))
+            sooner = behind[r : r + 1, lanes] * jnp.exp(-rate * (AHEAD - time))
+            for q in range(len(conv_sum)):
+                conv_sum[q] = conv_sum[q] + later
+                grad_sum[-1 - q] = grad_sum[-1 - q] + sooner
+                later = later * fall
+                sooner = sooner * fall
+        for q in range(len(conv_sum)):
+            conv_tiles[q].append(conv_sum[q])
+            grad_tiles[q].append(grad_sum[q])
+    conv_out = jnp.concatenate([jnp.concatenate(t, axis=1) for t in conv_tiles], axis=0)
+    grad_gated = jnp.concatenate([jnp.concatenate(t, axis=1) for t in grad_tiles], axis=0)
     hidden_ref[...] = (query * conv_out)[:block].astype(BF16)
     feat[0] = back * conv_out
     feat[1] = grad_gated * value_part
@@ -500,7 +527,8 @@
         flops=products(n_zl),
         hbm=2,
     )
-    from_left, from_right, total = lax.optimization_barrier((from_left, from_right, total))
+    from_left, _ = lax.optimization_barrier((from_left, total))
+    from_right, _ = lax.optimization_barrier((from_right, total))
     far_left = lax.ppermute(from_left[:half], "x", right)
     far_right = lax.ppermute(from_right[half:], "x", left)
     total = call(

time: 157 us -> 151 us (0.962)
  waiting for transfers between devices: 19.4 us -> 14.7 us
    ppermute x1, waiting for transfers between devices: 3.5 us -> 0.01 us  [shards(): far_right = lax.ppermute(from_right[half:], 'x', left)]
  transfers between devices with their start and end apart: 9 -> 9, of which waited for: 6 -> 4; matrix products, arithmetic and copies ran while one was open for 0% -> 0% of each run, Pallas kernels for 11% -> 11%
where the time goes in v10:
time: 151 us; the launch traced here: 148 us
  blocking collectives  69.8 us (46%)
  starting transfers between devices  36.6 us (24%)
  Pallas kernels  25 us (17%)
  waiting for transfers between devices  14.7 us (10%)
    all_to_all x1, blocking collectives, shards(): near_states = lax.all_to_all(send, ('zh', 'core'), 0, 0, tiled=True)  34.2 us
    pallas_call x11, Pallas kernels, call(): pl.pallas_call(kernel, out_shape=outs, scratch_shapes=scratch, in_specs=s...  25 us
    all_to_all x1, blocking collectives, shards(): pieces = lax.all_to_all(copies, 'zl', 0, 0, tiled=True)  21.5 us
    all_to_all x1, blocking collectives, shards(): summed = lax.all_to_all(summed, 'zl', 0, 0, tiled=True)  14 us
    all_to_all x1, starting transfers between devices, shards(): far_states = lax.all_to_all(send, 'y', 0, 0, tiled=True)  7.1 us
    all_to_all x1, waiting for transfers between devices, shards(): far_states = lax.all_to_all(send, 'y', 0, 0, tiled=True)  5.87 us
    ppermute x1, starting transfers between devices, shards(): far_right = lax.ppermute(to_right, 'x', right)  5.39 us
    ppermute x1, starting transfers between devices, shards(): from_left = lax.ppermute(pieces, 'x', right)  5.36 us
  transfers between devices with their start and end apart: 9, of which 4 were waited for; matrix products, arithmetic and copies ran while one was open for 0% of the time, Pallas kernels for 11%

profile of v10, /device:TPU:6, one launch (start us, length us, event | category | flops | bytes accessed | tf_op | source)
XLA Modules:
  0.0 148.0 jit_solution(16424044129150200846)
XLA Ops:
  0.6 1.3 shard_map.95
  1.9 21.5 %all_to_all.20.piece = bf16[4,256,256]{2,1,0:T(8,128)(2,1)S(1)} all-to-all(bf16[4,256,256]{2,1,0:T(8,128)(2,1)S(1)} %shard_map.95), channel_id=1, replica_groups=mesh['y'=8,'zh'=4,'core'=2,'x'=4,'zl'=4] {'zl'}, dimensions={0} | all-to-all | bytes 1048576 | tf_op jit(solution)/shard_map/all_to_all | solution.py:509
  23.5 2.7 %collective-permute-start.2 = (bf16[4,256,256]{2,1,0:T(8,128)(2,1)S(1)}, bf16[4,256,256]{2,1,0:T(8,128)(2,1)S(1)}, u32[]{:S(2)}, u32[]{:S(2)}) collective-permute-start(bf16[4,256,256]{2,1,0:T(8,128)(2,1)S(1)} %all_to_all.20.piece), channel_id=1, source_target_pairs={{0,12},{4,0},{8,4},{12,8},{1,13},{5,1},{9,5},{13,9},{2,14},{6,2},{... | collective-permute-start | bytes 1572872 | tf_op jit(solution)/shard_map/ppermute | solution.py:518
  26.2 5.4 %collective-permute-start = (bf16[4,256,256]{2,1,0:T(8,128)(2,1)S(1)}, bf16[4,256,256]{2,1,0:T(8,128)(2,1)S(1)}, u32[]{:S(2)}, u32[]{:S(2)}) collective-permute-start(bf16[4,256,256]{2,1,0:T(8,128)(2,1)S(1)} %all_to_all.20.piece), channel_id=1, source_target_pairs={{0,4},{4,8},{8,12},{12,0},{1,5},{5,9},{9,13},{13,1},{2,6},{6,10},{... | collective-permute-start | bytes 1572872 | tf_op jit(solution)/shard_map/ppermute | solution.py:517
  31.6 0.1 pad_add_fusion.place.place_ref
  31.6 2.6 %shard_map.96.old = f32[4,128,256]{2,1,0:T(8,128)S(1)} custom-call(s32[3]{0:T(128)S(1)} %pad_add_fusion.place.place_ref, bf16[4,256,256]{2,1,0:T(8,128)(2,1)S(1)} %all_to_all.20.piece, bf16[3,4096,256]{2,1,0:T(8,128)(2,1)} %bitcast.20, bf16[256,4096]{1,0:T(8,128)(2,1)} %weight_out.11), custom_call_target="tpu_custom_call" | custom-call | flops 268435456 | tf_op jit(solution)/shard_map/pallas_call | solution.py:312
  34.2 0.0 copy-start
  34.2 0.0 copy-start.1
  34.2 4.8 %collective-permute-done.2.right = bf16[4,256,256]{2,1,0:T(8,128)(2,1)S(1)} collective-permute-done((bf16[4,256,256]{2,1,0:T(8,128)(2,1)S(1)}, bf16[4,256,256]{2,1,0:T(8,128)(2,1)S(1)}, u32[]{:S(2)}, u32[]{:S(2)}) %collective-permute-start.2) | collective-permute-done | bytes 524320 | tf_op jit(solution)/shard_map/ppermute | solution.py:518
  39.1 1.9 %collective-permute-start.3 = (bf16[2,256,256]{2,1,0:T(8,128)(2,1)S(1)}, bf16[2,256,256]{2,1,0:T(8,128)(2,1)S(1)}, u32[]{:S(2)}, u32[]{:S(2)}) collective-permute-start(bf16[2,256,256]{2,1,0:T(8,128)(2,1)S(1)} %slice.13), channel_id=1, source_target_pairs={{0,12},{4,0},{8,4},{12,8},{1,13},{5,1},{9,5},{13,9},{2,14},{6,2},{... | collective-permute-start | bytes 786440 | tf_op jit(solution)/shard_map/ppermute | solution.py:533
  41.0 0.0 collective-permute-done.left
  41.1 5.1 %collective-permute-start.1 = (bf16[2,256,256]{2,1,0:T(8,128)(2,1)S(1)}, bf16[2,256,256]{2,1,0:T(8,128)(2,1)S(1)}, u32[]{:S(2)}, u32[]{:S(2)}) collective-permute-start(bf16[2,256,256]{2,1,0:T(8,128)(2,1)S(1)} %slice.12), channel_id=1, source_target_pairs={{0,4},{4,8},{8,12},{12,0},{1,5},{5,9},{9,13},{13,1},{2,6},{6,10},{... | collective-permute-start | bytes 786440 | tf_op jit(solution)/shard_map/ppermute | solution.py:532
  46.2 4.0 %shard_map.97.old = f32[4,128,256]{2,1,0:T(8,128)S(1)} custom-call(s32[3]{0:T(128)S(1)} %pad_add_fusion.place.place_ref, bf16[4,256,256]{2,1,0:T(8,128)(2,1)S(1)} %collective-permute-done.left, bf16[4,256,256]{2,1,0:T(8,128)(2,1)S(1)} %collective-permute-done.2.right, f32[4,128,256]{2,1,0:T(8,128)S(1)} %shard_map.96.old, bf16[3,4096,256]{2,1,0:T(8,128)(2,1)} %bitcast.21, ...), custom_call_target="tpu_custom_call" | custom-call | flops 536870912 | tf_op jit(solution)/shard_map/pallas_call | solution.py:312
  50.2 0.0 copy-start.2
  50.2 0.0 copy-start.3
  50.3 0.0 collective-permute-done.3.right
  50.3 0.0 collective-permute-done.1.left
  50.3 0.0 copy-done
  50.3 0.0 copy-done.1
  50.3 3.0 %shard_map.98 = (bf16[4,128,256]{2,1,0:T(8,128)(2,1)S(1)}, bf16[8,48,256]{2,1,0:T(8,128)(2,1)S(1)}) custom-call(s32[3]{0:T(128)S(1)} %pad_add_fusion.place.place_ref, bf16[2,256,256]{2,1,0:T(8,128)(2,1)S(1)} %collective-permute-done.1.left, bf16[2,256,256]{2,1,0:T(8,128)(2,1)S(1)} %collective-permute-done.3.right, f32[4,128,256]{2,1,0:T(8,128)S(1)} %shard_map.97.old, ...), custom_call_target="tpu_custom_call" | custom-call | flops 268435456 | tf_op jit(solution)/shard_map/pallas_call | solution.py:312
  53.3 34.2 %all_to_all.21.got_ref.near = bf16[8,48,256]{2,1,0:T(8,128)(2,1)S(1)} all-to-all(bf16[8,48,256]{2,1,0:T(8,128)(2,1)S(1)} %get-tuple-element.19), channel_id=1, replica_groups=mesh['y'=8,'zh'=4,'core'=2,'x'=4,'zl'=4] {'zh','core'}, dimensions={0} | all-to-all | bytes 393216 | tf_op jit(solution)/shard_map/all_to_all | solution.py:575
  87.5 1.3 shard_map.100
  88.9 7.1 %all-to-all-start.2 = ((bf16[8,32,256]{2,1,0:T(8,128)(2,1)}), bf16[8,32,256]{2,1,0:T(8,128)(2,1)S(1)}, u32[]{:S(2)}, u32[]{:S(2)}) async-start(bf16[8,32,256]{2,1,0:T(8,128)(2,1)} %shard_map.100), calls=%async_computation.2 | async-start | bytes 262144 | tf_op jit(solution)/shard_map/all_to_all | solution.py:585
  96.0 0.0 copy-done.2
  96.0 0.0 copy-done.3
  96.0 3.2 %shard_map.99 = (f32[136,256]{1,0:T(8,128)S(1)}, f32[136,256]{1,0:T(8,128)S(1)}) custom-call(bf16[4,128,256]{2,1,0:T(8,128)(2,1)S(1)} %get-tuple-element.16.proj_ref.proj, f32[3,3,256]{2,1,0:T(4,128)S(1)} %bitcast.14, f32[16,256]{1,0:T(8,128)S(1)} %bitcast.10, f32[16,256]{1,0:T(8,128)S(1)} %bitcast.16, f32[1,256]{1,0:T(1,128)S(1)} %bitcast.18), custom_call_target="tpu_custom_call" | custom-call | flops 3000000000 | tf_op jit(solution)/shard_map/pallas_call | solution.py:312
  99.2 5.9 %all-to-all-done.2.far = bf16[8,32,256]{2,1,0:T(8,128)(2,1)S(1)} async-done(((bf16[8,32,256]{2,1,0:T(8,128)(2,1)}), bf16[8,32,256]{2,1,0:T(8,128)(2,1)S(1)}, u32[]{:S(2)}, u32[]{:S(2)}) %all-to-all-start.2) | async-done | bytes 131104 | tf_op jit(solution)/shard_map/all_to_all | solution.py:585
  105.0 2.7 %shard_map.101 = (bf16[128,256]{1,0:T(8,128)(2,1)S(1)}, bf16[3,128,256]{2,1,0:T(8,128)(2,1)S(1)}, bf16[2,256,256]{2,1,0:T(8,128)(2,1)S(1)}, bf16[2,256,256]{2,1,0:T(8,128)(2,1)S(1)}) custom-call(s32[3]{0:T(128)S(1)} %pad_add_fusion.place.place_ref, bf16[4,128,256]{2,1,0:T(8,128)(2,1)S(1)} %get-tuple-element.16.proj_ref.proj, f32[3,3,256]{2,1,0:T(4,128)S(1)} %bitcast.15, ...), custom_call_target="tpu_custom_call" | custom-call | flops 268435456 | tf_op jit(solution)/shard_map/pallas_call | solution.py:312
  107.7 1.9 %collective-permute-start.6 = (bf16[2,256,256]{2,1,0:T(8,128)(2,1)S(1)}, bf16[2,256,256]{2,1,0:T(8,128)(2,1)S(1)}, u32[]{:S(2)}, u32[]{:S(2)}) collective-permute-start(bf16[2,256,256]{2,1,0:T(8,128)(2,1)S(1)} %get-tuple-element.25), channel_id=1, source_target_pairs={{0,12},{4,0},{8,4},{12,8},{1,13},{5,1},{9,5},{13,9},{2,14},{6,2},{... | collective-permute-start | bytes 786440 | tf_op jit(solution)/shard_map/ppermute | solution.py:612
  109.7 5.4 %collective-permute-start.4 = (bf16[2,256,256]{2,1,0:T(8,128)(2,1)S(1)}, bf16[2,256,256]{2,1,0:T(8,128)(2,1)S(1)}, u32[]{:S(2)}, u32[]{:S(2)}) collective-permute-start(bf16[2,256,256]{2,1,0:T(8,128)(2,1)S(1)} %get-tuple-element.23), channel_id=1, source_target_pairs={{0,4},{4,8},{8,12},{12,0},{1,5},{5,9},{9,13},{13,1},{2,6},{6,10},{... | collective-permute-start | bytes 786440 | tf_op jit(solution)/shard_map/ppermute | solution.py:611
  115.1 4.0 %shard_map.103 = (bf16[4,256,256]{2,1,0:T(8,128)(2,1)S(1)}, bf16[4,256,256]{2,1,0:T(8,128)(2,1)S(1)}) custom-call(s32[3]{0:T(128)S(1)} %pad_add_fusion.place.place_ref, bf16[128,256]{1,0:T(8,128)(2,1)S(1)} %get-tuple-element.20.hidden, bf16[3,128,256]{2,1,0:T(8,128)(2,1)S(1)} %get-tuple-element.21.grad, bf16[3,4096,256]{2,1,0:T(8,128)(2,1)} %bitcast.24, ...), custom_call_target="tpu_custom_call" | custom-call | flops 536870912 | tf_op jit(solution)/shard_map/pallas_call | solution.py:312
  119.1 0.0 collective-permute-done.6.got
  119.1 0.1 shard_map.105
  119.2 1.9 %collective-permute-start.7 = (bf16[4,256,256]{2,1,0:T(8,128)(2,1)S(1)}, bf16[4,256,256]{2,1,0:T(8,128)(2,1)S(1)}, u32[]{:S(2)}, u32[]{:S(2)}) collective-permute-start(bf16[4,256,256]{2,1,0:T(8,128)(2,1)S(1)} %shard_map.105), channel_id=1, source_target_pairs={{0,12},{4,0},{8,4},{12,8},{1,13},{5,1},{9,5},{13,9},{2,14},{6,2},{... | collective-permute-start | bytes 1572872 | tf_op jit(solution)/shard_map/ppermute | solution.py:627
  121.1 0.0 collective-permute-done.4.got
  121.2 0.1 shard_map.104
  121.2 5.1 %collective-permute-start.5 = (bf16[4,256,256]{2,1,0:T(8,128)(2,1)S(1)}, bf16[4,256,256]{2,1,0:T(8,128)(2,1)S(1)}, u32[]{:S(2)}, u32[]{:S(2)}) collective-permute-start(bf16[4,256,256]{2,1,0:T(8,128)(2,1)S(1)} %shard_map.104), channel_id=1, source_target_pairs={{0,4},{4,8},{8,12},{12,0},{1,5},{5,9},{9,13},{13,1},{2,6},{6,10},{... | collective-permute-start | bytes 1572872 | tf_op jit(solution)/shard_map/ppermute | solution.py:625
  126.4 2.7 %shard_map.102 = bf16[4,256,256]{2,1,0:T(8,128)(2,1)S(1)} custom-call(s32[3]{0:T(128)S(1)} %pad_add_fusion.place.place_ref, bf16[128,256]{1,0:T(8,128)(2,1)S(1)} %get-tuple-element.20.hidden, bf16[3,128,256]{2,1,0:T(8,128)(2,1)S(1)} %get-tuple-element.21.grad, bf16[3,4096,256]{2,1,0:T(8,128)(2,1)} %bitcast.25, bf16[256,4096]{1,0:T(8,128)(2,1)} %weight_out.11), custom_call_target="tpu_custom_call" | custom-call | flops 268435456 | tf_op jit(solution)/shard_map/pallas_call | solution.py:312
  129.1 2.4 %collective-permute-done.7 = bf16[4,256,256]{2,1,0:T(8,128)(2,1)S(1)} collective-permute-done((bf16[4,256,256]{2,1,0:T(8,128)(2,1)S(1)}, bf16[4,256,256]{2,1,0:T(8,128)(2,1)S(1)}, u32[]{:S(2)}, u32[]{:S(2)}) %collective-permute-start.7) | collective-permute-done | bytes 524320 | tf_op jit(solution)/shard_map/ppermute | solution.py:627
  131.5 1.5 %collective-permute-done.5 = bf16[4,256,256]{2,1,0:T(8,128)(2,1)S(1)} collective-permute-done((bf16[4,256,256]{2,1,0:T(8,128)(2,1)S(1)}, bf16[4,256,256]{2,1,0:T(8,128)(2,1)S(1)}, u32[]{:S(2)}, u32[]{:S(2)}) %collective-permute-start.5) | collective-permute-done | bytes 524320 | tf_op jit(solution)/shard_map/ppermute | solution.py:625
  133.1 0.2 add_convert_fusion
  133.3 14.0 %all_to_all.22 = bf16[4,256,256]{2,1,0:T(8,128)(2,1)S(1)} all-to-all(bf16[4,256,256]{2,1,0:T(8,128)(2,1)S(1)} %add_convert_fusion), channel_id=1, replica_groups=mesh['y'=8,'zh'=4,'core'=2,'x'=4,'zl'=4] {'zl'}, dimensions={0} | all-to-all | bytes 1048576 | tf_op jit(solution)/shard_map/all_to_all | solution.py:640
  147.3 0.1 reduce_sum.12
  147.4 0.7 fusion
  (2 shorter events, 0.0 us)
Async XLA Ops:
  23.5 15.6 %collective-permute-start.2 = (bf16[4,256,256]{2,1,0:T(8,128)(2,1)S(1)}, bf16[4,256,256]{2,1,0:T(8,128)(2,1)S(1)}, u32[]{:S(2)}, u32[]{:S(2)}) collective-permute-start(bf16[4,256,256]{2,1,0:T(8,128)(2,1)S(1)} %all_to_all.20.piece), channel_id=1, source_target_pairs={{0,12},{4,0},{8,4},{12,8},{1,13},{5,1},{9,5},{13,9},{2,14},{6,2},{... | collective-permute-start | bytes 1572872 | tf_op jit(solution)/shard_map/ppermute | solution.py:518
  26.2 14.8 %collective-permute-start = (bf16[4,256,256]{2,1,0:T(8,128)(2,1)S(1)}, bf16[4,256,256]{2,1,0:T(8,128)(2,1)S(1)}, u32[]{:S(2)}, u32[]{:S(2)}) collective-permute-start(bf16[4,256,256]{2,1,0:T(8,128)(2,1)S(1)} %all_to_all.20.piece), channel_id=1, source_target_pairs={{0,4},{4,8},{8,12},{12,0},{1,5},{5,9},{9,13},{13,1},{2,6},{6,10},{... | collective-permute-start | bytes 1572872 | tf_op jit(solution)/shard_map/ppermute | solution.py:517
  34.2 16.1 %copy-start = (f32[256,16]{0,1:T(8,128)S(1)}, f32[256,16]{0,1:T(8,128)}, u32[]{:S(2)}) copy-start(f32[256,16]{0,1:T(8,128)} %param.14) | copy-start | bytes 49156
  34.2 16.1 %copy-start.1 = (f32[3,256,3]{1,2,0:T(4,128)S(1)}, f32[3,256,3]{1,2,0:T(4,128)}, u32[]{:S(2)}) copy-start(f32[3,256,3]{1,2,0:T(4,128)} %param.12) | copy-start | bytes 27652
  39.1 11.2 %collective-permute-start.3 = (bf16[2,256,256]{2,1,0:T(8,128)(2,1)S(1)}, bf16[2,256,256]{2,1,0:T(8,128)(2,1)S(1)}, u32[]{:S(2)}, u32[]{:S(2)}) collective-permute-start(bf16[2,256,256]{2,1,0:T(8,128)(2,1)S(1)} %slice.13), channel_id=1, source_target_pairs={{0,12},{4,0},{8,4},{12,8},{1,13},{5,1},{9,5},{13,9},{2,14},{6,2},{... | collective-permute-start | bytes 786440 | tf_op jit(solution)/shard_map/ppermute | solution.py:533
  41.1 9.2 %collective-permute-start.1 = (bf16[2,256,256]{2,1,0:T(8,128)(2,1)S(1)}, bf16[2,256,256]{2,1,0:T(8,128)(2,1)S(1)}, u32[]{:S(2)}, u32[]{:S(2)}) collective-permute-start(bf16[2,256,256]{2,1,0:T(8,128)(2,1)S(1)} %slice.12), channel_id=1, source_target_pairs={{0,4},{4,8},{8,12},{12,0},{1,5},{5,9},{9,13},{13,1},{2,6},{6,10},{... | collective-permute-start | bytes 786440 | tf_op jit(solution)/shard_map/ppermute | solution.py:532
  50.2 45.7 %copy-start.2 = (f32[256,16]{0,1:T(8,128)S(1)}, f32[256,16]{0,1:T(8,128)}, u32[]{:S(2)}) copy-start(f32[256,16]{0,1:T(8,128)} %param.13) | copy-start | bytes 49156
  50.2 45.7 %copy-start.3 = (f32[256]{0:T(256)S(1)}, f32[256]{0:T(256)}, u32[]{:S(2)}) copy-start(f32[256]{0:T(256)} %param.15) | copy-start | bytes 3076
  88.9 16.2 %all-to-all-start.2 = ((bf16[8,32,256]{2,1,0:T(8,128)(2,1)}), bf16[8,32,256]{2,1,0:T(8,128)(2,1)S(1)}, u32[]{:S(2)}, u32[]{:S(2)}) async-start(bf16[8,32,256]{2,1,0:T(8,128)(2,1)} %shard_map.100), calls=%async_computation.2 | async-start | bytes 262144 | tf_op jit(solution)/shard_map/all_to_all | solution.py:585
  107.7 11.4 %collective-permute-start.6 = (bf16[2,256,256]{2,1,0:T(8,128)(2,1)S(1)}, bf16[2,256,256]{2,1,0:T(8,128)(2,1)S(1)}, u32[]{:S(2)}, u32[]{:S(2)}) collective-permute-start(bf16[2,256,256]{2,1,0:T(8,128)(2,1)S(1)} %get-tuple-element.25), channel_id=1, source_target_pairs={{0,12},{4,0},{8,4},{12,8},{1,13},{5,1},{9,5},{13,9},{2,14},{6,2},{... | collective-permute-start | bytes 786440 | tf_op jit(solution)/shard_map/ppermute | solution.py:612
  109.7 11.5 %collective-permute-start.4 = (bf16[2,256,256]{2,1,0:T(8,128)(2,1)S(1)}, bf16[2,256,256]{2,1,0:T(8,128)(2,1)S(1)}, u32[]{:S(2)}, u32[]{:S(2)}) collective-permute-start(bf16[2,256,256]{2,1,0:T(8,128)(2,1)S(1)} %get-tuple-element.23), channel_id=1, source_target_pairs={{0,4},{4,8},{8,12},{12,0},{1,5},{5,9},{9,13},{13,1},{2,6},{6,10},{... | collective-permute-start | bytes 786440 | tf_op jit(solution)/shard_map/ppermute | solution.py:611
  119.2 12.3 %collective-permute-start.7 = (bf16[4,256,256]{2,1,0:T(8,128)(2,1)S(1)}, bf16[4,256,256]{2,1,0:T(8,128)(2,1)S(1)}, u32[]{:S(2)}, u32[]{:S(2)}) collective-permute-start(bf16[4,256,256]{2,1,0:T(8,128)(2,1)S(1)} %shard_map.105), channel_id=1, source_target_pairs={{0,12},{4,0},{8,4},{12,8},{1,13},{5,1},{9,5},{13,9},{2,14},{6,2},{... | collective-permute-start | bytes 1572872 | tf_op jit(solution)/shard_map/ppermute | solution.py:627
  121.2 11.8 %collective-permute-start.5 = (bf16[4,256,256]{2,1,0:T(8,128)(2,1)S(1)}, bf16[4,256,256]{2,1,0:T(8,128)(2,1)S(1)}, u32[]{:S(2)}, u32[]{:S(2)}) collective-permute-start(bf16[4,256,256]{2,1,0:T(8,128)(2,1)S(1)} %shard_map.104), channel_id=1, source_target_pairs={{0,4},{4,8},{8,12},{12,0},{1,5},{5,9},{9,13},{13,1},{2,6},{6,10},{... | collective-permute-start | bytes 1572872 | tf_op jit(solution)/shard_map/ppermute | solution.py:625

commit v11 on v10

--- a/solution.py
+++ b/solution.py
@@ -356,6 +356,10 @@
     return ready
 
 
+def at_once(s):
+    pass
+
+
 def held_weights(count, part, width):
     return [
         pltpu.VMEM((count, PAIR * part, 3 * width), BF16),
@@ -364,7 +368,9 @@
     ]
 
 
-def project(sizes, offsets, place_ref, pieces, weights, old, total, held_in, held_out, sems):
+def project(
+    sizes, offsets, place_ref, pieces, weights, old, total, held_in, held_out, sems=None, also=None
+):
     n_x, n_zl = sizes["x"], sizes["zl"]
     block = pieces[0].shape[1] // 2
     width = total.shape[2]
@@ -373,7 +379,11 @@
         for piece, (k, start) in zip(pieces, offsets)
         for j in range(0, piece.shape[0], PAIR)
     ]
-    ready = load_weights([w[2] for w in work], *weights, held_in, held_out, sems)
+    ready = at_once
+    if sems is not None:
+        ready = load_weights([w[2] for w in work], *weights, held_in, held_out, sems)
+    if also is not None:
+        also()
     for s, (piece, j, _) in enumerate(work):
         run = range(j, j + PAIR)
         part_in = jnp.concatenate([piece[i, :block] for i in run], axis=1)
@@ -395,18 +405,28 @@
     project(sizes, [(0, 0)], place, [piece], (weight_in, weight_out), None, total, *held)
 
 
-def side_kernel(sizes, place, left, right, old, weight_in, weight_out, total, *held):
-    offsets = [(sizes["x"] - 1, 0), (1, 0)]
+def side_kernel(
+    sizes, place, left, right, old, weight_in, weight_out, total, far_in, far_out, *held
+):
+    n_x, n_zl = sizes["x"], sizes["zl"]
+    offsets = [(n_x - 1, 0), (1, 0)]
     weights = (weight_in, weight_out)
-    project(sizes, offsets, place, [left, right], weights, old, total, *held)
+    blocks = [lax.rem(place[2] + 2, n_x) * n_zl + j for j in range(0, n_zl, PAIR)]
+    waits = []
+
+    def fetch():
+        waits.append(load_weights(blocks, *weights, far_in, far_out, held[3], ahead=len(blocks)))
+
+    project(sizes, offsets, place, [left, right], weights, old, total, *held[:3], also=fetch)
+    for s in range(len(blocks)):
+        waits[0](s)
 
 
 def far_kernel(
-    sizes, place, left, right, old, taps, rates, weight_in, weight_out, proj, send, total, ext, pack, *held
+    sizes, place, left, right, old, taps, rates, far_in, far_out, proj, send, total, ext, pack
 ):
     offsets = [(2, 0), (2, left.shape[0])]
-    weights = (weight_in, weight_out)
-    project(sizes, offsets, place, [left, right], weights, old, total, *held)
+    project(sizes, offsets, place, [left, right], None, old, total, far_in, far_out)
     proj[...] = total[...].astype(BF16)
     state_kernel(proj, taps, rates, send, ext, pack)
 
@@ -428,33 +448,40 @@
             out[j + i, block:] = total[:, i * part : (i + 1) * part].astype(BF16)
 
 
-def partials_kernel(sizes, offsets, place, hidden, grad, weight_in, weight_out, *refs):
-    outs, held = refs[:-3], refs[-3:]
+def partials_kernel(sizes, offset, place, hidden, grad, weight_in, weight_out, out, *held):
     n_x, n_zl = sizes["x"], sizes["zl"]
-    blocks = [
-        lax.rem(place[2] + k, n_x) * n_zl + j
-        for k, out in zip(offsets, outs)
-        for j in range(0, out.shape[0], PAIR)
-    ]
+    base = lax.rem(place[2] + offset, n_x) * n_zl
+    blocks = [base + j for j in range(0, out.shape[0], PAIR)]
     ready = load_weights(blocks, weight_in, weight_out, *held)
-    start = 0
-    for out in outs:
-        partials(held, start, out, hidden, grad, ready)
-        start += out.shape[0] // PAIR
+    partials(held, 0, out, hidden, grad, ready)
+
+
+def side_partials_kernel(hidden, grad, side_in, side_out, to_right, to_left):
+    held = (side_in, side_out)
+    partials(held, 0, to_right, hidden, grad, at_once)
+    partials(held, to_right.shape[0] // PAIR, to_left, hidden, grad, at_once)
 
 
 def last_kernel(
     sizes, place, proj, taps, rates, res, skip, conv, grad, near, far, weight_in, weight_out,
-    hidden, out, to_right, to_left, ext, feat, *held,
+    hidden, out, to_right, to_left, side_in, side_out, ext, feat, *held,
 ):
     n_x, n_zl = sizes["x"], sizes["zl"]
-    blocks = [lax.rem(place[2] + 2, n_x) * n_zl + j for j in range(0, n_zl, PAIR)]
-    ready = load_weights(blocks, weight_in, weight_out, *held)
+    blocks, *side = [
+        [lax.rem(place[2] + k, n_x) * n_zl + j for j in range(0, n_zl, PAIR)]
+        for k in (2, 1, n_x - 1)
+    ]
+    side = side[0] + side[1]
+    weights = (weight_in, weight_out)
+    ready = load_weights(blocks, *weights, *held[:3], ahead=len(blocks))
+    ready_side = load_weights(side, *weights, side_in, side_out, held[3], ahead=len(side))
     finish_kernel(
         place, proj, taps, rates, res, skip, conv, grad, near, far, hidden, out, ext, feat
     )
     partials(held, 0, to_right, hidden, out, ready)
     partials(held, to_right.shape[0] // PAIR, to_left, hidden, out, ready)
+    for s in range(len(side)):
+        ready_side(s)
 
 
 def join_kernel(start, terms, got, out):
@@ -531,10 +558,15 @@
     from_right, _ = lax.optimization_barrier((from_right, total))
     far_left = lax.ppermute(from_left[:half], "x", right)
     far_right = lax.ppermute(from_right[half:], "x", left)
-    total = call(
+    runs = n_zl // PAIR
+    held_shapes = [
+        shape(runs, PAIR * part, 3 * width, dtype=BF16),
+        shape(runs, width, PAIR * part, dtype=BF16),
+    ]
+    total, far_in, far_out = call(
         functools.partial(side_kernel, sizes),
-        shape(4, block, width),
-        held_weights(2 * n_zl // PAIR, part, width),
+        [shape(4, block, width), *held_shapes],
+        held_weights(2 * runs, part, width) + [pltpu.SemaphoreType.DMA((runs, 4))],
         place,
         from_left,
         from_right,
@@ -549,17 +581,16 @@
     proj, send = call(
         functools.partial(far_kernel, sizes),
         [shape(4, block, width, dtype=BF16), shape(members, pack, width, dtype=BF16)],
-        [pltpu.VMEM((4, block, width), F32), ext, pltpu.VMEM((pack, width), F32)]
-        + held_weights(n_zl // PAIR, part, width),
+        [pltpu.VMEM((4, block, width), F32), ext, pltpu.VMEM((pack, width), F32)],
         place,
         far_left,
         far_right,
         total,
         taps,
         rates,
-        *weights,
+        far_in,
+        far_out,
         flops=products(n_zl),
-        hbm=2,
     )
     conv, grad = call(
         local_kernel,
@@ -585,15 +616,22 @@
     far_states = lax.all_to_all(send, "y", 0, 0, tiled=True)
     piece = shape(n_zl, 2 * block, part, dtype=BF16)
     half_piece = shape(half, 2 * block, part, dtype=BF16)
-    hidden, grad_proj, to_right, to_left = call(
+    side_shapes = [
+        shape(2 * runs, PAIR * part, 3 * width, dtype=BF16),
+        shape(2 * runs, width, PAIR * part, dtype=BF16),
+    ]
+    hidden, grad_proj, to_right, to_left, side_in, side_out = call(
         functools.partial(last_kernel, sizes),
         [
             shape(block, width, dtype=BF16),
             shape(3, block, width, dtype=BF16),
             half_piece,
             half_piece,
+            *side_shapes,
         ],
-        [ext, pltpu.VMEM((3, rows, width), F32)] + held_weights(n_zl // PAIR, part, width),
+        [ext, pltpu.VMEM((3, rows, width), F32)]
+        + held_weights(runs, part, width)
+        + [pltpu.SemaphoreType.DMA((2 * runs, 4))],
         place,
         proj,
         taps,
@@ -611,24 +649,23 @@
     far_right = lax.ppermute(to_right, "x", right)
     far_left = lax.ppermute(to_left, "x", left)
     to_right, to_left = call(
-        functools.partial(partials_kernel, sizes, [1, n_x - 1]),
+        side_partials_kernel,
         [piece, piece],
-        held_weights(2 * n_zl // PAIR, part, width),
-        place,
+        [],
         hidden,
         grad_proj,
-        *weights,
+        side_in,
+        side_out,
         flops=products(2 * n_zl),
-        hbm=2,
     )
     to_right = call(functools.partial(join_kernel, 0), piece, [], to_right, far_right)
     from_left = lax.ppermute(to_right, "x", right)
     to_left = call(functools.partial(join_kernel, half), piece, [], to_left, far_left)
     from_right = lax.ppermute(to_left, "x", left)
-    (own,) = call(
-        functools.partial(partials_kernel, sizes, [0]),
-        [piece],
-        held_weights(n_zl // PAIR, part, width),
+    own = call(
+        functools.partial(partials_kernel, sizes, 0),
+        piece,
+        held_weights(runs, part, width),
         place,
         hidden,
         grad_proj,

time: 151 us -> 149 us (0.987)
  the two profiles are of different devices: /device:TPU:6 before, /device:TPU:2 now
where the time goes in v11:
time: 149 us
  blocking collectives  68.4 us (46%)
  starting transfers between devices  34.2 us (23%)
  Pallas kernels  22.5 us (15%)
  waiting for transfers between devices  21.6 us (14%)
    all_to_all x1, blocking collectives, shards(): near_states = lax.all_to_all(send, ('zh', 'core'), 0, 0, tiled=True)  34.2 us
    pallas_call x11, Pallas kernels, call(): pl.pallas_call(kernel, out_shape=outs, scratch_shapes=scratch, in_specs=s...  22.5 us
    all_to_all x1, blocking collectives, shards(): pieces = lax.all_to_all(copies, 'zl', 0, 0, tiled=True)  21.5 us
    all_to_all x1, blocking collectives, shards(): summed = lax.all_to_all(summed, 'zl', 0, 0, tiled=True)  12.7 us
    all_to_all x1, starting transfers between devices, shards(): far_states = lax.all_to_all(send, 'y', 0, 0, tiled=True)  7.1 us
    ppermute x1, starting transfers between devices, shards(): from_right = lax.ppermute(pieces, 'x', left)  6.22 us
    all_to_all x1, waiting for transfers between devices, shards(): far_states = lax.all_to_all(send, 'y', 0, 0, tiled=True)  5.87 us
    ppermute x1, starting transfers between devices, shards(): far_left = lax.ppermute(to_left, 'x', left)  5.15 us
  transfers between devices with their start and end apart: 9, of which 7 were waited for; matrix products, arithmetic and copies ran while one was open for 0% of the time, Pallas kernels for 10%

profile of v11, /device:TPU:2, one launch (start us, length us, event | category | flops | bytes accessed | tf_op | source)
XLA Modules:
  0.0 148.6 jit_solution(12318627973320186983)
XLA Ops:
  0.6 1.3 shard_map.95
  1.9 21.5 %all_to_all.20.piece = bf16[4,256,256]{2,1,0:T(8,128)(2,1)S(1)} all-to-all(bf16[4,256,256]{2,1,0:T(8,128)(2,1)S(1)} %shard_map.95), channel_id=1, replica_groups=mesh['y'=8,'zh'=4,'core'=2,'x'=4,'zl'=4] {'zl'}, dimensions={0} | all-to-all | bytes 1048576 | tf_op jit(solution)/shard_map/all_to_all | solution.py:536
  23.5 6.2 %collective-permute-start.2 = (bf16[4,256,256]{2,1,0:T(8,128)(2,1)S(1)}, bf16[4,256,256]{2,1,0:T(8,128)(2,1)S(1)}, u32[]{:S(2)}, u32[]{:S(2)}) collective-permute-start(bf16[4,256,256]{2,1,0:T(8,128)(2,1)S(1)} %all_to_all.20.piece), channel_id=1, source_target_pairs={{0,12},{4,0},{8,4},{12,8},{1,13},{5,1},{9,5},{13,9},{2,14},{6,2},{... | collective-permute-start | bytes 1572872 | tf_op jit(solution)/shard_map/ppermute | solution.py:545
  29.7 1.9 %collective-permute-start = (bf16[4,256,256]{2,1,0:T(8,128)(2,1)S(1)}, bf16[4,256,256]{2,1,0:T(8,128)(2,1)S(1)}, u32[]{:S(2)}, u32[]{:S(2)}) collective-permute-start(bf16[4,256,256]{2,1,0:T(8,128)(2,1)S(1)} %all_to_all.20.piece), channel_id=1, source_target_pairs={{0,4},{4,8},{8,12},{12,0},{1,5},{5,9},{9,13},{13,1},{2,6},{6,10},{... | collective-permute-start | bytes 1572872 | tf_op jit(solution)/shard_map/ppermute | solution.py:544
  31.6 0.1 pad_add_fusion.place.place_ref
  31.7 2.6 %shard_map.96.old = f32[4,128,256]{2,1,0:T(8,128)S(1)} custom-call(s32[3]{0:T(128)S(1)} %pad_add_fusion.place.place_ref, bf16[4,256,256]{2,1,0:T(8,128)(2,1)S(1)} %all_to_all.20.piece, bf16[3,4096,256]{2,1,0:T(8,128)(2,1)} %bitcast.20, bf16[256,4096]{1,0:T(8,128)(2,1)} %weight_out.7), custom_call_target="tpu_custom_call" | custom-call | flops 268435456 | tf_op jit(solution)/shard_map/pallas_call | solution.py:312
  34.3 3.6 %collective-permute-done.2.right = bf16[4,256,256]{2,1,0:T(8,128)(2,1)S(1)} collective-permute-done((bf16[4,256,256]{2,1,0:T(8,128)(2,1)S(1)}, bf16[4,256,256]{2,1,0:T(8,128)(2,1)S(1)}, u32[]{:S(2)}, u32[]{:S(2)}) %collective-permute-start.2) | collective-permute-done | bytes 524320 | tf_op jit(solution)/shard_map/ppermute | solution.py:545
  37.9 2.9 %collective-permute-start.3 = (bf16[2,256,256]{2,1,0:T(8,128)(2,1)S(1)}, bf16[2,256,256]{2,1,0:T(8,128)(2,1)S(1)}, u32[]{:S(2)}, u32[]{:S(2)}) collective-permute-start(bf16[2,256,256]{2,1,0:T(8,128)(2,1)S(1)} %slice.13), channel_id=1, source_target_pairs={{0,12},{4,0},{8,4},{12,8},{1,13},{5,1},{9,5},{13,9},{2,14},{6,2},{... | collective-permute-start | bytes 786440 | tf_op jit(solution)/shard_map/ppermute | solution.py:560
  40.8 0.3 collective-permute-done.left
  41.1 0.0 copy-start
  41.1 0.0 copy-start.1
  41.1 2.7 %collective-permute-start.1 = (bf16[2,256,256]{2,1,0:T(8,128)(2,1)S(1)}, bf16[2,256,256]{2,1,0:T(8,128)(2,1)S(1)}, u32[]{:S(2)}, u32[]{:S(2)}) collective-permute-start(bf16[2,256,256]{2,1,0:T(8,128)(2,1)S(1)} %slice.12), channel_id=1, source_target_pairs={{0,4},{4,8},{8,12},{12,0},{1,5},{5,9},{9,13},{13,1},{2,6},{6,10},{... | collective-permute-start | bytes 786440 | tf_op jit(solution)/shard_map/ppermute | solution.py:559
  43.8 4.5 %shard_map.97 = (f32[4,128,256]{2,1,0:T(8,128)S(1)}, bf16[2,512,768]{2,1,0:T(8,128)(2,1)S(1)}, bf16[2,256,512]{2,1,0:T(8,128)(2,1)S(1)}) custom-call(s32[3]{0:T(128)S(1)} %pad_add_fusion.place.place_ref, bf16[4,256,256]{2,1,0:T(8,128)(2,1)S(1)} %collective-permute-done.left, bf16[4,256,256]{2,1,0:T(8,128)(2,1)S(1)} %collective-permute-done.2.right, ...), custom_call_target="tpu_custom_call" | custom-call | flops 536870912 | tf_op jit(solution)/shard_map/pallas_call | solution.py:312
  48.3 0.0 copy-start.2
  48.3 0.0 copy-start.3
  48.3 0.0 collective-permute-done.3.right
  48.4 2.3 %collective-permute-done.1.left = bf16[2,256,256]{2,1,0:T(8,128)(2,1)S(1)} collective-permute-done((bf16[2,256,256]{2,1,0:T(8,128)(2,1)S(1)}, bf16[2,256,256]{2,1,0:T(8,128)(2,1)S(1)}, u32[]{:S(2)}, u32[]{:S(2)}) %collective-permute-start.1) | collective-permute-done | bytes 262176 | tf_op jit(solution)/shard_map/ppermute | solution.py:559
  50.6 0.0 copy-done
  50.6 0.0 copy-done.1
  50.6 1.5 %shard_map.98 = (bf16[4,128,256]{2,1,0:T(8,128)(2,1)S(1)}, bf16[8,48,256]{2,1,0:T(8,128)(2,1)S(1)}) custom-call(s32[3]{0:T(128)S(1)} %pad_add_fusion.place.place_ref, bf16[2,256,256]{2,1,0:T(8,128)(2,1)S(1)} %collective-permute-done.1.left, bf16[2,256,256]{2,1,0:T(8,128)(2,1)S(1)} %collective-permute-done.3.right, f32[4,128,256]{2,1,0:T(8,128)S(1)} %get-tuple-element.21.old, ...), custom_call_target="tpu_custom_call" | custom-call | flops 268435456 | tf_op jit(solution)/shard_map/pallas_call | solution.py:312
  52.2 34.2 %all_to_all.21.got_ref.near = bf16[8,48,256]{2,1,0:T(8,128)(2,1)S(1)} all-to-all(bf16[8,48,256]{2,1,0:T(8,128)(2,1)S(1)} %get-tuple-element.27), channel_id=1, replica_groups=mesh['y'=8,'zh'=4,'core'=2,'x'=4,'zl'=4] {'zh','core'}, dimensions={0} | all-to-all | bytes 393216 | tf_op jit(solution)/shard_map/all_to_all | solution.py:606
  86.3 1.3 shard_map.100
  87.7 7.1 %all-to-all-start.2 = ((bf16[8,32,256]{2,1,0:T(8,128)(2,1)}), bf16[8,32,256]{2,1,0:T(8,128)(2,1)S(1)}, u32[]{:S(2)}, u32[]{:S(2)}) async-start(bf16[8,32,256]{2,1,0:T(8,128)(2,1)} %shard_map.100), calls=%async_computation.2 | async-start | bytes 262144 | tf_op jit(solution)/shard_map/all_to_all | solution.py:616
  94.8 0.0 copy-done.2
  94.8 0.0 copy-done.3
  94.8 3.2 %shard_map.99 = (f32[136,256]{1,0:T(8,128)S(1)}, f32[136,256]{1,0:T(8,128)S(1)}) custom-call(bf16[4,128,256]{2,1,0:T(8,128)(2,1)S(1)} %get-tuple-element.24.proj_ref.proj, f32[3,3,256]{2,1,0:T(4,128)S(1)} %bitcast.14, f32[16,256]{1,0:T(8,128)S(1)} %bitcast.10, f32[16,256]{1,0:T(8,128)S(1)} %bitcast.16, f32[1,256]{1,0:T(1,128)S(1)} %bitcast.18), custom_call_target="tpu_custom_call" | custom-call | flops 3000000000 | tf_op jit(solution)/shard_map/pallas_call | solution.py:312
  98.0 5.9 %all-to-all-done.2.far = bf16[8,32,256]{2,1,0:T(8,128)(2,1)S(1)} async-done(((bf16[8,32,256]{2,1,0:T(8,128)(2,1)}), bf16[8,32,256]{2,1,0:T(8,128)(2,1)S(1)}, u32[]{:S(2)}, u32[]{:S(2)}) %all-to-all-start.2) | async-done | bytes 131104 | tf_op jit(solution)/shard_map/all_to_all | solution.py:616
  103.9 3.9 %shard_map.101 = (bf16[128,256]{1,0:T(8,128)(2,1)S(1)}, bf16[3,128,256]{2,1,0:T(8,128)(2,1)S(1)}, bf16[2,256,256]{2,1,0:T(8,128)(2,1)S(1)}, bf16[2,256,256]{2,1,...) custom-call(s32[3]{0:T(128)S(1)} %pad_add_fusion.place.place_ref, ...), custom_call_target="tpu_custom_call" | custom-call | flops 268435456 | tf_op jit(solution)/shard_map/pallas_call | solution.py:312
  107.8 5.1 %collective-permute-start.6 = (bf16[2,256,256]{2,1,0:T(8,128)(2,1)S(1)}, bf16[2,256,256]{2,1,0:T(8,128)(2,1)S(1)}, u32[]{:S(2)}, u32[]{:S(2)}) collective-permute-start(bf16[2,256,256]{2,1,0:T(8,128)(2,1)S(1)} %get-tuple-element.35), channel_id=1, source_target_pairs={{0,12},{4,0},{8,4},{12,8},{1,13},{5,1},{9,5},{13,9},{2,14},{6,2},{... | collective-permute-start | bytes 786440 | tf_op jit(solution)/shard_map/ppermute | solution.py:650
  112.9 1.9 %collective-permute-start.4 = (bf16[2,256,256]{2,1,0:T(8,128)(2,1)S(1)}, bf16[2,256,256]{2,1,0:T(8,128)(2,1)S(1)}, u32[]{:S(2)}, u32[]{:S(2)}) collective-permute-start(bf16[2,256,256]{2,1,0:T(8,128)(2,1)S(1)} %get-tuple-element.33), channel_id=1, source_target_pairs={{0,4},{4,8},{8,12},{12,0},{1,5},{5,9},{9,13},{13,1},{2,6},{6,10},{... | collective-permute-start | bytes 786440 | tf_op jit(solution)/shard_map/ppermute | solution.py:649
  114.9 1.3 shard_map.103
  116.2 3.1 %collective-permute-done.6.got = bf16[2,256,256]{2,1,0:T(8,128)(2,1)S(1)} collective-permute-done((bf16[2,256,256]{2,1,0:T(8,128)(2,1)S(1)}, bf16[2,256,256]{2,1,0:T(8,128)(2,1)S(1)}, u32[]{:S(2)}, u32[]{:S(2)}) %collective-permute-start.6) | collective-permute-done | bytes 262176 | tf_op jit(solution)/shard_map/ppermute | solution.py:650
  119.3 0.1 shard_map.105
  119.4 4.4 %collective-permute-start.7 = (bf16[4,256,256]{2,1,0:T(8,128)(2,1)S(1)}, bf16[4,256,256]{2,1,0:T(8,128)(2,1)S(1)}, u32[]{:S(2)}, u32[]{:S(2)}) collective-permute-start(bf16[4,256,256]{2,1,0:T(8,128)(2,1)S(1)} %shard_map.105), channel_id=1, source_target_pairs={{0,12},{4,0},{8,4},{12,8},{1,13},{5,1},{9,5},{13,9},{2,14},{6,2},{... | collective-permute-start | bytes 1572872 | tf_op jit(solution)/shard_map/ppermute | solution.py:664
  123.8 0.0 collective-permute-done.4.got
  123.8 0.1 shard_map.104
  123.9 1.9 %collective-permute-start.5 = (bf16[4,256,256]{2,1,0:T(8,128)(2,1)S(1)}, bf16[4,256,256]{2,1,0:T(8,128)(2,1)S(1)}, u32[]{:S(2)}, u32[]{:S(2)}) collective-permute-start(bf16[4,256,256]{2,1,0:T(8,128)(2,1)S(1)} %shard_map.104), channel_id=1, source_target_pairs={{0,4},{4,8},{8,12},{12,0},{1,5},{5,9},{9,13},{13,1},{2,6},{6,10},{... | collective-permute-start | bytes 1572872 | tf_op jit(solution)/shard_map/ppermute | solution.py:662
  125.8 2.7 %shard_map.102 = bf16[4,256,256]{2,1,0:T(8,128)(2,1)S(1)} custom-call(s32[3]{0:T(128)S(1)} %pad_add_fusion.place.place_ref, bf16[128,256]{1,0:T(8,128)(2,1)S(1)} %get-tuple-element.28.hidden, bf16[3,128,256]{2,1,0:T(8,128)(2,1)S(1)} %get-tuple-element.29.grad, bf16[3,4096,256]{2,1,0:T(8,128)(2,1)} %bitcast.23, bf16[256,4096]{1,0:T(8,128)(2,1)} %weight_out.7), custom_call_target="tpu_custom_call" | custom-call | flops 268435456 | tf_op jit(solution)/shard_map/pallas_call | solution.py:312
  128.5 2.0 %collective-permute-done.7 = bf16[4,256,256]{2,1,0:T(8,128)(2,1)S(1)} collective-permute-done((bf16[4,256,256]{2,1,0:T(8,128)(2,1)S(1)}, bf16[4,256,256]{2,1,0:T(8,128)(2,1)S(1)}, u32[]{:S(2)}, u32[]{:S(2)}) %collective-permute-start.7) | collective-permute-done | bytes 524320 | tf_op jit(solution)/shard_map/ppermute | solution.py:664
  130.5 4.5 %collective-permute-done.5 = bf16[4,256,256]{2,1,0:T(8,128)(2,1)S(1)} collective-permute-done((bf16[4,256,256]{2,1,0:T(8,128)(2,1)S(1)}, bf16[4,256,256]{2,1,0:T(8,128)(2,1)S(1)}, u32[]{:S(2)}, u32[]{:S(2)}) %collective-permute-start.5) | collective-permute-done | bytes 524320 | tf_op jit(solution)/shard_map/ppermute | solution.py:662
  134.9 0.2 add_convert_fusion
  135.2 12.7 %all_to_all.22 = bf16[4,256,256]{2,1,0:T(8,128)(2,1)S(1)} all-to-all(bf16[4,256,256]{2,1,0:T(8,128)(2,1)S(1)} %add_convert_fusion), channel_id=1, replica_groups=mesh['y'=8,'zh'=4,'core'=2,'x'=4,'zl'=4] {'zl'}, dimensions={0} | all-to-all | bytes 1048576 | tf_op jit(solution)/shard_map/all_to_all | solution.py:677
  147.8 0.1 reduce_sum.12
  147.9 0.7 fusion
  (2 shorter events, 0.0 us)
Async XLA Ops:
  23.5 14.4 %collective-permute-start.2 = (bf16[4,256,256]{2,1,0:T(8,128)(2,1)S(1)}, bf16[4,256,256]{2,1,0:T(8,128)(2,1)S(1)}, u32[]{:S(2)}, u32[]{:S(2)}) collective-permute-start(bf16[4,256,256]{2,1,0:T(8,128)(2,1)S(1)} %all_to_all.20.piece), channel_id=1, source_target_pairs={{0,12},{4,0},{8,4},{12,8},{1,13},{5,1},{9,5},{13,9},{2,14},{6,2},{... | collective-permute-start | bytes 1572872 | tf_op jit(solution)/shard_map/ppermute | solution.py:545
  29.7 11.4 %collective-permute-start = (bf16[4,256,256]{2,1,0:T(8,128)(2,1)S(1)}, bf16[4,256,256]{2,1,0:T(8,128)(2,1)S(1)}, u32[]{:S(2)}, u32[]{:S(2)}) collective-permute-start(bf16[4,256,256]{2,1,0:T(8,128)(2,1)S(1)} %all_to_all.20.piece), channel_id=1, source_target_pairs={{0,4},{4,8},{8,12},{12,0},{1,5},{5,9},{9,13},{13,1},{2,6},{6,10},{... | collective-permute-start | bytes 1572872 | tf_op jit(solution)/shard_map/ppermute | solution.py:544
  37.9 10.5 %collective-permute-start.3 = (bf16[2,256,256]{2,1,0:T(8,128)(2,1)S(1)}, bf16[2,256,256]{2,1,0:T(8,128)(2,1)S(1)}, u32[]{:S(2)}, u32[]{:S(2)}) collective-permute-start(bf16[2,256,256]{2,1,0:T(8,128)(2,1)S(1)} %slice.13), channel_id=1, source_target_pairs={{0,12},{4,0},{8,4},{12,8},{1,13},{5,1},{9,5},{13,9},{2,14},{6,2},{... | collective-permute-start | bytes 786440 | tf_op jit(solution)/shard_map/ppermute | solution.py:560
  41.1 9.5 %copy-start = (f32[256,16]{0,1:T(8,128)S(1)}, f32[256,16]{0,1:T(8,128)}, u32[]{:S(2)}) copy-start(f32[256,16]{0,1:T(8,128)} %param.14) | copy-start | bytes 49156
  41.1 9.5 %copy-start.1 = (f32[3,256,3]{1,2,0:T(4,128)S(1)}, f32[3,256,3]{1,2,0:T(4,128)}, u32[]{:S(2)}) copy-start(f32[3,256,3]{1,2,0:T(4,128)} %param.12) | copy-start | bytes 27652
  41.1 9.5 %collective-permute-start.1 = (bf16[2,256,256]{2,1,0:T(8,128)(2,1)S(1)}, bf16[2,256,256]{2,1,0:T(8,128)(2,1)S(1)}, u32[]{:S(2)}, u32[]{:S(2)}) collective-permute-start(bf16[2,256,256]{2,1,0:T(8,128)(2,1)S(1)} %slice.12), channel_id=1, source_target_pairs={{0,4},{4,8},{8,12},{12,0},{1,5},{5,9},{9,13},{13,1},{2,6},{6,10},{... | collective-permute-start | bytes 786440 | tf_op jit(solution)/shard_map/ppermute | solution.py:559
  48.3 46.5 %copy-start.2 = (f32[256,16]{0,1:T(8,128)S(1)}, f32[256,16]{0,1:T(8,128)}, u32[]{:S(2)}) copy-start(f32[256,16]{0,1:T(8,128)} %param.13) | copy-start | bytes 49156
  48.3 46.5 %copy-start.3 = (f32[256]{0:T(256)S(1)}, f32[256]{0:T(256)}, u32[]{:S(2)}) copy-start(f32[256]{0:T(256)} %param.15) | copy-start | bytes 3076
  87.7 16.2 %all-to-all-start.2 = ((bf16[8,32,256]{2,1,0:T(8,128)(2,1)}), bf16[8,32,256]{2,1,0:T(8,128)(2,1)S(1)}, u32[]{:S(2)}, u32[]{:S(2)}) async-start(bf16[8,32,256]{2,1,0:T(8,128)(2,1)} %shard_map.100), calls=%async_computation.2 | async-start | bytes 262144 | tf_op jit(solution)/shard_map/all_to_all | solution.py:616
  107.8 11.5 %collective-permute-start.6 = (bf16[2,256,256]{2,1,0:T(8,128)(2,1)S(1)}, bf16[2,256,256]{2,1,0:T(8,128)(2,1)S(1)}, u32[]{:S(2)}, u32[]{:S(2)}) collective-permute-start(bf16[2,256,256]{2,1,0:T(8,128)(2,1)S(1)} %get-tuple-element.35), channel_id=1, source_target_pairs={{0,12},{4,0},{8,4},{12,8},{1,13},{5,1},{9,5},{13,9},{2,14},{6,2},{... | collective-permute-start | bytes 786440 | tf_op jit(solution)/shard_map/ppermute | solution.py:650
  112.9 10.9 %collective-permute-start.4 = (bf16[2,256,256]{2,1,0:T(8,128)(2,1)S(1)}, bf16[2,256,256]{2,1,0:T(8,128)(2,1)S(1)}, u32[]{:S(2)}, u32[]{:S(2)}) collective-permute-start(bf16[2,256,256]{2,1,0:T(8,128)(2,1)S(1)} %get-tuple-element.33), channel_id=1, source_target_pairs={{0,4},{4,8},{8,12},{12,0},{1,5},{5,9},{9,13},{13,1},{2,6},{6,10},{... | collective-permute-start | bytes 786440 | tf_op jit(solution)/shard_map/ppermute | solution.py:649
  119.4 11.1 %collective-permute-start.7 = (bf16[4,256,256]{2,1,0:T(8,128)(2,1)S(1)}, bf16[4,256,256]{2,1,0:T(8,128)(2,1)S(1)}, u32[]{:S(2)}, u32[]{:S(2)}) collective-permute-start(bf16[4,256,256]{2,1,0:T(8,128)(2,1)S(1)} %shard_map.105), channel_id=1, source_target_pairs={{0,12},{4,0},{8,4},{12,8},{1,13},{5,1},{9,5},{13,9},{2,14},{6,2},{... | collective-permute-start | bytes 1572872 | tf_op jit(solution)/shard_map/ppermute | solution.py:664
  123.9 11.1 %collective-permute-start.5 = (bf16[4,256,256]{2,1,0:T(8,128)(2,1)S(1)}, bf16[4,256,256]{2,1,0:T(8,128)(2,1)S(1)}, u32[]{:S(2)}, u32[]{:S(2)}) collective-permute-start(bf16[4,256,256]{2,1,0:T(8,128)(2,1)S(1)} %shard_map.104), channel_id=1, source_target_pairs={{0,4},{4,8},{8,12},{12,0},{1,5},{5,9},{9,13},{13,1},{2,6},{6,10},{... | collective-permute-start | bytes 1572872 | tf_op jit(solution)/shard_map/ppermute | solution.py:662

commit v12 on v11

--- a/solution.py
+++ b/solution.py
@@ -401,25 +401,46 @@
                 total[p] = (old if s == 0 else total)[p] + terms[p]
 
 
-def near_kernel(sizes, place, piece, weight_in, weight_out, total, *held):
-    project(sizes, [(0, 0)], place, [piece], (weight_in, weight_out), None, total, *held)
-
-
-def side_kernel(
-    sizes, place, left, right, old, weight_in, weight_out, total, far_in, far_out, *held
+def runs_of(sizes, place, offsets):
+    n_x, n_zl = sizes["x"], sizes["zl"]
+    return [
+        lax.rem(place[2] + k, n_x) * n_zl + j for k in offsets for j in range(0, n_zl, PAIR)
+    ]
+
+
+def fetch(blocks, weights, held):
+    ready = load_weights(blocks, *weights, *held, ahead=len(blocks))
+
+    def wait():
+        for s in range(len(blocks)):
+            ready(s)
+
+    return wait
+
+
+def near_kernel(
+    sizes, place, piece, weight_in, weight_out,
+    total, side_in, side_out, far_in, far_out, own_in, own_out, own_sems, side_sems, far_sems,
 ):
-    n_x, n_zl = sizes["x"], sizes["zl"]
-    offsets = [(n_x - 1, 0), (1, 0)]
     weights = (weight_in, weight_out)
-    blocks = [lax.rem(place[2] + 2, n_x) * n_zl + j for j in range(0, n_zl, PAIR)]
     waits = []
 
-    def fetch():
-        waits.append(load_weights(blocks, *weights, far_in, far_out, held[3], ahead=len(blocks)))
-
-    project(sizes, offsets, place, [left, right], weights, old, total, *held[:3], also=fetch)
-    for s in range(len(blocks)):
-        waits[0](s)
+    def also():
+        side = runs_of(sizes, place, [sizes["x"] - 1, 1])
+        waits.append(fetch(side, weights, (side_in, side_out, side_sems)))
+        far = runs_of(sizes, place, [2])
+        waits.append(fetch(far, weights, (far_in, far_out, far_sems)))
+
+    project(
+        sizes, [(0, 0)], place, [piece], weights, None, total, own_in, own_out, own_sems, also
+    )
+    for wait in waits:
+        wait()
+
+
+def side_kernel(sizes, place, left, right, old, side_in, side_out, total):
+    offsets = [(sizes["x"] - 1, 0), (1, 0)]
+    project(sizes, offsets, place, [left, right], None, old, total, side_in, side_out)
 
 
 def far_kernel(
@@ -448,12 +469,8 @@
             out[j + i, block:] = total[:, i * part : (i + 1) * part].astype(BF16)
 
 
-def partials_kernel(sizes, offset, place, hidden, grad, weight_in, weight_out, out, *held):
-    n_x, n_zl = sizes["x"], sizes["zl"]
-    base = lax.rem(place[2] + offset, n_x) * n_zl
-    blocks = [base + j for j in range(0, out.shape[0], PAIR)]
-    ready = load_weights(blocks, weight_in, weight_out, *held)
-    partials(held, 0, out, hidden, grad, ready)
+def own_partials_kernel(hidden, grad, own_in, own_out, out):
+    partials((own_in, own_out), 0, out, hidden, grad, at_once)
 
 
 def side_partials_kernel(hidden, grad, side_in, side_out, to_right, to_left):
@@ -463,25 +480,33 @@
 
 
 def last_kernel(
-    sizes, place, proj, taps, rates, res, skip, conv, grad, near, far, weight_in, weight_out,
-    hidden, out, to_right, to_left, side_in, side_out, ext, feat, *held,
+    place, proj, taps, rates, res, skip, conv, grad, near, far, far_in, far_out,
+    hidden, out, to_right, to_left, ext, feat,
 ):
-    n_x, n_zl = sizes["x"], sizes["zl"]
-    blocks, *side = [
-        [lax.rem(place[2] + k, n_x) * n_zl + j for j in range(0, n_zl, PAIR)]
-        for k in (2, 1, n_x - 1)
-    ]
-    side = side[0] + side[1]
-    weights = (weight_in, weight_out)
-    ready = load_weights(blocks, *weights, *held[:3], ahead=len(blocks))
-    ready_side = load_weights(side, *weights, side_in, side_out, held[3], ahead=len(side))
     finish_kernel(
         place, proj, taps, rates, res, skip, conv, grad, near, far, hidden, out, ext, feat
     )
-    partials(held, 0, to_right, hidden, out, ready)
-    partials(held, to_right.shape[0] // PAIR, to_left, hidden, out, ready)
-    for s in range(len(side)):
-        ready_side(s)
+    held = (far_in, far_out)
+    partials(held, 0, to_right, hidden, out, at_once)
+    partials(held, to_right.shape[0] // PAIR, to_left, hidden, out, at_once)
+
+
+def local_fetch_kernel(
+    sizes, place, proj, taps, rates, res, skip, weight_in, weight_out,
+    conv, grad, far_in, far_out, side_in, side_out, own_in, own_out,
+    ext, pad, filt, far_sems, side_sems, own_sems,
+):
+    weights = (weight_in, weight_out)
+    waits = [
+        fetch(runs_of(sizes, place, [2]), weights, (far_in, far_out, far_sems)),
+        fetch(
+            runs_of(sizes, place, [1, sizes["x"] - 1]), weights, (side_in, side_out, side_sems)
+        ),
+        fetch(runs_of(sizes, place, [0]), weights, (own_in, own_out, own_sems)),
+    ]
+    local_kernel(proj, taps, rates, res, skip, conv, grad, ext, pad, filt)
+    for wait in waits:
+        wait()
 
 
 def join_kernel(start, terms, got, out):
@@ -544,36 +569,43 @@
     from_left = lax.ppermute(pieces, "x", right)
     from_right = lax.ppermute(pieces, "x", left)
     weights = (in_hbm(input_weight.transpose(1, 0, 2)), in_hbm(output_weight))
-    total = call(
+    runs = n_zl // PAIR
+
+    def held_shapes(count):
+        return [
+            shape(count, PAIR * part, 3 * width, dtype=BF16),
+            shape(count, width, PAIR * part, dtype=BF16),
+        ]
+
+    def sems(count):
+        return pltpu.SemaphoreType.DMA((count, 4))
+
+    total, side_in, side_out, far_in, far_out = call(
         functools.partial(near_kernel, sizes),
-        shape(4, block, width),
-        held_weights(n_zl // PAIR, part, width),
+        [shape(4, block, width)] + held_shapes(2 * runs) + held_shapes(runs),
+        held_weights(runs, part, width) + [sems(2 * runs), sems(runs)],
         place,
         pieces,
         *weights,
-        flops=products(n_zl),
+        flops=16 * products(n_zl),
         hbm=2,
     )
-    from_left, _ = lax.optimization_barrier((from_left, total))
     from_right, _ = lax.optimization_barrier((from_right, total))
+    to_far = from_right[half:]
+    far_right = lax.ppermute(to_far, "x", left)
+    from_left, _ = lax.optimization_barrier((from_left, to_far))
     far_left = lax.ppermute(from_left[:half], "x", right)
-    far_right = lax.ppermute(from_right[half:], "x", left)
-    runs = n_zl // PAIR
-    held_shapes = [
-        shape(runs, PAIR * part, 3 * width, dtype=BF16),
-        shape(runs, width, PAIR * part, dtype=BF16),
-    ]
-    total, far_in, far_out = call(
+    total = call(
         functools.partial(side_kernel, sizes),
-        [shape(4, block, width), *held_shapes],
-        held_weights(2 * runs, part, width) + [pltpu.SemaphoreType.DMA((runs, 4))],
+        shape(4, block, width),
+        [],
         place,
         from_left,
         from_right,
         total,
-        *weights,
-        flops=products(2 * n_zl),
-        hbm=2,
+        side_in,
+        side_out,
+        flops=16 * products(n_zl),
     )
     ext = pltpu.VMEM((3, rows + TILE, width), F32)
     members = sizes["zh"] * sizes["core"]
@@ -592,16 +624,23 @@
         far_out,
         flops=products(n_zl),
     )
-    conv, grad = call(
-        local_kernel,
-        [shape(rows, width), shape(rows, width)],
-        [ext, pltpu.VMEM((2, rows + TILE, width), F32), pltpu.VMEM((rows, width), F32)],
+    conv, grad, far_in, far_out, side_in, side_out, own_in, own_out = call(
+        functools.partial(local_fetch_kernel, sizes),
+        [shape(rows, width), shape(rows, width)]
+        + held_shapes(runs)
+        + held_shapes(2 * runs)
+        + held_shapes(runs),
+        [ext, pltpu.VMEM((2, rows + TILE, width), F32), pltpu.VMEM((rows, width), F32)]
+        + [sems(runs), sems(2 * runs), sems(runs)],
+        place,
         proj,
         taps,
         rates,
         res,
         skip,
+        *weights,
         flops=3 * 10**9,
+        hbm=2,
     )
     near_states = lax.all_to_all(send, ("zh", "core"), 0, 0, tiled=True)
     send = call(
@@ -616,22 +655,15 @@
     far_states = lax.all_to_all(send, "y", 0, 0, tiled=True)
     piece = shape(n_zl, 2 * block, part, dtype=BF16)
     half_piece = shape(half, 2 * block, part, dtype=BF16)
-    side_shapes = [
-        shape(2 * runs, PAIR * part, 3 * width, dtype=BF16),
-        shape(2 * runs, width, PAIR * part, dtype=BF16),
-    ]
-    hidden, grad_proj, to_right, to_left, side_in, side_out = call(
-        functools.partial(last_kernel, sizes),
+    hidden, grad_proj, to_right, to_left = call(
+        last_kernel,
         [
             shape(block, width, dtype=BF16),
             shape(3, block, width, dtype=BF16),
             half_piece,
             half_piece,
-            *side_shapes,
         ],
-        [ext, pltpu.VMEM((3, rows, width), F32)]
-        + held_weights(runs, part, width)
-        + [pltpu.SemaphoreType.DMA((2 * runs, 4))],
+        [ext, pltpu.VMEM((3, rows, width), F32)],
         place,
         proj,
         taps,
@@ -642,9 +674,9 @@
         grad,
         near_states,
         far_states,
-        *weights,
+        far_in,
+        far_out,
         flops=products(n_zl),
-        hbm=2,
     )
     far_right = lax.ppermute(to_right, "x", right)
     far_left = lax.ppermute(to_left, "x", left)
@@ -663,15 +695,14 @@
     to_left = call(functools.partial(join_kernel, half), piece, [], to_left, far_left)
     from_right = lax.ppermute(to_left, "x", left)
     own = call(
-        functools.partial(partials_kernel, sizes, 0),
+        own_partials_kernel,
         piece,
-        held_weights(runs, part, width),
-        place,
+        [],
         hidden,
         grad_proj,
-        *weights,
+        own_in,
+        own_out,
         flops=products(n_zl),
-        hbm=2,
     )
     summed = sum(a.astype(F32) for a in (own, from_left, from_right)).astype(BF16)
     summed = lax.all_to_all(summed, "zl", 0, 0, tiled=True)

time: 149 us -> 157 us (1.054)
  the two profiles are of different devices: /device:TPU:2 before, /device:TPU:8 now
where the time goes in v12:
time: 157 us
  blocking collectives  69.8 us (44%)
  starting transfers between devices  33.4 us (21%)
  waiting for transfers between devices  19.7 us (13%)
  Pallas kernels  18.6 us (12%)
  local copies, waits for them, and re-layouts  13.9 us (9%)
    all_to_all x1, blocking collectives, shards(): near_states = lax.all_to_all(send, ('zh', 'core'), 0, 0, tiled=True)  34.2 us
    all_to_all x1, blocking collectives, shards(): pieces = lax.all_to_all(copies, 'zl', 0, 0, tiled=True)  21.5 us
    pallas_call x11, Pallas kernels, call(): pl.pallas_call(kernel, out_shape=outs, scratch_shapes=scratch, in_specs=s...  18.6 us
    all_to_all x1, blocking collectives, shards(): summed = lax.all_to_all(summed, 'zl', 0, 0, tiled=True)  14.1 us
    unnamed x42, local copies, waits for them, and re-layouts  13.2 us
    all_to_all x1, starting transfers between devices, shards(): far_states = lax.all_to_all(send, 'y', 0, 0, tiled=True)  7.54 us
    ppermute x1, waiting for transfers between devices, shards(): far_left = lax.ppermute(from_left[:half], 'x', right)  6.05 us
    ppermute x1, starting transfers between devices, shards(): far_right = lax.ppermute(to_far, 'x', left)  5.6 us
  transfers between devices with their start and end apart: 9, of which 5 were waited for; matrix products, arithmetic and copies ran while one was open for 0% of the time, Pallas kernels for 8%

profile of v12, /device:TPU:8, one launch (start us, length us, event | category | flops | bytes accessed | tf_op | source)
XLA Modules:
  0.0 156.6 jit_solution(6367805164316676850)
XLA Ops:
  0.6 1.3 shard_map.95
  1.9 21.5 %all_to_all.20.piece = bf16[4,256,256]{2,1,0:T(8,128)(2,1)S(1)} all-to-all(bf16[4,256,256]{2,1,0:T(8,128)(2,1)S(1)} %shard_map.95), channel_id=1, replica_groups=mesh['y'=8,'zh'=4,'core'=2,'x'=4,'zl'=4] {'zl'}, dimensions={0} | all-to-all | bytes 1048576 | tf_op jit(solution)/shard_map/all_to_all | solution.py:561
  23.5 4.7 %collective-permute-start.1 = (bf16[4,256,256]{2,1,0:T(8,128)(2,1)S(1)}, bf16[4,256,256]{2,1,0:T(8,128)(2,1)S(1)}, u32[]{:S(2)}, u32[]{:S(2)}) collective-permute-start(bf16[4,256,256]{2,1,0:T(8,128)(2,1)S(1)} %all_to_all.20.piece), channel_id=1, source_target_pairs={{0,12},{4,0},{8,4},{12,8},{1,13},{5,1},{9,5},{13,9},{2,14},{6,2},{... | collective-permute-start | bytes 1572872 | tf_op jit(solution)/shard_map/ppermute | solution.py:570
  28.1 1.9 %collective-permute-start = (bf16[4,256,256]{2,1,0:T(8,128)(2,1)S(1)}, bf16[4,256,256]{2,1,0:T(8,128)(2,1)S(1)}, u32[]{:S(2)}, u32[]{:S(2)}) collective-permute-start(bf16[4,256,256]{2,1,0:T(8,128)(2,1)S(1)} %all_to_all.20.piece), channel_id=1, source_target_pairs={{0,4},{4,8},{8,12},{12,0},{1,5},{5,9},{9,13},{13,1},{2,6},{6,10},{... | collective-permute-start | bytes 1572872 | tf_op jit(solution)/shard_map/ppermute | solution.py:569
  30.1 0.1 pad_add_fusion.place.place_ref
  30.2 4.5 %shard_map.96 = (f32[4,128,256]{2,1,0:T(8,128)S(1)}, bf16[4,512,768]{2,1,0:T(8,128)(2,1)S(1)}, bf16[4,256,512]{2,1,0:T(8,128)(2,1)S(1)}, bf16[2,512,768]{2,1,0:T(8,128)(2,1)S(1)}, bf16[2,256,512]{2,1,0:T(8,128)(2,1)S(1)}) custom-call(s32[3]{0:T(128)S(1)} %pad_add_fusion.place.place_ref, bf16[4,256,256]{2,1,0:T(8,128)(2,1)S(1)} %all_to_all.20.piece, ...), custom_call_target="tpu_custom_call" | custom-call | flops 4294967296 | tf_op jit(solution)/shard_map/pallas_call | solution.py:312
  34.6 3.5 %collective-permute-done.1.right = bf16[4,256,256]{2,1,0:T(8,128)(2,1)S(1)} collective-permute-done((bf16[4,256,256]{2,1,0:T(8,128)(2,1)S(1)}, bf16[4,256,256]{2,1,0:T(8,128)(2,1)S(1)}, u32[]{:S(2)}, u32[]{:S(2)}) %collective-permute-start.1) | collective-permute-done | bytes 524320 | tf_op jit(solution)/shard_map/ppermute | solution.py:570
  38.2 5.6 %collective-permute-start.3 = (bf16[2,256,256]{2,1,0:T(8,128)(2,1)S(1)}, bf16[2,256,256]{2,1,0:T(8,128)(2,1)S(1)}, u32[]{:S(2)}, u32[]{:S(2)}) collective-permute-start(bf16[2,256,256]{2,1,0:T(8,128)(2,1)S(1)} %slice.12), channel_id=1, source_target_pairs={{0,12},{4,0},{8,4},{12,8},{1,13},{5,1},{9,5},{13,9},{2,14},{6,2},{... | collective-permute-start | bytes 786440 | tf_op jit(solution)/shard_map/ppermute | solution.py:595
  43.8 1.9 %collective-permute-start.2 = (bf16[2,256,256]{2,1,0:T(8,128)(2,1)S(1)}, bf16[2,256,256]{2,1,0:T(8,128)(2,1)S(1)}, u32[]{:S(2)}, u32[]{:S(2)}) collective-permute-start(bf16[2,256,256]{2,1,0:T(8,128)(2,1)S(1)} %slice.13), channel_id=1, source_target_pairs={{0,4},{4,8},{8,12},{12,0},{1,5},{5,9},{9,13},{13,1},{2,6},{6,10},{... | collective-permute-start | bytes 786440 | tf_op jit(solution)/shard_map/ppermute | solution.py:597
  45.8 0.0 copy-start.13
  45.8 1.5 shard_map.97.old
  47.3 6.0 %collective-permute-done.2.left = bf16[2,256,256]{2,1,0:T(8,128)(2,1)S(1)} collective-permute-done((bf16[2,256,256]{2,1,0:T(8,128)(2,1)S(1)}, bf16[2,256,256]{2,1,0:T(8,128)(2,1)S(1)}, u32[]{:S(2)}, u32[]{:S(2)}) %collective-permute-start.2) | collective-permute-done | bytes 262176 | tf_op jit(solution)/shard_map/ppermute | solution.py:597
  53.3 0.0 copy-start.19
  53.4 1.5 shard_map.98
  54.9 0.7 copy-done.10
  55.6 34.2 %all_to_all.21.got_ref.near = bf16[8,48,256]{2,1,0:T(8,128)(2,1)S(1)} all-to-all(bf16[8,48,256]{2,1,0:T(8,128)(2,1)S(1)} %get-tuple-element.35), channel_id=1, replica_groups=mesh['y'=8,'zh'=4,'core'=2,'x'=4,'zl'=4] {'zh','core'}, dimensions={0} | all-to-all | bytes 393216 | tf_op jit(solution)/shard_map/all_to_all | solution.py:645
  89.8 1.3 shard_map.100
  91.1 7.5 %all-to-all-start.2 = ((bf16[8,32,256]{2,1,0:T(8,128)(2,1)}), bf16[8,32,256]{2,1,0:T(8,128)(2,1)S(1)}, u32[]{:S(2)}, u32[]{:S(2)}) async-start(bf16[8,32,256]{2,1,0:T(8,128)(2,1)} %shard_map.100), calls=%async_computation.2 | async-start | bytes 262144 | tf_op jit(solution)/shard_map/all_to_all | solution.py:655
  98.7 0.9 copy-done.11
  99.6 4.2 %shard_map.99 = (f32[136,256]{1,0:T(8,128)S(1)}, f32[136,256]{1,0:T(8,128)S(1)}, bf16[2,512,768]{2,1,0:T(8,128)(2,1)S(1)}, bf16[2,256,512]{2,1,0:T(8,128)(2,1)S(...) custom-call(s32[3]{0:T(128)S(1)} %pad_add_fusion.place.place_ref, ...), custom_call_target="tpu_custom_call" | custom-call | flops 3000000000 | tf_op jit(solution)/shard_map/pallas_call | solution.py:312
  103.9 1.1 copy-done
  105.0 1.2 copy-done.2
  106.2 1.0 copy-done.4
  107.2 0.8 copy-done.6
  108.0 0.8 copy-done.8
  108.8 0.7 copy-done.14
  109.5 0.6 copy-done.16
  110.1 1.4 copy-done.1
  111.5 1.0 copy-done.9
  112.6 0.9 copy-done.12
  113.5 0.9 copy-done.15
  114.4 0.9 copy-done.17
  115.4 2.1 %shard_map.101 = (bf16[128,256]{1,0:T(8,128)(2,1)S(1)}, bf16[3,128,256]{2,1,0:T(8,128)(2,1)S(1)}, bf16[2,256,256]{2,1,0:T(8,128)(2,1)S(1)}, bf16[2,256,256]{2,1,0:T(8,128)(2,1)S(1)}) custom-call(s32[3]{0:T(128)S(1)} %pad_add_fusion.place.place_ref, bf16[4,128,256]{2,1,0:T(8,128)(2,1)S(1)} %copy-done.12, f32[3,3,256]{2,1,0:T(4,128)S(1)} %bitcast.15, ...), custom_call_target="tpu_custom_call" | custom-call | flops 268435456 | tf_op jit(solution)/shard_map/pallas_call | solution.py:312
  117.4 1.9 %collective-permute-start.6 = (bf16[2,256,256]{2,1,0:T(8,128)(2,1)S(1)}, bf16[2,256,256]{2,1,0:T(8,128)(2,1)S(1)}, u32[]{:S(2)}, u32[]{:S(2)}) collective-permute-start(bf16[2,256,256]{2,1,0:T(8,128)(2,1)S(1)} %get-tuple-element.47), channel_id=1, source_target_pairs={{0,12},{4,0},{8,4},{12,8},{1,13},{5,1},{9,5},{13,9},{2,14},{6,2},{... | collective-permute-start | bytes 786440 | tf_op jit(solution)/shard_map/ppermute | solution.py:682
  119.4 3.9 %collective-permute-start.4 = (bf16[2,256,256]{2,1,0:T(8,128)(2,1)S(1)}, bf16[2,256,256]{2,1,0:T(8,128)(2,1)S(1)}, u32[]{:S(2)}, u32[]{:S(2)}) collective-permute-start(bf16[2,256,256]{2,1,0:T(8,128)(2,1)S(1)} %get-tuple-element.45), channel_id=1, source_target_pairs={{0,4},{4,8},{8,12},{12,0},{1,5},{5,9},{9,13},{13,1},{2,6},{6,10},{... | collective-permute-start | bytes 786440 | tf_op jit(solution)/shard_map/ppermute | solution.py:681
  123.3 1.3 shard_map.103
  124.7 2.5 %collective-permute-done.6.got = bf16[2,256,256]{2,1,0:T(8,128)(2,1)S(1)} collective-permute-done((bf16[2,256,256]{2,1,0:T(8,128)(2,1)S(1)}, bf16[2,256,256]{2,1,0:T(8,128)(2,1)S(1)}, u32[]{:S(2)}, u32[]{:S(2)}) %collective-permute-start.6) | collective-permute-done | bytes 262176 | tf_op jit(solution)/shard_map/ppermute | solution.py:682
  127.2 0.1 shard_map.105
  127.3 1.9 %collective-permute-start.7 = (bf16[4,256,256]{2,1,0:T(8,128)(2,1)S(1)}, bf16[4,256,256]{2,1,0:T(8,128)(2,1)S(1)}, u32[]{:S(2)}, u32[]{:S(2)}) collective-permute-start(bf16[4,256,256]{2,1,0:T(8,128)(2,1)S(1)} %shard_map.105), channel_id=1, source_target_pairs={{0,12},{4,0},{8,4},{12,8},{1,13},{5,1},{9,5},{13,9},{2,14},{6,2},{... | collective-permute-start | bytes 1572872 | tf_op jit(solution)/shard_map/ppermute | solution.py:696
  129.2 0.1 shard_map.104
  129.3 4.0 %collective-permute-start.5 = (bf16[4,256,256]{2,1,0:T(8,128)(2,1)S(1)}, bf16[4,256,256]{2,1,0:T(8,128)(2,1)S(1)}, u32[]{:S(2)}, u32[]{:S(2)}) collective-permute-start(bf16[4,256,256]{2,1,0:T(8,128)(2,1)S(1)} %shard_map.104), channel_id=1, source_target_pairs={{0,4},{4,8},{8,12},{12,0},{1,5},{5,9},{9,13},{13,1},{2,6},{6,10},{... | collective-permute-start | bytes 1572872 | tf_op jit(solution)/shard_map/ppermute | solution.py:694
  133.3 0.7 shard_map.102
  134.0 4.3 %collective-permute-done.7 = bf16[4,256,256]{2,1,0:T(8,128)(2,1)S(1)} collective-permute-done((bf16[4,256,256]{2,1,0:T(8,128)(2,1)S(1)}, bf16[4,256,256]{2,1,0:T(8,128)(2,1)S(1)}, u32[]{:S(2)}, u32[]{:S(2)}) %collective-permute-start.7) | collective-permute-done | bytes 524320 | tf_op jit(solution)/shard_map/ppermute | solution.py:696
  138.3 3.2 %collective-permute-done.5 = bf16[4,256,256]{2,1,0:T(8,128)(2,1)S(1)} collective-permute-done((bf16[4,256,256]{2,1,0:T(8,128)(2,1)S(1)}, bf16[4,256,256]{2,1,0:T(8,128)(2,1)S(1)}, u32[]{:S(2)}, u32[]{:S(2)}) %collective-permute-start.5) | collective-permute-done | bytes 524320 | tf_op jit(solution)/shard_map/ppermute | solution.py:694
  141.6 0.2 add_convert_fusion
  141.8 14.1 %all_to_all.22 = bf16[4,256,256]{2,1,0:T(8,128)(2,1)S(1)} all-to-all(bf16[4,256,256]{2,1,0:T(8,128)(2,1)S(1)} %add_convert_fusion), channel_id=1, replica_groups=mesh['y'=8,'zh'=4,'core'=2,'x'=4,'zl'=4] {'zl'}, dimensions={0} | all-to-all | bytes 1048576 | tf_op jit(solution)/shard_map/all_to_all | solution.py:708
  155.8 0.1 reduce_sum.12
  155.9 0.7 fusion
  (32 shorter events, 0.1 us)
Async XLA Ops:
  23.5 14.7 %collective-permute-start.1 = (bf16[4,256,256]{2,1,0:T(8,128)(2,1)S(1)}, bf16[4,256,256]{2,1,0:T(8,128)(2,1)S(1)}, u32[]{:S(2)}, u32[]{:S(2)}) collective-permute-start(bf16[4,256,256]{2,1,0:T(8,128)(2,1)S(1)} %all_to_all.20.piece), channel_id=1, source_target_pairs={{0,12},{4,0},{8,4},{12,8},{1,13},{5,1},{9,5},{13,9},{2,14},{6,2},{... | collective-permute-start | bytes 1572872 | tf_op jit(solution)/shard_map/ppermute | solution.py:570
  28.1 15.7 %collective-permute-start = (bf16[4,256,256]{2,1,0:T(8,128)(2,1)S(1)}, bf16[4,256,256]{2,1,0:T(8,128)(2,1)S(1)}, u32[]{:S(2)}, u32[]{:S(2)}) collective-permute-start(bf16[4,256,256]{2,1,0:T(8,128)(2,1)S(1)} %all_to_all.20.piece), channel_id=1, source_target_pairs={{0,4},{4,8},{8,12},{12,0},{1,5},{5,9},{9,13},{13,1},{2,6},{6,10},{... | collective-permute-start | bytes 1572872 | tf_op jit(solution)/shard_map/ppermute | solution.py:569
  38.2 15.1 %collective-permute-start.3 = (bf16[2,256,256]{2,1,0:T(8,128)(2,1)S(1)}, bf16[2,256,256]{2,1,0:T(8,128)(2,1)S(1)}, u32[]{:S(2)}, u32[]{:S(2)}) collective-permute-start(bf16[2,256,256]{2,1,0:T(8,128)(2,1)S(1)} %slice.12), channel_id=1, source_target_pairs={{0,12},{4,0},{8,4},{12,8},{1,13},{5,1},{9,5},{13,9},{2,14},{6,2},{... | collective-permute-start | bytes 786440 | tf_op jit(solution)/shard_map/ppermute | solution.py:595
  43.8 9.5 %collective-permute-start.2 = (bf16[2,256,256]{2,1,0:T(8,128)(2,1)S(1)}, bf16[2,256,256]{2,1,0:T(8,128)(2,1)S(1)}, u32[]{:S(2)}, u32[]{:S(2)}) collective-permute-start(bf16[2,256,256]{2,1,0:T(8,128)(2,1)S(1)} %slice.13), channel_id=1, source_target_pairs={{0,4},{4,8},{8,12},{12,0},{1,5},{5,9},{9,13},{13,1},{2,6},{6,10},{... | collective-permute-start | bytes 786440 | tf_op jit(solution)/shard_map/ppermute | solution.py:597
  45.8 7.6 %copy-start.13 = (f32[256,16]{0,1:T(8,128)S(1)}, f32[256,16]{0,1:T(8,128)}, u32[]{:S(2)}) copy-start(f32[256,16]{0,1:T(8,128)} %param.14) | copy-start | bytes 49156
  45.8 7.5 %copy-start.18 = (f32[3,256,3]{1,2,0:T(4,128)S(1)}, f32[3,256,3]{1,2,0:T(4,128)}, u32[]{:S(2)}) copy-start(f32[3,256,3]{1,2,0:T(4,128)} %param.12) | copy-start | bytes 27652
  53.3 45.3 %copy-start.19 = (f32[256,16]{0,1:T(8,128)S(1)}, f32[256,16]{0,1:T(8,128)}, u32[]{:S(2)}) copy-start(f32[256,16]{0,1:T(8,128)} %param.13) | copy-start | bytes 49156
  53.3 45.3 %copy-start.20 = (f32[256]{0:T(256)S(1)}, f32[256]{0:T(256)}, u32[]{:S(2)}) copy-start(f32[256]{0:T(256)} %param.15) | copy-start | bytes 3076
  54.9 0.7 copy-start.10
  91.1 19.0 %all-to-all-start.2 = ((bf16[8,32,256]{2,1,0:T(8,128)(2,1)}), bf16[8,32,256]{2,1,0:T(8,128)(2,1)S(1)}, u32[]{:S(2)}, u32[]{:S(2)}) async-start(bf16[8,32,256]{2,1,0:T(8,128)(2,1)} %shard_map.100), calls=%async_computation.2 | async-start | bytes 262144 | tf_op jit(solution)/shard_map/all_to_all | solution.py:655
  98.7 1.0 copy-start.11
  103.8 1.2 copy-start
  105.0 1.2 copy-start.2
  106.2 1.0 copy-start.4
  107.2 0.8 copy-start.6
  108.0 0.8 copy-start.8
  108.8 0.7 copy-start.14
  109.5 0.6 copy-start.16
  110.1 1.4 copy-start.1
  111.5 1.0 copy-start.9
  112.6 0.9 copy-start.12
  113.5 0.9 copy-start.15
  114.4 0.9 copy-start.17
  115.4 8.0 %copy-start.5 = (bf16[4,256,512]{2,1,0:T(8,128)(2,1)S(1)}, bf16[4,256,512]{2,1,0:T(8,128)(2,1)}, u32[]{:S(2)}) copy-start(bf16[4,256,512]{2,1,0:T(8,128)(2,1)} %copy-done.4) | copy-start | bytes 3145732
  117.4 9.7 %collective-permute-start.6 = (bf16[2,256,256]{2,1,0:T(8,128)(2,1)S(1)}, bf16[2,256,256]{2,1,0:T(8,128)(2,1)S(1)}, u32[]{:S(2)}, u32[]{:S(2)}) collective-permute-start(bf16[2,256,256]{2,1,0:T(8,128)(2,1)S(1)} %get-tuple-element.47), channel_id=1, source_target_pairs={{0,12},{4,0},{8,4},{12,8},{1,13},{5,1},{9,5},{13,9},{2,14},{6,2},{... | collective-permute-start | bytes 786440 | tf_op jit(solution)/shard_map/ppermute | solution.py:682
  119.4 9.8 %collective-permute-start.4 = (bf16[2,256,256]{2,1,0:T(8,128)(2,1)S(1)}, bf16[2,256,256]{2,1,0:T(8,128)(2,1)S(1)}, u32[]{:S(2)}, u32[]{:S(2)}) collective-permute-start(bf16[2,256,256]{2,1,0:T(8,128)(2,1)S(1)} %get-tuple-element.45), channel_id=1, source_target_pairs={{0,4},{4,8},{8,12},{12,0},{1,5},{5,9},{9,13},{13,1},{2,6},{6,10},{... | collective-permute-start | bytes 786440 | tf_op jit(solution)/shard_map/ppermute | solution.py:681
  124.6 8.6 %copy-start.3 = (bf16[2,512,768]{2,1,0:T(8,128)(2,1)S(1)}, bf16[2,512,768]{2,1,0:T(8,128)(2,1)}, u32[]{:S(2)}) copy-start(bf16[2,512,768]{2,1,0:T(8,128)(2,1)} %copy-done.2) | copy-start | bytes 4718596
  124.7 8.6 %copy-start.7 = (bf16[2,256,512]{2,1,0:T(8,128)(2,1)S(1)}, bf16[2,256,512]{2,1,0:T(8,128)(2,1)}, u32[]{:S(2)}) copy-start(bf16[2,256,512]{2,1,0:T(8,128)(2,1)} %copy-done.6) | copy-start | bytes 1572868
  127.3 11.1 %collective-permute-start.7 = (bf16[4,256,256]{2,1,0:T(8,128)(2,1)S(1)}, bf16[4,256,256]{2,1,0:T(8,128)(2,1)S(1)}, u32[]{:S(2)}, u32[]{:S(2)}) collective-permute-start(bf16[4,256,256]{2,1,0:T(8,128)(2,1)S(1)} %shard_map.105), channel_id=1, source_target_pairs={{0,12},{4,0},{8,4},{12,8},{1,13},{5,1},{9,5},{13,9},{2,14},{6,2},{... | collective-permute-start | bytes 1572872 | tf_op jit(solution)/shard_map/ppermute | solution.py:696
  129.3 12.3 %collective-permute-start.5 = (bf16[4,256,256]{2,1,0:T(8,128)(2,1)S(1)}, bf16[4,256,256]{2,1,0:T(8,128)(2,1)S(1)}, u32[]{:S(2)}, u32[]{:S(2)}) collective-permute-start(bf16[4,256,256]{2,1,0:T(8,128)(2,1)S(1)} %shard_map.104), channel_id=1, source_target_pairs={{0,4},{4,8},{8,12},{12,0},{1,5},{5,9},{9,13},{13,1},{2,6},{6,10},{... | collective-permute-start | bytes 1572872 | tf_op jit(solution)/shard_map/ppermute | solution.py:694

commit v13 on v11

--- a/solution.py
+++ b/solution.py
@@ -463,25 +463,35 @@
 
 
 def last_kernel(
-    sizes, place, proj, taps, rates, res, skip, conv, grad, near, far, weight_in, weight_out,
-    hidden, out, to_right, to_left, side_in, side_out, ext, feat, *held,
+    sizes, place, proj, taps, rates, res, skip, conv, grad, near, far, far_in, far_out,
+    weight_in, weight_out,
+    hidden, out, to_right, to_left, side_in, side_out, ext, feat, sems,
 ):
     n_x, n_zl = sizes["x"], sizes["zl"]
-    blocks, *side = [
-        [lax.rem(place[2] + k, n_x) * n_zl + j for j in range(0, n_zl, PAIR)]
-        for k in (2, 1, n_x - 1)
+    side = [
+        lax.rem(place[2] + k, n_x) * n_zl + j for k in (1, n_x - 1) for j in range(0, n_zl, PAIR)
     ]
-    side = side[0] + side[1]
-    weights = (weight_in, weight_out)
-    ready = load_weights(blocks, *weights, *held[:3], ahead=len(blocks))
-    ready_side = load_weights(side, *weights, side_in, side_out, held[3], ahead=len(side))
+    ready = load_weights(side, weight_in, weight_out, side_in, side_out, sems, ahead=len(side))
     finish_kernel(
         place, proj, taps, rates, res, skip, conv, grad, near, far, hidden, out, ext, feat
     )
-    partials(held, 0, to_right, hidden, out, ready)
-    partials(held, to_right.shape[0] // PAIR, to_left, hidden, out, ready)
+    held = (far_in, far_out)
+    partials(held, 0, to_right, hidden, out, at_once)
+    partials(held, to_right.shape[0] // PAIR, to_left, hidden, out, at_once)
     for s in range(len(side)):
-        ready_side(s)
+        ready(s)
+
+
+def local_fetch_kernel(
+    sizes, place, proj, taps, rates, res, skip, weight_in, weight_out,
+    conv, grad, far_in, far_out, ext, pad, filt, sems,
+):
+    n_x, n_zl = sizes["x"], sizes["zl"]
+    far = [lax.rem(place[2] + 2, n_x) * n_zl + j for j in range(0, n_zl, PAIR)]
+    ready = load_weights(far, weight_in, weight_out, far_in, far_out, sems, ahead=len(far))
+    local_kernel(proj, taps, rates, res, skip, conv, grad, ext, pad, filt)
+    for s in range(len(far)):
+        ready(s)
 
 
 def join_kernel(start, terms, got, out):
@@ -592,16 +602,24 @@
         far_out,
         flops=products(n_zl),
     )
-    conv, grad = call(
-        local_kernel,
-        [shape(rows, width), shape(rows, width)],
-        [ext, pltpu.VMEM((2, rows + TILE, width), F32), pltpu.VMEM((rows, width), F32)],
+    conv, grad, far_in, far_out = call(
+        functools.partial(local_fetch_kernel, sizes),
+        [shape(rows, width), shape(rows, width), *held_shapes],
+        [
+            ext,
+            pltpu.VMEM((2, rows + TILE, width), F32),
+            pltpu.VMEM((rows, width), F32),
+            pltpu.SemaphoreType.DMA((runs, 4)),
+        ],
+        place,
         proj,
         taps,
         rates,
         res,
         skip,
+        *weights,
         flops=3 * 10**9,
+        hbm=2,
     )
     near_states = lax.all_to_all(send, ("zh", "core"), 0, 0, tiled=True)
     send = call(
@@ -630,7 +648,6 @@
             *side_shapes,
         ],
         [ext, pltpu.VMEM((3, rows, width), F32)]
-        + held_weights(runs, part, width)
         + [pltpu.SemaphoreType.DMA((2 * runs, 4))],
         place,
         proj,
@@ -642,6 +659,8 @@
         grad,
         near_states,
         far_states,
+        far_in,
+        far_out,
         *weights,
         flops=products(n_zl),
         hbm=2,

time: 149 us -> 150 us (level)
  no operation moved by 1% of the time
where the time goes in v13:
time: 150 us; the launch traced here: 149 us
  blocking collectives  68.4 us (46%)
  starting transfers between devices  34.2 us (23%)
  Pallas kernels  23.3 us (16%)
  waiting for transfers between devices  21 us (14%)
    all_to_all x1, blocking collectives, shards(): near_states = lax.all_to_all(send, ('zh', 'core'), 0, 0, tiled=True)  34.2 us
    pallas_call x11, Pallas kernels, call(): pl.pallas_call(kernel, out_shape=outs, scratch_shapes=scratch, in_specs=s...  23.3 us
    all_to_all x1, blocking collectives, shards(): pieces = lax.all_to_all(copies, 'zl', 0, 0, tiled=True)  21.5 us
    all_to_all x1, blocking collectives, shards(): summed = lax.all_to_all(summed, 'zl', 0, 0, tiled=True)  12.7 us
    all_to_all x1, starting transfers between devices, shards(): far_states = lax.all_to_all(send, 'y', 0, 0, tiled=True)  7.1 us
    ppermute x1, starting transfers between devices, shards(): from_right = lax.ppermute(pieces, 'x', left)  6.22 us
    all_to_all x1, waiting for transfers between devices, shards(): far_states = lax.all_to_all(send, 'y', 0, 0, tiled=True)  5.24 us
    ppermute x1, starting transfers between devices, shards(): far_left = lax.ppermute(to_left, 'x', left)  5.16 us
  transfers between devices with their start and end apart: 9, of which 7 were waited for; matrix products, arithmetic and copies ran while one was open for 0% of the time, Pallas kernels for 10%

profile of v13, /device:TPU:2, one launch (start us, length us, event | category | flops | bytes accessed | tf_op | source)
XLA Modules:
  0.0 148.8 jit_solution(17172996170126680194)
XLA Ops:
  0.6 1.3 shard_map.95
  1.9 21.5 %all_to_all.20.piece = bf16[4,256,256]{2,1,0:T(8,128)(2,1)S(1)} all-to-all(bf16[4,256,256]{2,1,0:T(8,128)(2,1)S(1)} %shard_map.95), channel_id=1, replica_groups=mesh['y'=8,'zh'=4,'core'=2,'x'=4,'zl'=4] {'zl'}, dimensions={0} | all-to-all | bytes 1048576 | tf_op jit(solution)/shard_map/all_to_all | solution.py:546
  23.5 6.2 %collective-permute-start.2 = (bf16[4,256,256]{2,1,0:T(8,128)(2,1)S(1)}, bf16[4,256,256]{2,1,0:T(8,128)(2,1)S(1)}, u32[]{:S(2)}, u32[]{:S(2)}) collective-permute-start(bf16[4,256,256]{2,1,0:T(8,128)(2,1)S(1)} %all_to_all.20.piece), channel_id=1, source_target_pairs={{0,12},{4,0},{8,4},{12,8},{1,13},{5,1},{9,5},{13,9},{2,14},{6,2},{... | collective-permute-start | bytes 1572872 | tf_op jit(solution)/shard_map/ppermute | solution.py:555
  29.7 1.9 %collective-permute-start = (bf16[4,256,256]{2,1,0:T(8,128)(2,1)S(1)}, bf16[4,256,256]{2,1,0:T(8,128)(2,1)S(1)}, u32[]{:S(2)}, u32[]{:S(2)}) collective-permute-start(bf16[4,256,256]{2,1,0:T(8,128)(2,1)S(1)} %all_to_all.20.piece), channel_id=1, source_target_pairs={{0,4},{4,8},{8,12},{12,0},{1,5},{5,9},{9,13},{13,1},{2,6},{6,10},{... | collective-permute-start | bytes 1572872 | tf_op jit(solution)/shard_map/ppermute | solution.py:554
  31.6 0.1 pad_add_fusion.place.place_ref
  31.7 2.6 %shard_map.96.old = f32[4,128,256]{2,1,0:T(8,128)S(1)} custom-call(s32[3]{0:T(128)S(1)} %pad_add_fusion.place.place_ref, bf16[4,256,256]{2,1,0:T(8,128)(2,1)S(1)} %all_to_all.20.piece, bf16[3,4096,256]{2,1,0:T(8,128)(2,1)} %bitcast.20, bf16[256,4096]{1,0:T(8,128)(2,1)} %weight_out.9), custom_call_target="tpu_custom_call" | custom-call | flops 268435456 | tf_op jit(solution)/shard_map/pallas_call | solution.py:312
  34.3 3.6 %collective-permute-done.2.right = bf16[4,256,256]{2,1,0:T(8,128)(2,1)S(1)} collective-permute-done((bf16[4,256,256]{2,1,0:T(8,128)(2,1)S(1)}, bf16[4,256,256]{2,1,0:T(8,128)(2,1)S(1)}, u32[]{:S(2)}, u32[]{:S(2)}) %collective-permute-start.2) | collective-permute-done | bytes 524320 | tf_op jit(solution)/shard_map/ppermute | solution.py:555
  37.9 2.9 %collective-permute-start.3 = (bf16[2,256,256]{2,1,0:T(8,128)(2,1)S(1)}, bf16[2,256,256]{2,1,0:T(8,128)(2,1)S(1)}, u32[]{:S(2)}, u32[]{:S(2)}) collective-permute-start(bf16[2,256,256]{2,1,0:T(8,128)(2,1)S(1)} %slice.13), channel_id=1, source_target_pairs={{0,12},{4,0},{8,4},{12,8},{1,13},{5,1},{9,5},{13,9},{2,14},{6,2},{... | collective-permute-start | bytes 786440 | tf_op jit(solution)/shard_map/ppermute | solution.py:570
  40.8 0.3 collective-permute-done.left
  41.1 0.0 copy-start
  41.1 0.0 copy-start.1
  41.1 2.7 %collective-permute-start.1 = (bf16[2,256,256]{2,1,0:T(8,128)(2,1)S(1)}, bf16[2,256,256]{2,1,0:T(8,128)(2,1)S(1)}, u32[]{:S(2)}, u32[]{:S(2)}) collective-permute-start(bf16[2,256,256]{2,1,0:T(8,128)(2,1)S(1)} %slice.12), channel_id=1, source_target_pairs={{0,4},{4,8},{8,12},{12,0},{1,5},{5,9},{9,13},{13,1},{2,6},{6,10},{... | collective-permute-start | bytes 786440 | tf_op jit(solution)/shard_map/ppermute | solution.py:569
  43.8 4.5 %shard_map.97 = (f32[4,128,256]{2,1,0:T(8,128)S(1)}, bf16[2,512,768]{2,1,0:T(8,128)(2,1)S(1)}, bf16[2,256,512]{2,1,0:T(8,128)(2,1)S(1)}) custom-call(s32[3]{0:T(128)S(1)} %pad_add_fusion.place.place_ref, bf16[4,256,256]{2,1,0:T(8,128)(2,1)S(1)} %collective-permute-done.left, bf16[4,256,256]{2,1,0:T(8,128)(2,1)S(1)} %collective-permute-done.2.right, ...), custom_call_target="tpu_custom_call" | custom-call | flops 536870912 | tf_op jit(solution)/shard_map/pallas_call | solution.py:312
  48.3 0.0 collective-permute-done.3.right
  48.3 2.3 %collective-permute-done.1.left = bf16[2,256,256]{2,1,0:T(8,128)(2,1)S(1)} collective-permute-done((bf16[2,256,256]{2,1,0:T(8,128)(2,1)S(1)}, bf16[2,256,256]{2,1,0:T(8,128)(2,1)S(1)}, u32[]{:S(2)}, u32[]{:S(2)}) %collective-permute-start.1) | collective-permute-done | bytes 262176 | tf_op jit(solution)/shard_map/ppermute | solution.py:569
  50.6 0.0 copy-done
  50.6 0.0 copy-done.1
  50.6 0.0 copy-start.2
  50.6 0.0 copy-start.3
  50.6 1.5 %shard_map.98 = (bf16[4,128,256]{2,1,0:T(8,128)(2,1)S(1)}, bf16[8,48,256]{2,1,0:T(8,128)(2,1)S(1)}) custom-call(s32[3]{0:T(128)S(1)} %pad_add_fusion.place.place_ref, bf16[2,256,256]{2,1,0:T(8,128)(2,1)S(1)} %collective-permute-done.1.left, bf16[2,256,256]{2,1,0:T(8,128)(2,1)S(1)} %collective-permute-done.3.right, f32[4,128,256]{2,1,0:T(8,128)S(1)} %get-tuple-element.23.old, ...), custom_call_target="tpu_custom_call" | custom-call | flops 268435456 | tf_op jit(solution)/shard_map/pallas_call | solution.py:312
  52.2 34.2 %all_to_all.21.got_ref.near = bf16[8,48,256]{2,1,0:T(8,128)(2,1)S(1)} all-to-all(bf16[8,48,256]{2,1,0:T(8,128)(2,1)S(1)} %get-tuple-element.29), channel_id=1, replica_groups=mesh['y'=8,'zh'=4,'core'=2,'x'=4,'zl'=4] {'zh','core'}, dimensions={0} | all-to-all | bytes 393216 | tf_op jit(solution)/shard_map/all_to_all | solution.py:624
  86.3 1.3 shard_map.100
  87.7 7.1 %all-to-all-start.2 = ((bf16[8,32,256]{2,1,0:T(8,128)(2,1)}), bf16[8,32,256]{2,1,0:T(8,128)(2,1)S(1)}, u32[]{:S(2)}, u32[]{:S(2)}) async-start(bf16[8,32,256]{2,1,0:T(8,128)(2,1)} %shard_map.100), calls=%async_computation.2 | async-start | bytes 262144 | tf_op jit(solution)/shard_map/all_to_all | solution.py:634
  94.8 0.0 copy-done.2
  94.8 0.0 copy-done.3
  94.8 3.8 %shard_map.99 = (f32[136,256]{1,0:T(8,128)S(1)}, f32[136,256]{1,0:T(8,128)S(1)}, bf16[2,512,768]{2,1,0:T(8,128)(2,1)S(1)}, bf16[2,256,512]{2,1,0:T(8,128)(2,1)S(1)}) custom-call(s32[3]{0:T(128)S(1)} %pad_add_fusion.place.place_ref, bf16[4,128,256]{2,1,0:T(8,128)(2,1)S(1)} %get-tuple-element.26.proj, f32[3,3,256]{2,1,0:T(4,128)S(1)} %bitcast.14, ...), custom_call_target="tpu_custom_call" | custom-call | flops 3000000000 | tf_op jit(solution)/shard_map/pallas_call | solution.py:312
  98.6 5.2 %all-to-all-done.2.far = bf16[8,32,256]{2,1,0:T(8,128)(2,1)S(1)} async-done(((bf16[8,32,256]{2,1,0:T(8,128)(2,1)}), bf16[8,32,256]{2,1,0:T(8,128)(2,1)S(1)}, u32[]{:S(2)}, u32[]{:S(2)}) %all-to-all-start.2) | async-done | bytes 131104 | tf_op jit(solution)/shard_map/all_to_all | solution.py:634
  103.9 4.1 %shard_map.101 = (bf16[128,256]{1,0:T(8,128)(2,1)S(1)}, bf16[3,128,256]{2,1,0:T(8,128)(2,1)S(1)}, bf16[2,256,256]{2,1,0:T(8,128)(2,1)S(1)}, bf16[2,256,256]{2,1,...) custom-call(s32[3]{0:T(128)S(1)} %pad_add_fusion.place.place_ref, ...), custom_call_target="tpu_custom_call" | custom-call | flops 268435456 | tf_op jit(solution)/shard_map/pallas_call | solution.py:312
  108.0 5.2 %collective-permute-start.6 = (bf16[2,256,256]{2,1,0:T(8,128)(2,1)S(1)}, bf16[2,256,256]{2,1,0:T(8,128)(2,1)S(1)}, u32[]{:S(2)}, u32[]{:S(2)}) collective-permute-start(bf16[2,256,256]{2,1,0:T(8,128)(2,1)S(1)} %get-tuple-element.39), channel_id=1, source_target_pairs={{0,12},{4,0},{8,4},{12,8},{1,13},{5,1},{9,5},{13,9},{2,14},{6,2},{... | collective-permute-start | bytes 786440 | tf_op jit(solution)/shard_map/ppermute | solution.py:669
  113.2 1.9 %collective-permute-start.4 = (bf16[2,256,256]{2,1,0:T(8,128)(2,1)S(1)}, bf16[2,256,256]{2,1,0:T(8,128)(2,1)S(1)}, u32[]{:S(2)}, u32[]{:S(2)}) collective-permute-start(bf16[2,256,256]{2,1,0:T(8,128)(2,1)S(1)} %get-tuple-element.37), channel_id=1, source_target_pairs={{0,4},{4,8},{8,12},{12,0},{1,5},{5,9},{9,13},{13,1},{2,6},{6,10},{... | collective-permute-start | bytes 786440 | tf_op jit(solution)/shard_map/ppermute | solution.py:668
  115.1 1.3 shard_map.103
  116.4 3.1 %collective-permute-done.6.got = bf16[2,256,256]{2,1,0:T(8,128)(2,1)S(1)} collective-permute-done((bf16[2,256,256]{2,1,0:T(8,128)(2,1)S(1)}, bf16[2,256,256]{2,1,0:T(8,128)(2,1)S(1)}, u32[]{:S(2)}, u32[]{:S(2)}) %collective-permute-start.6) | collective-permute-done | bytes 262176 | tf_op jit(solution)/shard_map/ppermute | solution.py:669
  119.5 0.1 shard_map.105
  119.6 4.4 %collective-permute-start.7 = (bf16[4,256,256]{2,1,0:T(8,128)(2,1)S(1)}, bf16[4,256,256]{2,1,0:T(8,128)(2,1)S(1)}, u32[]{:S(2)}, u32[]{:S(2)}) collective-permute-start(bf16[4,256,256]{2,1,0:T(8,128)(2,1)S(1)} %shard_map.105), channel_id=1, source_target_pairs={{0,12},{4,0},{8,4},{12,8},{1,13},{5,1},{9,5},{13,9},{2,14},{6,2},{... | collective-permute-start | bytes 1572872 | tf_op jit(solution)/shard_map/ppermute | solution.py:683
  124.0 0.0 collective-permute-done.4.got
  124.0 0.1 shard_map.104
  124.1 1.9 %collective-permute-start.5 = (bf16[4,256,256]{2,1,0:T(8,128)(2,1)S(1)}, bf16[4,256,256]{2,1,0:T(8,128)(2,1)S(1)}, u32[]{:S(2)}, u32[]{:S(2)}) collective-permute-start(bf16[4,256,256]{2,1,0:T(8,128)(2,1)S(1)} %shard_map.104), channel_id=1, source_target_pairs={{0,4},{4,8},{8,12},{12,0},{1,5},{5,9},{9,13},{13,1},{2,6},{6,10},{... | collective-permute-start | bytes 1572872 | tf_op jit(solution)/shard_map/ppermute | solution.py:681
  126.0 2.7 %shard_map.102 = bf16[4,256,256]{2,1,0:T(8,128)(2,1)S(1)} custom-call(s32[3]{0:T(128)S(1)} %pad_add_fusion.place.place_ref, bf16[128,256]{1,0:T(8,128)(2,1)S(1)} %get-tuple-element.32.hidden, bf16[3,128,256]{2,1,0:T(8,128)(2,1)S(1)} %get-tuple-element.33.grad, bf16[3,4096,256]{2,1,0:T(8,128)(2,1)} %bitcast.24, bf16[256,4096]{1,0:T(8,128)(2,1)} %weight_out.9), custom_call_target="tpu_custom_call" | custom-call | flops 268435456 | tf_op jit(solution)/shard_map/pallas_call | solution.py:312
  128.7 2.0 %collective-permute-done.7 = bf16[4,256,256]{2,1,0:T(8,128)(2,1)S(1)} collective-permute-done((bf16[4,256,256]{2,1,0:T(8,128)(2,1)S(1)}, bf16[4,256,256]{2,1,0:T(8,128)(2,1)S(1)}, u32[]{:S(2)}, u32[]{:S(2)}) %collective-permute-start.7) | collective-permute-done | bytes 524320 | tf_op jit(solution)/shard_map/ppermute | solution.py:683
  130.7 4.5 %collective-permute-done.5 = bf16[4,256,256]{2,1,0:T(8,128)(2,1)S(1)} collective-permute-done((bf16[4,256,256]{2,1,0:T(8,128)(2,1)S(1)}, bf16[4,256,256]{2,1,0:T(8,128)(2,1)S(1)}, u32[]{:S(2)}, u32[]{:S(2)}) %collective-permute-start.5) | collective-permute-done | bytes 524320 | tf_op jit(solution)/shard_map/ppermute | solution.py:681
  135.2 0.2 add_convert_fusion
  135.4 12.7 %all_to_all.22 = bf16[4,256,256]{2,1,0:T(8,128)(2,1)S(1)} all-to-all(bf16[4,256,256]{2,1,0:T(8,128)(2,1)S(1)} %add_convert_fusion), channel_id=1, replica_groups=mesh['y'=8,'zh'=4,'core'=2,'x'=4,'zl'=4] {'zl'}, dimensions={0} | all-to-all | bytes 1048576 | tf_op jit(solution)/shard_map/all_to_all | solution.py:696
  148.1 0.1 reduce_sum.12
  148.2 0.7 fusion
  (2 shorter events, 0.0 us)
Async XLA Ops:
  23.5 14.4 %collective-permute-start.2 = (bf16[4,256,256]{2,1,0:T(8,128)(2,1)S(1)}, bf16[4,256,256]{2,1,0:T(8,128)(2,1)S(1)}, u32[]{:S(2)}, u32[]{:S(2)}) collective-permute-start(bf16[4,256,256]{2,1,0:T(8,128)(2,1)S(1)} %all_to_all.20.piece), channel_id=1, source_target_pairs={{0,12},{4,0},{8,4},{12,8},{1,13},{5,1},{9,5},{13,9},{2,14},{6,2},{... | collective-permute-start | bytes 1572872 | tf_op jit(solution)/shard_map/ppermute | solution.py:555
  29.7 11.4 %collective-permute-start = (bf16[4,256,256]{2,1,0:T(8,128)(2,1)S(1)}, bf16[4,256,256]{2,1,0:T(8,128)(2,1)S(1)}, u32[]{:S(2)}, u32[]{:S(2)}) collective-permute-start(bf16[4,256,256]{2,1,0:T(8,128)(2,1)S(1)} %all_to_all.20.piece), channel_id=1, source_target_pairs={{0,4},{4,8},{8,12},{12,0},{1,5},{5,9},{9,13},{13,1},{2,6},{6,10},{... | collective-permute-start | bytes 1572872 | tf_op jit(solution)/shard_map/ppermute | solution.py:554
  37.9 10.4 %collective-permute-start.3 = (bf16[2,256,256]{2,1,0:T(8,128)(2,1)S(1)}, bf16[2,256,256]{2,1,0:T(8,128)(2,1)S(1)}, u32[]{:S(2)}, u32[]{:S(2)}) collective-permute-start(bf16[2,256,256]{2,1,0:T(8,128)(2,1)S(1)} %slice.13), channel_id=1, source_target_pairs={{0,12},{4,0},{8,4},{12,8},{1,13},{5,1},{9,5},{13,9},{2,14},{6,2},{... | collective-permute-start | bytes 786440 | tf_op jit(solution)/shard_map/ppermute | solution.py:570
  41.1 9.5 %copy-start = (f32[256,16]{0,1:T(8,128)S(1)}, f32[256,16]{0,1:T(8,128)}, u32[]{:S(2)}) copy-start(f32[256,16]{0,1:T(8,128)} %param.14) | copy-start | bytes 49156
  41.1 9.5 %copy-start.1 = (f32[3,256,3]{1,2,0:T(4,128)S(1)}, f32[3,256,3]{1,2,0:T(4,128)}, u32[]{:S(2)}) copy-start(f32[3,256,3]{1,2,0:T(4,128)} %param.12) | copy-start | bytes 27652
  41.1 9.5 %collective-permute-start.1 = (bf16[2,256,256]{2,1,0:T(8,128)(2,1)S(1)}, bf16[2,256,256]{2,1,0:T(8,128)(2,1)S(1)}, u32[]{:S(2)}, u32[]{:S(2)}) collective-permute-start(bf16[2,256,256]{2,1,0:T(8,128)(2,1)S(1)} %slice.12), channel_id=1, source_target_pairs={{0,4},{4,8},{8,12},{12,0},{1,5},{5,9},{9,13},{13,1},{2,6},{6,10},{... | collective-permute-start | bytes 786440 | tf_op jit(solution)/shard_map/ppermute | solution.py:569
  50.6 44.2 %copy-start.2 = (f32[256,16]{0,1:T(8,128)S(1)}, f32[256,16]{0,1:T(8,128)}, u32[]{:S(2)}) copy-start(f32[256,16]{0,1:T(8,128)} %param.13) | copy-start | bytes 49156
  50.6 44.2 %copy-start.3 = (f32[256]{0:T(256)S(1)}, f32[256]{0:T(256)}, u32[]{:S(2)}) copy-start(f32[256]{0:T(256)} %param.15) | copy-start | bytes 3076
  87.7 16.2 %all-to-all-start.2 = ((bf16[8,32,256]{2,1,0:T(8,128)(2,1)}), bf16[8,32,256]{2,1,0:T(8,128)(2,1)S(1)}, u32[]{:S(2)}, u32[]{:S(2)}) async-start(bf16[8,32,256]{2,1,0:T(8,128)(2,1)} %shard_map.100), calls=%async_computation.2 | async-start | bytes 262144 | tf_op jit(solution)/shard_map/all_to_all | solution.py:634
  108.0 11.5 %collective-permute-start.6 = (bf16[2,256,256]{2,1,0:T(8,128)(2,1)S(1)}, bf16[2,256,256]{2,1,0:T(8,128)(2,1)S(1)}, u32[]{:S(2)}, u32[]{:S(2)}) collective-permute-start(bf16[2,256,256]{2,1,0:T(8,128)(2,1)S(1)} %get-tuple-element.39), channel_id=1, source_target_pairs={{0,12},{4,0},{8,4},{12,8},{1,13},{5,1},{9,5},{13,9},{2,14},{6,2},{... | collective-permute-start | bytes 786440 | tf_op jit(solution)/shard_map/ppermute | solution.py:669
  113.2 10.9 %collective-permute-start.4 = (bf16[2,256,256]{2,1,0:T(8,128)(2,1)S(1)}, bf16[2,256,256]{2,1,0:T(8,128)(2,1)S(1)}, u32[]{:S(2)}, u32[]{:S(2)}) collective-permute-start(bf16[2,256,256]{2,1,0:T(8,128)(2,1)S(1)} %get-tuple-element.37), channel_id=1, source_target_pairs={{0,4},{4,8},{8,12},{12,0},{1,5},{5,9},{9,13},{13,1},{2,6},{6,10},{... | collective-permute-start | bytes 786440 | tf_op jit(solution)/shard_map/ppermute | solution.py:668
  119.6 11.1 %collective-permute-start.7 = (bf16[4,256,256]{2,1,0:T(8,128)(2,1)S(1)}, bf16[4,256,256]{2,1,0:T(8,128)(2,1)S(1)}, u32[]{:S(2)}, u32[]{:S(2)}) collective-permute-start(bf16[4,256,256]{2,1,0:T(8,128)(2,1)S(1)} %shard_map.105), channel_id=1, source_target_pairs={{0,12},{4,0},{8,4},{12,8},{1,13},{5,1},{9,5},{13,9},{2,14},{6,2},{... | collective-permute-start | bytes 1572872 | tf_op jit(solution)/shard_map/ppermute | solution.py:683
  124.1 11.1 %collective-permute-start.5 = (bf16[4,256,256]{2,1,0:T(8,128)(2,1)S(1)}, bf16[4,256,256]{2,1,0:T(8,128)(2,1)S(1)}, u32[]{:S(2)}, u32[]{:S(2)}) collective-permute-start(bf16[4,256,256]{2,1,0:T(8,128)(2,1)S(1)} %shard_map.104), channel_id=1, source_target_pairs={{0,4},{4,8},{8,12},{12,0},{1,5},{5,9},{9,13},{13,1},{2,6},{6,10},{... | collective-permute-start | bytes 1572872 | tf_op jit(solution)/shard_map/ppermute | solution.py:681
